TPU v7x, 32 devices: a whole 2x2x4 slice. The times are simulated.
32 devices in a mesh: section: 2 (over core), head: 16 (over z, y, x).
Axes of the slice: x: 2, y: 2, z: 4, core: 2. Of those that a mesh axis runs over, the one named last changes fastest.
Arguments:
- inputs: bfloat16 [2, 1024, 2048], P(None, 'head'), may hold values from -6 to 6
- cotangent: bfloat16 [2, 1024, 2048], P(None, 'head'), may hold values from -6 to 6
- valid_lengths: int32 [2, 4], replicated, may hold values from 0 to 1024, as said below
- proj_in: float32 [2, 2048, 8256], P('section', None, 'head'), may hold values from -0.125 to 0.125
- proj_in_m: float32 [2, 2048, 8256], P('section', None, 'head'), may hold values from -1.2 to 1.2
- proj_in_v: float32 [2, 2048, 8256], P('section', None, 'head'), may hold values from 0.04 to 0.16
- proj_state: float32 [2, 2048, 256], P('section'), may hold values from -0.125 to 0.125
- proj_state_m: float32 [2, 2048, 256], P('section'), may hold values from -1.2 to 1.2
- proj_state_v: float32 [2, 2048, 256], P('section'), may hold values from 0.04 to 0.16
- proj_out: float32 [2, 4096, 2048], P('section', 'head'), may hold values from -0.09375 to 0.09375
- proj_out_m: float32 [2, 4096, 2048], P('section', 'head'), may hold values from -1.2 to 1.2
- proj_out_v: float32 [2, 4096, 2048], P('section', 'head'), may hold values from 0.04 to 0.16
- head_params: float32 [2, 64, 387], P('section', 'head')
- head_m: float32 [2, 64, 387], P('section', 'head'), may hold values from -2.4 to 2.4
- head_v: float32 [2, 64, 387], P('section', 'head'), may hold values from 0.16 to 0.64
- shared_params: float32 [2, 3328], P('section')
- shared_m: float32 [2, 3328], P('section'), may hold values from -2.4 to 2.4
- shared_v: float32 [2, 3328], P('section'), may hold values from 0.16 to 0.64
Outputs:
- layer_outputs: bfloat16 [2, 2, 1024, 2048], P('section', None, 'head')
- input_grads: float32 [2, 2, 1024, 2048], P('section', None, 'head')
- grad_norm: float32 [], replicated
- proj_in_new: float32 [2, 2048, 8256], P('section', None, 'head')
- proj_in_m_new: float32 [2, 2048, 8256], P('section', None, 'head')
- proj_in_v_new: float32 [2, 2048, 8256], P('section', None, 'head')
- proj_in_low: bfloat16 [2, 2048, 8256], P('section', None, 'head')
- proj_state_new: float32 [2, 2048, 256], P('section')
- proj_state_m_new: float32 [2, 2048, 256], P('section')
- proj_state_v_new: float32 [2, 2048, 256], P('section')
- proj_state_low: bfloat16 [2, 2048, 256], P('section')
- proj_out_new: float32 [2, 4096, 2048], P('section', 'head')
- proj_out_m_new: float32 [2, 4096, 2048], P('section', 'head')
- proj_out_v_new: float32 [2, 4096, 2048], P('section', 'head')
- proj_out_low: bfloat16 [2, 4096, 2048], P('section', 'head')
- head_new: float32 [2, 64, 387], P('section', 'head')
- head_m_new: float32 [2, 64, 387], P('section', 'head')
- head_v_new: float32 [2, 64, 387], P('section', 'head')
- shared_new: float32 [2, 3328], P('section')
- shared_m_new: float32 [2, 3328], P('section')
- shared_v_new: float32 [2, 3328], P('section')
Inputs may be any that keep to these rules, and one draw needn't show every extreme that they name: `valid_lengths`: entry c of a micro-batch's row is nonzero exactly where a sequence's padded span begins at block c; block 0 always begins one; a span runs to the next beginning or to the micro-batch's end. Outside the last micro-batch every span holds 1024 tokens or more and its valid length exceeds its span minus 256; the last micro-batch holds one sequence of 1024 valid tokens.
All inputs are finite; a program needn't handle non-finite values.
Results may differ from a plain program's by a relative error of at most 0.023.
The roundings to bfloat16 on the way count: a program that leaves them out, or rounds other values in their place, can miss the bound.
Values may be sent and summed in bfloat16 or wider, within the bound.
A program may use at most 384 MiB of HBM per device.

v0:
```python
import jax
import jax.numpy as jnp
from jax import lax
from jax.sharding import PartitionSpec as P

HEADS = 64
HDIM = 64
NSTATE = 128
CONV = 4
STRETCH = 256
ADAM_STEP = 5
PARAMS = 51698560


HIGH = lax.Precision.HIGHEST
EPS_NORM = 1e-05
ADAM_EPS = 1e-08
BETA_ONE = 0.5
BETA_TWO = 0.5
CLIP_COEF = 0.2
LEARN_MATRIX = 0.02
LEARN_VECTOR = 0.2
WEIGHT_DECAY = 0.1


def shifted_2(value, axis, steps):
    count = lax.axis_size(axis)
    initial, last = (max(0, -steps), min(count, count - steps))
    return lax.ppermute(value, axis, [(source, source + steps) for source in range(initial, last)])


def seq_layout(lengths_row):
    block_count = lengths_row.shape[0]
    block_idx = jnp.arange(block_count, dtype=jnp.int32)
    starts = lengths_row > 0
    start_block = lax.cummax(jnp.where(starts, block_idx, 0), axis=0)
    owner_mask = (start_block[:, None] == block_idx[None, :]).astype(jnp.int32)
    seq_length = jnp.sum(owner_mask * lengths_row[None, :], axis=1)
    token_idx = jnp.arange(block_count * STRETCH, dtype=jnp.int32)
    position = token_idx - jnp.repeat(start_block, STRETCH) * STRETCH
    live_mask = (position < jnp.repeat(seq_length, STRETCH)).astype(jnp.float32)
    return (position, live_mask, starts.astype(jnp.float32))


def causal_conv(values, conv_taps, conv_bias, position):
    running = conv_bias + conv_taps[0] * values
    for offset in range(1, CONV):
        pad_rows = jnp.zeros((offset,) + values.shape[1:], jnp.float32)
        shifted = jnp.concatenate([pad_rows, values[:-offset]], axis=0)
        in_seq = (position >= offset).astype(jnp.float32).reshape((-1,) + (1,) * (values.ndim - 1))
        running = running + conv_taps[offset] * shifted * in_seq
    return running


def block_scan(inner_act, step_size, decay_rate, writer, reader, resets):
    token_count, head_count, width = inner_act.shape
    blocks = token_count // STRETCH

    def advance(carry_state, pieces):
        block_inner, block_step, block_writer, block_reader, block_reset = pieces
        carry_state = carry_state * (1.0 - block_reset)
        log_decay = jnp.cumsum(block_step * decay_rate[None, :], axis=0)
        intersection = jnp.dot(block_reader, block_writer.T, precision=HIGH)
        causal_mask = jnp.arange(STRETCH)[:, None] >= jnp.arange(STRETCH)[None, :]
        log_gap = log_decay[:, None, :] - log_decay[None, :, :]
        decays = jnp.exp(jnp.where(causal_mask[:, :, None], log_gap, -jnp.inf))
        block_weights = intersection[:, :, None] * decays * block_step[None, :, :]
        within = jnp.einsum("ijh,jhp->ihp", block_weights, block_inner, precision=HIGH)
        carried = jnp.exp(log_decay)[:, :, None] * jnp.einsum(
            "in,hpn->ihp", block_reader, carry_state, precision=HIGH
        )
        tail_weight = jnp.exp(log_decay[-1][None, :] - log_decay) * block_step
        added_state = jnp.einsum(
            "jh,jhp,jn->hpn", tail_weight, block_inner, block_writer, precision=HIGH
        )
        new_state = jnp.exp(log_decay[-1])[:, None, None] * carry_state + added_state
        return (new_state, within + carried)

    start_state = jnp.zeros((head_count, width, NSTATE), jnp.float32)
    pieces = (
        inner_act.reshape(blocks, STRETCH, head_count, width),
        step_size.reshape(blocks, STRETCH, head_count),
        writer.reshape(blocks, STRETCH, NSTATE),
        reader.reshape(blocks, STRETCH, NSTATE),
        resets,
    )
    final_state, outputs = lax.scan(jax.checkpoint(advance), start_state, pieces)
    return outputs.reshape(token_count, head_count, width)


def mixer_core(projected, state_raw, head_part, shared_conv, position, resets):
    token_count = projected.shape[0]
    head_count = head_part.shape[0]
    columns = projected.reshape(token_count, head_count, 2 * HDIM + 1)
    gate_raw = columns[:, :, :HDIM]
    inner_raw = columns[:, :, HDIM : 2 * HDIM]
    step_raw = columns[:, :, 2 * HDIM]
    conv_taps = head_part[:, : CONV * HDIM].reshape(head_count, CONV, HDIM).transpose(1, 0, 2)
    conv_bias = head_part[:, (CONV + 1) * HDIM : (CONV + 2) * HDIM]
    step_bias = head_part[:, -3]
    decay_log = head_part[:, -2]
    skip_gain = head_part[:, -1]
    inner_act = jax.nn.silu(causal_conv(inner_raw, conv_taps, conv_bias, position))
    state_taps = shared_conv[: CONV * 2 * NSTATE].reshape(CONV, 2 * NSTATE)
    state_bias = shared_conv[CONV * 2 * NSTATE :]
    state_in = jax.nn.silu(causal_conv(state_raw, state_taps, state_bias, position))
    step_size = jax.nn.softplus(step_raw + step_bias[None, :])
    decay_rate = -jnp.exp(decay_log)
    scanned = block_scan(
        inner_act, step_size, decay_rate, state_in[:, :NSTATE], state_in[:, NSTATE:], resets
    )
    mixed_out = scanned + skip_gain[None, :, None] * inner_act
    gated_out = (mixed_out * jax.nn.silu(gate_raw)).reshape(token_count, head_count * HDIM)
    squares = jnp.sum(gated_out * gated_out, axis=1)
    return (gated_out, squares)


def input_norm(residual, in_gain):
    return (
        residual
        * lax.rsqrt(jnp.mean(residual * residual, axis=1, keepdims=True) + EPS_NORM)
        * in_gain
    )


def output_norm(gated_out, squares, out_gain):
    return gated_out * lax.rsqrt(squares / (HEADS * HDIM) + EPS_NORM)[:, None] * out_gain


def row_product(left_rows, right_matrix):
    return jnp.dot(left_rows, right_matrix, preferred_element_type=jnp.float32)


def row_product_back(left_rows, right_matrix):
    return jnp.einsum("tk,dk->td", left_rows, right_matrix, preferred_element_type=jnp.float32)


def select_micro(buffer, micro_pick):
    return lax.dynamic_index_in_dim(buffer, micro_pick, 0, keepdims=False)


def store_micro(buffer, micro_pick, live_now, value):
    previous = select_micro(buffer, micro_pick)
    return lax.dynamic_update_index_in_dim(
        buffer, jnp.where(live_now, value, previous), micro_pick, 0
    )


def adam_update(weight, moment, second, gradient, rate, decay):
    moment_new = BETA_ONE * moment + (1.0 - BETA_ONE) * gradient
    second_new = BETA_TWO * second + (1.0 - BETA_TWO) * gradient * gradient
    corrected = moment_new / (1.0 - BETA_ONE**ADAM_STEP)
    corrected_sq = second_new / (1.0 - BETA_TWO**ADAM_STEP)
    weight_new = weight - rate * (corrected / (jnp.sqrt(corrected_sq) + ADAM_EPS) + decay * weight)
    return (weight_new, moment_new, second_new)


def shards(
    inputs,
    cotangent,
    valid_lengths,
    proj_in,
    proj_in_m,
    proj_in_v,
    proj_state,
    proj_state_m,
    proj_state_v,
    proj_out,
    proj_out_m,
    proj_out_v,
    head_params,
    head_m,
    head_v,
    shared_params,
    shared_m,
    shared_v,
):
    section_idx = lax.axis_index("section")
    head_idx = lax.axis_index("head")
    micro_count = inputs.shape[0]
    shard_rows = inputs.shape[1]
    model_width = inputs.shape[2]
    row_start = head_idx * shard_rows
    weight_in = proj_in[0]
    weight_state = proj_state[0]
    weight_out = proj_out[0]
    head_part = head_params[0]
    shared_part = shared_params[0]
    low_in = weight_in.astype(jnp.bfloat16)
    low_state = weight_state.astype(jnp.bfloat16)
    low_out = weight_out.astype(jnp.bfloat16)
    conv_length = 2 * CONV * NSTATE + 2 * NSTATE
    shared_conv = shared_part[:conv_length]
    in_gain = shared_part[conv_length:]
    out_gain = head_part[:, CONV * HDIM : (CONV + 1) * HDIM].reshape(-1)
    positions, live_masks, reset_rows = jax.vmap(seq_layout)(valid_lengths)
    token_count = positions.shape[1]
    keep_res = jnp.zeros((micro_count, shard_rows, model_width), jnp.float32)
    keep_proj = jnp.zeros((micro_count, token_count, weight_in.shape[1]), jnp.float32)
    keep_state = jnp.zeros((micro_count, token_count, weight_state.shape[1]), jnp.float32)
    keep_squares = jnp.zeros((micro_count, token_count), jnp.float32)
    layer_outs = jnp.zeros((micro_count, shard_rows, model_width), jnp.bfloat16)
    keep_rows = jnp.zeros((micro_count, token_count, model_width), jnp.bfloat16)
    received = jnp.zeros((shard_rows, model_width), jnp.bfloat16)
    for tick_idx in range(micro_count + 1):
        micro_now = tick_idx - section_idx
        live_now = (micro_now >= 0) & (micro_now < micro_count)
        micro_pick = jnp.clip(micro_now, 0, micro_count - 1)
        position = select_micro(positions, micro_pick)
        live_mask = select_micro(live_masks, micro_pick)
        resets = select_micro(reset_rows, micro_pick)
        fed = select_micro(inputs, micro_pick)
        residual = jnp.where(section_idx == 0, fed, received).astype(jnp.float32)
        normed_rows = input_norm(residual, in_gain).astype(jnp.bfloat16)
        state_own = jnp.dot(normed_rows, low_state, preferred_element_type=jnp.float32).astype(
            jnp.bfloat16
        )
        gathered, state_low = (
            lax.all_gather(normed_rows, "head", axis=0, tiled=True),
            lax.all_gather(state_own, "head", axis=0, tiled=True),
        )
        projected = jnp.dot(gathered, low_in, preferred_element_type=jnp.float32)
        state_raw = state_low.astype(jnp.float32)
        gated_out, squares = mixer_core(
            projected, state_raw, head_part, shared_conv, position, resets
        )
        squares = lax.psum(squares, "head")
        scaled = output_norm(gated_out, squares, out_gain).astype(jnp.bfloat16)
        branch = lax.psum_scatter(
            row_product(scaled, low_out), "head", scatter_dimension=0, tiled=True
        )
        live_rows = lax.dynamic_slice_in_dim(live_mask, row_start, shard_rows)
        layer_out = (residual + live_rows[:, None] * branch).astype(jnp.bfloat16)
        keep_res = store_micro(keep_res, micro_pick, live_now, residual)
        keep_proj = store_micro(keep_proj, micro_pick, live_now, projected)
        keep_state = store_micro(keep_state, micro_pick, live_now, state_raw)
        keep_squares = store_micro(keep_squares, micro_pick, live_now, squares)
        layer_outs = store_micro(layer_outs, micro_pick, live_now, layer_out)
        keep_rows = store_micro(keep_rows, micro_pick, live_now, gathered)
        received = shifted_2(layer_out, "section", 1)
    acc_in_w = jnp.zeros_like(weight_in)
    acc_state_w = jnp.zeros_like(weight_state)
    acc_out_w = jnp.zeros_like(weight_out)
    acc_head = jnp.zeros_like(head_part)
    acc_shared = jnp.zeros_like(shared_part)
    grad_buffer = jnp.zeros((micro_count, shard_rows, model_width), jnp.float32)
    returned = jnp.zeros((shard_rows, model_width), jnp.bfloat16)
    for tick_idx in range(micro_count + 1):
        micro_now = tick_idx - (1 - section_idx)
        live_now = (micro_now >= 0) & (micro_now < micro_count)
        live_scale = live_now.astype(jnp.float32)
        micro_pick = jnp.clip(micro_now, 0, micro_count - 1)
        position = select_micro(positions, micro_pick)
        live_mask = select_micro(live_masks, micro_pick)
        resets = select_micro(reset_rows, micro_pick)
        upstream = jnp.where(
            section_idx == 1, select_micro(cotangent, micro_pick), returned
        ).astype(jnp.float32)
        residual = select_micro(keep_res, micro_pick)
        projected = select_micro(keep_proj, micro_pick)
        state_raw = select_micro(keep_state, micro_pick)
        squares = select_micro(keep_squares, micro_pick)
        own_normed = input_norm(residual, in_gain).astype(jnp.bfloat16)
        gathered = select_micro(keep_rows, micro_pick)
        live_rows = lax.dynamic_slice_in_dim(live_mask, row_start, shard_rows)
        out_grad = (live_rows[:, None] * upstream).astype(jnp.bfloat16)
        grad_full = lax.all_gather(out_grad, "head", axis=0, tiled=True)

        def core_apply(proj_arg, state_arg, head_arg, conv_arg):
            return mixer_core(proj_arg, state_arg, head_arg, conv_arg, position, resets)

        core_result, core_pull = jax.vjp(core_apply, projected, state_raw, head_part, shared_conv)
        normed_out, norm_pull = jax.vjp(output_norm, core_result[0], squares, out_gain)
        scaled = normed_out.astype(jnp.bfloat16)
        grad_out_w = jnp.einsum("tk,td->kd", scaled, grad_full, preferred_element_type=jnp.float32)
        grad_scaled = jnp.einsum(
            "td,kd->tk", grad_full, low_out, preferred_element_type=jnp.float32
        )
        grad_gated, grad_squares, grad_out_gain = norm_pull(grad_scaled)
        grad_squares = lax.psum(grad_squares, "head")
        grad_proj, grad_state_raw, grad_head, grad_conv = core_pull((grad_gated, grad_squares))
        own_state_grad = lax.psum_scatter(
            grad_state_raw, "head", scatter_dimension=0, tiled=True
        ).astype(jnp.bfloat16)
        low_grad_proj = grad_proj.astype(jnp.bfloat16)
        grad_in_w = jnp.einsum(
            "td,tk->dk", gathered, low_grad_proj, preferred_element_type=jnp.float32
        )
        grad_state_w = jnp.einsum(
            "td,tk->dk", own_normed, own_state_grad, preferred_element_type=jnp.float32
        )
        grad_normed = lax.psum_scatter(
            row_product_back(low_grad_proj, low_in), "head", scatter_dimension=0, tiled=True
        )
        grad_normed = grad_normed + jnp.einsum(
            "tk,dk->td", own_state_grad, low_state, preferred_element_type=jnp.float32
        )
        normed_value, in_pull = jax.vjp(input_norm, residual, in_gain)
        grad_res, grad_in_gain = in_pull(grad_normed)
        grad_res = grad_res + upstream
        grad_head = grad_head.at[:, CONV * HDIM : (CONV + 1) * HDIM].add(
            grad_out_gain.reshape(head_part.shape[0], HDIM)
        )
        acc_in_w = acc_in_w + live_scale * grad_in_w
        acc_state_w = acc_state_w + live_scale * grad_state_w
        acc_out_w = acc_out_w + live_scale * grad_out_w
        acc_head = acc_head + live_scale * grad_head
        acc_shared = acc_shared + live_scale * jnp.concatenate([grad_conv, grad_in_gain])
        grad_buffer = store_micro(grad_buffer, micro_pick, live_now, grad_res)
        returned = shifted_2(grad_res.astype(jnp.bfloat16), "section", -1)
    shared_grad, state_grad = lax.psum((acc_shared, acc_state_w), "head")
    local_sq = (
        jnp.sum(acc_in_w * acc_in_w) + jnp.sum(acc_out_w * acc_out_w) + jnp.sum(acc_head * acc_head)
    )
    local_sq = local_sq + (
        jnp.sum(state_grad * state_grad) + jnp.sum(shared_grad * shared_grad)
    ) / lax.axis_size("head")
    norm_sq = lax.psum(local_sq, ("section", "head"))
    grad_norm = jnp.sqrt(norm_sq)
    threshold = CLIP_COEF * PARAMS**0.5
    clip_scale = threshold / jnp.maximum(grad_norm, threshold)
    new_in = adam_update(
        weight_in, proj_in_m[0], proj_in_v[0], clip_scale * acc_in_w, LEARN_MATRIX, WEIGHT_DECAY
    )
    new_state = adam_update(
        weight_state,
        proj_state_m[0],
        proj_state_v[0],
        clip_scale * state_grad,
        LEARN_MATRIX,
        WEIGHT_DECAY,
    )
    new_out = adam_update(
        weight_out, proj_out_m[0], proj_out_v[0], clip_scale * acc_out_w, LEARN_MATRIX, WEIGHT_DECAY
    )
    new_head = adam_update(
        head_part, head_m[0], head_v[0], clip_scale * acc_head, LEARN_VECTOR, 0.0
    )
    new_shared = adam_update(
        shared_part, shared_m[0], shared_v[0], clip_scale * shared_grad, LEARN_VECTOR, 0.0
    )
    return (
        layer_outs[None],
        grad_buffer[None],
        grad_norm,
        new_in[0][None],
        new_in[1][None],
        new_in[2][None],
        new_in[0][None].astype(jnp.bfloat16),
        new_state[0][None],
        new_state[1][None],
        new_state[2][None],
        new_state[0][None].astype(jnp.bfloat16),
        new_out[0][None],
        new_out[1][None],
        new_out[2][None],
        new_out[0][None].astype(jnp.bfloat16),
        new_head[0][None],
        new_head[1][None],
        new_head[2][None],
        new_shared[0][None],
        new_shared[1][None],
        new_shared[2][None],
    )


def solution(mesh):
    in_specs = (
        P(None, "head", None),
        P(None, "head", None),
        P(),
        P("section", None, "head"),
        P("section", None, "head"),
        P("section", None, "head"),
        P("section", None, None),
        P("section", None, None),
        P("section", None, None),
        P("section", "head", None),
        P("section", "head", None),
        P("section", "head", None),
        P("section", "head", None),
        P("section", "head", None),
        P("section", "head", None),
        P("section", None),
        P("section", None),
        P("section", None),
    )
    out_specs = (
        P("section", None, "head", None),
        P("section", None, "head", None),
        P(),
        P("section", None, "head"),
        P("section", None, "head"),
        P("section", None, "head"),
        P("section", None, "head"),
        P("section", None, None),
        P("section", None, None),
        P("section", None, None),
        P("section", None, None),
        P("section", "head", None),
        P("section", "head", None),
        P("section", "head", None),
        P("section", "head", None),
        P("section", "head", None),
        P("section", "head", None),
        P("section", "head", None),
        P("section", None),
        P("section", None),
        P("section", None),
    )
    return jax.shard_map(shards, mesh=mesh, in_specs=in_specs, out_specs=out_specs, check_vma=False)
```

profile of v0, /device:TPU:13, one launch (start us, length us, event | category | flops | bytes accessed | tf_op | source)
XLA Modules:
  0.0 3526.2 jit_solution(9607444074299756189)
XLA Ops:
  13.0 27.8 all_gather.28
  50.3 39.3 %all-gather.7.cloned.1.call-done = bf16[1024,2048]{1,0:T(8,128)(2,1)} async-done(((bf16[64,2048]{1,0:T(8,128)(2,1)}), bf16[1024,2048]{1,0:T(8,128)(2,1)}) %all-gather.7.cloned.1.call-update) | async-done | bytes 4194320 | tf_op jit(solution)/shard_map/all_gather | solution.py:219
  93.3 7.0 bitcast_dynamic-update-slice_fusion.8
  111.2 67.1 %while.165 = (s32[]{:T(128)}, f32[4,64,128]{2,1,0:T(8,128)S(1)}, f32[4,256,4,64]{1,0,3,2:T(4,128)}, f32[4,256,4]{1,2,0:T(4,128)S(1)}, f32[4]{0:T(128)}, /*index=...) while((s32[]{:T(128)}, f32[4,64,128]{2,1,0:T(8,128)S(1)}, ...), condition=%wide.region_6.7_spmd.clone, body=%wide.region_3.6_spmd.clone.sunk | while | flops 504957952 | bytes 4536984 | solution.py:87
  184.5 24.1 psum.63
  216.3 190.4 %reduce-scatter.10.cloned.1.call-done = f32[64,2048]{1,0:T(8,128)} async-done(((f32[1024,2048]{1,0:T(8,128)}), f32[64,2048]{1,0:T(8,128)}) %reduce-scatter.10.cloned.1.call-update) | async-done | bytes 524304 | tf_op jit(solution)/shard_map/reduce_scatter | solution.py:229
  419.9 31.0 all_gather.30
  454.1 39.0 %all-gather.9.cloned.1.call-done = bf16[1024,2048]{1,0:T(8,128)(2,1)} async-done(((bf16[64,2048]{1,0:T(8,128)(2,1)}), bf16[1024,2048]{1,0:T(8,128)(2,1)}) %all-gather.9.cloned.1.call-update) | async-done | bytes 4194320 | tf_op jit(solution)/shard_map/all_gather | solution.py:219
  493.1 8.9 bitcast_dynamic-update-slice_fusion.7
  513.6 91.0 %while.166 = (s32[]{:T(128)}, f32[4,64,128]{2,1,0:T(8,128)S(1)}, f32[4,256,4,64]{1,0,3,2:T(4,128)}, f32[4,256,4]{1,2,0:T(4,128)}, f32[4]{0:T(128)}, /*index=5*/f...) while((s32[]{:T(128)}, f32[4,64,128]{2,1,0:T(8,128)S(1)}, ...), condition=%wide.region_14.15_spmd.clone, body=%wide.region_11.14_spmd.clone.sunk | while | flops 504957952 | bytes 4553500 | solution.py:87
  610.4 24.4 psum.64
  644.0 190.4 %reduce-scatter.12.cloned.1.call-done = f32[64,2048]{1,0:T(8,128)} async-done(((f32[1024,2048]{1,0:T(8,128)}), f32[64,2048]{1,0:T(8,128)}) %reduce-scatter.12.cloned.1.call-update) | async-done | bytes 524304 | tf_op jit(solution)/shard_map/reduce_scatter | solution.py:229
  844.2 7.1 convert_element_type.545
  858.6 30.5 all_gather.32
  903.6 18.1 all-gather.11.cloned.1.call-done
  921.7 9.0 bitcast_dynamic-update-slice_fusion.6
  992.5 71.7 %while.167 = (s32[]{:T(128)}, f32[4,64,128]{2,1,0:T(8,128)S(1)}, f32[4,256,4,64]{1,0,3,2:T(4,128)}, f32[4,256,4]{1,2,0:T(4,128)}, f32[4]{0:T(128)}, /*index=5*/f...) while((s32[]{:T(128)}, f32[4,64,128]{2,1,0:T(8,128)S(1)}, ...), condition=%wide.region_22.23_spmd.clone, body=%wide.region_19.22_spmd.clone.sunk | while | flops 504957952 | bytes 4536996 | solution.py:87
  1076.3 70.6 %while.168 = (s32[]{:T(128)}, f32[4,64,128]{2,1,0:T(8,128)S(1)}, f32[4,256,4,64]{1,0,3,2:T(4,128)}, f32[4,4,64,128]{3,2,1,0:T(8,128)}, f32[4,256,4]{1,2,0:T(4,12...) while((s32[]{:T(128)}, f32[4,64,128]{2,1,0:T(8,128)S(1)}, ...), condition=%wide.region_29.31_spmd.clone, body=%wide.region_26.30_spmd.clone.sunk | while | flops 504925184 | bytes 4214456 | solution.py:87
  1154.6 23.6 psum.65
  1185.6 29.8 psum.66
  1218.4 74.4 %while.170 = (s32[]{:T(128)}, f32[4,64,128]{2,1,0:T(8,128)S(1)}, f32[4,256,4,64]{1,0,3,2:T(4,128)}, f32[4,4,64,128]{3,2,1,0:T(8,128)}, f32[4,256,4]{1,2,0:T(4,12...) while((s32[]{:T(128)}, f32[4,64,128]{2,1,0:T(8,128)S(1)}, ...), condition=%wide.region_53.55_spmd.clone, body=%wide.region_50.54_spmd.clone.sunk | while | flops 504925184 | bytes 4214964 | solution.py:87
  1308.6 225.8 %while.169 = (s32[]{:T(128)}, f32[4]{0:T(128)}, f32[4,64,128]{2,1,0:T(8,128)}, f32[4,256,4,64]{1,0,3,2:T(4,128)}, f32[4,256,4]{1,2,0:T(4,128)}, /*index=5*/f32[4...) while((s32[]{:T(128)}, f32[4]{0:T(128)}, ...), condition=%wide.region_45.47_spmd.clone, body=%wide.region_32.46_spmd.clone.sunk | while | flops 1213644800 | bytes 12642824 | solution.py:87
  1550.3 74.3 %while.172 = (s32[]{:T(128)}, f32[4,64,128]{2,1,0:T(8,128)S(1)}, f32[4,256,4,64]{1,0,3,2:T(4,128)}, f32[4,4,64,128]{3,2,1,0:T(8,128)}, f32[4,256,4]{1,2,0:T(4,12...) while((s32[]{:T(128)}, f32[4,64,128]{2,1,0:T(8,128)S(1)}, ...), condition=%wide.region_77.79_spmd.clone, body=%wide.region_74.78_spmd.clone.sunk | while | flops 504925184 | bytes 4214964 | solution.py:87
  1640.6 9.5 fusion.374
  1651.5 55.4 %reduce-scatter.18.cloned.1.call-done = f32[64,256]{1,0:T(8,128)} async-done(((f32[1024,256]{1,0:T(8,128)}), f32[64,256]{1,0:T(8,128)}) %reduce-scatter.18.cloned.1.call-update) | async-done | bytes 65552 | tf_op jit(solution)/shard_map/reduce_scatter | solution.py:282
  1706.9 198.5 %reduce-scatter.16.cloned.1.call-done = f32[64,2048]{1,0:T(8,128)} async-done(((f32[1024,2048]{1,0:T(8,128)}), f32[64,2048]{1,0:T(8,128)}) %reduce-scatter.16.cloned.1.call-update) | async-done | bytes 524304 | tf_op jit(solution)/shard_map/reduce_scatter | solution.py:292
  1914.5 75.9 %all-gather.15.cloned.1.call-done = bf16[1024,2048]{1,0:T(8,128)(2,1)} async-done(((bf16[64,2048]{1,0:T(8,128)(2,1)}), bf16[1024,2048]{1,0:T(8,128)(2,1)}) %all-gather.15.cloned.1.call-update) | async-done | bytes 4194320 | tf_op jit(solution)/shard_map/all_gather | solution.py:267
  1996.5 24.3 psum.67
  2033.3 155.1 %while.171 = (s32[]{:T(128)}, f32[4]{0:T(128)}, f32[4,64,128]{2,1,0:T(8,128)S(1)}, f32[4,256,4,64]{1,0,3,2:T(4,128)}, f32[4,256,4]{1,2,0:T(4,128)}, /*index=5*/f...) while((s32[]{:T(128)}, f32[4]{0:T(128)}, ...), condition=%wide.region_69.71_spmd.clone, body=%wide.region_56.70_spmd.clone.sunk | while | flops 1213644800 | bytes 12643008 | solution.py:87
  2210.7 9.5 fusion.372
  2220.9 50.6 %reduce-scatter.22.cloned.1.call-done = f32[64,256]{1,0:T(8,128)} async-done(((f32[1024,256]{1,0:T(8,128)}), f32[64,256]{1,0:T(8,128)}) %reduce-scatter.22.cloned.1.call-update) | async-done | bytes 65552 | tf_op jit(solution)/shard_map/reduce_scatter | solution.py:282
  2271.5 198.7 %reduce-scatter.20.cloned.1.call-done = f32[64,2048]{1,0:T(8,128)} async-done(((f32[1024,2048]{1,0:T(8,128)}), f32[64,2048]{1,0:T(8,128)}) %reduce-scatter.20.cloned.1.call-update) | async-done | bytes 524304 | tf_op jit(solution)/shard_map/reduce_scatter | solution.py:292
  2479.4 75.9 %all-gather.17.cloned.1.call-done = bf16[1024,2048]{1,0:T(8,128)(2,1)} async-done(((bf16[64,2048]{1,0:T(8,128)(2,1)}), bf16[1024,2048]{1,0:T(8,128)(2,1)}) %all-gather.17.cloned.1.call-update) | async-done | bytes 4194320 | tf_op jit(solution)/shard_map/all_gather | solution.py:267
  2561.2 24.1 psum.68
  2597.9 154.6 %while.173 = (s32[]{:T(128)}, f32[4]{0:T(128)}, f32[4,64,128]{2,1,0:T(8,128)S(1)}, f32[4,256,4,64]{1,0,3,2:T(4,128)}, f32[4,256,4]{1,2,0:T(4,128)}, /*index=5*/f...) while((s32[]{:T(128)}, f32[4]{0:T(128)}, ...), condition=%wide.region_93.95_spmd.clone, body=%wide.region_80.94_spmd.clone.sunk | while | flops 1213644800 | bytes 12643008 | solution.py:87
  2777.2 53.1 %reduce-scatter.26.cloned.1.call-done = f32[64,256]{1,0:T(8,128)} async-done(((f32[1024,256]{1,0:T(8,128)}), f32[64,256]{1,0:T(8,128)}) %reduce-scatter.26.cloned.1.call-update) | async-done | bytes 65552 | tf_op jit(solution)/shard_map/reduce_scatter | solution.py:282
  2842.4 9.5 fusion.370
  2869.9 7.8 bitcast_dynamic-update-slice_fusion.3
  2878.0 150.4 %reduce-scatter.14.cloned.1.call-done = f32[64,2048]{1,0:T(8,128)} async-done(((f32[1024,2048]{1,0:T(8,128)}), f32[64,2048]{1,0:T(8,128)}) %reduce-scatter.14.cloned.1.call-update) | async-done | bytes 524304 | tf_op jit(solution)/shard_map/reduce_scatter | solution.py:229
  3067.7 94.5 %all-reduce.122.cloned.1.call-done = f32[2048,256]{1,0:T(8,128)} async-done(((f32[2048,256]{1,0:T(8,128)}), f32[2048,256]{1,0:T(8,128)}) %all-reduce.122.cloned.1.call-update) | async-done | bytes 2097168 | tf_op jit(solution)/shard_map/psum | solution.py:311
  3164.9 178.1 %reduce-scatter.24.cloned.1.call-done = f32[64,2048]{1,0:T(8,128)} async-done(((f32[1024,2048]{1,0:T(8,128)}), f32[64,2048]{1,0:T(8,128)}) %reduce-scatter.24.cloned.1.call-update) | async-done | bytes 524304 | tf_op jit(solution)/shard_map/reduce_scatter | solution.py:292
  3344.7 51.5 %psum.70 = f32[3328]{0:T(1024)S(1)} all-reduce(f32[3328]{0:T(1024)S(1)} %fusion.523), channel_id=1, replica_groups=mesh['section'=2,'head'=16] {'head'}, use_global_device_ids=true, to_apply=%region_146.148 | all-reduce | flops 3328 | bytes 26624 | tf_op jit(solution)/shard_map/psum | solution.py:311
  3398.1 62.0 %psum.71 = f32[]{:T(128)} all-reduce(f32[]{:T(128)S(6)} %add.1223), channel_id=1, replica_groups=mesh['section'=2,'head'=16] {'section','head'}, use_global_device_ids=true, to_apply=%region_148.150 | all-reduce | flops 1 | bytes 8 | tf_op jit(solution)/shard_map/psum | solution.py:318
  3460.8 15.1 convert_bitcast_fusion
  3475.9 8.6 copy.861
  3484.5 8.6 copy.862
  3493.1 9.0 copy.863
  3503.9 7.6 convert_bitcast_fusion.1
  (2266 shorter events, 1397.9 us)
Async XLA Ops:
  7.2 82.4 %all-gather.7.cloned.1.call-start = ((), (), s32[]{:S(2)}) async-start(), calls=%async_computation.9 | async-start | bytes 4456448 | tf_op jit(solution)/shard_map/all_gather | solution.py:219
  10.9 395.7 %reduce-scatter.10.cloned.1.call-start = ((), (), s32[]{:S(2)}) async-start(), calls=%async_computation.10 | async-start | bytes 8912896 | tf_op jit(solution)/shard_map/reduce_scatter | solution.py:229
  43.8 137.2 %copy-start.223 = (f32[4]{0:T(128)}, f32[4]{0:T(128)S(1)}, u32[]{:S(2)}) copy-start(f32[4]{0:T(128)S(1)} %get-tuple-element.2634) | copy-start | bytes 52
  46.0 163.2 %copy-start.217 = (f32[4,64]{1,0:T(4,128)}, f32[4,64]{1,0:T(4,128)S(1)}, u32[]{:S(2)}) copy-start(f32[4,64]{1,0:T(4,128)S(1)} %get-tuple-element.3095) | copy-start | bytes 3076
  46.9 462.9 %copy-start.137 = (f32[1,4,64]{2,0,1:T(1,128)}, f32[1,4,64]{2,0,1:T(1,128)S(1)}, u32[]{:S(2)}) copy-start(f32[1,4,64]{2,0,1:T(1,128)S(1)} %get-tuple-element.3097) | copy-start | bytes 3076
  46.9 462.9 %copy-start.142 = (f32[1,4,64]{2,0,1:T(1,128)}, f32[1,4,64]{2,0,1:T(1,128)S(1)}, u32[]{:S(2)}) copy-start(f32[1,4,64]{2,0,1:T(1,128)S(1)} %get-tuple-element.3098) | copy-start | bytes 3076
  215.2 192.3 %copy-start.70 = (bf16[2,64,2048]{2,1,0:T(8,128)(2,1)S(1)}, bf16[2,64,2048]{2,1,0:T(8,128)(2,1)}, u32[]{:S(2)}) copy-start(bf16[2,64,2048]{2,1,0:T(8,128)(2,1)} %param.43) | copy-start | bytes 1572868
  215.2 277.9 %all-gather.9.cloned.1.call-start = ((), (), s32[]{:S(2)}) async-start(), calls=%async_computation.11 | async-start | bytes 4456448 | tf_op jit(solution)/shard_map/all_gather | solution.py:219
  409.4 3.4 collective-permute-start
  413.9 420.5 %reduce-scatter.12.cloned.1.call-start = ((), (), s32[]{:S(2)}) async-start(), calls=%async_computation.12 | async-start | bytes 8912896 | tf_op jit(solution)/shard_map/reduce_scatter | solution.py:229
  642.9 191.5 %copy-start.306 = (f32[64]{0:T(128)S(1)}, f32[64]{0:T(128)}, u32[]{:S(2)}) copy-start(f32[64]{0:T(128)} %get-tuple-element.3075) | copy-start | bytes 772
  642.9 197.3 %copy-start.71 = (bf16[2,64,2048]{2,1,0:T(8,128)(2,1)S(1)}, bf16[2,64,2048]{2,1,0:T(8,128)(2,1)}, u32[]{:S(2)}) copy-start(bf16[2,64,2048]{2,1,0:T(8,128)(2,1)} %param.43) | copy-start | bytes 1572868
  643.0 278.7 %all-gather.11.cloned.1.call-start = ((), (), s32[]{:S(2)}) async-start(), calls=%async_computation.13 | async-start | bytes 4456448 | tf_op jit(solution)/shard_map/all_gather | solution.py:219
  836.5 3.8 collective-permute-start.1
  841.9 337.6 %all-gather.13.cloned.1.call-start = ((), (), s32[]{:S(2)}) async-start(), calls=%async_computation.15 | async-start | bytes 4456448 | tf_op jit(solution)/shard_map/all_gather | solution.py:267
  842.8 864.1 %reduce-scatter.18.cloned.1.call-start = ((), (), s32[]{:S(2)}) async-start(), calls=%async_computation.17 | async-start | bytes 1114112 | tf_op jit(solution)/shard_map/reduce_scatter | solution.py:282
  1628.3 277.1 %reduce-scatter.16.cloned.1.call-start = ((), (), s32[]{:S(2)}) async-start(), calls=%async_computation.16 | async-start | bytes 8912896 | tf_op jit(solution)/shard_map/reduce_scatter | solution.py:292
  1650.1 340.3 %all-gather.15.cloned.1.call-start = ((), (), s32[]{:S(2)}) async-start(), calls=%async_computation.18 | async-start | bytes 4456448 | tf_op jit(solution)/shard_map/all_gather | solution.py:267
  1651.5 257.6 %copy-start.285 = (f32[64]{0:T(128)}, f32[64]{0:T(128)S(1)}, u32[]{:S(2)}) copy-start(f32[64]{0:T(128)S(1)} %fusion.548) | copy-start | bytes 772
  1651.5 262.2 %copy-start.315 = (f32[64]{0:T(128)S(1)}, f32[64]{0:T(128)}, u32[]{:S(2)}) copy-start(f32[64]{0:T(128)} %get-tuple-element.3072) | copy-start | bytes 772
  1909.0 3.9 collective-permute-start.2
  1914.4 357.0 %reduce-scatter.22.cloned.1.call-start = ((), (), s32[]{:S(2)}) async-start(), calls=%async_computation.20 | async-start | bytes 1114112 | tf_op jit(solution)/shard_map/reduce_scatter | solution.py:282
  2202.2 268.0 %reduce-scatter.20.cloned.1.call-start = ((), (), s32[]{:S(2)}) async-start(), calls=%async_computation.19 | async-start | bytes 8912896 | tf_op jit(solution)/shard_map/reduce_scatter | solution.py:292
  2220.2 250.0 %copy-start.2 = (f32[2,64,2048]{2,1,0:T(8,128)S(1)}, f32[2,64,2048]{2,1,0:T(8,128)}, u32[]{:S(2)}) copy-start(f32[2,64,2048]{2,1,0:T(8,128)} %copy-done) | copy-start | bytes 3145732
  2220.2 252.6 %copy-start.116 = (bf16[64,2048]{1,0:T(8,128)(2,1)S(1)}, bf16[64,2048]{1,0:T(8,128)(2,1)}, u32[]{:S(2)}) copy-start(bf16[64,2048]{1,0:T(8,128)(2,1)} %copy-done.115) | copy-start | bytes 786436
  2220.3 335.0 %all-gather.17.cloned.1.call-start = ((), (), s32[]{:S(2)}) async-start(), calls=%async_computation.21 | async-start | bytes 4456448 | tf_op jit(solution)/shard_map/all_gather | solution.py:267
  2220.9 253.0 %copy-start.289 = (f32[64]{0:T(128)}, f32[64]{0:T(128)S(1)}, u32[]{:S(2)}) copy-start(f32[64]{0:T(128)S(1)} %fusion.549) | copy-start | bytes 772
  2220.9 257.6 %copy-start.314 = (f32[64]{0:T(128)S(1)}, f32[64]{0:T(128)}, u32[]{:S(2)}) copy-start(f32[64]{0:T(128)} %get-tuple-element.3071) | copy-start | bytes 772
  2473.9 3.9 collective-permute-start.3
  2479.3 351.1 %reduce-scatter.26.cloned.1.call-start = ((), (), s32[]{:S(2)}) async-start(), calls=%async_computation.23 | async-start | bytes 1114112 | tf_op jit(solution)/shard_map/reduce_scatter | solution.py:282
  2760.6 267.8 %reduce-scatter.14.cloned.1.call-start = ((), (), s32[]{:S(2)}) async-start(), calls=%async_computation.14 | async-start | bytes 8912896 | tf_op jit(solution)/shard_map/reduce_scatter | solution.py:229
  2766.8 395.4 %all-reduce.122.cloned.1.call-start = ((), (), s32[]{:S(2)}) async-start(), calls=%async_computation.24 | async-start | bytes 4194304 | tf_op jit(solution)/shard_map/psum | solution.py:311
  2833.9 509.1 %reduce-scatter.24.cloned.1.call-start = ((), (), s32[]{:S(2)}) async-start(), calls=%async_computation.22 | async-start | bytes 8912896 | tf_op jit(solution)/shard_map/reduce_scatter | solution.py:292
  2877.7 150.7 %copy-start.91 = (bf16[64,2048]{1,0:T(8,128)(2,1)S(1)}, bf16[64,2048]{1,0:T(8,128)(2,1)}, u32[]{:S(2)}) copy-start(bf16[64,2048]{1,0:T(8,128)(2,1)} %copy-done.90) | copy-start | bytes 786436
  2877.7 150.7 %copy-start.307 = (f32[64]{0:T(128)S(1)}, f32[64]{0:T(128)}, u32[]{:S(2)}) copy-start(f32[64]{0:T(128)} %get-tuple-element.3074) | copy-start | bytes 772
  2877.7 152.0 %copy-start.319 = (f32[256]{0:T(256)S(1)}, f32[256]{0:T(256)}, u32[]{:S(2)}) copy-start(f32[256]{0:T(256)} %get-tuple-element.2612) | copy-start | bytes 3076
  2877.7 152.1 %copy-start.275 = (f32[4,64]{1,0:T(4,128)S(1)}, f32[4,64]{1,0:T(4,128)}, u32[]{:S(2)}) copy-start(f32[4,64]{1,0:T(4,128)} %get-tuple-element.2630) | copy-start | bytes 3076
  2877.7 152.1 %copy-start.278 = (f32[4,64]{1,0:T(4,128)S(1)}, f32[4,64]{1,0:T(4,128)}, u32[]{:S(2)}) copy-start(f32[4,64]{1,0:T(4,128)} %get-tuple-element.2912) | copy-start | bytes 3076
  2877.7 152.1 %copy-start.279 = (f32[4,64]{1,0:T(4,128)S(1)}, f32[4,64]{1,0:T(4,128)}, u32[]{:S(2)}) copy-start(f32[4,64]{1,0:T(4,128)} %get-tuple-element.2915) | copy-start | bytes 3076
  2877.7 152.1 %copy-start.280 = (f32[4,64]{1,0:T(4,128)S(1)}, f32[4,64]{1,0:T(4,128)}, u32[]{:S(2)}) copy-start(f32[4,64]{1,0:T(4,128)} %get-tuple-element.3041) | copy-start | bytes 3076
  2877.8 152.2 %copy-start.310 = (f32[4]{0:T(128)S(1)}, f32[4]{0:T(128)}, u32[]{:S(2)}) copy-start(f32[4]{0:T(128)} %get-tuple-element.2910) | copy-start | bytes 52
  2877.8 152.2 %copy-start.316 = (f32[4]{0:T(128)S(1)}, f32[4]{0:T(128)}, u32[]{:S(2)}) copy-start(f32[4]{0:T(128)} %get-tuple-element.2908) | copy-start | bytes 52
  3058.9 284.1 %copy-start.288 = (f32[64]{0:T(128)S(1)}, f32[64]{0:T(128)}, u32[]{:S(2)}) copy-start(f32[64]{0:T(128)} %copy-done.287) | copy-start | bytes 772
  3065.0 278.0 %copy-start.6 = (bf16[2048,256]{1,0:T(8,128)(2,1)S(1)}, bf16[2048,256]{1,0:T(8,128)(2,1)}, u32[]{:S(2)}) copy-start(bf16[2048,256]{1,0:T(8,128)(2,1)} %copy-done.4) | copy-start | bytes 3145732
  3065.0 278.0 %copy-start.127 = (f32[64,256]{1,0:T(8,128)S(1)}, f32[64,256]{1,0:T(8,128)}, u32[]{:S(2)}) copy-start(f32[64,256]{1,0:T(8,128)} %reduce-scatter.26.cloned.1.call-done) | copy-start | bytes 196612
  3067.7 276.9 %copy-start.252 = (f32[2048]{0:T(1024)S(1)}, f32[2048]{0:T(1024)}, u32[]{:S(2)}) copy-start(f32[2048]{0:T(1024)} %get-tuple-element.2620) | copy-start | bytes 24580
  3067.7 276.9 %copy-start.253 = (f32[2048]{0:T(1024)S(1)}, f32[2048]{0:T(1024)}, u32[]{:S(2)}) copy-start(f32[2048]{0:T(1024)} %get-tuple-element.2618) | copy-start | bytes 24580
  3067.7 330.3 %copy-start.322 = (f32[64]{0:T(128)S(1)}, f32[64]{0:T(128)}, u32[]{:S(2)}) copy-start(f32[64]{0:T(128)} %get-tuple-element.2625) | copy-start | bytes 772
  (374 other events, 2319.6 us)
Sparse Core Ops, SparseCore 0:
  11.4 78.1 all-gather.6
  215.3 191.2 reduce-scatter.9
  414.0 78.9 all-gather.8
  643.1 191.3 reduce-scatter.11
  842.0 79.5 all-gather.10
  924.3 74.9 all-gather.12
  1628.4 78.3 reduce-scatter.17
  1709.3 196.0 reduce-scatter.15
  1914.6 75.8 all-gather.14
  2202.3 69.1 reduce-scatter.21
  2273.8 196.3 reduce-scatter.19
  2479.4 75.8 all-gather.16
  2760.8 69.5 reduce-scatter.25
  2832.6 195.7 reduce-scatter.13
  3035.2 126.9 all-reduce.121
  3164.3 178.6 reduce-scatter.23
where the time goes:
time: 3550 us; the launch traced here: 3530 us
  waiting for transfers between devices  1610 us (45%)
  local copies, waits for them, and re-layouts  676 us (19%)
  matrix products  419 us (12%)
  other arithmetic  404 us (11%)
  blocking collectives  353 us (10%)
    reduce_scatter x3, waiting for transfers between devices, shards(): lax.psum_scatter(row_product_back(low_grad_proj, low_in), 'head', scatter...  575 us
    reduce_scatter x3, waiting for transfers between devices, shards(): lax.psum_scatter(row_product(scaled, low_out), 'head', scatter_dimension=...  531 us
    dynamic_update_slice x72, local copies, waits for them, and re-layouts, block_scan(): lax.scan(jax.checkpoint(advance), start_state, pieces)  261 us
    reduce_scatter x3, waiting for transfers between devices, shards(): lax.psum_scatter(grad_state_raw, 'head', scatter_dimension=0, tiled=True)  159 us
    another operation x147, other arithmetic  155 us
    all_gather x3, waiting for transfers between devices, shards(): grad_full = lax.all_gather(out_grad, 'head', axis=0, tiled=True)  152 us
    dot_general x48, matrix products, advance(): jnp.einsum('ijh,jhp->ihp', block_weights, block_inner, precision=HIGH)  99 us
    all_gather x3, waiting for transfers between devices, shards(): lax.all_gather(normed_rows, 'head', axis=0, tiled=True)  96.3 us
  transfers between devices with their start and end apart: 20, of which 19 were waited for; matrix products, arithmetic and copies ran while one was open for 12% of the time, Pallas kernels for 0%

commit v1 on v0

v1 whole, which is shorter than its diff:
```python
import itertools

import jax
import jax.numpy as jnp
import numpy as np
from jax import lax
from jax.experimental import pallas as pl
from jax.experimental.pallas import tpu as pltpu
from jax.sharding import PartitionSpec as P

HEADS = 64
HDIM = 64
NSTATE = 128
CONV = 4
STRETCH = 256
ADAM_STEP = 5
PARAMS = 51698560

HIGH = lax.Precision.HIGHEST
EPS_NORM = 1e-05
ADAM_EPS = 1e-08
BETA_ONE = 0.5
BETA_TWO = 0.5
CLIP_COEF = 0.2
LEARN_MATRIX = 0.02
LEARN_VECTOR = 0.2
WEIGHT_DECAY = 0.1

F32 = jnp.float32
BF16 = jnp.bfloat16
MESH = pl.DeviceIdType.MESH
LANES = 128
CHUNK = 128
COLS = HDIM * 2 + 1
GAIN_ROW = 9
VMEM_LIMIT = 56 << 20


def seq_layout(lengths_row):
    block_count = lengths_row.shape[0]
    block_idx = jnp.arange(block_count, dtype=jnp.int32)
    starts = lengths_row > 0
    start_block = lax.cummax(jnp.where(starts, block_idx, 0), axis=0)
    owner_mask = (start_block[:, None] == block_idx[None, :]).astype(jnp.int32)
    seq_length = jnp.sum(owner_mask * lengths_row[None, :], axis=1)
    return (start_block, seq_length, starts.astype(jnp.float32))


def chip_dims(count):
    side = 4 if count % 64 == 0 else 2
    if count % (side * side) != 0:
        return (count, 1, 1)
    return (count // (side * side), side, side)


def place(dims):
    me = lax.axis_index("head")
    return (me // (dims[1] * dims[2]), (me // dims[2]) % dims[1], me % dims[2])


def linear(dims, spot):
    return (spot[0] * dims[1] + spot[1]) * dims[2] + spot[2]


def moved(dims, spot, shifts):
    return tuple(s if d == 0 else (s + d) % n for s, d, n in zip(spot, shifts, dims))


def shift_of(order, offsets):
    out = [0, 0, 0]
    for axis, off in zip(order, offsets):
        out[axis] = off
    return out


def greet_axes(dims, spot):
    barrier = pltpu.get_barrier_semaphore()
    count = 0
    for axis in range(3):
        for off in range(1, dims[axis]):
            peer = linear(dims, moved(dims, spot, shift_of((axis,), (off,))))
            pl.semaphore_signal(
                barrier, inc=1, device_id={"head": peer}, device_id_type=MESH
            )
            count += 1
    if count:
        pl.semaphore_wait(barrier, count)


def greet_all(count):
    barrier = pltpu.get_barrier_semaphore()
    me = lax.axis_index("head")
    for off in range(1, count):
        pl.semaphore_signal(
            barrier, inc=1, device_id={"head": (me + off) % count}, device_id_type=MESH
        )
    if count > 1:
        pl.semaphore_wait(barrier, count - 1)


def rows_at(shard, rows):
    return pl.ds(pl.multiple_of(shard * rows, rows), rows)


def column_parts(width):
    tiles = width // LANES
    late = max(tiles // 8, 0)
    early = (tiles - 2 * late) // 2
    sizes = [early, tiles - 2 * late - early, late, late]
    orders = [(0, 2, 1), (0, 1, 2), (2, 1, 0), (1, 2, 0)]
    parts, start = [], 0
    for size, order in zip(sizes, orders):
        if size:
            parts.append((start, size * LANES, order))
            start += size * LANES
    return parts


def guarded(preds, action):
    preds = [pred for pred in preds if pred is not None]
    if not preds:
        action()
        return
    cond = preds[0]()
    for pred in preds[1:]:
        cond = jnp.logical_and(cond, pred())
    pl.when(cond)(action)


def gather_steps(dims, parts, rows, own_ref, all_ref, send_sem, recv_sem):
    spot = place(dims)
    me = linear(dims, spot)
    waits = []
    counter = [0] * len(parts)

    def lined(axis):
        return axis == 0 and dims[0] > 2 and dims[1] == 2

    def above(axis, dist):
        return lambda: spot[axis] + dist < dims[axis]

    def below(axis, dist):
        return lambda: spot[axis] >= dist

    def sources(part, pos):
        axis = parts[part][2][pos]
        if not lined(axis):
            return [(off, None) for off in range(1, dims[axis])]
        out = []
        for dist in range(1, dims[axis]):
            out.append((dist, above(axis, dist)))
            out.append((-dist, below(axis, dist)))
        return out

    def block(part, offsets):
        start, width, order = parts[part]
        shard = linear(dims, moved(dims, spot, shift_of(order, offsets)))
        return shard, all_ref.at[rows_at(shard, rows), pl.ds(start, width)]

    def push(part, offsets, pos, preds, src, came):
        axis = parts[part][2][pos]
        shard, dst = block(part, offsets)
        up, down = (1, above(axis, 1)), (-1, below(axis, 1))
        if lined(axis):
            targets = [up, down] if came == 0 else [down] if came > 0 else [up]
        else:
            targets = [(off, None) for off in range(1, dims[axis])] if came == 0 else []
        for off, pred in targets:
            peer = linear(dims, moved(dims, spot, shift_of((axis,), (off,))))
            number = counter[part]
            counter[part] += 1

            def begin(peer=peer, number=number):
                pltpu.make_async_remote_copy(
                    src_ref=dst if src is None else src,
                    dst_ref=dst,
                    send_sem=send_sem.at[part, number],
                    recv_sem=recv_sem.at[part, shard],
                    device_id={"head": peer},
                    device_id_type=MESH,
                ).start()

            guarded([pred], begin)
            waits.append((preds + [pred], part, number))

    def visit(part, offsets, preds, pos, came):
        def body():
            shard, dst = block(part, offsets)
            pltpu.make_async_remote_copy(
                src_ref=dst,
                dst_ref=dst,
                send_sem=send_sem.at[part, 0],
                recv_sem=recv_sem.at[part, shard],
                device_id={"head": me},
                device_id_type=MESH,
            ).wait_recv()
            push(part, offsets, pos, preds, None, came)
            for later in range(pos + 1, 3):
                push(part, offsets, later, preds, None, 0)

        guarded(preds, body)

    for pos in range(3):
        for part, (start, width, _) in enumerate(parts):
            push(part, (0, 0, 0), pos, [], own_ref.at[:, pl.ds(start, width)], 0)
    todo = []
    for part in range(len(parts)):
        first, second, third = (sources(part, pos) for pos in range(3))
        for k, (oa, pa) in enumerate(first):
            todo.append(((0, k, part), part, (oa, 0, 0), [pa], 0, oa))
        for ka, (oa, pa) in enumerate([(0, None)] + first):
            for k, (ob, pb) in enumerate(second):
                todo.append(((1, ka + k, part), part, (oa, ob, 0), [pa, pb], 1, ob))
            for kb, (ob, pb) in enumerate([(0, None)] + second):
                for k, (oc, pc) in enumerate(third):
                    todo.append(
                        ((2, ka + kb + k, part), part, (oa, ob, oc), [pa, pb, pc], 2, oc)
                    )
    todo.sort(key=lambda entry: entry[0])
    for _, part, offsets, preds, pos, came in todo:
        visit(part, offsets, preds, pos, came)
    for preds, part, number in waits:

        def settle(part=part, number=number):
            start, width, _ = parts[part]
            ref = own_ref.at[:, pl.ds(start, width)]
            pltpu.make_async_remote_copy(
                src_ref=ref,
                dst_ref=ref,
                send_sem=send_sem.at[part, number],
                recv_sem=recv_sem.at[part, 0],
                device_id={"head": me},
                device_id_type=MESH,
            ).wait_send()

        guarded(preds, settle)


def gather_sends(dims):
    return 3 * dims[0] * dims[1] * dims[2]


def scatter_steps(dims, parts, rows, in_ref, out_ref, box_ref, send_sem, recv_sem):
    spot = place(dims)
    me = linear(dims, spot)
    sends = []
    big = max(dims)

    def size(part, pos):
        return dims[parts[part][2][pos]]

    def slot_one(part, ea, ob, oc):
        return ((ea - 1) * size(part, 1) + ob) * size(part, 2) + oc

    def slot_two(part, eb, oc):
        base = (size(part, 0) - 1) * size(part, 1) * size(part, 2)
        return base + (eb - 1) * size(part, 2) + oc

    def slot_three(part, ec):
        return slot_two(part, size(part, 1), 0) + ec - 1

    def cols(part):
        return pl.ds(parts[part][0], parts[part][1])

    def mine(part, offsets):
        shard = linear(dims, moved(dims, spot, shift_of(parts[part][2], offsets)))
        return in_ref.at[rows_at(shard, rows), cols(part)]

    def send(part, src, pos, off, slot):
        peer = linear(dims, moved(dims, spot, shift_of((parts[part][2][pos],), (off,))))
        copy = pltpu.make_async_remote_copy(
            src_ref=src,
            dst_ref=box_ref.at[slot, :, cols(part)],
            send_sem=send_sem.at[part, slot],
            recv_sem=recv_sem.at[part, slot],
            device_id={"head": peer},
            device_id_type=MESH,
        )
        copy.start()
        sends.append(copy)

    def arrived(part, slot):
        ref = box_ref.at[slot, :, cols(part)]
        pltpu.make_async_remote_copy(
            src_ref=ref,
            dst_ref=ref,
            send_sem=send_sem.at[part, slot],
            recv_sem=recv_sem.at[part, slot],
            device_id={"head": me},
            device_id_type=MESH,
        ).wait_recv()
        return ref[...].astype(F32)

    every = range(len(parts))
    ranks = sorted(
        itertools.product(range(big), range(big)), key=lambda t: (t[0] == 0, t[1] == 0)
    )
    for ob, oc in ranks:
        for off in range(1, big):
            for part in every:
                if off < size(part, 0) and ob < size(part, 1) and oc < size(part, 2):
                    slot = slot_one(part, size(part, 0) - off, ob, oc)
                    send(part, mine(part, (off, ob, oc)), 0, off, slot)
    for ob, oc in ranks:
        for part in every:
            if ob == 0 or ob >= size(part, 1) or oc >= size(part, 2):
                continue
            total = mine(part, (0, ob, oc))[...].astype(F32)
            for ea in range(1, size(part, 0)):
                total = total + arrived(part, slot_one(part, ea, ob, oc))
            hold = mine(part, (0, ob, oc))
            if size(part, 0) > 1:
                hold = box_ref.at[slot_one(part, 1, ob, oc), :, cols(part)]
                hold[...] = total.astype(box_ref.dtype)
            send(part, hold, 1, ob, slot_two(part, size(part, 1) - ob, oc))
    for oc in list(range(1, big)) + [0]:
        for part in every:
            if oc >= size(part, 2):
                continue
            total = mine(part, (0, 0, oc))[...].astype(F32)
            for ea in range(1, size(part, 0)):
                total = total + arrived(part, slot_one(part, ea, 0, oc))
            for eb in range(1, size(part, 1)):
                total = total + arrived(part, slot_two(part, eb, oc))
            if oc == 0:
                for ec in range(1, size(part, 2)):
                    total = total + arrived(part, slot_three(part, ec))
                out_ref[:, cols(part)] = total
                continue
            hold = mine(part, (0, 0, oc))
            if size(part, 0) > 1:
                hold = box_ref.at[slot_one(part, 1, 0, oc), :, cols(part)]
            elif size(part, 1) > 1:
                hold = box_ref.at[slot_two(part, 1, oc), :, cols(part)]
            if size(part, 0) > 1 or size(part, 1) > 1:
                hold[...] = total.astype(box_ref.dtype)
            send(part, hold, 2, oc, slot_three(part, size(part, 2) - oc))
    return sends


def start_direct(count, own_ref_of, box_ref, send_sem, recv_sem):
    me = lax.axis_index("head")
    copies = []
    for off in range(1, count):
        peer = (me + off) % count
        copy = pltpu.make_async_remote_copy(
            src_ref=own_ref_of(peer),
            dst_ref=box_ref.at[me],
            send_sem=send_sem.at[off],
            recv_sem=recv_sem.at[count - off],
            device_id={"head": peer},
            device_id_type=MESH,
        )
        copy.start()
        copies.append(copy)
    return copies


def wait_direct(count, box_ref, copies, recv_sem, send_sem):
    me = lax.axis_index("head")
    for off in range(1, count):
        ref = box_ref.at[(me + off) % count]
        pltpu.make_async_remote_copy(
            src_ref=ref,
            dst_ref=ref,
            send_sem=send_sem.at[off],
            recv_sem=recv_sem.at[off],
            device_id={"head": me},
            device_id_type=MESH,
        ).wait_recv()
    for copy in copies:
        copy.wait_send()


VMEM_SPEC = pl.BlockSpec(memory_space=pltpu.VMEM)
ANY_SPEC = pl.BlockSpec(memory_space=pl.ANY)
DMA = pltpu.SemaphoreType.DMA


def gather_rows(count, own, stats, collective_id):
    dims = chip_dims(count)
    rows, width = own.shape
    parts = column_parts(width)

    def kernel(*refs):
        if stats is None:
            own_ref, all_ref, send_sem, recv_sem, local_sem = refs
        else:
            (own_ref, stat_ref, all_ref, box_ref, send_sem, recv_sem, local_sem) = refs[:7]
            small_send, small_recv = refs[7:]
        spot = place(dims)
        me = linear(dims, spot)
        if stats is None:
            greet_axes(dims, spot)
        else:
            greet_all(count)
        local = pltpu.make_async_copy(own_ref, all_ref.at[rows_at(me, rows)], local_sem)
        local.start()
        if stats is not None:
            copies = start_direct(count, lambda peer: stat_ref, box_ref, small_send, small_recv)
            box_ref[me] = stat_ref[...]
        gather_steps(dims, parts, rows, own_ref, all_ref, send_sem, recv_sem)
        if stats is not None:
            wait_direct(count, box_ref, copies, small_recv, small_send)
        local.wait()

    out_shape = [jax.ShapeDtypeStruct((count * rows, width), own.dtype)]
    out_specs = [ANY_SPEC]
    scratch = [
        DMA((len(parts), gather_sends(dims))),
        DMA((len(parts), count)),
        DMA,
    ]
    operands = [own]
    if stats is not None:
        out_shape.append(jax.ShapeDtypeStruct((count,) + stats.shape, stats.dtype))
        out_specs.append(VMEM_SPEC)
        scratch += [DMA((count,)), DMA((count,))]
        operands.append(stats)
    return pl.pallas_call(
        kernel,
        out_shape=out_shape,
        in_specs=[VMEM_SPEC] * len(operands),
        out_specs=out_specs,
        scratch_shapes=scratch,
        compiler_params=pltpu.CompilerParams(
            collective_id=collective_id, has_side_effects=True, vmem_limit_bytes=VMEM_LIMIT
        ),
        name="gather_rows",
    )(*operands)


def scatter_rows(count, partial, small, collective_id):
    dims = chip_dims(count)
    width = partial.shape[1]
    rows = partial.shape[0] // count
    parts = [(s, w, tuple(reversed(order))) for s, w, order in column_parts(width)]

    def kernel(*refs):
        if small is None:
            in_ref, out_ref, box_ref, send_sem, recv_sem = refs
        else:
            in_ref, small_ref, out_ref, sums_ref, box_ref, send_sem, recv_sem = refs[:7]
            small_send, small_recv = refs[7:]
        me = lax.axis_index("head")
        spot = place(dims)
        if small is None:
            greet_axes(dims, spot)
        else:
            greet_all(count)
            copies = start_direct(
                count, lambda peer: small_ref.at[peer], sums_ref, small_send, small_recv
            )
            sums_ref[me] = small_ref[me]
        sends = scatter_steps(dims, parts, rows, in_ref, out_ref, box_ref, send_sem, recv_sem)
        if small is not None:
            wait_direct(count, sums_ref, copies, small_recv, small_send)
        for copy in sends:
            copy.wait_send()

    out_shape = [jax.ShapeDtypeStruct((rows, width), F32)]
    scratch = [
        pltpu.VMEM((max(count - 1, 1), rows, width), partial.dtype),
        DMA((len(parts), max(count - 1, 1))),
        DMA((len(parts), max(count - 1, 1))),
    ]
    operands = [partial]
    if small is not None:
        out_shape.append(jax.ShapeDtypeStruct(small.shape, small.dtype))
        scratch += [DMA((count,)), DMA((count,))]
        operands.append(small)
    return pl.pallas_call(
        kernel,
        out_shape=out_shape,
        in_specs=[VMEM_SPEC] * len(operands),
        out_specs=[VMEM_SPEC] * len(out_shape),
        scratch_shapes=scratch,
        compiler_params=pltpu.CompilerParams(
            collective_id=collective_id, has_side_effects=True, vmem_limit_bytes=VMEM_LIMIT
        ),
        name="scatter_rows",
    )(*operands)


def gather_small(count, block, collective_id):
    def kernel(in_ref, box_ref, send_sem, recv_sem):
        greet_all(count)
        copies = start_direct(count, lambda peer: in_ref, box_ref, send_sem, recv_sem)
        box_ref[lax.axis_index("head")] = in_ref[...]
        wait_direct(count, box_ref, copies, recv_sem, send_sem)

    return pl.pallas_call(
        kernel,
        out_shape=jax.ShapeDtypeStruct((count,) + block.shape, block.dtype),
        in_specs=[VMEM_SPEC],
        out_specs=VMEM_SPEC,
        scratch_shapes=[DMA((count,)), DMA((count,))],
        compiler_params=pltpu.CompilerParams(
            collective_id=collective_id, has_side_effects=True
        ),
        name="gather_small",
    )(block)


def greet_other():
    barrier = pltpu.get_barrier_semaphore()
    other = 1 - lax.axis_index("section")
    pl.semaphore_signal(barrier, inc=1, device_id={"section": other}, device_id_type=MESH)
    pl.semaphore_wait(barrier, 1)
    return other


def both_sections(arrays, collective_id):
    number = len(arrays)

    def kernel(*refs):
        ins, outs = refs[:number], refs[number : 2 * number]
        send_sem, recv_sem, local_sem = refs[2 * number :]
        section = lax.axis_index("section")
        locals_ = [
            pltpu.make_async_copy(ins[k], outs[k].at[section], local_sem.at[k])
            for k in range(number)
        ]
        for local in locals_:
            local.start()
        other = greet_other()
        copies = []
        for k in range(number):
            locals_[k].wait()
            copy = pltpu.make_async_remote_copy(
                src_ref=outs[k].at[section],
                dst_ref=outs[k].at[section],
                send_sem=send_sem.at[k],
                recv_sem=recv_sem.at[k],
                device_id={"section": other},
                device_id_type=MESH,
            )
            copy.start()
            copies.append(copy)
        for copy in copies:
            copy.wait()

    return pl.pallas_call(
        kernel,
        out_shape=[jax.ShapeDtypeStruct((2,) + a.shape, a.dtype) for a in arrays],
        in_specs=[ANY_SPEC] * number,
        out_specs=[VMEM_SPEC] * number,
        scratch_shapes=[DMA((number,))] * 3,
        compiler_params=pltpu.CompilerParams(
            collective_id=collective_id, has_side_effects=True, vmem_limit_bytes=VMEM_LIMIT
        ),
        name="both_sections",
    )(*arrays)


def trade_sections(sums, stacks, collective_id):
    pairs = sums + stacks
    number, summed = len(pairs), len(sums)

    def kernel(*refs):
        ins, outs = refs[: 2 * number], refs[2 * number : 3 * number]
        boxes = refs[3 * number : 3 * number + summed]
        send_sem, recv_sem = refs[3 * number + summed :]
        section = lax.axis_index("section")
        other = greet_other()

        def go(mine, theirs):
            copies = []
            for k in range(number):
                copy = pltpu.make_async_remote_copy(
                    src_ref=theirs[k],
                    dst_ref=boxes[k] if k < summed else outs[k].at[section],
                    send_sem=send_sem.at[k],
                    recv_sem=recv_sem.at[k],
                    device_id={"section": other},
                    device_id_type=MESH,
                )
                copy.start()
                copies.append(copy)
            for k in range(summed, number):
                outs[k][section] = mine[k][...]
            for k in range(number):
                copies[k].wait()
                if k < summed:
                    outs[k][...] = mine[k][...].astype(F32) + boxes[k][...].astype(F32)

        pl.when(section == 0)(lambda: go(ins[0::2], ins[1::2]))
        pl.when(section == 1)(lambda: go(ins[1::2], ins[0::2]))

    shapes = [jax.ShapeDtypeStruct(a.shape, F32) for a, _ in sums]
    shapes += [jax.ShapeDtypeStruct((2,) + a.shape, a.dtype) for a, _ in stacks]
    return pl.pallas_call(
        kernel,
        out_shape=shapes,
        in_specs=[VMEM_SPEC] * (2 * number),
        out_specs=[VMEM_SPEC] * number,
        scratch_shapes=[pltpu.VMEM(a.shape, a.dtype) for a, _ in sums] + [DMA((number,))] * 2,
        compiler_params=pltpu.CompilerParams(
            collective_id=collective_id, has_side_effects=True, vmem_limit_bytes=VMEM_LIMIT
        ),
        name="trade_sections",
    )(*[a for pair in pairs for a in pair])


class Sizes:
    def __init__(self, heads, tokens, width):
        self.heads = heads
        self.padded = heads + heads % 2
        self.channels = self.padded * HDIM
        self.conv = self.channels + 2 * NSTATE
        self.cols = 2 * self.channels + 2 * NSTATE + LANES
        self.dt = 2 * self.channels + 2 * NSTATE
        self.master = heads * COLS
        self.master_pad = -(-self.master // LANES) * LANES
        self.grad_rows = self.master_pad + 2 * NSTATE
        self.tokens = tokens
        self.width = width
        self.blocks = tokens // STRETCH

    def order(self):
        table = np.zeros((self.grad_rows, self.cols), np.float32)
        for head in range(self.heads):
            for j in range(HDIM):
                table[head * COLS + j, head * HDIM + j] = 1
                table[head * COLS + HDIM + j, self.channels + head * HDIM + j] = 1
            table[head * COLS + 2 * HDIM, self.dt + head] = 1
        for j in range(2 * NSTATE):
            table[self.master_pad + j, 2 * self.channels + j] = 1
        return jnp.asarray(table, BF16)

    def head_sum(self):
        table = np.zeros((self.channels, LANES), np.float32)
        for head in range(self.padded):
            table[head * HDIM : (head + 1) * HDIM, head] = 1
        return jnp.asarray(table, F32)


def nt(left, right, precision=None):
    return lax.dot_general(
        left, right, (((1,), (1,)), ((), ())), precision=precision, preferred_element_type=F32
    )


def tn(left, right, precision=None):
    return lax.dot_general(
        left, right, (((0,), (0,)), ((), ())), precision=precision, preferred_element_type=F32
    )


def nn(left, right, precision=None):
    return jnp.dot(left, right, precision=precision, preferred_element_type=F32)


def softplus(value):
    return jnp.maximum(value, 0.0) + jnp.log1p(jnp.exp(-jnp.abs(value)))


def sigmoid(value):
    return 1.0 / (1.0 + jnp.exp(-value))


def halves(left, right):
    rows = left.shape[0]
    lane = lax.broadcasted_iota(jnp.int32, (rows, LANES), 1)
    return jnp.where(lane < HDIM, left, right)


def lower_mask(size):
    row = lax.broadcasted_iota(jnp.int32, (size, size), 0)
    col = lax.broadcasted_iota(jnp.int32, (size, size), 1)
    return row >= col


def step_rows(log_decay, step):
    lane = lax.broadcasted_iota(jnp.int32, log_decay.shape, 1)
    both = jnp.where(lane < 8, log_decay, pltpu.roll(step, 8, 1))
    return jnp.transpose(jnp.where(lane < 16, both, 0.0))


def prepare_weights(sz, proj_in, proj_state, order):
    rows = min(256, sz.width)

    def kernel(in_ref, state_ref, order_ref, out_ref):
        low = in_ref[...].astype(BF16)
        table = order_ref[: sz.master, :]
        out_ref[...] = nn(low, table).astype(BF16)
        out_ref[:, 2 * sz.channels : sz.dt] = state_ref[...].astype(BF16)

    return pl.pallas_call(
        kernel,
        out_shape=jax.ShapeDtypeStruct((sz.width, sz.cols), BF16),
        grid=(sz.width // rows,),
        in_specs=[
            pl.BlockSpec((rows, sz.master), lambda i: (i, 0)),
            pl.BlockSpec((rows, 2 * NSTATE), lambda i: (i, 0)),
            pl.BlockSpec((sz.grad_rows, sz.cols), lambda i: (0, 0)),
        ],
        out_specs=pl.BlockSpec((rows, sz.cols), lambda i: (i, 0)),
        compiler_params=pltpu.CompilerParams(vmem_limit_bytes=VMEM_LIMIT),
        name="prepare_weights",
    )(proj_in, proj_state, order)


def pack_params(sz, head_part, shared_part):
    heads = sz.heads
    pad = ((0, 0), (0, sz.channels - heads * HDIM))
    taps = head_part[:, : CONV * HDIM].reshape(heads, CONV, HDIM).transpose(1, 0, 2)
    taps = jnp.pad(taps.reshape(CONV, heads * HDIM), pad)
    bias = head_part[:, (CONV + 1) * HDIM : (CONV + 2) * HDIM].reshape(1, -1)
    gain = head_part[:, CONV * HDIM : (CONV + 1) * HDIM].reshape(1, -1)
    skip = jnp.repeat(head_part[:, -1], HDIM).reshape(1, -1)
    state_taps = shared_part[: CONV * 2 * NSTATE].reshape(CONV, 2 * NSTATE)
    state_bias = shared_part[CONV * 2 * NSTATE : (CONV + 1) * 2 * NSTATE].reshape(1, -1)
    in_gain = shared_part[(CONV + 1) * 2 * NSTATE :].reshape(1, -1)

    def row(value):
        return jnp.pad(value, ((0, 0), (0, sz.width - value.shape[1])))

    rows = [
        row(jnp.concatenate([taps, state_taps], axis=1)),
        row(jnp.concatenate([jnp.pad(bias, pad), state_bias], axis=1)),
        row(gain),
        row(skip),
        row(head_part[:, -3].reshape(1, -1)),
        row(-jnp.exp(head_part[:, -2]).reshape(1, -1)),
        in_gain,
        jnp.zeros((16 - GAIN_ROW - 1, sz.width), F32),
    ]
    return jnp.concatenate(rows, axis=0)


def forward_core(sz, layer, resets, gathered, weights, weight_out, pack, rows):
    block, chunk, chans = STRETCH, CHUNK, sz.channels
    subs = block // chunk
    shards = block // rows

    def kernel(
        reset_ref, h_ref, w_ref, wo_ref, pk_ref, part_ref, sq_ref, p_ref, y_ref, s_ref,
        conv_ref, state_ref,
    ):
        c = pl.program_id(0)
        keep = 1.0 - reset_ref[c]

        @pl.when(c == 0)
        def _():
            conv_ref[...] = jnp.zeros_like(conv_ref)
            state_ref[...] = jnp.zeros_like(state_ref)

        p_ref[...] = nn(h_ref[...], w_ref[...])
        inner = p_ref[:, chans : 2 * chans]
        state_raw = p_ref[:, 2 * chans : sz.dt].astype(BF16).astype(F32)
        conv_ref[0:8, :] = conv_ref[block : block + 8, :] * keep
        conv_ref[8 : 8 + block, :chans] = inner
        conv_ref[8 : 8 + block, chans:] = state_raw
        pre = pk_ref[CONV : CONV + 1, : sz.conv] + pk_ref[0:1, : sz.conv] * conv_ref[8 : 8 + block, :]
        for tap in range(1, CONV):
            pre = pre + pk_ref[tap : tap + 1, : sz.conv] * conv_ref[8 - tap : 8 - tap + block, :]
        act = pre * sigmoid(pre)
        step = softplus(p_ref[:, sz.dt :] + pk_ref[7:8, :LANES])
        decay = step * pk_ref[8:9, :LANES]
        mask = lower_mask(chunk)
        lower = mask.astype(F32)
        lane = lax.broadcasted_iota(jnp.int32, (chunk, LANES), 1)
        for sub in range(subs):
            span = slice(sub * chunk, (sub + 1) * chunk)
            if sub == 0:
                state_ref[...] = state_ref[...] * keep
            s_ref[sub] = state_ref[...]
            dt = step[span]
            log_decay = nn(lower, decay[span], HIGH)
            flat = step_rows(log_decay, dt)
            writer = act[span, chans : chans + NSTATE].astype(BF16)
            reader = act[span, chans + NSTATE :].astype(BF16)
            cross = nt(reader, writer)
            for pair in range(sz.padded // 2):
                cols = slice(pair * LANES, (pair + 1) * LANES)
                x = act[span, cols]
                total = jnp.zeros((chunk, LANES), F32)
                for side in range(2):
                    head = 2 * pair + side
                    gap = log_decay[:, head : head + 1] - flat[head : head + 1, :]
                    weight = cross * jnp.exp(jnp.where(mask, gap, -1e30)) * flat[8 + head : 9 + head, :]
                    part = jnp.where((lane < HDIM) == (side == 0), x, 0.0).astype(BF16)
                    total = total + nn(weight.astype(BF16), part)
                logs = halves(log_decay[:, 2 * pair : 2 * pair + 1], log_decay[:, 2 * pair + 1 : 2 * pair + 2])
                dts = halves(dt[:, 2 * pair : 2 * pair + 1], dt[:, 2 * pair + 1 : 2 * pair + 2])
                old = state_ref[:, cols]
                total = total + jnp.exp(logs) * nn(reader, old.astype(BF16))
                last = logs[chunk - 1 : chunk, :]
                moved_in = (x * jnp.exp(last - logs) * dts).astype(BF16)
                state_ref[:, cols] = jnp.exp(last) * old + tn(writer, moved_in)
                y_ref[span, cols] = total + pk_ref[6:7, cols] * x
        z = p_ref[:, :chans]
        gated = y_ref[...] * z * sigmoid(z)
        square = nt(jnp.ones((8, chans), F32), gated * gated, HIGH)
        for k in range(shards):
            sq_ref[k] = square[:, k * rows : (k + 1) * rows]
        low = (gated * pk_ref[5:6, :chans]).astype(BF16)
        part_ref[...] = nn(low, wo_ref[...]).astype(BF16)

    width = sz.width
    return pl.pallas_call(
        kernel,
        grid=(sz.blocks,),
        out_shape=[
            jax.ShapeDtypeStruct((sz.tokens, width), BF16),
            jax.ShapeDtypeStruct((sz.tokens // rows, 8, rows), F32),
            jax.ShapeDtypeStruct((sz.tokens, sz.cols), F32),
            jax.ShapeDtypeStruct((sz.tokens, chans), F32),
            jax.ShapeDtypeStruct((sz.tokens // chunk, NSTATE, chans), F32),
        ],
        in_specs=[
            pl.BlockSpec(memory_space=pltpu.SMEM),
            pl.BlockSpec((block, width), lambda c: (c, 0)),
            pl.BlockSpec((None, width, sz.cols), lambda c: (layer, 0, 0)),
            pl.BlockSpec((None, chans, width), lambda c: (layer, 0, 0)),
            pl.BlockSpec((None, 16, width), lambda c: (layer, 0, 0)),
        ],
        out_specs=[
            pl.BlockSpec((block, width), lambda c: (c, 0)),
            pl.BlockSpec((shards, 8, rows), lambda c: (c, 0, 0)),
            pl.BlockSpec((block, sz.cols), lambda c: (c, 0)),
            pl.BlockSpec((block, chans), lambda c: (c, 0)),
            pl.BlockSpec((subs, NSTATE, chans), lambda c: (c, 0, 0)),
        ],
        scratch_shapes=[
            pltpu.VMEM((block + 8, sz.conv), F32),
            pltpu.VMEM((NSTATE, chans), F32),
        ],
        compiler_params=pltpu.CompilerParams(vmem_limit_bytes=VMEM_LIMIT),
        name="forward_core",
    )(resets, gathered, weights, weight_out, pack)


def backward_core(sz, layer, resets, grads, proj, mixed, states, stats, weights, weight_out, pack, order):
    block, chunk, chans = STRETCH, CHUNK, sz.channels
    subs = block // chunk
    blocks = sz.blocks

    def kernel(
        reset_ref, g_ref, p_ref, halo_ref, y_ref, s_ref, st_ref, w_ref, wo_ref, pk_ref, order_ref, sum_ref,
        gh_ref, gt_ref, q_ref, acc_ref,
        conv_ref, dpre_ref, dact_ref, dlog_ref, ddt_ref, dstate_ref,
    ):
        i = pl.program_id(0)
        c = blocks - 1 - i
        keep = 1.0 - reset_ref[c]
        after = 1.0 - reset_ref[jnp.minimum(c + 1, blocks - 1)]

        @pl.when(i == 0)
        def _():
            dpre_ref[...] = jnp.zeros_like(dpre_ref)
            dstate_ref[...] = jnp.zeros_like(dstate_ref)
            acc_ref[...] = jnp.zeros_like(acc_ref)

        conv_ref[0:8, :chans] = halo_ref[:, chans : 2 * chans] * keep
        conv_ref[0:8, chans:] = halo_ref[:, 2 * chans : sz.dt].astype(BF16).astype(F32) * keep
        conv_ref[8 : 8 + block, :chans] = p_ref[:, chans : 2 * chans]
        conv_ref[8 : 8 + block, chans:] = p_ref[:, 2 * chans : sz.dt].astype(BF16).astype(F32)
        pre = pk_ref[CONV : CONV + 1, : sz.conv] + pk_ref[0:1, : sz.conv] * conv_ref[8 : 8 + block, :]
        for tap in range(1, CONV):
            pre = pre + pk_ref[tap : tap + 1, : sz.conv] * conv_ref[8 - tap : 8 - tap + block, :]
        gate = sigmoid(pre)
        act = pre * gate
        slope = gate * (1.0 + pre * (1.0 - gate))
        step_in = p_ref[:, sz.dt :] + pk_ref[7:8, :LANES]
        step = softplus(step_in)
        rate = pk_ref[8:9, :LANES]
        decay = step * rate
        z = p_ref[:, :chans]
        zgate = sigmoid(z)
        zsilu = z * zgate
        y = y_ref[...]
        gated = y * zsilu
        gain = pk_ref[5:6, :chans]
        skip = pk_ref[6:7, :chans]
        scale = st_ref[:, 0:1]
        along = st_ref[:, 1:2]
        grad_q = nt(g_ref[...], wo_ref[...])
        q_ref[...] = (gated * scale * gain).astype(BF16)
        acc_ref[5:6, :chans] += jnp.sum(grad_q * gated * scale, axis=0, keepdims=True)
        dgated = grad_q * gain * scale - gated * (scale * scale * along * (1.0 / (HEADS * HDIM)))
        dy = dgated * zsilu
        dz = dgated * y * zgate * (1.0 + z * (1.0 - zgate))
        x_all = act[:, :chans]
        acc_ref[6:7, :chans] += jnp.sum(dy * x_all, axis=0, keepdims=True)
        scan_dot = nn(dy * (y - skip * x_all), sum_ref[...], HIGH)
        mask = lower_mask(chunk)
        lower = mask.astype(F32)
        lane = lax.broadcasted_iota(jnp.int32, (chunk, LANES), 1)
        for sub in reversed(range(subs)):
            span = slice(sub * chunk, (sub + 1) * chunk)
            dt = step[span]
            log_decay = nn(lower, decay[span], HIGH)
            flat = step_rows(log_decay, dt)
            writer = act[span, chans : chans + NSTATE].astype(BF16)
            reader = act[span, chans + NSTATE :].astype(BF16)
            cross = nt(reader, writer)
            cross_grad = jnp.zeros((chunk, chunk), F32)
            dreader = jnp.zeros((chunk, NSTATE), F32)
            dwriter = jnp.zeros((chunk, NSTATE), F32)
            fall = jnp.zeros((LANES, chunk), F32)
            row = lax.broadcasted_iota(jnp.int32, (LANES, chunk), 0)
            reach = []
            carried = []
            for pair in range(sz.padded // 2):
                cols = slice(pair * LANES, (pair + 1) * LANES)
                x = act[span, cols]
                g = dy[span, cols]
                logs = halves(log_decay[:, 2 * pair : 2 * pair + 1], log_decay[:, 2 * pair + 1 : 2 * pair + 2])
                dts = halves(dt[:, 2 * pair : 2 * pair + 1], dt[:, 2 * pair + 1 : 2 * pair + 2])
                last = logs[chunk - 1 : chunk, :]
                old = s_ref[sub, :, cols]
                dnew = dstate_ref[:, cols]
                old_low, dnew_low = old.astype(BF16), dnew.astype(BF16)
                faded = (g * jnp.exp(logs)).astype(BF16)
                tail = jnp.exp(last - logs)
                dreader = dreader + nt(faded, old_low)
                ahead = nn(writer, dnew_low)
                dx = g * skip[:, cols] + ahead * tail * dts
                dwriter = dwriter + nt((x * tail * dts).astype(BF16), dnew_low)
                reach.append(x * ahead * tail)
                carried.append(jnp.sum(old * dnew, axis=0, keepdims=True) * jnp.exp(last))
                dstate_ref[:, cols] = jnp.exp(last) * dnew + tn(reader, faded)
                x_low = x.astype(BF16)
                for side in range(2):
                    head = 2 * pair + side
                    own = (lane < HDIM) == (side == 0)
                    g_own = jnp.where(own, g, 0.0).astype(BF16)
                    gap = log_decay[:, head : head + 1] - flat[head : head + 1, :]
                    decays = jnp.exp(jnp.where(mask, gap, -1e30))
                    steps = flat[8 + head : 9 + head, :]
                    spread = nt(g_own, x_low) * decays
                    weight = cross * decays * steps
                    dx = dx + tn(weight.astype(BF16), g_own)
                    cross_grad = cross_grad + spread * steps
                    sums = jnp.sum(spread * cross, axis=0, keepdims=True)
                    fall = fall + jnp.where(row == head, sums, 0.0)
                dact_ref[span, cols] = dx
            cross_low = cross_grad.astype(BF16)
            dact_ref[span, chans : chans + NSTATE] = dwriter + tn(cross_low, reader)
            dact_ref[span, chans + NSTATE :] = dreader + nn(cross_low, writer)
            reach = nn(jnp.concatenate(reach, axis=1), sum_ref[...], HIGH)
            carried = nn(jnp.concatenate(carried, axis=1), sum_ref[...], HIGH)
            direct = jnp.transpose(fall) + reach
            given = dt * reach
            dlog = scan_dot[span] - dt * direct
            ends = jnp.sum(given, axis=0, keepdims=True) + carried
            at_end = lax.broadcasted_iota(jnp.int32, (chunk, LANES), 0) == chunk - 1
            dlog = dlog + jnp.where(at_end, ends, 0.0)
            ddecay = tn(lower, dlog, HIGH)
            ddt_ref[span, :] = direct + ddecay * rate
            acc_ref[8:9, :LANES] += jnp.sum(ddecay * dt, axis=0, keepdims=True)
        dstate_ref[...] = dstate_ref[...] * keep
        ddt_raw = ddt_ref[...] * sigmoid(step_in)
        acc_ref[7:8, :LANES] += jnp.sum(ddt_raw, axis=0, keepdims=True)
        dpre_ref[block : block + 8, :] = dpre_ref[0:8, :] * after
        dpre_ref[0:block, :] = dact_ref[...] * slope
        raw = conv_ref[8 : 8 + block, :]
        acc_ref[CONV : CONV + 1, : sz.conv] += jnp.sum(dpre_ref[0:block, :], axis=0, keepdims=True)
        draw = jnp.zeros((block, sz.conv), F32)
        for tap in range(CONV):
            later = dpre_ref[tap : tap + block, :]
            draw = draw + pk_ref[tap : tap + 1, : sz.conv] * later
            acc_ref[tap : tap + 1, : sz.conv] += jnp.sum(raw * later, axis=0, keepdims=True)
        low = jnp.concatenate(
            [dz.astype(BF16), draw.astype(BF16), ddt_raw.astype(BF16)], axis=1
        )
        gh_ref[...] = nt(low, w_ref[...]).astype(BF16)
        gt_ref[...] = nt(order_ref[...], low).astype(BF16)

    width = sz.width
    back = blocks - 1
    per = block // 8
    return pl.pallas_call(
        kernel,
        grid=(blocks,),
        out_shape=[
            jax.ShapeDtypeStruct((sz.tokens, width), BF16),
            jax.ShapeDtypeStruct((sz.grad_rows, sz.tokens), BF16),
            jax.ShapeDtypeStruct((sz.tokens, chans), BF16),
            jax.ShapeDtypeStruct((16, width), F32),
        ],
        in_specs=[
            pl.BlockSpec(memory_space=pltpu.SMEM),
            pl.BlockSpec((block, width), lambda i: (back - i, 0)),
            pl.BlockSpec((block, sz.cols), lambda i: (back - i, 0)),
            pl.BlockSpec((8, sz.cols), lambda i: (jnp.maximum((back - i) * per - 1, 0), 0)),
            pl.BlockSpec((block, chans), lambda i: (back - i, 0)),
            pl.BlockSpec((subs, NSTATE, chans), lambda i: (back - i, 0, 0)),
            pl.BlockSpec((block, LANES), lambda i: (back - i, 0)),
            pl.BlockSpec((None, width, sz.cols), lambda i: (layer, 0, 0)),
            pl.BlockSpec((None, chans, width), lambda i: (layer, 0, 0)),
            pl.BlockSpec((None, 16, width), lambda i: (layer, 0, 0)),
            pl.BlockSpec((sz.grad_rows, sz.cols), lambda i: (0, 0)),
            pl.BlockSpec((chans, LANES), lambda i: (0, 0)),
        ],
        out_specs=[
            pl.BlockSpec((block, width), lambda i: (back - i, 0)),
            pl.BlockSpec((sz.grad_rows, block), lambda i: (0, back - i)),
            pl.BlockSpec((block, chans), lambda i: (back - i, 0)),
            pl.BlockSpec((16, width), lambda i: (0, 0)),
        ],
        scratch_shapes=[
            pltpu.VMEM((block + 8, sz.conv), F32),
            pltpu.VMEM((block + 8, sz.conv), F32),
            pltpu.VMEM((block, sz.conv), F32),
            pltpu.VMEM((chunk, LANES), F32),
            pltpu.VMEM((block, LANES), F32),
            pltpu.VMEM((NSTATE, chans), F32),
        ],
        compiler_params=pltpu.CompilerParams(vmem_limit_bytes=VMEM_LIMIT),
        name="backward_core",
    )(resets, grads, proj, proj, mixed, states, stats, weights, weight_out, pack, order, sz.head_sum())


def weight_grads(sz, grads_t, gathered, scaled, out_grads):
    cols = 256

    def kernel(gt_ref, h_ref, q_ref, g_ref, in_ref, out_ref):
        in_ref[...] = nn(gt_ref[...], h_ref[...]).astype(BF16)
        out_ref[...] = tn(q_ref[...], g_ref[...]).astype(BF16)

    tokens, width, chans = sz.tokens, sz.width, sz.channels
    return pl.pallas_call(
        kernel,
        grid=(width // cols,),
        out_shape=[
            jax.ShapeDtypeStruct((sz.grad_rows, width), BF16),
            jax.ShapeDtypeStruct((chans, width), BF16),
        ],
        in_specs=[
            pl.BlockSpec((sz.grad_rows, tokens), lambda i: (0, 0)),
            pl.BlockSpec((tokens, cols), lambda i: (0, i)),
            pl.BlockSpec((tokens, chans), lambda i: (0, 0)),
            pl.BlockSpec((tokens, cols), lambda i: (0, i)),
        ],
        out_specs=[
            pl.BlockSpec((sz.grad_rows, cols), lambda i: (0, i)),
            pl.BlockSpec((chans, cols), lambda i: (0, i)),
        ],
        compiler_params=pltpu.CompilerParams(vmem_limit_bytes=VMEM_LIMIT),
        name="weight_grads",
    )(grads_t, gathered, scaled, out_grads)


def input_norm(residual, in_gain):
    return (
        residual
        * lax.rsqrt(jnp.mean(residual * residual, axis=1, keepdims=True) + EPS_NORM)
        * in_gain
    )


def adam_update(weight, moment, second, gradient, rate, decay):
    moment_new = BETA_ONE * moment + (1.0 - BETA_ONE) * gradient
    second_new = BETA_TWO * second + (1.0 - BETA_TWO) * gradient * gradient
    corrected = moment_new / (1.0 - BETA_ONE**ADAM_STEP)
    corrected_sq = second_new / (1.0 - BETA_TWO**ADAM_STEP)
    weight_new = weight - rate * (corrected / (jnp.sqrt(corrected_sq) + ADAM_EPS) + decay * weight)
    return (weight_new, moment_new, second_new)


def shards(
    inputs,
    cotangent,
    valid_lengths,
    proj_in,
    proj_in_m,
    proj_in_v,
    proj_state,
    proj_state_m,
    proj_state_v,
    proj_out,
    proj_out_m,
    proj_out_v,
    head_params,
    head_m,
    head_v,
    shared_params,
    shared_m,
    shared_v,
):
    section = lax.axis_index("section")
    head_idx = lax.axis_index("head")
    count = lax.axis_size("head")
    rows, width = inputs.shape[1], inputs.shape[2]
    heads = head_params.shape[1]
    tokens = rows * count
    sz = Sizes(heads, tokens, width)
    order = sz.order()
    start_block, seq_length, resets = seq_layout(
        lax.dynamic_index_in_dim(valid_lengths, section, 0, keepdims=False)
    )
    token = head_idx * rows + jnp.arange(rows, dtype=jnp.int32)
    own_block = token // STRETCH
    position = token - start_block[own_block] * STRETCH
    live = (position < seq_length[own_block]).astype(F32)[:, None]
    first_in = lax.dynamic_index_in_dim(inputs, section, 0, keepdims=False).astype(F32)
    last_grad = lax.dynamic_index_in_dim(cotangent, section, 0, keepdims=False).astype(F32)
    own_weights = prepare_weights(sz, proj_in[0], proj_state[0], order)
    own_out = proj_out[0].astype(BF16)
    own_out = jnp.pad(own_out, ((0, sz.channels - own_out.shape[0]), (0, 0)))
    own_pack = pack_params(sz, head_params[0], shared_params[0])
    weights, weight_out, pack = both_sections([own_weights, own_out, own_pack], 0)

    kept = []
    residual = first_in
    for layer in range(2):
        in_gain = pack[layer, GAIN_ROW]
        normed = input_norm(residual, in_gain).astype(BF16)
        (gathered,) = gather_rows(count, normed, None, 1)
        partial, squares, proj, mixed, states = forward_core(
            sz, layer, resets, gathered, weights, weight_out, pack, rows
        )
        summed, all_squares = scatter_rows(count, partial, squares, 2)
        scale = lax.rsqrt(jnp.sum(all_squares, axis=0)[0] / (HEADS * HDIM) + EPS_NORM)
        branch = summed * scale[:, None]
        result = (residual + live * branch).astype(BF16)
        kept.append((residual, in_gain, gathered, proj, mixed, states, scale, branch, result))
        residual = result.astype(F32)

    upstream = last_grad
    made = [None, None]
    input_grads = [None, None]
    for layer in (1, 0):
        residual, in_gain, gathered, proj, mixed, states, scale, branch, _ = kept[layer]
        out_grad = (live * upstream).astype(BF16)
        along = jnp.sum(out_grad.astype(F32) * branch, axis=1)
        stats = jnp.stack([scale, along])
        stats = jnp.pad(stats, ((0, 6), (0, LANES - rows)))
        out_grads, all_stats = gather_rows(count, out_grad, stats, 3)
        all_stats = all_stats[:, :2, :rows].transpose(0, 2, 1).reshape(tokens, 2)
        all_stats = jnp.pad(all_stats, ((0, 0), (0, LANES - 2)))
        grad_rows, grads_t, scaled, small = backward_core(
            sz, layer, resets, out_grads, proj, mixed, states, all_stats, weights, weight_out, pack, order
        )
        (grad_normed,) = scatter_rows(count, grad_rows, None, 4)
        in_t, out_w = weight_grads(sz, grads_t, gathered, scaled, out_grads)
        _, in_pull = jax.vjp(input_norm, residual, in_gain)
        grad_res, grad_in_gain = in_pull(grad_normed)
        small = jnp.concatenate(
            [small[:GAIN_ROW], grad_in_gain[None], small[GAIN_ROW + 1 :]], axis=0
        )
        made[layer] = [in_t, out_w, small]
        grad_res = grad_res + upstream
        input_grads[layer] = grad_res
        upstream = grad_res.astype(BF16).astype(F32)

    sum_t, sum_out, small, layer_outs, grad_buffer = trade_sections(
        list(zip(made[0], made[1])),
        [(kept[0][8], kept[1][8]), (input_grads[0], input_grads[1])],
        5,
    )
    grad_in = sum_t[: sz.master].T
    grad_out = sum_out[: heads * HDIM]

    state_part = sum_t[sz.master_pad :].astype(BF16)
    share_rows = 16 * count
    (state_own,) = scatter_rows(count, state_part.reshape(share_rows, -1), None, 6)
    (state_all,) = gather_rows(count, state_own.astype(BF16), None, 7)
    grad_state = state_all.reshape(state_part.shape).astype(F32).T
    chans = heads * HDIM
    conv_rows = small[: CONV + 1, sz.channels : sz.conv].reshape(-1)
    shared_own = jnp.concatenate([conv_rows, small[GAIN_ROW]])
    shared_rows = -(-shared_own.shape[0] // (8 * LANES)) * 8
    shared_own = jnp.pad(shared_own, (0, shared_rows * LANES - shared_own.shape[0]))
    shared_all = gather_small(count, shared_own.reshape(shared_rows, LANES), 8)
    grad_shared = jnp.sum(shared_all, axis=0).reshape(-1)[: shared_params.shape[1]]
    head_part = head_params[0]
    taps = small[:CONV, :chans].reshape(CONV, heads, HDIM).transpose(1, 0, 2).reshape(heads, -1)
    grad_head = jnp.concatenate(
        [
            taps,
            small[5, :chans].reshape(heads, HDIM),
            small[CONV, :chans].reshape(heads, HDIM),
            small[7, :heads][:, None],
            (small[8, :heads] * -jnp.exp(head_part[:, -2]))[:, None],
            jnp.sum(small[6, :chans].reshape(heads, HDIM), axis=1)[:, None],
        ],
        axis=1,
    )
    local_sq = (
        jnp.sum(sum_t[: sz.master] ** 2) + jnp.sum(grad_out * grad_out) + jnp.sum(grad_head * grad_head)
    )
    local_sq = local_sq + (jnp.sum(grad_state * grad_state) + jnp.sum(grad_shared * grad_shared)) / count
    sums = gather_small(count, jnp.full((8, LANES), local_sq, F32), 9)
    section_sq = jnp.sum(sums[:, 0, 0])
    norm_sq = section_sq + lax.ppermute(section_sq, "section", [(0, 1), (1, 0)])
    grad_norm = jnp.sqrt(norm_sq)
    threshold = CLIP_COEF * PARAMS**0.5
    clip_scale = threshold / jnp.maximum(grad_norm, threshold)
    new_in = adam_update(
        proj_in[0], proj_in_m[0], proj_in_v[0], clip_scale * grad_in, LEARN_MATRIX, WEIGHT_DECAY
    )
    new_state = adam_update(
        proj_state[0], proj_state_m[0], proj_state_v[0], clip_scale * grad_state, LEARN_MATRIX, WEIGHT_DECAY
    )
    new_out = adam_update(
        proj_out[0], proj_out_m[0], proj_out_v[0], clip_scale * grad_out, LEARN_MATRIX, WEIGHT_DECAY
    )
    new_head = adam_update(
        head_part, head_m[0], head_v[0], clip_scale * grad_head, LEARN_VECTOR, 0.0
    )
    new_shared = adam_update(
        shared_params[0], shared_m[0], shared_v[0], clip_scale * grad_shared, LEARN_VECTOR, 0.0
    )
    return (
        layer_outs[None],
        grad_buffer[None],
        grad_norm,
        new_in[0][None],
        new_in[1][None],
        new_in[2][None],
        new_in[0][None].astype(BF16),
        new_state[0][None],
        new_state[1][None],
        new_state[2][None],
        new_state[0][None].astype(BF16),
        new_out[0][None],
        new_out[1][None],
        new_out[2][None],
        new_out[0][None].astype(BF16),
        new_head[0][None],
        new_head[1][None],
        new_head[2][None],
        new_shared[0][None],
        new_shared[1][None],
        new_shared[2][None],
    )


def solution(mesh):
    in_specs = (
        P(None, "head", None),
        P(None, "head", None),
        P(),
        P("section", None, "head"),
        P("section", None, "head"),
        P("section", None, "head"),
        P("section", None, None),
        P("section", None, None),
        P("section", None, None),
        P("section", "head", None),
        P("section", "head", None),
        P("section", "head", None),
        P("section", "head", None),
        P("section", "head", None),
        P("section", "head", None),
        P("section", None),
        P("section", None),
        P("section", None),
    )
    out_specs = (
        P("section", None, "head", None),
        P("section", None, "head", None),
        P(),
        P("section", None, "head"),
        P("section", None, "head"),
        P("section", None, "head"),
        P("section", None, "head"),
        P("section", None, None),
        P("section", None, None),
        P("section", None, None),
        P("section", None, None),
        P("section", "head", None),
        P("section", "head", None),
        P("section", "head", None),
        P("section", "head", None),
        P("section", "head", None),
        P("section", "head", None),
        P("section", "head", None),
        P("section", None),
        P("section", None),
        P("section", None),
    )
    return jax.shard_map(shards, mesh=mesh, in_specs=in_specs, out_specs=out_specs, check_vma=False)
```

time: 3550 us -> 724 us (0.20)
  waiting for transfers between devices: 1610 us -> 0.01 us
  local copies, waits for them, and re-layouts: 676 us -> 72.3 us
  Pallas kernels: 0 us -> 553 us
  matrix products: 419 us -> 0 us
  blocking collectives: 353 us -> 0 us
  other arithmetic: 404 us -> 69.7 us
    reduce_scatter x9 -> x0, waiting for transfers between devices: 1270 us -> none  [the longest x3 575 us: shards(): lax.psum_scatter(row_product_back(low_grad_proj, low_in), 'head', scatter...]
    pallas_call x0 -> x21, Pallas kernels: none -> 553 us  [the longest x5 214 us: scatter_rows(): pl.pallas_call(kernel, out_shape=out_shape, in_specs=[VMEM_SPEC] * len(op...]
    dot_general x243 -> x0, matrix products: 419 us -> none  [the longest x48 99 us: advance(): jnp.einsum('ijh,jhp->ihp', block_weights, block_inner, precision=HIGH)]
    psum x8 -> x0, blocking collectives: 264 us -> none  [the longest x3 78.2 us: shards(): grad_squares = lax.psum(grad_squares, 'head')]
    dynamic_update_slice x75 -> x0, local copies, waits for them, and re-layouts: 262 us -> none  [the longest x72 261 us: block_scan(): lax.scan(jax.checkpoint(advance), start_state, pieces)]
    all_gather x6 -> x0, waiting for transfers between devices: 248 us -> none  [the longest x3 152 us: shards(): grad_full = lax.all_gather(out_grad, 'head', axis=0, tiled=True)]
    another operation x160 -> x3, other arithmetic: 158 us -> 1.43 us  [the longest x2 1.25 us: shards(): stats = jnp.stack([scale, along])]
    psum x1 -> x0, waiting for transfers between devices: 94.5 us -> none  [shards(): shared_grad, state_grad = lax.psum((acc_shared, acc_state_w), 'head')]
  transfers between devices with their start and end apart: 20 -> 1, of which waited for: 19 -> 0; matrix products, arithmetic and copies ran while one was open for 12% -> 1% of each run, Pallas kernels for 0% -> 0%
where the time goes in v1:
time: 724 us; the launch traced here: 712 us
  Pallas kernels  553 us (76%)
  local copies, waits for them, and re-layouts  72.3 us (10%)
  other arithmetic  69.7 us (10%)
  starting transfers between devices  10.6 us (1%)
    pallas_call x5, Pallas kernels, scatter_rows(): pl.pallas_call(kernel, out_shape=out_shape, in_specs=[VMEM_SPEC] * len(op...  214 us
    pallas_call x5, Pallas kernels, gather_rows(): pl.pallas_call(kernel, out_shape=out_shape, in_specs=[VMEM_SPEC] * len(op...  163 us
    unnamed x53, local copies, waits for them, and re-layouts  53.9 us
    pallas_call x2, Pallas kernels, backward_core(): pl.pallas_call(kernel, grid=(blocks,), out_shape=[jax.ShapeDtypeStruct((s...  53.8 us
    pallas_call x2, Pallas kernels, forward_core(): pl.pallas_call(kernel, grid=(sz.blocks,), out_shape=[jax.ShapeDtypeStruct...  32.5 us
    pallas_call x2, Pallas kernels, gather_small(): pl.pallas_call(kernel, out_shape=jax.ShapeDtypeStruct((count,) + block.sh...  22.8 us
    pallas_call x2, Pallas kernels, weight_grads(): pl.pallas_call(kernel, grid=(width // cols,), out_shape=[jax.ShapeDtypeSt...  22.5 us
    pallas_call x1, Pallas kernels, trade_sections(): pl.pallas_call(kernel, out_shape=shapes, in_specs=[VMEM_SPEC] * (2 * numb...  20.7 us
  transfers between devices with their start and end apart: 1, of which 0 were waited for; matrix products, arithmetic and copies ran while one was open for 1% of the time, Pallas kernels for 0%

profile of v1, /device:TPU:13, one launch (start us, length us, event | category | flops | bytes accessed | tf_op | source)
XLA Modules:
  0.0 712.3 jit_solution(10025620018228299118)
XLA Ops:
  6.3 11.5 %copy.143 = f32[1,2048,516]{2,1,0:T(8,128)} copy(f32[1,2048,516]{1,0,2:T(1,128)} %param.24) | data formatting | bytes 8454144
  19.0 9.6 %prepare_weights.1.refs_0_ = bf16[2048,896]{1,0:T(8,128)(2,1)} custom-call(f32[2048,516]{1,0:T(8,128)} %bitcast.215, f32[2048,256]{1,0:T(8,128)} %bitcast.217, bf16[896,896]{1,0:T(8,128)(2,1)} %constant.118.clone.order_ref), custom_call_target="tpu_custom_call" | custom-call | tf_op jit(solution)/shard_map/prepare_weights/pallas_call | solution.py:689
  28.6 1.4 concatenate.49.refs_2_
  30.0 14.2 %both_sections.1 = (bf16[2,2048,896]{2,1,0:T(8,128)(2,1)}, bf16[2,256,2048]{2,1,0:T(8,128)(2,1)}, f32[2,16,2048]{2,1,0:T(8,128)}) custom-call(bf16[2048,896]{1,0:T(8,128)(2,1)} %prepare_weights.1.refs_0_, bf16[256,2048]{1,0:T(8,128)(2,1)} %bitcast_convert_fusion.refs_1_, f32[16,2048]{1,0:T(8,128)} %concatenate.49.refs_2_), custom_call_target="tpu_custom_call" | custom-call | tf_op jit(solution)/shard_map/both_sections/pallas_call | solution.py:543
  46.1 38.5 %gather_rows.5.h_ref = bf16[1024,2048]{1,0:T(8,128)(2,1)} custom-call(bf16[64,2048]{1,0:T(8,128)(2,1)} %fusion.19.refs_0_), custom_call_target="tpu_custom_call" | custom-call | tf_op jit(solution)/shard_map/gather_rows/pallas_call | solution.py:420
  84.6 16.3 %forward_core.2 = (bf16[1024,2048]{1,0:T(8,128)(2,1)}, f32[16,8,64]{2,1,0:T(8,128)}, f32[1024,896]{1,0:T(8,128)}, f32[1024,256]{1,0:T(8,128)}, f32[8,128,256]{2,1,0:T(8,128)}) custom-call(f32[4]{0:T(128)} %get-tuple-element.210.reset_ref, bf16[1024,2048]{1,0:T(8,128)(2,1)} %gather_rows.5.h_ref, bf16[2,2048,896]{2,1,0:T(8,128)(2,1)} %get-tuple-element.60.w_ref, ...), custom_call_target="tpu_custom_call" | custom-call | tf_op jit(solution)/shard_map/forward_core/pallas_call | solution.py:802
  100.8 52.1 %scatter_rows.5 = (f32[64,2048]{1,0:T(8,128)}, f32[16,8,64]{2,1,0:T(8,128)}) custom-call(bf16[1024,2048]{1,0:T(8,128)(2,1)} %get-tuple-element.62.refs_0_, f32[16,8,64]{2,1,0:T(8,128)} %get-tuple-element.63.refs_1_), custom_call_target="tpu_custom_call" | custom-call | tf_op jit(solution)/shard_map/scatter_rows/pallas_call | solution.py:472
  155.4 5.2 compare_convert_fusion
  160.6 1.3 fusion.25
  162.8 34.3 %gather_rows.6.h_ref = bf16[1024,2048]{1,0:T(8,128)(2,1)} custom-call(bf16[64,2048]{1,0:T(8,128)(2,1)} %fusion.21.refs_0_), custom_call_target="tpu_custom_call" | custom-call | tf_op jit(solution)/shard_map/gather_rows/pallas_call | solution.py:420
  197.1 16.3 %forward_core.3 = (bf16[1024,2048]{1,0:T(8,128)(2,1)}, f32[16,8,64]{2,1,0:T(8,128)}, f32[1024,896]{1,0:T(8,128)}, f32[1024,256]{1,0:T(8,128)}, f32[8,128,256]{2,1,0:T(8,128)}) custom-call(f32[4]{0:T(128)} %get-tuple-element.210.reset_ref, bf16[1024,2048]{1,0:T(8,128)(2,1)} %gather_rows.6.h_ref, bf16[2,2048,896]{2,1,0:T(8,128)(2,1)} %get-tuple-element.60.w_ref, ...), custom_call_target="tpu_custom_call" | custom-call | tf_op jit(solution)/shard_map/forward_core/pallas_call | solution.py:802
  213.3 51.7 %scatter_rows.6 = (f32[64,2048]{1,0:T(8,128)}, f32[16,8,64]{2,1,0:T(8,128)}) custom-call(bf16[1024,2048]{1,0:T(8,128)(2,1)} %get-tuple-element.66.refs_0_, f32[16,8,64]{2,1,0:T(8,128)} %get-tuple-element.67.refs_1_), custom_call_target="tpu_custom_call" | custom-call | tf_op jit(solution)/shard_map/scatter_rows/pallas_call | solution.py:472
  266.0 2.2 multiply_reduce_fusion.3
  268.8 36.4 %gather_rows.7 = (bf16[1024,2048]{1,0:T(8,128)(2,1)}, f32[16,8,128]{2,1,0:T(8,128)}) custom-call(bf16[64,2048]{1,0:T(8,128)(2,1)} %get-tuple-element.207.refs_0_, f32[8,128]{1,0:T(8,128)} %select_maximum_fusion.3.refs_1_), custom_call_target="tpu_custom_call" | custom-call | tf_op jit(solution)/shard_map/gather_rows/pallas_call | solution.py:420
  307.1 26.9 %backward_core.2 = (bf16[1024,2048]{1,0:T(8,128)(2,1)}, bf16[896,1024]{1,0:T(8,128)(2,1)}, bf16[1024,256]{1,0:T(8,128)(2,1)}, f32[16,2048]{1,0:T(8,128)}) custom-call(f32[4]{0:T(128)} %get-tuple-element.210.reset_ref, bf16[1024,2048]{1,0:T(8,128)(2,1)} %get-tuple-element.70.g_ref, f32[1024,896]{1,0:T(8,128)} %get-tuple-element.71.p_ref.halo_ref, ...), custom_call_target="tpu_custom_call" | custom-call | tf_op jit(solution)/shard_map/backward_core/pallas_call | solution.py:975
  334.0 49.0 %scatter_rows.7 = f32[64,2048]{1,0:T(8,128)} custom-call(bf16[1024,2048]{1,0:T(8,128)(2,1)} %get-tuple-element.75.refs_0_), custom_call_target="tpu_custom_call" | custom-call | tf_op jit(solution)/shard_map/scatter_rows/pallas_call | solution.py:472
  383.0 1.3 fusion.22
  384.4 2.1 multiply_reduce_fusion.2
  387.1 35.6 %gather_rows.8 = (bf16[1024,2048]{1,0:T(8,128)(2,1)}, f32[16,8,128]{2,1,0:T(8,128)}) custom-call(bf16[64,2048]{1,0:T(8,128)(2,1)} %get-tuple-element.204.refs_0_, f32[8,128]{1,0:T(8,128)} %select_maximum_fusion.2.refs_1_), custom_call_target="tpu_custom_call" | custom-call | tf_op jit(solution)/shard_map/gather_rows/pallas_call | solution.py:420
  424.7 26.9 %backward_core.3 = (bf16[1024,2048]{1,0:T(8,128)(2,1)}, bf16[896,1024]{1,0:T(8,128)(2,1)}, bf16[1024,256]{1,0:T(8,128)(2,1)}, f32[16,2048]{1,0:T(8,128)}) custom-call(f32[4]{0:T(128)} %get-tuple-element.210.reset_ref, bf16[1024,2048]{1,0:T(8,128)(2,1)} %get-tuple-element.76.g_ref, f32[1024,896]{1,0:T(8,128)} %get-tuple-element.77.p_ref.halo_ref, ...), custom_call_target="tpu_custom_call" | custom-call | tf_op jit(solution)/shard_map/backward_core/pallas_call | solution.py:975
  451.6 46.6 %scatter_rows.8 = f32[64,2048]{1,0:T(8,128)} custom-call(bf16[1024,2048]{1,0:T(8,128)(2,1)} %get-tuple-element.90.refs_0_), custom_call_target="tpu_custom_call" | custom-call | tf_op jit(solution)/shard_map/scatter_rows/pallas_call | solution.py:472
  498.2 1.3 fusion.30
  499.6 2.0 convert_add_fusion.3.refs_8_
  501.6 11.2 %weight_grads.3 = (bf16[896,2048]{1,0:T(8,128)(2,1)}, bf16[256,2048]{1,0:T(8,128)(2,1)}) custom-call(bf16[896,1024]{1,0:T(8,128)(2,1)} %get-tuple-element.84.gt_ref, bf16[1024,2048]{1,0:T(8,128)(2,1)} %gather_rows.6.h_ref, bf16[1024,256]{1,0:T(8,128)(2,1)} %get-tuple-element.85.q_ref, bf16[1024,2048]{1,0:T(8,128)(2,1)} %get-tuple-element.70.g_ref), custom_call_target="tpu_custom_call" | custom-call | tf_op jit(solution)/shard_map/weight_grads/pallas_call | solution.py:1025
  512.9 11.3 %weight_grads.2 = (bf16[896,2048]{1,0:T(8,128)(2,1)}, bf16[256,2048]{1,0:T(8,128)(2,1)}) custom-call(bf16[896,1024]{1,0:T(8,128)(2,1)} %get-tuple-element.81.gt_ref, bf16[1024,2048]{1,0:T(8,128)(2,1)} %gather_rows.5.h_ref, bf16[1024,256]{1,0:T(8,128)(2,1)} %get-tuple-element.82.q_ref, bf16[1024,2048]{1,0:T(8,128)(2,1)} %get-tuple-element.76.g_ref), custom_call_target="tpu_custom_call" | custom-call | tf_op jit(solution)/shard_map/weight_grads/pallas_call | solution.py:1025
  524.9 20.7 %trade_sections.1 = (f32[896,2048]{1,0:T(8,128)}, f32[256,2048]{1,0:T(8,128)}, f32[16,2048]{1,0:T(8,128)}, bf16[2,64,2048]{2,1,0:T(8,128)(2,1)}, f32[2,64,2048]{2,1,0:T(8,128)}) custom-call(bf16[896,2048]{1,0:T(8,128)(2,1)} %get-tuple-element.83.refs_0_, bf16[896,2048]{1,0:T(8,128)(2,1)} %get-tuple-element.86.refs_1_, ...), custom_call_target="tpu_custom_call" | custom-call | tf_op jit(solution)/shard_map/trade_sections/pallas_call | solution.py:592
  549.4 2.7 slice.189.refs_0_
  552.1 3.9 multiply_reduce_fusion
  556.6 12.5 %gather_small.2 = f32[16,32,128]{2,1,0:T(8,128)} custom-call(f32[32,128]{1,0:T(8,128)} %fusion.33.in_ref), custom_call_target="tpu_custom_call" | custom-call | tf_op jit(solution)/shard_map/gather_small/pallas_call | solution.py:492
  570.7 14.2 %scatter_rows.9 = f32[16,2048]{1,0:T(8,128)} custom-call(bf16[256,2048]{1,0:T(8,128)(2,1)} %slice.189.refs_0_), custom_call_target="tpu_custom_call" | custom-call | tf_op jit(solution)/shard_map/scatter_rows/pallas_call | solution.py:472
  584.9 1.5 convert_element_type.120.refs_0_
  586.4 18.1 %gather_rows.9 = bf16[256,2048]{1,0:T(8,128)(2,1)} custom-call(bf16[16,2048]{1,0:T(8,128)(2,1)} %convert_element_type.120.refs_0_), custom_call_target="tpu_custom_call" | custom-call | tf_op jit(solution)/shard_map/gather_rows/pallas_call | solution.py:420
  604.5 2.4 fusion.3
  613.5 10.3 %gather_small.3 = f32[16,8,128]{2,1,0:T(8,128)} custom-call(f32[8,128]{1,0:T(8,128)} %broadcast_in_dim.84.in_ref), custom_call_target="tpu_custom_call" | custom-call | tf_op jit(solution)/shard_map/gather_small/pallas_call | solution.py:492
  623.8 1.5 slice_reduce_fusion
  625.3 10.6 %collective-permute-start = (f32[]{:T(128)}, f32[]{:T(128)}, u32[]{:S(2)}, u32[]{:S(2)}) collective-permute-start(f32[]{:T(128)} %slice_reduce_fusion), channel_id=1, source_target_pairs={{0,16},{16,0},{1,17},{17,1},{2,18},{18,2},{3,19},{19,3},{4,20},{20... | collective-permute-start | bytes 20 | tf_op jit(solution)/shard_map/ppermute | solution.py:1189
  635.9 1.9 copy.117
  638.2 2.9 copy.129
  641.1 3.0 copy.130
  645.5 6.9 convert_bitcast_fusion.2
  652.4 2.9 copy.137
  655.3 3.0 copy.138
  658.3 1.8 copy.139
  661.4 14.3 %convert_bitcast_fusion = (bf16[1,2048,516]{1,2,0:T(8,128)(2,1)}, f32[2048,516]{0,1:T(8,128)}, f32[1,2048,516]{1,2,0:T(8,128)S(1)}, f32[1,2048,516]{1,2,0:T(8,128)}) fusion(f32[1,2048,516]{1,0,2:T(1,128)} %param.26, f32[896,2048]{1,0:T(8,128)} %get-tuple-element.94, f32[]{:T(128)S(6)} %div.110, f32[1,2048,516]{1,0,2:T(1,128)} %param.25, ...), kind=kLoop, calls=%fused_computation.16 | loop fusion | flops 16908288 | bytes 31703044 | tf_op jit(solution)/shard_map/convert_element_type | solution.py:1215
  675.7 8.6 %copy.134 = f32[1,2048,516]{1,0,2:T(1,128)} copy(f32[1,2048,516]{1,2,0:T(8,128)} %bitcast.216) | data formatting | bytes 8454144
  684.2 8.6 %copy.135 = f32[1,2048,516]{1,0,2:T(1,128)} copy(f32[1,2048,516]{1,2,0:T(8,128)} %get-tuple-element.213) | data formatting | bytes 8454144
  692.8 6.6 copy.136
  699.4 8.4 %convert_bitcast_fusion.1 = (bf16[1,256,2048]{2,1,0:T(8,128)(2,1)}, f32[256,2048]{1,0:T(8,128)}, f32[1,256,2048]{2,1,0:T(8,128)}, f32[1,256,2048]{2,1,0:T(8,128)}) fusion(f32[1,256,2048]{2,1,0:T(8,128)} %param.32, f32[256,2048]{1,0:T(8,128)} %get-tuple-element.95, f32[]{:T(128)S(6)} %div.110, f32[1,256,2048]{2,1,0:T(8,128)} %param.31, f32[1,256,2048]{2,1,0:T(8,128)} %param.30), kind=kLoop, calls=%fused_computation.38 | loop fusion | flops 8388608 | bytes 15728644 | tf_op jit(solution)/shard_map/convert_element_type | solution.py:1223
  (132 shorter events, 33.0 us)
Async XLA Ops:
  6.3 11.5 %copy-start.2 = (f32[1,256,2048]{2,1,0:T(8,128)S(1)}, f32[1,256,2048]{2,1,0:T(8,128)}, u32[]{:S(2)}) copy-start(f32[1,256,2048]{2,1,0:T(8,128)} %param.30) | copy-start | bytes 6291460
  17.8 1.1 slice-start
  19.0 9.6 %slice-start.1 = ((f32[1,3328]{1,0:T(1,128)}), f32[1,2048]{1,0:T(1,128)S(1)}, s32[]{:S(2)}) async-start(f32[1,3328]{1,0:T(1,128)} %param.36), calls=%async_computation.1 | async-start | bytes 16384 | tf_op jit(solution)/shard_map/slice | solution.py:714
  30.0 15.1 %copy-start.7 = (bf16[2,64,2048]{2,1,0:T(8,128)(2,1)S(1)}, bf16[2,64,2048]{2,1,0:T(8,128)(2,1)}, u32[]{:S(2)}) copy-start(bf16[2,64,2048]{2,1,0:T(8,128)(2,1)} %param.21) | copy-start | bytes 1572868
  161.9 222.4 %copy-start.1 = (bf16[64,2048]{1,0:T(8,128)(2,1)}, bf16[64,2048]{1,0:T(8,128)(2,1)S(1)}, u32[]{:S(2)}) copy-start(bf16[64,2048]{1,0:T(8,128)(2,1)S(1)} %get-tuple-element.209.refs_6_) | copy-start | bytes 786436
  213.3 52.7 %copy-start.10 = (bf16[2,64,2048]{2,1,0:T(8,128)(2,1)S(1)}, bf16[2,64,2048]{2,1,0:T(8,128)(2,1)}, u32[]{:S(2)}) copy-start(bf16[2,64,2048]{2,1,0:T(8,128)(2,1)} %param.22) | copy-start | bytes 1572868
  333.9 50.4 %copy-start.8 = (f32[64,2048]{1,0:T(8,128)S(1)}, f32[64,2048]{1,0:T(8,128)}, u32[]{:S(2)}) copy-start(f32[64,2048]{1,0:T(8,128)} %get-tuple-element.64) | copy-start | bytes 1572868
  386.5 113.1 %copy-start.5 = (f32[64,2048]{1,0:T(8,128)}, f32[64,2048]{1,0:T(8,128)S(1)}, u32[]{:S(2)}) copy-start(f32[64,2048]{1,0:T(8,128)S(1)} %get-tuple-element.205.refs_9_) | copy-start | bytes 1572868
  451.6 48.0 %copy-start.13 = (f32[16,2048]{1,0:T(8,128)S(1)}, f32[16,2048]{1,0:T(8,128)}, u32[]{:S(2)}) copy-start(f32[16,2048]{1,0:T(8,128)} %get-tuple-element.89) | copy-start | bytes 393220
  451.6 48.0 %copy-start.12 = (f32[16,2048]{1,0:T(8,128)S(1)}, f32[16,2048]{1,0:T(8,128)}, u32[]{:S(2)}) copy-start(f32[16,2048]{1,0:T(8,128)} %get-tuple-element.91) | copy-start | bytes 393220
  556.6 51.0 %copy-start.14 = (f32[1,4,387]{2,1,0:T(4,128)S(1)}, f32[1,4,387]{2,1,0:T(4,128)}, u32[]{:S(2)}) copy-start(f32[1,4,387]{2,1,0:T(4,128)} %param.33) | copy-start | bytes 18580
  556.6 51.9 %copy-start.3 = (f32[256,2048]{1,0:T(8,128)S(1)}, f32[256,2048]{1,0:T(8,128)}, u32[]{:S(2)}) copy-start(f32[256,2048]{1,0:T(8,128)} %get-tuple-element.95) | copy-start | bytes 6291460
  625.3 18.9 %collective-permute-start = (f32[]{:T(128)}, f32[]{:T(128)}, u32[]{:S(2)}, u32[]{:S(2)}) collective-permute-start(f32[]{:T(128)} %slice_reduce_fusion), channel_id=1, source_target_pairs={{0,16},{16,0},{1,17},{17,1},{2,18},{18,2},{3,19},{19,3},{4,20},{20... | collective-permute-start | bytes 20 | tf_op jit(solution)/shard_map/ppermute | solution.py:1189
  641.1 4.4 copy-start
  655.2 3.0 copy-start.4
  658.3 1.8 copy-start.6
  699.4 8.4 %copy-start.15 = (f32[1,3328]{1,0:T(1,128)S(1)}, f32[1,3328]{1,0:T(1,128)}, u32[]{:S(2)}) copy-start(f32[1,3328]{1,0:T(1,128)} %param.36) | copy-start | bytes 39940
  699.4 8.4 %copy-start.16 = (f32[1,3328]{1,0:T(1,128)S(1)}, f32[1,3328]{1,0:T(1,128)}, u32[]{:S(2)}) copy-start(f32[1,3328]{1,0:T(1,128)} %param.37) | copy-start | bytes 39940
  699.4 8.4 %copy-start.17 = (f32[1,3328]{1,0:T(1,128)S(1)}, f32[1,3328]{1,0:T(1,128)}, u32[]{:S(2)}) copy-start(f32[1,3328]{1,0:T(1,128)} %param.38) | copy-start | bytes 39940
  699.4 9.1 %copy-start.18 = (f32[1,4,387]{2,1,0:T(4,128)S(1)}, f32[1,4,387]{2,1,0:T(4,128)}, u32[]{:S(2)}) copy-start(f32[1,4,387]{2,1,0:T(4,128)} %param.34) | copy-start | bytes 18580
  699.4 9.1 %copy-start.19 = (f32[1,4,387]{2,1,0:T(4,128)S(1)}, f32[1,4,387]{2,1,0:T(4,128)}, u32[]{:S(2)}) copy-start(f32[1,4,387]{2,1,0:T(4,128)} %param.35) | copy-start | bytes 18580
  699.4 9.8 %copy-start.11 = (bf16[2,64,2048]{2,1,0:T(8,128)(2,1)S(1)}, bf16[2,64,2048]{2,1,0:T(8,128)(2,1)}, u32[]{:S(2)}) copy-start(bf16[2,64,2048]{2,1,0:T(8,128)(2,1)} %get-tuple-element.92) | copy-start | bytes 1572868
  699.4 10.5 %copy-start.9 = (f32[2,64,2048]{2,1,0:T(8,128)S(1)}, f32[2,64,2048]{2,1,0:T(8,128)}, u32[]{:S(2)}) copy-start(f32[2,64,2048]{2,1,0:T(8,128)} %get-tuple-element.93) | copy-start | bytes 3145732

commit v2 on v1

--- a/solution.py
+++ b/solution.py
@@ -102,18 +102,26 @@
     return pl.ds(pl.multiple_of(shard * rows, rows), rows)
 
 
-def column_parts(width):
+def column_parts(width, shares):
     tiles = width // LANES
-    late = max(tiles // 8, 0)
-    early = (tiles - 2 * late) // 2
-    sizes = [early, tiles - 2 * late - early, late, late]
-    orders = [(0, 2, 1), (0, 1, 2), (2, 1, 0), (1, 2, 0)]
-    parts, start = [], 0
-    for size, order in zip(sizes, orders):
-        if size:
-            parts.append((start, size * LANES, order))
-            start += size * LANES
+    parts, start, taken = [], 0, 0
+    for share, order, group in shares:
+        taken += share
+        stop = tiles * taken // 16 * LANES
+        if stop > start:
+            parts.append((start, stop - start, order, group))
+            start = stop
     return parts
+
+
+GATHER = ((2, (2, 1, 0), 0), (2, (1, 2, 0), 0), (6, (0, 2, 1), 0), (6, (0, 1, 2), 0))
+GATHER_SMALL = ((8, (0, 2, 1), 0), (8, (0, 1, 2), 0))
+SCATTER = (
+    (1, (2, 0, 1), 0), (1, (1, 0, 2), 0), (1, (0, 1, 2), 0), (1, (0, 2, 1), 0),
+    (3, (2, 1, 0), 0), (3, (1, 2, 0), 0), (3, (2, 1, 0), 1), (3, (1, 2, 0), 1),
+)
+SCATTER_SMALL = ((8, (2, 1, 0), 0), (8, (1, 2, 0), 0))
+SCATTER_PACE = (0.3, 0.9, 0.7, 2.0)
 
 
 def guarded(preds, action):
@@ -153,7 +161,7 @@
         return out
 
     def block(part, offsets):
-        start, width, order = parts[part]
+        start, width, order, _ = parts[part]
         shard = linear(dims, moved(dims, spot, shift_of(order, offsets)))
         return shard, all_ref.at[rows_at(shard, rows), pl.ds(start, width)]
 
@@ -201,7 +209,7 @@
         guarded(preds, body)
 
     for pos in range(3):
-        for part, (start, width, _) in enumerate(parts):
+        for part, (start, width, _, _) in enumerate(parts):
             push(part, (0, 0, 0), pos, [], own_ref.at[:, pl.ds(start, width)], 0)
     todo = []
     for part in range(len(parts)):
@@ -216,13 +224,13 @@
                     todo.append(
                         ((2, ka + kb + k, part), part, (oa, ob, oc), [pa, pb, pc], 2, oc)
                     )
-    todo.sort(key=lambda entry: entry[0])
+    todo.sort(key=lambda entry: (sum(abs(off) for off in entry[2]), entry[0]))
     for _, part, offsets, preds, pos, came in todo:
         visit(part, offsets, preds, pos, came)
     for preds, part, number in waits:
 
         def settle(part=part, number=number):
-            start, width, _ = parts[part]
+            start, width, _, _ = parts[part]
             ref = own_ref.at[:, pl.ds(start, width)]
             pltpu.make_async_remote_copy(
                 src_ref=ref,
@@ -244,7 +252,6 @@
     spot = place(dims)
     me = linear(dims, spot)
     sends = []
-    big = max(dims)
 
     def size(part, pos):
         return dims[parts[part][2][pos]]
@@ -291,50 +298,56 @@
         ).wait_recv()
         return ref[...].astype(F32)
 
-    every = range(len(parts))
-    ranks = sorted(
-        itertools.product(range(big), range(big)), key=lambda t: (t[0] == 0, t[1] == 0)
-    )
-    for ob, oc in ranks:
-        for off in range(1, big):
-            for part in every:
-                if off < size(part, 0) and ob < size(part, 1) and oc < size(part, 2):
-                    slot = slot_one(part, size(part, 0) - off, ob, oc)
-                    send(part, mine(part, (off, ob, oc)), 0, off, slot)
-    for ob, oc in ranks:
-        for part in every:
-            if ob == 0 or ob >= size(part, 1) or oc >= size(part, 2):
-                continue
-            total = mine(part, (0, ob, oc))[...].astype(F32)
-            for ea in range(1, size(part, 0)):
-                total = total + arrived(part, slot_one(part, ea, ob, oc))
-            hold = mine(part, (0, ob, oc))
-            if size(part, 0) > 1:
-                hold = box_ref.at[slot_one(part, 1, ob, oc), :, cols(part)]
-                hold[...] = total.astype(box_ref.dtype)
-            send(part, hold, 1, ob, slot_two(part, size(part, 1) - ob, oc))
-    for oc in list(range(1, big)) + [0]:
-        for part in every:
-            if oc >= size(part, 2):
-                continue
-            total = mine(part, (0, 0, oc))[...].astype(F32)
-            for ea in range(1, size(part, 0)):
-                total = total + arrived(part, slot_one(part, ea, 0, oc))
-            for eb in range(1, size(part, 1)):
-                total = total + arrived(part, slot_two(part, eb, oc))
-            if oc == 0:
-                for ec in range(1, size(part, 2)):
-                    total = total + arrived(part, slot_three(part, ec))
-                out_ref[:, cols(part)] = total
-                continue
-            hold = mine(part, (0, 0, oc))
-            if size(part, 0) > 1:
-                hold = box_ref.at[slot_one(part, 1, 0, oc), :, cols(part)]
-            elif size(part, 1) > 1:
-                hold = box_ref.at[slot_two(part, 1, oc), :, cols(part)]
-            if size(part, 0) > 1 or size(part, 1) > 1:
-                hold[...] = total.astype(box_ref.dtype)
-            send(part, hold, 2, oc, slot_three(part, size(part, 2) - oc))
+    def combined(part, ob, oc, stages):
+        total = mine(part, (0, ob, oc))[...].astype(F32)
+        for ea in range(1, size(part, 0)):
+            total = total + arrived(part, slot_one(part, ea, ob, oc))
+        for eb in range(1, size(part, 1)) if stages > 1 else ():
+            total = total + arrived(part, slot_two(part, eb, oc))
+        for ec in range(1, size(part, 2)) if stages > 2 else ():
+            total = total + arrived(part, slot_three(part, ec))
+        return total
+
+    def put_by(part, ob, oc, total):
+        if size(part, 0) > 1:
+            hold = box_ref.at[slot_one(part, 1, ob, oc), :, cols(part)]
+        elif size(part, 1) > 1 and ob == 0:
+            hold = box_ref.at[slot_two(part, 1, oc), :, cols(part)]
+        else:
+            return mine(part, (0, ob, oc))
+        hold[...] = total.astype(box_ref.dtype)
+        return hold
+
+    def first(part, ob, oc, off):
+        slot = slot_one(part, size(part, 0) - off, ob, oc)
+        send(part, mine(part, (off, ob, oc)), 0, off, slot)
+
+    def second(part, ob, oc, _):
+        hold = put_by(part, ob, oc, combined(part, ob, oc, 1))
+        send(part, hold, 1, ob, slot_two(part, size(part, 1) - ob, oc))
+
+    def third(part, _, oc, __):
+        hold = put_by(part, 0, oc, combined(part, 0, oc, 2))
+        send(part, hold, 2, oc, slot_three(part, size(part, 2) - oc))
+
+    def last(part, _, __, ___):
+        out_ref[:, cols(part)] = combined(part, 0, 0, 3)
+
+    lag, rest, turn, end = SCATTER_PACE
+    program = []
+    for part, (_, _, _, group) in enumerate(parts):
+        for ob, oc in itertools.product(range(size(part, 1)), range(size(part, 2))):
+            for off in range(1, size(part, 0)):
+                rank = (0.0 if ob else rest) + group * lag
+                program.append((rank, oc == 0, off, part, first, ob, oc))
+            if ob:
+                program.append((turn + group * lag, oc == 0, 0, part, second, ob, oc))
+        for oc in range(1, size(part, 2)):
+            program.append((end + group * lag, False, 0, part, third, 0, oc))
+        program.append((3.0 + group * lag, True, 0, part, last, 0, 0))
+    program.sort(key=lambda step: step[:4])
+    for _, _, off, part, action, ob, oc in program:
+        action(part, ob, oc, off)
     return sends
 
 
@@ -377,129 +390,308 @@
 DMA = pltpu.SemaphoreType.DMA
 
 
+def params(collective_id):
+    return pltpu.CompilerParams(
+        collective_id=collective_id, has_side_effects=True, vmem_limit_bytes=VMEM_LIMIT
+    )
+
+
+def gather_scratch(parts, dims, count):
+    return [DMA((len(parts), gather_sends(dims))), DMA((len(parts), count)), DMA]
+
+
+def run_gather(count, parts, own_ref, all_ref, sems, stat=None):
+    dims = chip_dims(count)
+    rows = own_ref.shape[0]
+    me = lax.axis_index("head")
+    send_sem, recv_sem, local_sem = sems
+    local = pltpu.make_async_copy(own_ref, all_ref.at[rows_at(me, rows)], local_sem)
+    local.start()
+    if stat is not None:
+        stat_ref, box_ref, small_send, small_recv = stat
+        copies = start_direct(count, lambda peer: stat_ref, box_ref, small_send, small_recv)
+        box_ref[me] = stat_ref[...]
+    gather_steps(dims, parts, rows, own_ref, all_ref, send_sem, recv_sem)
+    if stat is not None:
+        wait_direct(count, box_ref, copies, small_recv, small_send)
+    local.wait()
+
+
 def gather_rows(count, own, stats, collective_id):
     dims = chip_dims(count)
     rows, width = own.shape
-    parts = column_parts(width)
+    parts = column_parts(width, GATHER_SMALL)
+
+    def kernel(own_ref, stat_ref, all_ref, box_ref, *sems):
+        greet_all(count)
+        run_gather(count, parts, own_ref, all_ref, sems[:3], (stat_ref, box_ref) + sems[3:])
+
+    return pl.pallas_call(
+        kernel,
+        out_shape=[
+            jax.ShapeDtypeStruct((count * rows, width), own.dtype),
+            jax.ShapeDtypeStruct((count,) + stats.shape, stats.dtype),
+        ],
+        in_specs=[VMEM_SPEC] * 2,
+        out_specs=[ANY_SPEC, VMEM_SPEC],
+        scratch_shapes=gather_scratch(parts, dims, count) + [DMA((count,)), DMA((count,))],
+        compiler_params=params(collective_id),
+        name="gather_rows",
+    )(own, stats)
+
+
+def scatter_scratch(parts, count, rows, width):
+    slots = max(count - 1, 1)
+    return [pltpu.VMEM((slots, rows, width), BF16), DMA((len(parts), slots)), DMA((len(parts), slots))]
+
+
+def scatter_rows(count, partial, small, collective_id):
+    dims = chip_dims(count)
+    width = partial.shape[1]
+    rows = partial.shape[0] // count
+    parts = column_parts(width, SCATTER_SMALL)
+
+    def kernel(in_ref, small_ref, out_ref, sums_ref, box_ref, send_sem, recv_sem, small_send, small_recv):
+        me = lax.axis_index("head")
+        greet_all(count)
+        copies = start_direct(
+            count, lambda peer: small_ref.at[peer], sums_ref, small_send, small_recv
+        )
+        sums_ref[me] = small_ref[me]
+        sends = scatter_steps(dims, parts, rows, in_ref, out_ref, box_ref, send_sem, recv_sem)
+        wait_direct(count, sums_ref, copies, small_recv, small_send)
+        for copy in sends:
+            copy.wait_send()
+
+    return pl.pallas_call(
+        kernel,
+        out_shape=[
+            jax.ShapeDtypeStruct((rows, width), F32),
+            jax.ShapeDtypeStruct(small.shape, small.dtype),
+        ],
+        in_specs=[VMEM_SPEC] * 2,
+        out_specs=[VMEM_SPEC] * 2,
+        scratch_shapes=scatter_scratch(parts, count, rows, width) + [DMA((count,)), DMA((count,))],
+        compiler_params=params(collective_id),
+        name="scatter_rows",
+    )(partial, small)
+
+
+def norm_rows(value, gain):
+    mean = jnp.mean(value * value, axis=1, keepdims=True)
+    return value * lax.rsqrt(mean + EPS_NORM) * gain
+
+
+def norm_rows_back(value, gain, grad):
+    width = value.shape[1]
+    scale = lax.rsqrt(jnp.mean(value * value, axis=1, keepdims=True) + EPS_NORM)
+    scaled = grad * gain
+    dot = jnp.sum(scaled * value, axis=1, keepdims=True)
+    back = scaled * scale - value * (scale * scale * scale * dot * (1.0 / width))
+    return back, jnp.sum(grad * value * scale, axis=0, keepdims=True)
+
+
+def opening(count, sz, own_weights, own_out, own_pack, first, collective_id):
+    dims = chip_dims(count)
+    rows, width = first.shape
+    parts = column_parts(width, GATHER)
+
+    def kernel(w_ref, wo_ref, pk_ref, x_ref, ws_ref, wos_ref, pks_ref, all_ref, own_ref, *sems):
+        section = lax.axis_index("section")
+        other = 1 - section
+        barrier = pltpu.get_barrier_semaphore()
+        pl.semaphore_signal(barrier, inc=1, device_id={"section": other}, device_id_type=MESH)
+        me = lax.axis_index("head")
+        for off in range(1, count):
+            pl.semaphore_signal(
+                barrier, inc=1, device_id={"head": (me + off) % count}, device_id_type=MESH
+            )
+        pl.semaphore_wait(barrier, count)
+        pair_send, pair_recv, pair_local = sems[3:]
+        copies = []
+        for k, (src, dst) in enumerate(((pk_ref, pks_ref), (w_ref, ws_ref), (wo_ref, wos_ref))):
+            copy = pltpu.make_async_remote_copy(
+                src_ref=src,
+                dst_ref=dst.at[section],
+                send_sem=pair_send.at[k],
+                recv_sem=pair_recv.at[k],
+                device_id={"section": other},
+                device_id_type=MESH,
+            )
+            copy.start()
+            copies.append(copy)
+            if k > 0:
+                local = pltpu.make_async_copy(src, dst.at[section], pair_local.at[k])
+                local.start()
+                copies.append(local)
+        pks_ref[section] = pk_ref[...]
+        copies[0].wait()
+        gain = pks_ref[0, GAIN_ROW : GAIN_ROW + 1, :]
+        own_ref[...] = norm_rows(x_ref[...].astype(F32), gain).astype(BF16)
+        run_gather(count, parts, own_ref, all_ref, sems[:3])
+        for copy in copies[1:]:
+            copy.wait()
+
+    return pl.pallas_call(
+        kernel,
+        out_shape=[
+            jax.ShapeDtypeStruct((2,) + own_weights.shape, BF16),
+            jax.ShapeDtypeStruct((2,) + own_out.shape, BF16),
+            jax.ShapeDtypeStruct((2,) + own_pack.shape, F32),
+            jax.ShapeDtypeStruct((count * rows, width), BF16),
+        ],
+        in_specs=[VMEM_SPEC] * 4,
+        out_specs=[ANY_SPEC, ANY_SPEC, VMEM_SPEC, ANY_SPEC],
+        scratch_shapes=[pltpu.VMEM((rows, width), BF16)]
+        + gather_scratch(parts, dims, count)
+        + [DMA((3,))] * 3,
+        compiler_params=params(collective_id),
+        name="opening",
+    )(own_weights, own_out, own_pack, first)
+
+
+def column_of(tile, rows):
+    row = lax.broadcasted_iota(jnp.int32, (rows, rows), 0)
+    lane = lax.broadcasted_iota(jnp.int32, (rows, rows), 1)
+    return nt((row == lane).astype(F32), tile, HIGH)[:, 0:1]
+
+
+def write_stats(stat_ref, squares, out_grad, branch, rows):
+    dot = nt(jnp.ones((8, branch.shape[1]), F32), out_grad * branch, HIGH)
+    scale = lax.rsqrt(squares / (HEADS * HDIM) + EPS_NORM)
+    row = lax.broadcasted_iota(jnp.int32, (8, rows), 0)
+    stat_ref[...] = jnp.zeros_like(stat_ref)
+    stat_ref[:, :rows] = jnp.where(row == 0, scale, jnp.where(row == 1, dot, 0.0))
+
+
+def after_forward(count, sz, layer, partial, squares, residual, live, pack, cotangent, collective_id):
+    dims = chip_dims(count)
+    rows, width = residual.shape
+    parts, back = column_parts(width, GATHER), column_parts(width, SCATTER)
+    turn = cotangent is not None
 
     def kernel(*refs):
-        if stats is None:
-            own_ref, all_ref, send_sem, recv_sem, local_sem = refs
+        refs = list(refs)
+        in_ref, sq_ref, u_ref, live_ref, pk_ref = (refs.pop(0) for _ in range(5))
+        cot_ref = refs.pop(0) if turn else None
+        result_ref, branch_ref, total_ref, all_ref = (refs.pop(0) for _ in range(4))
+        stats_ref = refs.pop(0) if turn else None
+        sums_ref, own_ref, box_ref, rs_send, rs_recv = (refs.pop(0) for _ in range(5))
+        ag_sems = [refs.pop(0) for _ in range(3)]
+        small_send, small_recv = refs.pop(0), refs.pop(0)
+        me = lax.axis_index("head")
+        greet_all(count)
+        copies = start_direct(count, lambda peer: sq_ref.at[peer], sums_ref, small_send, small_recv)
+        sums_ref[me] = sq_ref[me]
+        sends = scatter_steps(dims, back, rows, in_ref, branch_ref, box_ref, rs_send, rs_recv)
+        wait_direct(count, sums_ref, copies, small_recv, small_send)
+        total = jnp.sum(sums_ref[...], axis=0)
+        total_ref[...] = total
+        scale = lax.rsqrt(column_of(total, rows) / (HEADS * HDIM) + EPS_NORM)
+        branch = branch_ref[...] * scale
+        branch_ref[...] = branch
+        live_col = live_ref[:, 0:1]
+        result = (u_ref[...].astype(F32) + live_col * branch).astype(BF16)
+        result_ref[...] = result
+        stat = None
+        if turn:
+            stat_ref, stat_send, stat_recv = refs
+            out_grad = (live_col * cot_ref[...].astype(F32)).astype(BF16)
+            own_ref[...] = out_grad
+            write_stats(stat_ref, total, out_grad.astype(F32), branch, rows)
+            stat = (stat_ref, stats_ref, stat_send, stat_recv)
         else:
-            (own_ref, stat_ref, all_ref, box_ref, send_sem, recv_sem, local_sem) = refs[:7]
-            small_send, small_recv = refs[7:]
-        spot = place(dims)
-        me = linear(dims, spot)
-        if stats is None:
-            greet_axes(dims, spot)
-        else:
-            greet_all(count)
-        local = pltpu.make_async_copy(own_ref, all_ref.at[rows_at(me, rows)], local_sem)
-        local.start()
-        if stats is not None:
-            copies = start_direct(count, lambda peer: stat_ref, box_ref, small_send, small_recv)
-            box_ref[me] = stat_ref[...]
-        gather_steps(dims, parts, rows, own_ref, all_ref, send_sem, recv_sem)
-        if stats is not None:
-            wait_direct(count, box_ref, copies, small_recv, small_send)
-        local.wait()
-
-    out_shape = [jax.ShapeDtypeStruct((count * rows, width), own.dtype)]
-    out_specs = [ANY_SPEC]
-    scratch = [
-        DMA((len(parts), gather_sends(dims))),
-        DMA((len(parts), count)),
-        DMA,
+            gain = pk_ref[layer + 1, GAIN_ROW : GAIN_ROW + 1, :]
+            own_ref[...] = norm_rows(result.astype(F32), gain).astype(BF16)
+        run_gather(count, parts, own_ref, all_ref, ag_sems, stat)
+        for copy in sends:
+            copy.wait_send()
+
+    out_shape = [
+        jax.ShapeDtypeStruct((rows, width), BF16),
+        jax.ShapeDtypeStruct((rows, width), F32),
+        jax.ShapeDtypeStruct((8, rows), F32),
+        jax.ShapeDtypeStruct((count * rows, width), BF16),
     ]
-    operands = [own]
-    if stats is not None:
-        out_shape.append(jax.ShapeDtypeStruct((count,) + stats.shape, stats.dtype))
+    out_specs = [VMEM_SPEC, VMEM_SPEC, VMEM_SPEC, ANY_SPEC]
+    scratch = [pltpu.VMEM((count, 8, rows), F32), pltpu.VMEM((rows, width), BF16)]
+    scratch += scatter_scratch(back, count, rows, width) + gather_scratch(parts, dims, count)
+    scratch += [DMA((count,))] * 2
+    operands = [partial, squares, residual, live, pack]
+    if turn:
+        out_shape.append(jax.ShapeDtypeStruct((count, 8, LANES), F32))
         out_specs.append(VMEM_SPEC)
-        scratch += [DMA((count,)), DMA((count,))]
-        operands.append(stats)
+        scratch += [pltpu.VMEM((8, LANES), F32)] + [DMA((count,))] * 2
+        operands.append(cotangent)
     return pl.pallas_call(
         kernel,
         out_shape=out_shape,
         in_specs=[VMEM_SPEC] * len(operands),
         out_specs=out_specs,
         scratch_shapes=scratch,
-        compiler_params=pltpu.CompilerParams(
-            collective_id=collective_id, has_side_effects=True, vmem_limit_bytes=VMEM_LIMIT
-        ),
-        name="gather_rows",
+        compiler_params=params(collective_id),
+        name="after_forward",
     )(*operands)
 
 
-def scatter_rows(count, partial, small, collective_id):
+def after_backward(count, sz, layer, partial, residual, upstream, live, pack, below, collective_id):
     dims = chip_dims(count)
-    width = partial.shape[1]
-    rows = partial.shape[0] // count
-    parts = [(s, w, tuple(reversed(order))) for s, w, order in column_parts(width)]
+    rows, width = residual.shape
+    parts, back = column_parts(width, GATHER), column_parts(width, SCATTER)
+    more = below is not None
 
     def kernel(*refs):
-        if small is None:
-            in_ref, out_ref, box_ref, send_sem, recv_sem = refs
-        else:
-            in_ref, small_ref, out_ref, sums_ref, box_ref, send_sem, recv_sem = refs[:7]
-            small_send, small_recv = refs[7:]
-        me = lax.axis_index("head")
-        spot = place(dims)
-        if small is None:
-            greet_axes(dims, spot)
-        else:
-            greet_all(count)
-            copies = start_direct(
-                count, lambda peer: small_ref.at[peer], sums_ref, small_send, small_recv
-            )
-            sums_ref[me] = small_ref[me]
-        sends = scatter_steps(dims, parts, rows, in_ref, out_ref, box_ref, send_sem, recv_sem)
-        if small is not None:
-            wait_direct(count, sums_ref, copies, small_recv, small_send)
+        refs = list(refs)
+        in_ref, u_ref, up_ref, live_ref, pk_ref = (refs.pop(0) for _ in range(5))
+        if more:
+            branch_ref, total_ref = refs.pop(0), refs.pop(0)
+        grad_ref, low_ref, gain_ref = (refs.pop(0) for _ in range(3))
+        if more:
+            all_ref, stats_ref = refs.pop(0), refs.pop(0)
+        box_ref, rs_send, rs_recv = (refs.pop(0) for _ in range(3))
+        greet_all(count) if more else greet_axes(dims, place(dims))
+        sends = scatter_steps(dims, back, rows, in_ref, grad_ref, box_ref, rs_send, rs_recv)
+        gain = pk_ref[layer, GAIN_ROW : GAIN_ROW + 1, :]
+        grad, gain_grad = norm_rows_back(u_ref[...].astype(F32), gain, grad_ref[...])
+        grad = grad + up_ref[...].astype(F32)
+        grad_ref[...] = grad
+        low_ref[...] = grad.astype(BF16)
+        gain_ref[...] = gain_grad
+        if more:
+            own_ref, stat_ref, stat_send, stat_recv = (refs.pop(0) for _ in range(4))
+            out_grad = (live_ref[:, 0:1] * grad.astype(BF16).astype(F32)).astype(BF16)
+            own_ref[...] = out_grad
+            write_stats(stat_ref, total_ref[...], out_grad.astype(F32), branch_ref[...], rows)
+            run_gather(count, parts, own_ref, all_ref, refs, (stat_ref, stats_ref, stat_send, stat_recv))
         for copy in sends:
             copy.wait_send()
 
-    out_shape = [jax.ShapeDtypeStruct((rows, width), F32)]
-    scratch = [
-        pltpu.VMEM((max(count - 1, 1), rows, width), partial.dtype),
-        DMA((len(parts), max(count - 1, 1))),
-        DMA((len(parts), max(count - 1, 1))),
+    out_shape = [
+        jax.ShapeDtypeStruct((rows, width), F32),
+        jax.ShapeDtypeStruct((rows, width), BF16),
+        jax.ShapeDtypeStruct((1, width), F32),
     ]
-    operands = [partial]
-    if small is not None:
-        out_shape.append(jax.ShapeDtypeStruct(small.shape, small.dtype))
-        scratch += [DMA((count,)), DMA((count,))]
-        operands.append(small)
+    out_specs = [VMEM_SPEC] * 3
+    scratch = scatter_scratch(back, count, rows, width)
+    operands = [partial, residual, upstream, live, pack]
+    if more:
+        out_shape += [
+            jax.ShapeDtypeStruct((count * rows, width), BF16),
+            jax.ShapeDtypeStruct((count, 8, LANES), F32),
+        ]
+        out_specs += [ANY_SPEC, VMEM_SPEC]
+        scratch += [pltpu.VMEM((rows, width), BF16), pltpu.VMEM((8, LANES), F32)]
+        scratch += [DMA((count,))] * 2 + gather_scratch(parts, dims, count)
+        operands += list(below)
     return pl.pallas_call(
         kernel,
         out_shape=out_shape,
         in_specs=[VMEM_SPEC] * len(operands),
-        out_specs=[VMEM_SPEC] * len(out_shape),
+        out_specs=out_specs,
         scratch_shapes=scratch,
-        compiler_params=pltpu.CompilerParams(
-            collective_id=collective_id, has_side_effects=True, vmem_limit_bytes=VMEM_LIMIT
-        ),
-        name="scatter_rows",
+        compiler_params=params(collective_id),
+        name="after_backward",
     )(*operands)
-
-
-def gather_small(count, block, collective_id):
-    def kernel(in_ref, box_ref, send_sem, recv_sem):
-        greet_all(count)
-        copies = start_direct(count, lambda peer: in_ref, box_ref, send_sem, recv_sem)
-        box_ref[lax.axis_index("head")] = in_ref[...]
-        wait_direct(count, box_ref, copies, recv_sem, send_sem)
-
-    return pl.pallas_call(
-        kernel,
-        out_shape=jax.ShapeDtypeStruct((count,) + block.shape, block.dtype),
-        in_specs=[VMEM_SPEC],
-        out_specs=VMEM_SPEC,
-        scratch_shapes=[DMA((count,)), DMA((count,))],
-        compiler_params=pltpu.CompilerParams(
-            collective_id=collective_id, has_side_effects=True
-        ),
-        name="gather_small",
-    )(block)
 
 
 def greet_other():
@@ -510,57 +702,33 @@
     return other
 
 
-def both_sections(arrays, collective_id):
-    number = len(arrays)
-
-    def kernel(*refs):
-        ins, outs = refs[:number], refs[number : 2 * number]
-        send_sem, recv_sem, local_sem = refs[2 * number :]
-        section = lax.axis_index("section")
-        locals_ = [
-            pltpu.make_async_copy(ins[k], outs[k].at[section], local_sem.at[k])
-            for k in range(number)
-        ]
-        for local in locals_:
-            local.start()
-        other = greet_other()
-        copies = []
-        for k in range(number):
-            locals_[k].wait()
-            copy = pltpu.make_async_remote_copy(
-                src_ref=outs[k].at[section],
-                dst_ref=outs[k].at[section],
-                send_sem=send_sem.at[k],
-                recv_sem=recv_sem.at[k],
-                device_id={"section": other},
-                device_id_type=MESH,
-            )
-            copy.start()
-            copies.append(copy)
-        for copy in copies:
-            copy.wait()
-
-    return pl.pallas_call(
-        kernel,
-        out_shape=[jax.ShapeDtypeStruct((2,) + a.shape, a.dtype) for a in arrays],
-        in_specs=[ANY_SPEC] * number,
-        out_specs=[VMEM_SPEC] * number,
-        scratch_shapes=[DMA((number,))] * 3,
-        compiler_params=pltpu.CompilerParams(
-            collective_id=collective_id, has_side_effects=True, vmem_limit_bytes=VMEM_LIMIT
-        ),
-        name="both_sections",
-    )(*arrays)
-
-
-def trade_sections(sums, stacks, collective_id):
+def add_up(out_ref, mine_ref, got_ref, squares_ref):
+    rows, width = out_ref.shape
+    step = 16 if rows % 16 == 0 else rows
+
+    def body(i, carry):
+        span = pl.ds(pl.multiple_of(i * step, step), step)
+        total = mine_ref[span, :].astype(F32) + got_ref[span, :].astype(F32)
+        out_ref[span, :] = total
+        if squares_ref is not None:
+            part = total * total
+            for k in range(0, step, 8):
+                squares_ref[...] += part[k : k + 8]
+        return carry
+
+    lax.fori_loop(0, rows // step, body, 0)
+
+
+def trade_sections(sums, stacks, squared, collective_id):
     pairs = sums + stacks
     number, summed = len(pairs), len(sums)
 
     def kernel(*refs):
         ins, outs = refs[: 2 * number], refs[2 * number : 3 * number]
-        boxes = refs[3 * number : 3 * number + summed]
-        send_sem, recv_sem = refs[3 * number + summed :]
+        squares_ref = refs[3 * number]
+        boxes = refs[3 * number + 1 : 3 * number + 1 + summed]
+        send_sem, recv_sem = refs[3 * number + 1 + summed :]
+        squares_ref[...] = jnp.zeros_like(squares_ref)
         section = lax.axis_index("section")
         other = greet_other()
 
@@ -582,18 +750,19 @@
             for k in range(number):
                 copies[k].wait()
                 if k < summed:
-                    outs[k][...] = mine[k][...].astype(F32) + boxes[k][...].astype(F32)
+                    add_up(outs[k], mine[k], boxes[k], squares_ref if k < squared else None)
 
         pl.when(section == 0)(lambda: go(ins[0::2], ins[1::2]))
         pl.when(section == 1)(lambda: go(ins[1::2], ins[0::2]))
 
     shapes = [jax.ShapeDtypeStruct(a.shape, F32) for a, _ in sums]
     shapes += [jax.ShapeDtypeStruct((2,) + a.shape, a.dtype) for a, _ in stacks]
+    shapes.append(jax.ShapeDtypeStruct((8, sums[0][0].shape[1]), F32))
     return pl.pallas_call(
         kernel,
         out_shape=shapes,
         in_specs=[VMEM_SPEC] * (2 * number),
-        out_specs=[VMEM_SPEC] * number,
+        out_specs=[VMEM_SPEC] * len(shapes),
         scratch_shapes=[pltpu.VMEM(a.shape, a.dtype) for a, _ in sums] + [DMA((number,))] * 2,
         compiler_params=pltpu.CompilerParams(
             collective_id=collective_id, has_side_effects=True, vmem_limit_bytes=VMEM_LIMIT
@@ -651,6 +820,32 @@
     return jnp.dot(left, right, precision=precision, preferred_element_type=F32)
 
 
+def split(value):
+    high = value.astype(BF16)
+    return high, (value - high.astype(F32)).astype(BF16)
+
+
+def fine(dot, left, right, left_axis, right_axis):
+    left_high, left_low = split(left)
+    right_high, right_low = split(right)
+    return dot(
+        jnp.concatenate([left_high, left_low, left_high], axis=left_axis),
+        jnp.concatenate([right_high, right_high, right_low], axis=right_axis),
+    )
+
+
+def nt3(left, right):
+    return fine(nt, left, right, 1, 1)
+
+
+def tn3(left, right):
+    return fine(tn, left, right, 0, 0)
+
+
+def nn3(left, right):
+    return fine(nn, left, right, 1, 0)
+
+
 def softplus(value):
     return jnp.maximum(value, 0.0) + jnp.log1p(jnp.exp(-jnp.abs(value)))
 
@@ -677,28 +872,39 @@
     return jnp.transpose(jnp.where(lane < 16, both, 0.0))
 
 
-def prepare_weights(sz, proj_in, proj_state, order):
-    rows = min(256, sz.width)
-
-    def kernel(in_ref, state_ref, order_ref, out_ref):
-        low = in_ref[...].astype(BF16)
-        table = order_ref[: sz.master, :]
-        out_ref[...] = nn(low, table).astype(BF16)
-        out_ref[:, 2 * sz.channels : sz.dt] = state_ref[...].astype(BF16)
+def prepare_weights(sz, proj_in_t, proj_state, order):
+    cols = 256
+    full = sz.master // 16 * 16
+
+    def kernel(in_ref, state_ref, order_ref, out_ref, low_ref):
+        low_ref[:full, :] = in_ref[:full, 0, :].astype(BF16)
+        if full < sz.master_pad:
+            low_ref[full:, :] = jnp.zeros((sz.master_pad - full, cols), BF16)
+        if full < sz.master:
+            low_ref[full : full + 16, :] = jnp.concatenate(
+                [in_ref[full : sz.master, 0, :], jnp.zeros((full + 16 - sz.master, cols), F32)], axis=0
+            ).astype(BF16)
+        table = order_ref[: sz.master_pad, :]
+        out_ref[...] = tn(table, low_ref[...]).astype(BF16)
+        row = lax.broadcasted_iota(jnp.int32, (2 * NSTATE, 2 * NSTATE), 0)
+        col = lax.broadcasted_iota(jnp.int32, (2 * NSTATE, 2 * NSTATE), 1)
+        one = (row == col).astype(BF16)
+        out_ref[2 * sz.channels : sz.dt, :] = nt(one, state_ref[...].astype(BF16)).astype(BF16)
 
     return pl.pallas_call(
         kernel,
-        out_shape=jax.ShapeDtypeStruct((sz.width, sz.cols), BF16),
-        grid=(sz.width // rows,),
+        out_shape=jax.ShapeDtypeStruct((sz.cols, sz.width), BF16),
+        grid=(sz.width // cols,),
         in_specs=[
-            pl.BlockSpec((rows, sz.master), lambda i: (i, 0)),
-            pl.BlockSpec((rows, 2 * NSTATE), lambda i: (i, 0)),
+            pl.BlockSpec((sz.master, 1, cols), lambda i: (0, 0, i)),
+            pl.BlockSpec((cols, 2 * NSTATE), lambda i: (i, 0)),
             pl.BlockSpec((sz.grad_rows, sz.cols), lambda i: (0, 0)),
         ],
-        out_specs=pl.BlockSpec((rows, sz.cols), lambda i: (i, 0)),
+        out_specs=pl.BlockSpec((sz.cols, cols), lambda i: (0, i)),
+        scratch_shapes=[pltpu.VMEM((sz.master_pad, cols), BF16)],
         compiler_params=pltpu.CompilerParams(vmem_limit_bytes=VMEM_LIMIT),
         name="prepare_weights",
-    )(proj_in, proj_state, order)
+    )(proj_in_t, proj_state, order)
 
 
 def pack_params(sz, head_part, shared_part):
@@ -729,6 +935,12 @@
     return jnp.concatenate(rows, axis=0)
 
 
+def to_columns(tile, rows):
+    row = lax.broadcasted_iota(jnp.int32, (rows, LANES), 0)
+    lane = lax.broadcasted_iota(jnp.int32, (rows, LANES), 1)
+    return nt((row == lane).astype(F32), tile, HIGH)
+
+
 def forward_core(sz, layer, resets, gathered, weights, weight_out, pack, rows):
     block, chunk, chans = STRETCH, CHUNK, sz.channels
     subs = block // chunk
@@ -746,7 +958,7 @@
             conv_ref[...] = jnp.zeros_like(conv_ref)
             state_ref[...] = jnp.zeros_like(state_ref)
 
-        p_ref[...] = nn(h_ref[...], w_ref[...])
+        p_ref[...] = nt(h_ref[...], w_ref[...])
         inner = p_ref[:, chans : 2 * chans]
         state_raw = p_ref[:, 2 * chans : sz.dt].astype(BF16).astype(F32)
         conv_ref[0:8, :] = conv_ref[block : block + 8, :] * keep
@@ -769,9 +981,9 @@
             dt = step[span]
             log_decay = nn(lower, decay[span], HIGH)
             flat = step_rows(log_decay, dt)
-            writer = act[span, chans : chans + NSTATE].astype(BF16)
-            reader = act[span, chans + NSTATE :].astype(BF16)
-            cross = nt(reader, writer)
+            writer = act[span, chans : chans + NSTATE]
+            reader = act[span, chans + NSTATE :]
+            cross = nt3(reader, writer)
             for pair in range(sz.padded // 2):
                 cols = slice(pair * LANES, (pair + 1) * LANES)
                 x = act[span, cols]
@@ -780,23 +992,23 @@
                     head = 2 * pair + side
                     gap = log_decay[:, head : head + 1] - flat[head : head + 1, :]
                     weight = cross * jnp.exp(jnp.where(mask, gap, -1e30)) * flat[8 + head : 9 + head, :]
-                    part = jnp.where((lane < HDIM) == (side == 0), x, 0.0).astype(BF16)
-                    total = total + nn(weight.astype(BF16), part)
+                    part = jnp.where((lane < HDIM) == (side == 0), x, 0.0)
+                    total = total + nn3(weight, part)
                 logs = halves(log_decay[:, 2 * pair : 2 * pair + 1], log_decay[:, 2 * pair + 1 : 2 * pair + 2])
                 dts = halves(dt[:, 2 * pair : 2 * pair + 1], dt[:, 2 * pair + 1 : 2 * pair + 2])
                 old = state_ref[:, cols]
-                total = total + jnp.exp(logs) * nn(reader, old.astype(BF16))
+                total = total + jnp.exp(logs) * nn3(reader, old)
                 last = logs[chunk - 1 : chunk, :]
-                moved_in = (x * jnp.exp(last - logs) * dts).astype(BF16)
-                state_ref[:, cols] = jnp.exp(last) * old + tn(writer, moved_in)
+                moved_in = x * jnp.exp(last - logs) * dts
+                state_ref[:, cols] = jnp.exp(last) * old + tn3(writer, moved_in)
                 y_ref[span, cols] = total + pk_ref[6:7, cols] * x
         z = p_ref[:, :chans]
         gated = y_ref[...] * z * sigmoid(z)
         square = nt(jnp.ones((8, chans), F32), gated * gated, HIGH)
         for k in range(shards):
             sq_ref[k] = square[:, k * rows : (k + 1) * rows]
-        low = (gated * pk_ref[5:6, :chans]).astype(BF16)
-        part_ref[...] = nn(low, wo_ref[...]).astype(BF16)
+        high, low = split(gated * pk_ref[5:6, :chans])
+        part_ref[...] = (nn(high, wo_ref[...]) + nn(low, wo_ref[...])).astype(BF16)
 
     width = sz.width
     return pl.pallas_call(
@@ -812,7 +1024,7 @@
         in_specs=[
             pl.BlockSpec(memory_space=pltpu.SMEM),
             pl.BlockSpec((block, width), lambda c: (c, 0)),
-            pl.BlockSpec((None, width, sz.cols), lambda c: (layer, 0, 0)),
+            pl.BlockSpec((None, sz.cols, width), lambda c: (layer, 0, 0)),
             pl.BlockSpec((None, chans, width), lambda c: (layer, 0, 0)),
             pl.BlockSpec((None, 16, width), lambda c: (layer, 0, 0)),
         ],
@@ -832,7 +1044,7 @@
     )(resets, gathered, weights, weight_out, pack)
 
 
-def backward_core(sz, layer, resets, grads, proj, mixed, states, stats, weights, weight_out, pack, order):
+def backward_core(sz, layer, resets, grads, proj, mixed, states, stats, weights, weight_out, pack, order, rows):
     block, chunk, chans = STRETCH, CHUNK, sz.channels
     subs = block // chunk
     blocks = sz.blocks
@@ -874,8 +1086,10 @@
         gated = y * zsilu
         gain = pk_ref[5:6, :chans]
         skip = pk_ref[6:7, :chans]
-        scale = st_ref[:, 0:1]
-        along = st_ref[:, 1:2]
+        columns = [to_columns(st_ref[k], rows) for k in range(block // rows)]
+        columns = jnp.concatenate(columns, axis=0)
+        scale = columns[:, 0:1]
+        along = columns[:, 1:2]
         grad_q = nt(g_ref[...], wo_ref[...])
         q_ref[...] = (gated * scale * gain).astype(BF16)
         acc_ref[5:6, :chans] += jnp.sum(grad_q * gated * scale, axis=0, keepdims=True)
@@ -893,9 +1107,9 @@
             dt = step[span]
             log_decay = nn(lower, decay[span], HIGH)
             flat = step_rows(log_decay, dt)
-            writer = act[span, chans : chans + NSTATE].astype(BF16)
-            reader = act[span, chans + NSTATE :].astype(BF16)
-            cross = nt(reader, writer)
+            writer = act[span, chans : chans + NSTATE]
+            reader = act[span, chans + NSTATE :]
+            cross = nt3(reader, writer)
             cross_grad = jnp.zeros((chunk, chunk), F32)
             dreader = jnp.zeros((chunk, NSTATE), F32)
             dwriter = jnp.zeros((chunk, NSTATE), F32)
@@ -912,34 +1126,31 @@
                 last = logs[chunk - 1 : chunk, :]
                 old = s_ref[sub, :, cols]
                 dnew = dstate_ref[:, cols]
-                old_low, dnew_low = old.astype(BF16), dnew.astype(BF16)
-                faded = (g * jnp.exp(logs)).astype(BF16)
+                faded = g * jnp.exp(logs)
                 tail = jnp.exp(last - logs)
-                dreader = dreader + nt(faded, old_low)
-                ahead = nn(writer, dnew_low)
+                dreader = dreader + nt3(faded, old)
+                ahead = nn3(writer, dnew)
                 dx = g * skip[:, cols] + ahead * tail * dts
-                dwriter = dwriter + nt((x * tail * dts).astype(BF16), dnew_low)
+                dwriter = dwriter + nt3(x * tail * dts, dnew)
                 reach.append(x * ahead * tail)
                 carried.append(jnp.sum(old * dnew, axis=0, keepdims=True) * jnp.exp(last))
-                dstate_ref[:, cols] = jnp.exp(last) * dnew + tn(reader, faded)
-                x_low = x.astype(BF16)
+                dstate_ref[:, cols] = jnp.exp(last) * dnew + tn3(reader, faded)
                 for side in range(2):
                     head = 2 * pair + side
                     own = (lane < HDIM) == (side == 0)
-                    g_own = jnp.where(own, g, 0.0).astype(BF16)
+                    g_own = jnp.where(own, g, 0.0)
                     gap = log_decay[:, head : head + 1] - flat[head : head + 1, :]
                     decays = jnp.exp(jnp.where(mask, gap, -1e30))
                     steps = flat[8 + head : 9 + head, :]
-                    spread = nt(g_own, x_low) * decays
+                    spread = nt3(g_own, x) * decays
                     weight = cross * decays * steps
-                    dx = dx + tn(weight.astype(BF16), g_own)
+                    dx = dx + tn3(weight, g_own)
                     cross_grad = cross_grad + spread * steps
                     sums = jnp.sum(spread * cross, axis=0, keepdims=True)
                     fall = fall + jnp.where(row == head, sums, 0.0)
                 dact_ref[span, cols] = dx
-            cross_low = cross_grad.astype(BF16)
-            dact_ref[span, chans : chans + NSTATE] = dwriter + tn(cross_low, reader)
-            dact_ref[span, chans + NSTATE :] = dreader + nn(cross_low, writer)
+            dact_ref[span, chans : chans + NSTATE] = dwriter + tn3(cross_grad, reader)
+            dact_ref[span, chans + NSTATE :] = dreader + nn3(cross_grad, writer)
             reach = nn(jnp.concatenate(reach, axis=1), sum_ref[...], HIGH)
             carried = nn(jnp.concatenate(carried, axis=1), sum_ref[...], HIGH)
             direct = jnp.transpose(fall) + reach
@@ -966,7 +1177,7 @@
         low = jnp.concatenate(
             [dz.astype(BF16), draw.astype(BF16), ddt_raw.astype(BF16)], axis=1
         )
-        gh_ref[...] = nt(low, w_ref[...]).astype(BF16)
+        gh_ref[...] = nn(low, w_ref[...]).astype(BF16)
         gt_ref[...] = nt(order_ref[...], low).astype(BF16)
 
     width = sz.width
@@ -988,8 +1199,8 @@
             pl.BlockSpec((8, sz.cols), lambda i: (jnp.maximum((back - i) * per - 1, 0), 0)),
             pl.BlockSpec((block, chans), lambda i: (back - i, 0)),
             pl.BlockSpec((subs, NSTATE, chans), lambda i: (back - i, 0, 0)),
-            pl.BlockSpec((block, LANES), lambda i: (back - i, 0)),
-            pl.BlockSpec((None, width, sz.cols), lambda i: (layer, 0, 0)),
+            pl.BlockSpec((block // rows, 8, LANES), lambda i: (back - i, 0, 0)),
+            pl.BlockSpec((None, sz.cols, width), lambda i: (layer, 0, 0)),
             pl.BlockSpec((None, chans, width), lambda i: (layer, 0, 0)),
             pl.BlockSpec((None, 16, width), lambda i: (layer, 0, 0)),
             pl.BlockSpec((sz.grad_rows, sz.cols), lambda i: (0, 0)),
@@ -1017,8 +1228,11 @@
 def weight_grads(sz, grads_t, gathered, scaled, out_grads):
     cols = 256
 
-    def kernel(gt_ref, h_ref, q_ref, g_ref, in_ref, out_ref):
-        in_ref[...] = nn(gt_ref[...], h_ref[...]).astype(BF16)
+    split_row = sz.master_pad
+
+    def kernel(gt_ref, h_ref, q_ref, g_ref, in_ref, state_ref, out_ref):
+        in_ref[...] = nn(gt_ref[:split_row, :], h_ref[...]).astype(BF16)
+        state_ref[...] = nn(gt_ref[split_row:, :], h_ref[...])
         out_ref[...] = tn(q_ref[...], g_ref[...]).astype(BF16)
 
     tokens, width, chans = sz.tokens, sz.width, sz.channels
@@ -1026,7 +1240,8 @@
         kernel,
         grid=(width // cols,),
         out_shape=[
-            jax.ShapeDtypeStruct((sz.grad_rows, width), BF16),
+            jax.ShapeDtypeStruct((sz.master_pad, width), BF16),
+            jax.ShapeDtypeStruct((2 * NSTATE, width), F32),
             jax.ShapeDtypeStruct((chans, width), BF16),
         ],
         in_specs=[
@@ -1036,20 +1251,13 @@
             pl.BlockSpec((tokens, cols), lambda i: (0, i)),
         ],
         out_specs=[
-            pl.BlockSpec((sz.grad_rows, cols), lambda i: (0, i)),
+            pl.BlockSpec((sz.master_pad, cols), lambda i: (0, i)),
+            pl.BlockSpec((2 * NSTATE, cols), lambda i: (0, i)),
             pl.BlockSpec((chans, cols), lambda i: (0, i)),
         ],
         compiler_params=pltpu.CompilerParams(vmem_limit_bytes=VMEM_LIMIT),
         name="weight_grads",
     )(grads_t, gathered, scaled, out_grads)
-
-
-def input_norm(residual, in_gain):
-    return (
-        residual
-        * lax.rsqrt(jnp.mean(residual * residual, axis=1, keepdims=True) + EPS_NORM)
-        * in_gain
-    )
 
 
 def adam_update(weight, moment, second, gradient, rate, decay):
@@ -1059,6 +1267,81 @@
     corrected_sq = second_new / (1.0 - BETA_TWO**ADAM_STEP)
     weight_new = weight - rate * (corrected / (jnp.sqrt(corrected_sq) + ADAM_EPS) + decay * weight)
     return (weight_new, moment_new, second_new)
+
+
+def adam_in(sz, clip, grad, weight, moment, second):
+    block = LANES
+    width = sz.width
+
+    def kernel(clip_ref, g_ref, w_ref, m_ref, v_ref, wn_ref, mn_ref, vn_ref, low_ref):
+        scale = clip_ref[0]
+
+        def body(i, carry):
+            made = []
+            for half in range(2):
+                span = pl.ds(pl.multiple_of(i * 16 + half * 8, 8), 8)
+                new = adam_update(
+                    w_ref[span, 0, :], m_ref[span, 0, :], v_ref[span, 0, :],
+                    scale * g_ref[span, :], LEARN_MATRIX, WEIGHT_DECAY,
+                )
+                wn_ref[span, 0, :] = new[0]
+                mn_ref[span, 0, :] = new[1]
+                vn_ref[span, 0, :] = new[2]
+                made.append(new[0])
+            low_ref[pl.ds(pl.multiple_of(i * 16, 16), 16), :] = jnp.concatenate(made, axis=0).astype(BF16)
+            return carry
+
+        lax.fori_loop(0, block // 16, body, 0)
+
+    view = pl.BlockSpec((block, 1, width), lambda i: (i, 0, 0))
+    flat = pl.BlockSpec((block, width), lambda i: (i, 0))
+    shape = jax.ShapeDtypeStruct((sz.master, 1, width), F32)
+    return pl.pallas_call(
+        kernel,
+        grid=(sz.master_pad // block,),
+        out_shape=[shape, shape, shape, jax.ShapeDtypeStruct((sz.master, width), BF16)],
+        in_specs=[pl.BlockSpec(memory_space=pltpu.SMEM), flat, view, view, view],
+        out_specs=[view, view, view, flat],
+        compiler_params=pltpu.CompilerParams(vmem_limit_bytes=VMEM_LIMIT),
+        name="adam_in",
+    )(clip, grad, weight, moment, second)
+
+
+def adam_plain(clip, grad, weight, moment, second, transposed):
+    rows, width = weight.shape
+    block = min(256 if transposed else 64, rows)
+
+    def kernel(clip_ref, g_ref, w_ref, m_ref, v_ref, wn_ref, mn_ref, vn_ref, low_ref):
+        if transposed:
+            row = lax.broadcasted_iota(jnp.int32, (width, width), 0)
+            col = lax.broadcasted_iota(jnp.int32, (width, width), 1)
+            grad_value = tn(g_ref[...], (row == col).astype(BF16))
+        else:
+            grad_value = g_ref[...]
+        new = adam_update(
+            w_ref[...], m_ref[...], v_ref[...], clip_ref[0] * grad_value, LEARN_MATRIX, WEIGHT_DECAY
+        )
+        wn_ref[...], mn_ref[...], vn_ref[...] = new
+        low_ref[...] = new[0].astype(BF16)
+
+    flat = pl.BlockSpec((block, width), lambda i: (i, 0))
+    turned = pl.BlockSpec((width, block), lambda i: (0, i))
+    shape = jax.ShapeDtypeStruct((rows, width), F32)
+    return pl.pallas_call(
+        kernel,
+        grid=(rows // block,),
+        out_shape=[shape, shape, shape, jax.ShapeDtypeStruct((rows, width), BF16)],
+        in_specs=[
+            pl.BlockSpec(memory_space=pltpu.SMEM), turned if transposed else flat, flat, flat, flat
+        ],
+        out_specs=[flat] * 4,
+        compiler_params=pltpu.CompilerParams(vmem_limit_bytes=VMEM_LIMIT),
+        name="adam_plain",
+    )(clip, grad, weight, moment, second)
+
+
+def columns_first(array):
+    return jnp.transpose(array, (2, 0, 1))
 
 
 def shards(
@@ -1092,81 +1375,69 @@
     start_block, seq_length, resets = seq_layout(
         lax.dynamic_index_in_dim(valid_lengths, section, 0, keepdims=False)
     )
-    token = head_idx * rows + jnp.arange(rows, dtype=jnp.int32)
-    own_block = token // STRETCH
-    position = token - start_block[own_block] * STRETCH
-    live = (position < seq_length[own_block]).astype(F32)[:, None]
-    first_in = lax.dynamic_index_in_dim(inputs, section, 0, keepdims=False).astype(F32)
-    last_grad = lax.dynamic_index_in_dim(cotangent, section, 0, keepdims=False).astype(F32)
-    own_weights = prepare_weights(sz, proj_in[0], proj_state[0], order)
+    token = head_idx * rows + lax.broadcasted_iota(jnp.int32, (rows, LANES), 0)
+    live = jnp.zeros((rows, LANES), F32)
+    for block in range(sz.blocks):
+        inside = (token // STRETCH == block) & (token - start_block[block] * STRETCH < seq_length[block])
+        live = jnp.where(inside, 1.0, live)
+    first = lax.dynamic_index_in_dim(inputs, section, 0, keepdims=False)
+    cot = lax.dynamic_index_in_dim(cotangent, section, 0, keepdims=False)
+    own_weights = prepare_weights(sz, columns_first(proj_in), proj_state[0], order)
     own_out = proj_out[0].astype(BF16)
     own_out = jnp.pad(own_out, ((0, sz.channels - own_out.shape[0]), (0, 0)))
     own_pack = pack_params(sz, head_params[0], shared_params[0])
-    weights, weight_out, pack = both_sections([own_weights, own_out, own_pack], 0)
-
-    kept = []
-    residual = first_in
-    for layer in range(2):
-        in_gain = pack[layer, GAIN_ROW]
-        normed = input_norm(residual, in_gain).astype(BF16)
-        (gathered,) = gather_rows(count, normed, None, 1)
-        partial, squares, proj, mixed, states = forward_core(
-            sz, layer, resets, gathered, weights, weight_out, pack, rows
+    weights, weight_out, pack, rows_zero = opening(
+        count, sz, own_weights, own_out, own_pack, first, 0
+    )
+    def run_forward(layer, gathered):
+        return forward_core(sz, layer, resets, gathered, weights, weight_out, pack, rows)
+
+    def run_backward(layer, out_grads, kept, stats):
+        _, _, proj, mixed, states = kept
+        return backward_core(
+            sz, layer, resets, out_grads, proj, mixed, states, stats, weights, weight_out, pack, order, rows
         )
-        summed, all_squares = scatter_rows(count, partial, squares, 2)
-        scale = lax.rsqrt(jnp.sum(all_squares, axis=0)[0] / (HEADS * HDIM) + EPS_NORM)
-        branch = summed * scale[:, None]
-        result = (residual + live * branch).astype(BF16)
-        kept.append((residual, in_gain, gathered, proj, mixed, states, scale, branch, result))
-        residual = result.astype(F32)
-
-    upstream = last_grad
-    made = [None, None]
-    input_grads = [None, None]
-    for layer in (1, 0):
-        residual, in_gain, gathered, proj, mixed, states, scale, branch, _ = kept[layer]
-        out_grad = (live * upstream).astype(BF16)
-        along = jnp.sum(out_grad.astype(F32) * branch, axis=1)
-        stats = jnp.stack([scale, along])
-        stats = jnp.pad(stats, ((0, 6), (0, LANES - rows)))
-        out_grads, all_stats = gather_rows(count, out_grad, stats, 3)
-        all_stats = all_stats[:, :2, :rows].transpose(0, 2, 1).reshape(tokens, 2)
-        all_stats = jnp.pad(all_stats, ((0, 0), (0, LANES - 2)))
-        grad_rows, grads_t, scaled, small = backward_core(
-            sz, layer, resets, out_grads, proj, mixed, states, all_stats, weights, weight_out, pack, order
-        )
-        (grad_normed,) = scatter_rows(count, grad_rows, None, 4)
-        in_t, out_w = weight_grads(sz, grads_t, gathered, scaled, out_grads)
-        _, in_pull = jax.vjp(input_norm, residual, in_gain)
-        grad_res, grad_in_gain = in_pull(grad_normed)
-        small = jnp.concatenate(
-            [small[:GAIN_ROW], grad_in_gain[None], small[GAIN_ROW + 1 :]], axis=0
-        )
-        made[layer] = [in_t, out_w, small]
-        grad_res = grad_res + upstream
-        input_grads[layer] = grad_res
-        upstream = grad_res.astype(BF16).astype(F32)
-
-    sum_t, sum_out, small, layer_outs, grad_buffer = trade_sections(
-        list(zip(made[0], made[1])),
-        [(kept[0][8], kept[1][8]), (input_grads[0], input_grads[1])],
-        5,
-    )
-    grad_in = sum_t[: sz.master].T
-    grad_out = sum_out[: heads * HDIM]
-
-    state_part = sum_t[sz.master_pad :].astype(BF16)
-    share_rows = 16 * count
-    (state_own,) = scatter_rows(count, state_part.reshape(share_rows, -1), None, 6)
-    (state_all,) = gather_rows(count, state_own.astype(BF16), None, 7)
-    grad_state = state_all.reshape(state_part.shape).astype(F32).T
+
+    kept_zero = run_forward(0, rows_zero)
+    result_zero, branch_zero, total_zero, rows_one = after_forward(
+        count, sz, 0, kept_zero[0], kept_zero[1], first, live, pack, None, 1
+    )
+    kept_one = run_forward(1, rows_one)
+    result_one, _, _, out_grads_one, stats_one = after_forward(
+        count, sz, 1, kept_one[0], kept_one[1], result_zero, live, pack, cot, 2
+    )
+    back_one = run_backward(1, out_grads_one, kept_one, stats_one)
+    grad_one, low_one, gain_one, out_grads_zero, stats_zero = after_backward(
+        count, sz, 1, back_one[0], result_zero, cot, live, pack, (branch_zero, total_zero), 3
+    )
+    back_zero = run_backward(0, out_grads_zero, kept_zero, stats_zero)
+    grad_zero, _, gain_zero = after_backward(
+        count, sz, 0, back_zero[0], first, low_one, live, pack, None, 4
+    )
+    made_zero = list(weight_grads(sz, back_zero[1], rows_zero, back_zero[2], out_grads_zero))
+    made_one = list(weight_grads(sz, back_one[1], rows_one, back_one[2], out_grads_one))
+
+    def with_gain(small, gain):
+        return jnp.concatenate([small[:GAIN_ROW], gain, small[GAIN_ROW + 1 :]], axis=0)
+
+    lower = [made_zero[0], made_zero[2], made_zero[1], with_gain(back_zero[3], gain_zero)]
+    upper = [made_one[0], made_one[2], made_one[1], with_gain(back_one[3], gain_one)]
+    grad_in, grad_out, state_sum, small, layer_outs, grad_buffer, squares = trade_sections(
+        list(zip(lower, upper)), [(result_zero, result_one), (grad_zero, grad_one)], 2, 5
+    )
+
+    state_part = state_sum.astype(BF16)
     chans = heads * HDIM
+    shared_len = shared_params.shape[1]
+    lines = -(-shared_len // (count * LANES))
     conv_rows = small[: CONV + 1, sz.channels : sz.conv].reshape(-1)
     shared_own = jnp.concatenate([conv_rows, small[GAIN_ROW]])
-    shared_rows = -(-shared_own.shape[0] // (8 * LANES)) * 8
-    shared_own = jnp.pad(shared_own, (0, shared_rows * LANES - shared_own.shape[0]))
-    shared_all = gather_small(count, shared_own.reshape(shared_rows, LANES), 8)
-    grad_shared = jnp.sum(shared_all, axis=0).reshape(-1)[: shared_params.shape[1]]
+    shared_own = jnp.pad(shared_own, (0, count * lines * LANES - shared_len))
+    shared_own = jnp.pad(shared_own.reshape(count, lines, LANES), ((0, 0), (0, 8 - lines), (0, 0)))
+    state_own, shared_parts = scatter_rows(
+        count, state_part.reshape(16 * count, -1), shared_own, 6
+    )
+    shared_piece = jnp.sum(shared_parts, axis=0)
     head_part = head_params[0]
     taps = small[:CONV, :chans].reshape(CONV, heads, HDIM).transpose(1, 0, 2).reshape(heads, -1)
     grad_head = jnp.concatenate(
@@ -1180,24 +1451,26 @@
         ],
         axis=1,
     )
-    local_sq = (
-        jnp.sum(sum_t[: sz.master] ** 2) + jnp.sum(grad_out * grad_out) + jnp.sum(grad_head * grad_head)
-    )
-    local_sq = local_sq + (jnp.sum(grad_state * grad_state) + jnp.sum(grad_shared * grad_shared)) / count
-    sums = gather_small(count, jnp.full((8, LANES), local_sq, F32), 9)
-    section_sq = jnp.sum(sums[:, 0, 0])
+    local_sq = jnp.sum(squares) + jnp.sum(grad_head * grad_head)
+    local_sq = local_sq + jnp.sum(state_own * state_own) + jnp.sum(shared_piece * shared_piece)
+    stats = shared_piece.at[7].set(local_sq)
+    state_all, all_stats = gather_rows(count, state_own.astype(BF16), stats, 7)
+    grad_state = state_all.reshape(state_part.shape)
+    grad_shared = all_stats[:, :lines].reshape(-1)[:shared_len]
+    section_sq = jnp.sum(all_stats[:, 7, 0])
     norm_sq = section_sq + lax.ppermute(section_sq, "section", [(0, 1), (1, 0)])
     grad_norm = jnp.sqrt(norm_sq)
     threshold = CLIP_COEF * PARAMS**0.5
     clip_scale = threshold / jnp.maximum(grad_norm, threshold)
-    new_in = adam_update(
-        proj_in[0], proj_in_m[0], proj_in_v[0], clip_scale * grad_in, LEARN_MATRIX, WEIGHT_DECAY
-    )
-    new_state = adam_update(
-        proj_state[0], proj_state_m[0], proj_state_v[0], clip_scale * grad_state, LEARN_MATRIX, WEIGHT_DECAY
-    )
-    new_out = adam_update(
-        proj_out[0], proj_out_m[0], proj_out_v[0], clip_scale * grad_out, LEARN_MATRIX, WEIGHT_DECAY
+    clip = clip_scale.reshape(1)
+    new_in = adam_in(
+        sz, clip, grad_in, columns_first(proj_in), columns_first(proj_in_m), columns_first(proj_in_v)
+    )
+    new_out = adam_plain(
+        clip, grad_out, proj_out[0], proj_out_m[0], proj_out_v[0], False
+    )
+    new_state = adam_plain(
+        clip, grad_state, proj_state[0], proj_state_m[0], proj_state_v[0], True
     )
     new_head = adam_update(
         head_part, head_m[0], head_v[0], clip_scale * grad_head, LEARN_VECTOR, 0.0
@@ -1205,22 +1478,23 @@
     new_shared = adam_update(
         shared_params[0], shared_m[0], shared_v[0], clip_scale * grad_shared, LEARN_VECTOR, 0.0
     )
+    back_view = [jnp.transpose(array, (1, 2, 0)) for array in new_in[:3]]
     return (
         layer_outs[None],
         grad_buffer[None],
         grad_norm,
-        new_in[0][None],
-        new_in[1][None],
-        new_in[2][None],
-        new_in[0][None].astype(BF16),
+        back_view[0],
+        back_view[1],
+        back_view[2],
+        new_in[3].T[None],
         new_state[0][None],
         new_state[1][None],
         new_state[2][None],
-        new_state[0][None].astype(BF16),
+        new_state[3][None],
         new_out[0][None],
         new_out[1][None],
         new_out[2][None],
-        new_out[0][None].astype(BF16),
+        new_out[3][None],
         new_head[0][None],
         new_head[1][None],
         new_head[2][None],

time: 724 us -> 598 us (0.83)
  the two profiles are of different devices: /device:TPU:13 before, /device:TPU:0 now
where the time goes in v2:
time: 598 us; the launch traced here: 588 us
  Pallas kernels  539 us (90%)
  other arithmetic  23.1 us (4%)
  local copies, waits for them, and re-layouts  16 us (3%)
  between operations  9.15 us (2%)
    pallas_call x2, Pallas kernels, after_forward(): pl.pallas_call(kernel, out_shape=out_shape, in_specs=[VMEM_SPEC] * len(op...  156 us
    pallas_call x2, Pallas kernels, after_backward(): pl.pallas_call(kernel, out_shape=out_shape, in_specs=[VMEM_SPEC] * len(op...  107 us
    pallas_call x2, Pallas kernels, backward_core(): pl.pallas_call(kernel, grid=(blocks,), out_shape=[jax.ShapeDtypeStruct((s...  60 us
    pallas_call x1, Pallas kernels, opening(): pl.pallas_call(kernel, out_shape=[jax.ShapeDtypeStruct((2,) + own_weights...  45.3 us
    pallas_call x2, Pallas kernels, forward_core(): pl.pallas_call(kernel, grid=(sz.blocks,), out_shape=[jax.ShapeDtypeStruct...  38.2 us
    pallas_call x1, Pallas kernels, gather_rows(): pl.pallas_call(kernel, out_shape=[jax.ShapeDtypeStruct((count * rows, wid...  23.2 us
    pallas_call x2, Pallas kernels, weight_grads(): pl.pallas_call(kernel, grid=(width // cols,), out_shape=[jax.ShapeDtypeSt...  22.2 us
    pallas_call x1, Pallas kernels, scatter_rows(): pl.pallas_call(kernel, out_shape=[jax.ShapeDtypeStruct((rows, width), F32...  21.5 us
  transfers between devices with their start and end apart: 1, of which 1 were waited for; matrix products, arithmetic and copies ran while one was open for 0% of the time, Pallas kernels for 0%

profile of v2, /device:TPU:0, one launch (start us, length us, event | category | flops | bytes accessed | tf_op | source)
XLA Modules:
  0.0 588.0 jit_solution(12680123319909193136)
XLA Ops:
  0.7 0.8 bitcast_select_fusion
  1.5 1.2 compare_convert_fusion
  2.7 1.0 fusion.9
  3.7 0.7 slice.150
  4.4 0.7 slice_reduce_fusion.1
  5.1 0.8 fusion.14
  10.6 2.7 bitcast_convert_fusion.wo_ref
  14.7 0.8 dynamic-slice_bitcast_fusion
  15.5 11.8 %prepare_weights.1.w_ref = bf16[896,2048]{1,0:T(8,128)(2,1)} custom-call(f32[516,1,2048]{2,1,0:T(1,128)} %bitcast.70, f32[2048,256]{1,0:T(8,128)} %bitcast.73, bf16[896,896]{1,0:T(8,128)(2,1)} %constant.123.clone.order_ref), custom_call_target="tpu_custom_call" | custom-call | tf_op jit(solution)/shard_map/prepare_weights/pallas_call | solution.py:894
  27.3 1.3 subtract_compare_fusion.1
  28.6 1.4 concatenate.51.pk_ref
  30.0 45.3 %opening.1 = (bf16[2,896,2048]{2,1,0:T(8,128)(2,1)}, bf16[2,256,2048]{2,1,0:T(8,128)(2,1)}, f32[2,16,2048]{2,1,0:T(8,128)}, bf16[1024,2048]{1,0:T(8,128)(2,1)}) custom-call(bf16[896,2048]{1,0:T(8,128)(2,1)} %prepare_weights.1.w_ref, bf16[256,2048]{1,0:T(8,128)(2,1)} %bitcast_convert_fusion.wo_ref, f32[16,2048]{1,0:T(8,128)} %concatenate.51.pk_ref, ...), custom_call_target="tpu_custom_call" | custom-call | tf_op jit(solution)/shard_map/opening/pallas_call | solution.py:535
  75.3 19.1 %forward_core.2 = (bf16[1024,2048]{1,0:T(8,128)(2,1)}, f32[16,8,64]{2,1,0:T(8,128)}, f32[1024,896]{1,0:T(8,128)}, f32[1024,256]{1,0:T(8,128)}, f32[8,128,256]{2,1,0:T(8,128)}) custom-call(f32[4]{0:T(128)} %get-tuple-element.175.reset_ref, bf16[1024,2048]{1,0:T(8,128)(2,1)} %get-tuple-element.98.h_ref, bf16[2,896,2048]{2,1,0:T(8,128)(2,1)} %get-tuple-element.99.w_ref, ...), custom_call_target="tpu_custom_call" | custom-call | tf_op jit(solution)/shard_map/forward_core/pallas_call | solution.py:1014
  94.4 0.7 select_select_fusion.refs_3_
  95.1 79.1 %after_forward.2 = (bf16[64,2048]{1,0:T(8,128)(2,1)}, f32[64,2048]{1,0:T(8,128)}, f32[8,64]{1,0:T(8,128)}, bf16[1024,2048]{1,0:T(8,128)(2,1)}) custom-call(bf16[1024,2048]{1,0:T(8,128)(2,1)} %get-tuple-element.102.refs_0_, f32[16,8,64]{2,1,0:T(8,128)} %get-tuple-element.103.refs_1_, bf16[64,2048]{1,0:T(8,128)(2,1)} %get-tuple-element.197.x_ref.refs_2_.refs_1_, ...), custom_call_target="tpu_custom_call" | custom-call | tf_op jit(solution)/shard_map/after_forward/pallas_call | solution.py:626
  174.2 19.1 %forward_core.3 = (bf16[1024,2048]{1,0:T(8,128)(2,1)}, f32[16,8,64]{2,1,0:T(8,128)}, f32[1024,896]{1,0:T(8,128)}, f32[1024,256]{1,0:T(8,128)}, f32[8,128,256]{2,1,0:T(8,128)}) custom-call(f32[4]{0:T(128)} %get-tuple-element.175.reset_ref, bf16[1024,2048]{1,0:T(8,128)(2,1)} %get-tuple-element.104.h_ref, bf16[2,896,2048]{2,1,0:T(8,128)(2,1)} %get-tuple-element.99.w_ref, ...), custom_call_target="tpu_custom_call" | custom-call | tf_op jit(solution)/shard_map/forward_core/pallas_call | solution.py:1014
  193.3 77.1 %after_forward.3 = (bf16[64,2048]{1,0:T(8,128)(2,1)}, f32[64,2048]{1,0:T(8,128)}, f32[8,64]{1,0:T(8,128)}, bf16[1024,2048]{1,0:T(8,128)(2,1)}, f32[16,8,128]{2,1,0:T(8,128)}) custom-call(bf16[1024,2048]{1,0:T(8,128)(2,1)} %get-tuple-element.105.refs_0_, f32[16,8,64]{2,1,0:T(8,128)} %get-tuple-element.106.refs_1_, ...), custom_call_target="tpu_custom_call" | custom-call | tf_op jit(solution)/shard_map/after_forward/pallas_call | solution.py:626
  270.4 30.0 %backward_core.2 = (bf16[1024,2048]{1,0:T(8,128)(2,1)}, bf16[896,1024]{1,0:T(8,128)(2,1)}, bf16[1024,256]{1,0:T(8,128)(2,1)}, f32[16,2048]{1,0:T(8,128)}) custom-call(f32[4]{0:T(128)} %get-tuple-element.175.reset_ref, bf16[1024,2048]{1,0:T(8,128)(2,1)} %get-tuple-element.108.g_ref, f32[1024,896]{1,0:T(8,128)} %get-tuple-element.109.p_ref.halo_ref, ...), custom_call_target="tpu_custom_call" | custom-call | tf_op jit(solution)/shard_map/backward_core/pallas_call | solution.py:1186
  300.4 0.8 slice.139
  301.2 71.7 %after_backward.2 = (f32[64,2048]{1,0:T(8,128)}, bf16[64,2048]{1,0:T(8,128)(2,1)}, f32[1,2048]{1,0:T(1,128)}, bf16[1024,2048]{1,0:T(8,128)(2,1)}, f32[16,8,128]{2,1,0:T(8,128)}) custom-call(bf16[1024,2048]{1,0:T(8,128)(2,1)} %get-tuple-element.113.refs_0_, bf16[64,2048]{1,0:T(8,128)(2,1)} %get-tuple-element.107.refs_2_.refs_1_.refs_8_, ...), custom_call_target="tpu_custom_call" | custom-call | tf_op jit(solution)/shard_map/after_backward/pallas_call | solution.py:686
  372.9 30.0 %backward_core.3 = (bf16[1024,2048]{1,0:T(8,128)(2,1)}, bf16[896,1024]{1,0:T(8,128)(2,1)}, bf16[1024,256]{1,0:T(8,128)(2,1)}, f32[16,2048]{1,0:T(8,128)}) custom-call(f32[4]{0:T(128)} %get-tuple-element.175.reset_ref, bf16[1024,2048]{1,0:T(8,128)(2,1)} %get-tuple-element.116.g_ref, f32[1024,896]{1,0:T(8,128)} %get-tuple-element.117.p_ref.halo_ref, ...), custom_call_target="tpu_custom_call" | custom-call | tf_op jit(solution)/shard_map/backward_core/pallas_call | solution.py:1186
  403.0 0.8 slice.137
  403.8 11.1 %weight_grads.3 = (bf16[640,2048]{1,0:T(8,128)(2,1)}, f32[256,2048]{1,0:T(8,128)}, bf16[256,2048]{1,0:T(8,128)(2,1)}) custom-call(bf16[896,1024]{1,0:T(8,128)(2,1)} %get-tuple-element.124.gt_ref, bf16[1024,2048]{1,0:T(8,128)(2,1)} %get-tuple-element.104.h_ref, bf16[1024,256]{1,0:T(8,128)(2,1)} %get-tuple-element.125.q_ref, ...), custom_call_target="tpu_custom_call" | custom-call | tf_op jit(solution)/shard_map/weight_grads/pallas_call | solution.py:1239
  414.9 35.7 %after_backward.3 = (f32[64,2048]{1,0:T(8,128)}, bf16[64,2048]{1,0:T(8,128)(2,1)}, f32[1,2048]{1,0:T(1,128)}) custom-call(bf16[1024,2048]{1,0:T(8,128)(2,1)} %get-tuple-element.132.refs_0_, bf16[64,2048]{1,0:T(8,128)(2,1)} %get-tuple-element.197.x_ref.refs_2_.refs_1_, bf16[64,2048]{1,0:T(8,128)(2,1)} %get-tuple-element.133.refs_2_, ...), custom_call_target="tpu_custom_call" | custom-call | tf_op jit(solution)/shard_map/after_backward/pallas_call | solution.py:686
  450.6 11.2 %weight_grads.2 = (bf16[640,2048]{1,0:T(8,128)(2,1)}, f32[256,2048]{1,0:T(8,128)}, bf16[256,2048]{1,0:T(8,128)(2,1)}) custom-call(bf16[896,1024]{1,0:T(8,128)(2,1)} %get-tuple-element.121.gt_ref, bf16[1024,2048]{1,0:T(8,128)(2,1)} %get-tuple-element.98.h_ref, bf16[1024,256]{1,0:T(8,128)(2,1)} %get-tuple-element.122.q_ref, ...), custom_call_target="tpu_custom_call" | custom-call | tf_op jit(solution)/shard_map/weight_grads/pallas_call | solution.py:1239
  461.8 0.7 pad_maximum_fusion.1.refs_7_
  462.5 0.7 pad_maximum_fusion.refs_6_
  463.2 20.3 %trade_sections.1 = (f32[640,2048]{1,0:T(8,128)}, f32[256,2048]{1,0:T(8,128)}, f32[256,2048]{1,0:T(8,128)}, f32[16,2048]{1,0:T(8,128)}, bf16[2,64,2048]{2,1,0:T(...) custom-call(bf16[640,2048]{1,0:T(8,128)(2,1)} %get-tuple-element.123.refs_0_, ...), custom_call_target="tpu_custom_call" | custom-call | tf_op jit(solution)/shard_map/trade_sections/pallas_call | solution.py:761
  483.5 0.7 slice_bitcast_fusion.1
  484.2 0.7 slice.142
  484.9 0.8 slice_reduce_fusion.4
  485.7 0.8 slice.141
  486.5 0.7 slice.140
  487.2 1.5 reduce_sum.74
  491.0 2.8 convert_element_type.29.in_ref
  493.8 21.5 %scatter_rows.1 = (f32[16,2048]{1,0:T(8,128)}, f32[16,8,128]{2,1,0:T(8,128)}) custom-call(bf16[256,2048]{1,0:T(8,128)(2,1)} %convert_element_type.29.in_ref, f32[16,8,128]{2,1,0:T(8,128)} %pad.39.small_ref), custom_call_target="tpu_custom_call" | custom-call | tf_op jit(solution)/shard_map/scatter_rows/pallas_call | solution.py:466
  515.3 2.2 multiply_reduce_fusion
  517.5 0.9 reduce_sum.73
  522.2 23.2 %gather_rows.1 = (bf16[256,2048]{1,0:T(8,128)(2,1)}, f32[16,8,128]{2,1,0:T(8,128)}) custom-call(bf16[16,2048]{1,0:T(8,128)(2,1)} %get-tuple-element.183.own_ref, f32[8,128]{1,0:T(8,128)} %copy-done.8), custom_call_target="tpu_custom_call" | custom-call | tf_op jit(solution)/shard_map/gather_rows/pallas_call | solution.py:429
  545.4 1.5 slice_reduce_fusion
  547.4 0.7 collective-permute-done
  549.5 0.8 slice_multiply_fusion
  551.0 0.7 multiply_subtract_fusion
  551.7 9.6 %adam_plain.2 = (f32[2048,256]{1,0:T(8,128)}, f32[2048,256]{1,0:T(8,128)}, f32[2048,256]{1,0:T(8,128)}, bf16[2048,256]{1,0:T(8,128)(2,1)}) custom-call(f32[1]{0:T(128)} %bitcast.26.clip_ref, bf16[256,2048]{1,0:T(8,128)(2,1)} %get-tuple-element.153.g_ref, f32[2048,256]{1,0:T(8,128)} %bitcast.74, f32[2048,256]{1,0:T(8,128)} %bitcast.77, f32[2048,256]{1,0:T(8,128)} %bitcast.78), custom_call_target="tpu_custom_call" | custom-call | tf_op jit(solution)/shard_map/adam_plain/pallas_call | solution.py:1330
  561.3 16.0 %adam_in.1 = (f32[516,1,2048]{2,1,0:T(1,128)}, f32[516,1,2048]{2,1,0:T(1,128)}, f32[516,1,2048]{2,1,0:T(1,128)}, bf16[516,2048]{1,0:T(8,128)(2,1)}) custom-call(f32[1]{0:T(128)} %bitcast.26.clip_ref, f32[640,2048]{1,0:T(8,128)} %get-tuple-element.148.g_ref, f32[516,1,2048]{2,1,0:T(1,128)} %bitcast.71, f32[516,1,2048]{2,1,0:T(1,128)} %bitcast.75, ...), custom_call_target="tpu_custom_call" | custom-call | tf_op jit(solution)/shard_map/adam_in/pallas_call | solution.py:1299
  577.4 7.3 %adam_plain.3 = (f32[256,2048]{1,0:T(8,128)}, f32[256,2048]{1,0:T(8,128)}, f32[256,2048]{1,0:T(8,128)}, bf16[256,2048]{1,0:T(8,128)(2,1)}) custom-call(f32[1]{0:T(128)} %bitcast.26.clip_ref, f32[256,2048]{1,0:T(8,128)} %get-tuple-element.158.g_ref, f32[256,2048]{1,0:T(8,128)} %bitcast.72, f32[256,2048]{1,0:T(8,128)} %bitcast.79, f32[256,2048]{1,0:T(8,128)} %bitcast.80), custom_call_target="tpu_custom_call" | custom-call | tf_op jit(solution)/shard_map/adam_plain/pallas_call | solution.py:1330
  584.6 0.8 copy.84
  585.4 1.0 copy.85
  (83 shorter events, 8.1 us)
Async XLA Ops:
  0.7 14.0 %slice-start = ((f32[1,3328]{1,0:T(1,128)}), f32[1,256]{1,0:T(1,128)S(1)}, s32[]{:S(2)}) async-start(f32[1,3328]{1,0:T(1,128)} %param.38), calls=%async_computation | async-start | bytes 2048 | tf_op jit(solution)/shard_map/slice | solution.py:919
  0.7 14.0 %copy-start.4 = (bf16[2,64,2048]{2,1,0:T(8,128)(2,1)S(1)}, bf16[2,64,2048]{2,1,0:T(8,128)(2,1)}, u32[]{:S(2)}) copy-start(bf16[2,64,2048]{2,1,0:T(8,128)(2,1)} %param.24) | copy-start | bytes 1572868
  0.7 14.0 %copy-start.5 = (bf16[2,64,2048]{2,1,0:T(8,128)(2,1)S(1)}, bf16[2,64,2048]{2,1,0:T(8,128)(2,1)}, u32[]{:S(2)}) copy-start(bf16[2,64,2048]{2,1,0:T(8,128)(2,1)} %param.23) | copy-start | bytes 1572868
  15.5 13.1 %slice-start.1 = ((f32[1,3328]{1,0:T(1,128)}), f32[1,2048]{1,0:T(1,128)S(1)}, s32[]{:S(2)}) async-start(f32[1,3328]{1,0:T(1,128)} %param.38), calls=%async_computation.1 | async-start | bytes 16384 | tf_op jit(solution)/shard_map/slice | solution.py:920
  450.6 11.2 %copy-start.2 = (f32[16,2048]{1,0:T(8,128)S(1)}, f32[16,2048]{1,0:T(8,128)}, u32[]{:S(2)}) copy-start(f32[16,2048]{1,0:T(8,128)} %get-tuple-element.135) | copy-start | bytes 393220
  450.6 11.2 %copy-start.13 = (f32[1,2048]{1,0:T(1,128)S(1)}, f32[1,2048]{1,0:T(1,128)}, u32[]{:S(2)}) copy-start(f32[1,2048]{1,0:T(1,128)} %get-tuple-element.136) | copy-start | bytes 24580
  450.6 11.9 %copy-start.3 = (f32[16,2048]{1,0:T(8,128)S(1)}, f32[16,2048]{1,0:T(8,128)}, u32[]{:S(2)}) copy-start(f32[16,2048]{1,0:T(8,128)} %get-tuple-element.131) | copy-start | bytes 393220
  450.6 11.9 %copy-start.14 = (f32[1,2048]{1,0:T(1,128)S(1)}, f32[1,2048]{1,0:T(1,128)}, u32[]{:S(2)}) copy-start(f32[1,2048]{1,0:T(1,128)} %get-tuple-element.134) | copy-start | bytes 24580
  463.2 25.6 %copy-start.6 = (f32[1,4,387]{2,1,0:T(4,128)S(1)}, f32[1,4,387]{2,1,0:T(4,128)}, u32[]{:S(2)}) copy-start(f32[1,4,387]{2,1,0:T(4,128)} %param.35) | copy-start | bytes 18580
  491.0 59.4 %copy-start.11 = (f32[1,4,387]{2,1,0:T(4,128)S(1)}, f32[1,4,387]{2,1,0:T(4,128)}, u32[]{:S(2)}) copy-start(f32[1,4,387]{2,1,0:T(4,128)} %param.36) | copy-start | bytes 18580
  491.0 59.4 %copy-start.12 = (f32[1,4,387]{2,1,0:T(4,128)S(1)}, f32[1,4,387]{2,1,0:T(4,128)}, u32[]{:S(2)}) copy-start(f32[1,4,387]{2,1,0:T(4,128)} %param.37) | copy-start | bytes 18580
  491.0 60.0 %copy-start.7 = (f32[1,3328]{1,0:T(1,128)S(1)}, f32[1,3328]{1,0:T(1,128)}, u32[]{:S(2)}) copy-start(f32[1,3328]{1,0:T(1,128)} %param.38) | copy-start | bytes 39940
  491.0 60.0 %copy-start.9 = (f32[1,3328]{1,0:T(1,128)S(1)}, f32[1,3328]{1,0:T(1,128)}, u32[]{:S(2)}) copy-start(f32[1,3328]{1,0:T(1,128)} %param.39) | copy-start | bytes 39940
  491.0 60.0 %copy-start.10 = (f32[1,3328]{1,0:T(1,128)S(1)}, f32[1,3328]{1,0:T(1,128)}, u32[]{:S(2)}) copy-start(f32[1,3328]{1,0:T(1,128)} %param.40) | copy-start | bytes 39940
  521.6 0.6 copy-start.8
  546.9 1.2 collective-permute-start
  577.3 7.3 %copy-start.1 = (bf16[2,64,2048]{2,1,0:T(8,128)(2,1)S(1)}, bf16[2,64,2048]{2,1,0:T(8,128)(2,1)}, u32[]{:S(2)}) copy-start(bf16[2,64,2048]{2,1,0:T(8,128)(2,1)} %get-tuple-element.140) | copy-start | bytes 1572868
  577.3 8.1 %copy-start = (f32[2,64,2048]{2,1,0:T(8,128)S(1)}, f32[2,64,2048]{2,1,0:T(8,128)}, u32[]{:S(2)}) copy-start(f32[2,64,2048]{2,1,0:T(8,128)} %get-tuple-element.141) | copy-start | bytes 3145732

commit v3 on v2

v3 whole, which is shorter than its diff:
```python
import itertools

import jax
import jax.numpy as jnp
import numpy as np
from jax import lax
from jax.experimental import pallas as pl
from jax.experimental.pallas import tpu as pltpu
from jax.sharding import PartitionSpec as P

HEADS = 64
HDIM = 64
NSTATE = 128
CONV = 4
STRETCH = 256
ADAM_STEP = 5
PARAMS = 51698560

HIGH = lax.Precision.HIGHEST
EPS_NORM = 1e-05
ADAM_EPS = 1e-08
BETA_ONE = 0.5
BETA_TWO = 0.5
CLIP_COEF = 0.2
LEARN_MATRIX = 0.02
LEARN_VECTOR = 0.2
WEIGHT_DECAY = 0.1

F32 = jnp.float32
BF16 = jnp.bfloat16
MESH = pl.DeviceIdType.MESH
LANES = 128
CHUNK = 128
COLS = HDIM * 2 + 1
GAIN_ROW = 9
VMEM_LIMIT = 56 << 20


def seq_layout(lengths_row):
    block_count = lengths_row.shape[0]
    block_idx = jnp.arange(block_count, dtype=jnp.int32)
    starts = lengths_row > 0
    start_block = lax.cummax(jnp.where(starts, block_idx, 0), axis=0)
    owner_mask = (start_block[:, None] == block_idx[None, :]).astype(jnp.int32)
    seq_length = jnp.sum(owner_mask * lengths_row[None, :], axis=1)
    return (start_block, seq_length, starts.astype(jnp.float32))


def chip_dims(count):
    side = 4 if count % 64 == 0 else 2
    if count % (side * side) != 0:
        return (count, 1, 1)
    return (count // (side * side), side, side)


def place(dims):
    me = lax.axis_index("head")
    return (me // (dims[1] * dims[2]), (me // dims[2]) % dims[1], me % dims[2])


def linear(dims, spot):
    return (spot[0] * dims[1] + spot[1]) * dims[2] + spot[2]


def moved(dims, spot, shifts):
    return tuple(s if d == 0 else (s + d) % n for s, d, n in zip(spot, shifts, dims))


def shift_of(order, offsets):
    out = [0, 0, 0]
    for axis, off in zip(order, offsets):
        out[axis] = off
    return out


def greet_axes(dims, spot):
    barrier = pltpu.get_barrier_semaphore()
    count = 0
    for axis in range(3):
        for off in range(1, dims[axis]):
            peer = linear(dims, moved(dims, spot, shift_of((axis,), (off,))))
            pl.semaphore_signal(
                barrier, inc=1, device_id={"head": peer}, device_id_type=MESH
            )
            count += 1
    if count:
        pl.semaphore_wait(barrier, count)


def greet_all(count, pair=None):
    barrier = pltpu.get_barrier_semaphore()
    me = lax.axis_index("head")
    if pair is not None:
        other = 1 - lax.axis_index(pair)
        pl.semaphore_signal(barrier, inc=1, device_id={pair: other}, device_id_type=MESH)
    for off in range(1, count):
        pl.semaphore_signal(
            barrier, inc=1, device_id={"head": (me + off) % count}, device_id_type=MESH
        )
    expected = count - 1 + (pair is not None)
    if expected:
        pl.semaphore_wait(barrier, expected)


def rows_at(shard, rows):
    return pl.ds(pl.multiple_of(shard * rows, rows), rows)


def column_parts(width, shares):
    tiles = width // LANES
    parts, start, taken = [], 0, 0
    for share, order, group in shares:
        taken += share
        stop = tiles * taken // 16 * LANES
        if stop > start:
            parts.append((start, stop - start, order, group))
            start = stop
    return parts


GATHER = ((2, (2, 1, 0), 0), (2, (1, 2, 0), 0), (6, (0, 2, 1), 0), (6, (0, 1, 2), 0))
GATHER_SMALL = ((8, (0, 2, 1), 0), (8, (0, 1, 2), 0))
SCATTER = (
    (1, (2, 0, 1), 0), (1, (1, 0, 2), 0), (1, (0, 1, 2), 0), (1, (0, 2, 1), 0),
    (3, (2, 1, 0), 0), (3, (1, 2, 0), 0), (3, (2, 1, 0), 1), (3, (1, 2, 0), 1),
)
SCATTER_SMALL = ((8, (2, 1, 0), 0), (8, (1, 2, 0), 0))
SCATTER_PACE = (0.3, 0.9, 0.7, 2.0)


def guarded(preds, action):
    preds = [pred for pred in preds if pred is not None]
    if not preds:
        action()
        return
    cond = preds[0]()
    for pred in preds[1:]:
        cond = jnp.logical_and(cond, pred())
    pl.when(cond)(action)


def gather_steps(dims, parts, rows, own_ref, all_ref, send_sem, recv_sem, between=()):
    spot = place(dims)
    me = linear(dims, spot)
    waits = []
    counter = [0] * len(parts)

    def lined(axis):
        return axis == 0 and dims[0] > 2 and dims[1] == 2

    def above(axis, dist):
        return lambda: spot[axis] + dist < dims[axis]

    def below(axis, dist):
        return lambda: spot[axis] >= dist

    def sources(part, pos):
        axis = parts[part][2][pos]
        if not lined(axis):
            return [(off, None) for off in range(1, dims[axis])]
        out = []
        for dist in range(1, dims[axis]):
            out.append((dist, above(axis, dist)))
            out.append((-dist, below(axis, dist)))
        return out

    def block(part, offsets):
        start, width, order, _ = parts[part]
        shard = linear(dims, moved(dims, spot, shift_of(order, offsets)))
        return shard, all_ref.at[rows_at(shard, rows), pl.ds(start, width)]

    def push(part, offsets, pos, preds, src, came):
        axis = parts[part][2][pos]
        shard, dst = block(part, offsets)
        up, down = (1, above(axis, 1)), (-1, below(axis, 1))
        if lined(axis):
            targets = [up, down] if came == 0 else [down] if came > 0 else [up]
        else:
            targets = [(off, None) for off in range(1, dims[axis])] if came == 0 else []
        for off, pred in targets:
            peer = linear(dims, moved(dims, spot, shift_of((axis,), (off,))))
            number = counter[part]
            counter[part] += 1

            def begin(peer=peer, number=number):
                pltpu.make_async_remote_copy(
                    src_ref=dst if src is None else src,
                    dst_ref=dst,
                    send_sem=send_sem.at[part, number],
                    recv_sem=recv_sem.at[part, shard],
                    device_id={"head": peer},
                    device_id_type=MESH,
                ).start()

            guarded([pred], begin)
            waits.append((preds + [pred], part, number))

    def visit(part, offsets, preds, pos, came):
        def body():
            shard, dst = block(part, offsets)
            pltpu.make_async_remote_copy(
                src_ref=dst,
                dst_ref=dst,
                send_sem=send_sem.at[part, 0],
                recv_sem=recv_sem.at[part, shard],
                device_id={"head": me},
                device_id_type=MESH,
            ).wait_recv()
            push(part, offsets, pos, preds, None, came)
            for later in range(pos + 1, 3):
                push(part, offsets, later, preds, None, 0)

        guarded(preds, body)

    for pos in range(3):
        for part, (start, width, _, _) in enumerate(parts):
            push(part, (0, 0, 0), pos, [], own_ref.at[:, pl.ds(start, width)], 0)
    todo = []
    for part in range(len(parts)):
        first, second, third = (sources(part, pos) for pos in range(3))
        for k, (oa, pa) in enumerate(first):
            todo.append(((0, k, part), part, (oa, 0, 0), [pa], 0, oa))
        for ka, (oa, pa) in enumerate([(0, None)] + first):
            for k, (ob, pb) in enumerate(second):
                todo.append(((1, ka + k, part), part, (oa, ob, 0), [pa, pb], 1, ob))
            for kb, (ob, pb) in enumerate([(0, None)] + second):
                for k, (oc, pc) in enumerate(third):
                    todo.append(
                        ((2, ka + kb + k, part), part, (oa, ob, oc), [pa, pb, pc], 2, oc)
                    )
    todo.sort(key=lambda entry: (sum(abs(off) for off in entry[2]), entry[0]))
    between = list(between)
    for _, part, offsets, preds, pos, came in todo:
        if between:
            between.pop(0)()
        visit(part, offsets, preds, pos, came)
    for work in between:
        work()
    for preds, part, number in waits:

        def settle(part=part, number=number):
            start, width, _, _ = parts[part]
            ref = own_ref.at[:, pl.ds(start, width)]
            pltpu.make_async_remote_copy(
                src_ref=ref,
                dst_ref=ref,
                send_sem=send_sem.at[part, number],
                recv_sem=recv_sem.at[part, 0],
                device_id={"head": me},
                device_id_type=MESH,
            ).wait_send()

        guarded(preds, settle)


def gather_sends(dims):
    return 3 * dims[0] * dims[1] * dims[2]


def scatter_steps(dims, parts, rows, in_ref, out_ref, box_ref, send_sem, recv_sem):
    spot = place(dims)
    me = linear(dims, spot)
    sends = []

    def size(part, pos):
        return dims[parts[part][2][pos]]

    def slot_one(part, ea, ob, oc):
        return ((ea - 1) * size(part, 1) + ob) * size(part, 2) + oc

    def slot_two(part, eb, oc):
        base = (size(part, 0) - 1) * size(part, 1) * size(part, 2)
        return base + (eb - 1) * size(part, 2) + oc

    def slot_three(part, ec):
        return slot_two(part, size(part, 1), 0) + ec - 1

    def cols(part):
        return pl.ds(parts[part][0], parts[part][1])

    def mine(part, offsets):
        shard = linear(dims, moved(dims, spot, shift_of(parts[part][2], offsets)))
        return in_ref.at[rows_at(shard, rows), cols(part)]

    def send(part, src, pos, off, slot):
        peer = linear(dims, moved(dims, spot, shift_of((parts[part][2][pos],), (off,))))
        copy = pltpu.make_async_remote_copy(
            src_ref=src,
            dst_ref=box_ref.at[slot, :, cols(part)],
            send_sem=send_sem.at[part, slot],
            recv_sem=recv_sem.at[part, slot],
            device_id={"head": peer},
            device_id_type=MESH,
        )
        copy.start()
        sends.append(copy)

    def arrived(part, slot):
        ref = box_ref.at[slot, :, cols(part)]
        pltpu.make_async_remote_copy(
            src_ref=ref,
            dst_ref=ref,
            send_sem=send_sem.at[part, slot],
            recv_sem=recv_sem.at[part, slot],
            device_id={"head": me},
            device_id_type=MESH,
        ).wait_recv()
        return ref[...].astype(F32)

    def combined(part, ob, oc, stages):
        total = mine(part, (0, ob, oc))[...].astype(F32)
        for ea in range(1, size(part, 0)):
            total = total + arrived(part, slot_one(part, ea, ob, oc))
        for eb in range(1, size(part, 1)) if stages > 1 else ():
            total = total + arrived(part, slot_two(part, eb, oc))
        for ec in range(1, size(part, 2)) if stages > 2 else ():
            total = total + arrived(part, slot_three(part, ec))
        return total

    def put_by(part, ob, oc, total):
        if size(part, 0) > 1:
            hold = box_ref.at[slot_one(part, 1, ob, oc), :, cols(part)]
        elif size(part, 1) > 1 and ob == 0:
            hold = box_ref.at[slot_two(part, 1, oc), :, cols(part)]
        else:
            return mine(part, (0, ob, oc))
        hold[...] = total.astype(box_ref.dtype)
        return hold

    def first(part, ob, oc, off):
        slot = slot_one(part, size(part, 0) - off, ob, oc)
        send(part, mine(part, (off, ob, oc)), 0, off, slot)

    def second(part, ob, oc, _):
        hold = put_by(part, ob, oc, combined(part, ob, oc, 1))
        send(part, hold, 1, ob, slot_two(part, size(part, 1) - ob, oc))

    def third(part, _, oc, __):
        hold = put_by(part, 0, oc, combined(part, 0, oc, 2))
        send(part, hold, 2, oc, slot_three(part, size(part, 2) - oc))

    def last(part, _, __, ___):
        out_ref[:, cols(part)] = combined(part, 0, 0, 3)

    lag, rest, turn, end = SCATTER_PACE
    program = []
    for part, (_, _, _, group) in enumerate(parts):
        for ob, oc in itertools.product(range(size(part, 1)), range(size(part, 2))):
            for off in range(1, size(part, 0)):
                rank = (0.0 if ob else rest) + group * lag
                program.append((rank, oc == 0, off, part, first, ob, oc))
            if ob:
                program.append((turn + group * lag, oc == 0, 0, part, second, ob, oc))
        for oc in range(1, size(part, 2)):
            program.append((end + group * lag, False, 0, part, third, 0, oc))
        program.append((3.0 + group * lag, True, 0, part, last, 0, 0))
    program.sort(key=lambda step: step[:4])
    for _, _, off, part, action, ob, oc in program:
        action(part, ob, oc, off)
    return sends


class PlaneScatter:
    def __init__(self, dims, rows, width):
        self.dims, self.rows, self.half = dims, rows, width // 2
        self.orders = ((2, 1), (1, 2))
        self.width = width
        depth = dims[0]
        most = max(dims[1], dims[2])
        self.one = depth * (most - 1) * most
        self.two = depth * (most - 1)
        self.slots = max(self.one + self.two + depth, 1)

    def scratch(self):
        return [
            pltpu.VMEM((self.slots, self.rows, self.width), BF16),
            DMA((2, self.slots)),
            DMA((2, self.slots)),
        ]

    def bind(self, part_ref, out_ref, box_ref, send_sem, recv_sem):
        self.part_ref, self.out_ref, self.box_ref = part_ref, out_ref, box_ref
        self.send_sem, self.recv_sem = send_sem, recv_sem
        self.spot = place(self.dims)
        self.me = linear(self.dims, self.spot)

    def sizes(self, part):
        a, b = self.orders[part]
        return self.dims[a], self.dims[b]

    def slot_one(self, part, plane, ea, ob):
        size_a, size_b = self.sizes(part)
        return (plane * (size_a - 1) + ea - 1) * size_b + ob

    def slot_two(self, part, plane, eb):
        return self.one + plane * (self.sizes(part)[1] - 1) + eb - 1

    def slot_three(self, plane):
        return self.one + self.two + plane

    def cols(self, part):
        return pl.ds(part * self.half, self.half)

    def mine(self, part, plane, oa, ob):
        shift = shift_of(self.orders[part], (oa, ob))
        spot = moved(self.dims, (plane, self.spot[1], self.spot[2]), shift)
        return self.part_ref.at[rows_at(linear(self.dims, spot), self.rows), self.cols(part)]

    def copy(self, part, src, slot, sent, peer):
        return pltpu.make_async_remote_copy(
            src_ref=src,
            dst_ref=self.box_ref.at[slot, :, self.cols(part)],
            send_sem=self.send_sem.at[part, sent],
            recv_sem=self.recv_sem.at[part, slot],
            device_id={"head": peer},
            device_id_type=MESH,
        )

    def peer(self, part, pos, off):
        shift = shift_of((self.orders[part][pos],), (off,))
        return linear(self.dims, moved(self.dims, self.spot, shift))

    def arrived(self, part, slot):
        ref = self.box_ref.at[slot, :, self.cols(part)]
        self.copy(part, ref, slot, slot, self.me).wait_recv()
        return ref[...].astype(F32)

    def first(self, plane):
        for inner in (1, 0):
            for part in range(2):
                size_a, size_b = self.sizes(part)
                for ob in range(size_b):
                    if (ob != 0) != bool(inner):
                        continue
                    for off in range(1, size_a):
                        slot = self.slot_one(part, plane, size_a - off, ob)
                        src = self.mine(part, plane, off, ob)
                        self.copy(part, src, slot, slot, self.peer(part, 0, off)).start()

    def second(self, plane):
        for part in range(2):
            size_a, size_b = self.sizes(part)
            for ob in range(1, size_b):
                hold = self.mine(part, plane, 0, ob)
                total = hold[...].astype(F32)
                for ea in range(1, size_a):
                    total = total + self.arrived(part, self.slot_one(part, plane, ea, ob))
                hold[...] = total.astype(BF16)
                slot = self.slot_two(part, plane, size_b - ob)
                self.copy(part, hold, slot, slot, self.peer(part, 1, ob)).start()

    def third(self, plane):
        depth = self.spot[0]
        for part in range(2):
            size_a, size_b = self.sizes(part)
            hold = self.mine(part, plane, 0, 0)
            total = hold[...].astype(F32)
            for ea in range(1, size_a):
                total = total + self.arrived(part, self.slot_one(part, plane, ea, 0))
            for eb in range(1, size_b):
                total = total + self.arrived(part, self.slot_two(part, plane, eb))

            @pl.when(plane == depth)
            def _(part=part, total=total):
                self.out_ref[:, self.cols(part)] = total

            @pl.when(plane != depth)
            def _(part=part, total=total, hold=hold):
                hold[...] = total.astype(BF16)
                peer = linear(self.dims, (plane, self.spot[1], self.spot[2]))
                self.copy(part, hold, self.slot_three(depth), self.slot_three(plane), peer).start()

    def last(self):
        for part in range(2):
            total = self.out_ref[:, self.cols(part)]
            for off in range(1, self.dims[0]):
                plane = (self.spot[0] + off) % self.dims[0]
                total = total + self.arrived(part, self.slot_three(plane))
            self.out_ref[:, self.cols(part)] = total

    def step(self, number, made, plane_of):
        for back, action in ((0, self.first), (1, self.second), (2, self.third)):
            k = made - 1 - back
            if isinstance(made, int):
                if 0 <= k < number:
                    action(plane_of(k))
            else:
                pl.when(k >= 0)(lambda k=k, action=action: action(plane_of(k)))

    def finish(self, number, plane_of):
        for extra in (1, 2):
            self.step(number, number + extra, plane_of)
        self.last()

    def drain(self):
        ref_of = lambda part: self.box_ref.at[0, :, self.cols(part)]
        for part in range(2):
            size_a, size_b = self.sizes(part)
            for plane in range(self.dims[0]):
                slots = [self.slot_one(part, plane, ea, ob) for ea in range(1, size_a) for ob in range(size_b)]
                slots += [self.slot_two(part, plane, eb) for eb in range(1, size_b)]
                for slot in slots:
                    self.copy(part, ref_of(part), slot, slot, self.me).wait_send()
            for off in range(1, self.dims[0]):
                slot = self.slot_three((self.spot[0] + off) % self.dims[0])
                self.copy(part, ref_of(part), slot, slot, self.me).wait_send()


def start_direct(count, own_ref_of, box_ref, send_sem, recv_sem):
    me = lax.axis_index("head")
    copies = []
    for off in range(1, count):
        peer = (me + off) % count
        copy = pltpu.make_async_remote_copy(
            src_ref=own_ref_of(peer),
            dst_ref=box_ref.at[me],
            send_sem=send_sem.at[off],
            recv_sem=recv_sem.at[count - off],
            device_id={"head": peer},
            device_id_type=MESH,
        )
        copy.start()
        copies.append(copy)
    return copies


def wait_direct(count, box_ref, copies, recv_sem, send_sem):
    me = lax.axis_index("head")
    for off in range(1, count):
        ref = box_ref.at[(me + off) % count]
        pltpu.make_async_remote_copy(
            src_ref=ref,
            dst_ref=ref,
            send_sem=send_sem.at[off],
            recv_sem=recv_sem.at[off],
            device_id={"head": me},
            device_id_type=MESH,
        ).wait_recv()
    for copy in copies:
        copy.wait_send()


VMEM_SPEC = pl.BlockSpec(memory_space=pltpu.VMEM)
ANY_SPEC = pl.BlockSpec(memory_space=pl.ANY)
DMA = pltpu.SemaphoreType.DMA


def params(collective_id):
    return pltpu.CompilerParams(
        collective_id=collective_id, has_side_effects=True, vmem_limit_bytes=VMEM_LIMIT
    )


def gather_scratch(parts, dims, count):
    return [DMA((len(parts), gather_sends(dims))), DMA((len(parts), count)), DMA]


def run_gather(count, parts, own_ref, all_ref, sems, stat=None, between=()):
    dims = chip_dims(count)
    rows = own_ref.shape[0]
    me = lax.axis_index("head")
    send_sem, recv_sem, local_sem = sems
    local = pltpu.make_async_copy(own_ref, all_ref.at[rows_at(me, rows)], local_sem)
    local.start()
    if stat is not None:
        stat_ref, box_ref, small_send, small_recv = stat
        copies = start_direct(count, lambda peer: stat_ref, box_ref, small_send, small_recv)
        box_ref[me] = stat_ref[...]
    gather_steps(dims, parts, rows, own_ref, all_ref, send_sem, recv_sem, between)
    if stat is not None:
        wait_direct(count, box_ref, copies, small_recv, small_send)
    local.wait()


def scatter_scratch(parts, count, rows, width):
    slots = max(count - 1, 1)
    return [pltpu.VMEM((slots, rows, width), BF16), DMA((len(parts), slots)), DMA((len(parts), slots))]


def finish_sums(count, sz, state_part, small, squares, pack, head_sum, collective_id):
    dims = chip_dims(count)
    width = state_part.shape[1]
    rows = state_part.shape[0] // count
    back, parts = column_parts(width, SCATTER_SMALL), column_parts(width, GATHER_SMALL)
    chans, state = sz.channels, 2 * NSTATE
    pieces = sz.width // LANES
    threshold = CLIP_COEF * PARAMS**0.5

    def kernel(*refs):
        refs = list(refs)
        take = lambda number: [refs.pop(0) for _ in range(number)]
        in_ref, small_ref, squares_ref, pks_ref, sum_ref = take(5)
        all_ref, stats_ref, norm_ref = take(3)
        share_ref, sums_ref, out_ref, own_ref, stat_ref, mine_ref, got_ref = take(7)
        scatter_refs, ag_sems = take(3), take(3)
        small_send, small_recv, stat_send, stat_recv, pair_send, pair_recv = take(6)
        me = lax.axis_index("head")
        section = lax.axis_index("section")
        share_ref[...] = jnp.zeros_like(share_ref)
        share_ref[0:1, :] = small_ref[GAIN_ROW : GAIN_ROW + 1, :]
        share_ref[1 : CONV + 2, :state] = small_ref[: CONV + 1, chans : chans + state]

        def piece(peer):
            return share_ref.at[:, pl.ds(pl.multiple_of((peer % pieces) * LANES, LANES), LANES)]

        greet_all(count, "section")
        copies = start_direct(count, piece, sums_ref, small_send, small_recv)
        sums_ref[me] = piece(me)[...]
        sends = scatter_steps(dims, back, rows, in_ref, out_ref, *scatter_refs)
        wait_direct(count, sums_ref, copies, small_recv, small_send)
        shared = jnp.sum(sums_ref[...], axis=0)
        shared_sq = jnp.where(me < pieces, jnp.sum(shared * shared), 0.0)
        state_own = out_ref[...]
        own_ref[...] = state_own.astype(BF16)
        taps = small_ref[: CONV + 2, :chans]
        skip = nn(small_ref[6:7, :chans], sum_ref[...], HIGH)
        bias = small_ref[7:8, :LANES]
        rate = small_ref[8:9, :LANES] * pks_ref[section, 8:9, :LANES]
        lane = lax.broadcasted_iota(jnp.int32, (1, LANES), 1)
        of_heads = jnp.where(lane < sz.heads, bias * bias + rate * rate + skip * skip, 0.0)
        if chans > sz.heads * HDIM:
            taps = taps[:, : sz.heads * HDIM]
        total = jnp.sum(squares_ref[...]) + jnp.sum(taps * taps) + jnp.sum(of_heads)
        total = total + jnp.sum(state_own * state_own) + shared_sq
        row = lax.broadcasted_iota(jnp.int32, (8, LANES), 0)
        stat_ref[...] = jnp.where(row == 7, total, shared)
        run_gather(count, parts, own_ref, all_ref, ag_sems, (stat_ref, stats_ref, stat_send, stat_recv))
        section_sq = stats_ref[0, 7:8, :]
        for k in range(1, count):
            section_sq = section_sq + stats_ref[k, 7:8, :]
        mine_ref[...] = jnp.broadcast_to(section_sq, (8, LANES))
        pair = pltpu.make_async_remote_copy(
            src_ref=mine_ref,
            dst_ref=got_ref,
            send_sem=pair_send,
            recv_sem=pair_recv,
            device_id={"section": 1 - section},
            device_id_type=MESH,
        )
        pair.start()
        pair.wait()
        norm = jnp.sqrt(mine_ref[...] + got_ref[...])
        norm_ref[...] = jnp.where(row == 0, norm, threshold / jnp.maximum(norm, threshold))
        for copy in sends:
            copy.wait_send()

    return pl.pallas_call(
        kernel,
        out_shape=[
            jax.ShapeDtypeStruct(state_part.shape, BF16),
            jax.ShapeDtypeStruct((count, 8, LANES), F32),
            jax.ShapeDtypeStruct((8, LANES), F32),
        ],
        in_specs=[VMEM_SPEC] * 5,
        out_specs=[ANY_SPEC, VMEM_SPEC, VMEM_SPEC],
        scratch_shapes=[
            pltpu.VMEM((8, sz.width), F32),
            pltpu.VMEM((count, 8, LANES), F32),
            pltpu.VMEM((rows, width), F32),
            pltpu.VMEM((rows, width), BF16),
        ]
        + [pltpu.VMEM((8, LANES), F32)] * 3
        + scatter_scratch(back, count, rows, width)
        + gather_scratch(parts, dims, count)
        + [DMA((count,))] * 4
        + [DMA, DMA],
        compiler_params=params(collective_id),
        name="finish_sums",
    )(state_part, small, squares, pack, head_sum)


def norm_rows(value, gain):
    mean = jnp.mean(value * value, axis=1, keepdims=True)
    return value * lax.rsqrt(mean + EPS_NORM) * gain


def norm_rows_back(value, gain, grad):
    width = value.shape[1]
    scale = lax.rsqrt(jnp.mean(value * value, axis=1, keepdims=True) + EPS_NORM)
    scaled = grad * gain
    dot = jnp.sum(scaled * value, axis=1, keepdims=True)
    back = scaled * scale - value * (scale * scale * scale * dot * (1.0 / width))
    return back, jnp.sum(grad * value * scale, axis=0, keepdims=True)


def write_pack(sz, pack_ref, head_ref, shared_ref):
    chans, state = sz.channels, 2 * NSTATE
    pack_ref[...] = jnp.zeros_like(pack_ref)
    lane = lax.broadcasted_iota(jnp.int32, (1, LANES), 1)
    bias_row = jnp.zeros((1, LANES), F32)
    rate_row = jnp.zeros((1, LANES), F32)
    rates = -jnp.exp(head_ref[:, (CONV + 2) * HDIM :])
    for head in range(sz.heads):
        cols = slice(head * HDIM, (head + 1) * HDIM)
        for tap in range(CONV):
            pack_ref[tap : tap + 1, cols] = head_ref[head : head + 1, tap * HDIM : (tap + 1) * HDIM]
        pack_ref[5:6, cols] = head_ref[head : head + 1, CONV * HDIM : (CONV + 1) * HDIM]
        pack_ref[CONV : CONV + 1, cols] = head_ref[head : head + 1, (CONV + 1) * HDIM : (CONV + 2) * HDIM]
        last = (CONV + 2) * HDIM
        pack_ref[6:7, cols] = jnp.broadcast_to(head_ref[head : head + 1, last + 2 : last + 3], (1, HDIM))
        bias_row = jnp.where(lane == head, head_ref[head : head + 1, last : last + 1], bias_row)
        rate_row = jnp.where(lane == head, rates[head : head + 1, 1:2], rate_row)
    pack_ref[7:8, :LANES] = bias_row
    pack_ref[8:9, :LANES] = rate_row
    for tap in range(CONV + 1):
        pack_ref[tap : tap + 1, chans : chans + state] = shared_ref[:, tap * state : (tap + 1) * state]
    pack_ref[GAIN_ROW : GAIN_ROW + 1, :] = shared_ref[:, (CONV + 1) * state :]


def opening(count, sz, proj_in_t, proj_state, proj_out, head_part, shared_part, order, first, collective_id):
    dims = chip_dims(count)
    rows, width = first.shape
    parts = column_parts(width, GATHER)
    cols = 256
    steps = width // cols
    full = sz.master // 16 * 16
    own_rows = proj_out.shape[0]

    def kernel(*refs):
        refs = list(refs)
        take = lambda number: [refs.pop(0) for _ in range(number)]
        in_hbm, state_hbm, out_hbm, order_hbm, head_ref, shared_ref, x_ref = take(7)
        ws_ref, wos_ref, pks_ref, all_ref = take(4)
        own_ref, in_ref, state_ref, out_ref, order_ref, low_ref, w_ref, wo_ref = take(8)
        ag_sems = take(3)
        load_sem, pair_send, pair_recv, pair_local = take(4)
        section = lax.axis_index("section")
        other = 1 - section
        loads = [
            pltpu.make_async_copy(src, dst, load_sem.at[k])
            for k, (src, dst) in enumerate(
                ((order_hbm, order_ref), (in_hbm, in_ref), (state_hbm, state_ref), (out_hbm, out_ref))
            )
        ]
        for copy in loads:
            copy.start()
        write_pack(sz, pks_ref.at[section], head_ref, shared_ref)
        greet_all(count, "section")
        sent = []

        def share(src, dst, k):
            copy = pltpu.make_async_remote_copy(
                src_ref=src,
                dst_ref=dst,
                send_sem=pair_send.at[k],
                recv_sem=pair_recv.at[k],
                device_id={"section": other},
                device_id_type=MESH,
            )
            copy.start()
            return copy

        pack_copy = share(pks_ref.at[section], pks_ref.at[section], 0)
        pack_copy.wait()
        gain = pks_ref[0, GAIN_ROW : GAIN_ROW + 1, :]
        own_ref[...] = norm_rows(x_ref[...].astype(F32), gain).astype(BF16)

        def keep(src, dst, k):
            local = pltpu.make_async_copy(src, dst, pair_local.at[k])
            local.start()
            sent.extend([share(src, dst, k), local])

        def low_out():
            for copy in loads:
                copy.wait()
            if own_rows < sz.channels:
                wo_ref[...] = jnp.zeros_like(wo_ref)
            wo_ref[:own_rows, :] = out_ref[...].astype(BF16)
            keep(wo_ref, wos_ref.at[section], 1)

        def low_in(step):
            span = slice(step * cols, (step + 1) * cols)
            low_ref[:full, :] = in_ref[:full, 0, span].astype(BF16)
            if full < sz.master_pad:
                low_ref[full:, :] = jnp.zeros((sz.master_pad - full, cols), BF16)
            if full < sz.master:
                low_ref[full : full + 16, :] = jnp.concatenate(
                    [in_ref[full : sz.master, 0, span], jnp.zeros((full + 16 - sz.master, cols), F32)], axis=0
                ).astype(BF16)
            w_ref[:, span] = tn(order_ref[: sz.master_pad, :], low_ref[...]).astype(BF16)
            row = lax.broadcasted_iota(jnp.int32, (2 * NSTATE, 2 * NSTATE), 0)
            col = lax.broadcasted_iota(jnp.int32, (2 * NSTATE, 2 * NSTATE), 1)
            one = (row == col).astype(BF16)
            w_ref[2 * sz.channels : sz.dt, span] = nt(one, state_ref[span, :].astype(BF16)).astype(BF16)
            keep(w_ref.at[:, span], ws_ref.at[section, :, span], 2 + step)

        work = [low_out] + [lambda step=step: low_in(step) for step in range(steps)]
        run_gather(count, parts, own_ref, all_ref, ag_sems, None, work)
        for copy in sent:
            copy.wait()

    return pl.pallas_call(
        kernel,
        out_shape=[
            jax.ShapeDtypeStruct((2, sz.cols, width), BF16),
            jax.ShapeDtypeStruct((2, sz.channels, width), BF16),
            jax.ShapeDtypeStruct((2, 16, width), F32),
            jax.ShapeDtypeStruct((count * rows, width), BF16),
        ],
        in_specs=[ANY_SPEC] * 4 + [VMEM_SPEC] * 3,
        out_specs=[ANY_SPEC, ANY_SPEC, VMEM_SPEC, ANY_SPEC],
        scratch_shapes=[
            pltpu.VMEM((rows, width), BF16),
            pltpu.VMEM(proj_in_t.shape, F32),
            pltpu.VMEM(proj_state.shape, F32),
            pltpu.VMEM(proj_out.shape, F32),
            pltpu.VMEM(order.shape, BF16),
            pltpu.VMEM((sz.master_pad, cols), BF16),
            pltpu.VMEM((sz.cols, width), BF16),
            pltpu.VMEM((sz.channels, width), BF16),
        ]
        + gather_scratch(parts, dims, count)
        + [DMA((4,)), DMA((2 + steps,)), DMA((2 + steps,)), DMA((2 + steps,))],
        compiler_params=params(collective_id),
        name="opening",
    )(proj_in_t, proj_state, proj_out, order, head_part, shared_part, first)


def column_of(tile, rows):
    row = lax.broadcasted_iota(jnp.int32, (rows, rows), 0)
    lane = lax.broadcasted_iota(jnp.int32, (rows, rows), 1)
    return nt((row == lane).astype(F32), tile, HIGH)[:, 0:1]


def write_stats(stat_ref, squares, out_grad, branch, rows):
    dot = nt(jnp.ones((8, branch.shape[1]), F32), out_grad * branch, HIGH)
    scale = lax.rsqrt(squares / (HEADS * HDIM) + EPS_NORM)
    row = lax.broadcasted_iota(jnp.int32, (8, rows), 0)
    stat_ref[...] = jnp.zeros_like(stat_ref)
    stat_ref[:, :rows] = jnp.where(row == 0, scale, jnp.where(row == 1, dot, 0.0))


def greet_other():
    barrier = pltpu.get_barrier_semaphore()
    other = 1 - lax.axis_index("section")
    pl.semaphore_signal(barrier, inc=1, device_id={"section": other}, device_id_type=MESH)
    pl.semaphore_wait(barrier, 1)
    return other


def add_up(out_ref, mine_ref, got_ref, squares_ref):
    rows, width = out_ref.shape
    step = 16 if rows % 16 == 0 else rows

    def body(i, carry):
        span = pl.ds(pl.multiple_of(i * step, step), step)
        total = mine_ref[span, :].astype(F32) + got_ref[span, :].astype(F32)
        out_ref[span, :] = total
        if squares_ref is not None:
            part = total * total
            for k in range(0, step, 8):
                squares_ref[...] += part[k : k + 8]
        return carry

    lax.fori_loop(0, rows // step, body, 0)


def trade_sections(sums, stacks, squared, collective_id):
    pairs = sums + stacks
    number, summed = len(pairs), len(sums)

    def kernel(*refs):
        ins, outs = refs[: 2 * number], refs[2 * number : 3 * number]
        squares_ref = refs[3 * number]
        boxes = refs[3 * number + 1 : 3 * number + 1 + summed]
        send_sem, recv_sem = refs[3 * number + 1 + summed :]
        squares_ref[...] = jnp.zeros_like(squares_ref)
        section = lax.axis_index("section")
        other = greet_other()

        def go(mine, theirs):
            copies = []
            for k in range(number):
                copy = pltpu.make_async_remote_copy(
                    src_ref=theirs[k],
                    dst_ref=boxes[k] if k < summed else outs[k].at[section],
                    send_sem=send_sem.at[k],
                    recv_sem=recv_sem.at[k],
                    device_id={"section": other},
                    device_id_type=MESH,
                )
                copy.start()
                copies.append(copy)
            for k in range(summed, number):
                outs[k][section] = mine[k][...]
            for k in range(number):
                copies[k].wait()
                if k < summed:
                    add_up(outs[k], mine[k], boxes[k], squares_ref if k < squared else None)

        pl.when(section == 0)(lambda: go(ins[0::2], ins[1::2]))
        pl.when(section == 1)(lambda: go(ins[1::2], ins[0::2]))

    shapes = [jax.ShapeDtypeStruct(a.shape, F32) for a, _ in sums]
    shapes += [jax.ShapeDtypeStruct((2,) + a.shape, a.dtype) for a, _ in stacks]
    shapes.append(jax.ShapeDtypeStruct((8, sums[0][0].shape[1]), F32))
    return pl.pallas_call(
        kernel,
        out_shape=shapes,
        in_specs=[VMEM_SPEC] * (2 * number),
        out_specs=[VMEM_SPEC] * len(shapes),
        scratch_shapes=[pltpu.VMEM(a.shape, a.dtype) for a, _ in sums] + [DMA((number,))] * 2,
        compiler_params=pltpu.CompilerParams(
            collective_id=collective_id, has_side_effects=True, vmem_limit_bytes=VMEM_LIMIT
        ),
        name="trade_sections",
    )(*[a for pair in pairs for a in pair])


class Sizes:
    def __init__(self, heads, tokens, width):
        self.heads = heads
        self.padded = heads + heads % 2
        self.channels = self.padded * HDIM
        self.conv = self.channels + 2 * NSTATE
        self.cols = 2 * self.channels + 2 * NSTATE + LANES
        self.dt = 2 * self.channels + 2 * NSTATE
        self.master = heads * COLS
        self.master_pad = -(-self.master // LANES) * LANES
        self.grad_rows = self.master_pad + 2 * NSTATE
        self.tokens = tokens
        self.width = width
        self.blocks = tokens // STRETCH

    def order(self):
        table = np.zeros((self.grad_rows, self.cols), np.float32)
        for head in range(self.heads):
            for j in range(HDIM):
                table[head * COLS + j, head * HDIM + j] = 1
                table[head * COLS + HDIM + j, self.channels + head * HDIM + j] = 1
            table[head * COLS + 2 * HDIM, self.dt + head] = 1
        for j in range(2 * NSTATE):
            table[self.master_pad + j, 2 * self.channels + j] = 1
        return jnp.asarray(table, BF16)

    def head_sum(self):
        table = np.zeros((self.channels, LANES), np.float32)
        for head in range(self.padded):
            table[head * HDIM : (head + 1) * HDIM, head] = 1
        return jnp.asarray(table, F32)


def nt(left, right, precision=None):
    return lax.dot_general(
        left, right, (((1,), (1,)), ((), ())), precision=precision, preferred_element_type=F32
    )


def tn(left, right, precision=None):
    return lax.dot_general(
        left, right, (((0,), (0,)), ((), ())), precision=precision, preferred_element_type=F32
    )


def nn(left, right, precision=None):
    return jnp.dot(left, right, precision=precision, preferred_element_type=F32)


def split(value):
    high = value.astype(BF16)
    return high, (value - high.astype(F32)).astype(BF16)


def fine(dot, left, right, left_axis, right_axis):
    left_high, left_low = split(left)
    right_high, right_low = split(right)
    return dot(
        jnp.concatenate([left_high, left_low, left_high], axis=left_axis),
        jnp.concatenate([right_high, right_high, right_low], axis=right_axis),
    )


def nt3(left, right):
    return fine(nt, left, right, 1, 1)


def tn3(left, right):
    return fine(tn, left, right, 0, 0)


def nn3(left, right):
    return fine(nn, left, right, 1, 0)


def softplus(value):
    return jnp.maximum(value, 0.0) + jnp.log1p(jnp.exp(-jnp.abs(value)))


def sigmoid(value):
    return 1.0 / (1.0 + jnp.exp(-value))


def halves(left, right):
    rows = left.shape[0]
    lane = lax.broadcasted_iota(jnp.int32, (rows, LANES), 1)
    return jnp.where(lane < HDIM, left, right)


def lower_mask(size):
    row = lax.broadcasted_iota(jnp.int32, (size, size), 0)
    col = lax.broadcasted_iota(jnp.int32, (size, size), 1)
    return row >= col


def step_rows(log_decay, step):
    lane = lax.broadcasted_iota(jnp.int32, log_decay.shape, 1)
    both = jnp.where(lane < 8, log_decay, pltpu.roll(step, 8, 1))
    return jnp.transpose(jnp.where(lane < 16, both, 0.0))


def to_columns(tile, rows):
    row = lax.broadcasted_iota(jnp.int32, (rows, LANES), 0)
    lane = lax.broadcasted_iota(jnp.int32, (rows, LANES), 1)
    return nt((row == lane).astype(F32), tile, HIGH)


def forward_phase(count, sz, layer, resets, gathered, weights, weight_out, pack, residual, live, cotangent, collective_id):
    block, chunk, chans = STRETCH, CHUNK, sz.channels
    dims = chip_dims(count)
    rows, width = residual.shape
    subs = block // chunk
    shards = block // rows
    blocks = sz.blocks
    planes = dims[0]
    per = blocks // planes
    parts = column_parts(width, GATHER)
    scatter = PlaneScatter(dims, rows, width)
    turn = cotangent is not None

    def kernel(*refs):
        refs = list(refs)
        take = lambda number: [refs.pop(0) for _ in range(number)]
        reset_ref, rows_ref, ws_ref, wos_ref, pks_ref, u_ref, live_ref = take(7)
        cot_ref = refs.pop(0) if turn else None
        result_ref, branch_ref, total_ref, next_ref, p_out, y_out, s_out = take(7)
        stats_ref = refs.pop(0) if turn else None
        conv_ref, state_ref, w_ref, wo_ref, h_buf, p_buf, y_buf, s_buf, part_ref, sq_ref = take(10)
        load_sem, store_sem, weight_sem = take(3)
        sums_ref, own_ref = take(2)
        scatter_refs = take(3)
        ag_sems = take(3)
        small_send, small_recv = take(2)
        pk_ref = pks_ref.at[layer]

        def load(c):
            span = pl.ds(pl.multiple_of(c * block, block), block)
            return pltpu.make_async_copy(rows_ref.at[span, :], h_buf.at[c % 2], load_sem.at[c % 2])

        def stores(c):
            slot = c % 2
            span = pl.ds(pl.multiple_of(c * block, block), block)
            return [
                pltpu.make_async_copy(p_buf.at[slot], p_out.at[span, :], store_sem.at[0, slot]),
                pltpu.make_async_copy(y_buf.at[slot], y_out.at[span, :], store_sem.at[1, slot]),
                pltpu.make_async_copy(s_buf.at[slot], s_out.at[pl.ds(c * subs, subs)], store_sem.at[2, slot]),
            ]

        load(0).start()
        weight_copies = [
            pltpu.make_async_copy(ws_ref.at[layer], w_ref, weight_sem.at[0]),
            pltpu.make_async_copy(wos_ref.at[layer], wo_ref, weight_sem.at[1]),
        ]
        for copy in weight_copies:
            copy.start()
        greet_all(count)
        conv_ref[...] = jnp.zeros_like(conv_ref)
        state_ref[...] = jnp.zeros_like(state_ref)
        scatter.bind(part_ref, branch_ref, *scatter_refs)
        for copy in weight_copies:
            copy.wait()

        def one_block(c, carry):
            slot = c % 2
            keep = 1.0 - reset_ref[c]
            span_all = pl.ds(pl.multiple_of(c * block, block), block)
            pl.when(c + 1 < blocks)(lambda: load(c + 1).start())
            load(c).wait()

            @pl.when(c >= 2)
            def _():
                for copy in stores(c - 2):
                    copy.wait()

            h_ref, p_ref, y_ref, s_ref = (buf.at[slot] for buf in (h_buf, p_buf, y_buf, s_buf))
            p_ref[...] = nt(h_ref[...], w_ref[...])
            inner = p_ref[:, chans : 2 * chans]
            state_raw = p_ref[:, 2 * chans : sz.dt].astype(BF16).astype(F32)
            conv_ref[0:8, :] = conv_ref[block : block + 8, :] * keep
            conv_ref[8 : 8 + block, :chans] = inner
            conv_ref[8 : 8 + block, chans:] = state_raw
            pre = pk_ref[CONV : CONV + 1, : sz.conv] + pk_ref[0:1, : sz.conv] * conv_ref[8 : 8 + block, :]
            for tap in range(1, CONV):
                pre = pre + pk_ref[tap : tap + 1, : sz.conv] * conv_ref[8 - tap : 8 - tap + block, :]
            act = pre * sigmoid(pre)
            step = softplus(p_ref[:, sz.dt :] + pk_ref[7:8, :LANES])
            decay = step * pk_ref[8:9, :LANES]
            mask = lower_mask(chunk)
            lower = mask.astype(F32)
            lane = lax.broadcasted_iota(jnp.int32, (chunk, LANES), 1)
            for sub in range(subs):
                span = slice(sub * chunk, (sub + 1) * chunk)
                if sub == 0:
                    state_ref[...] = state_ref[...] * keep
                s_ref[sub] = state_ref[...]
                dt = step[span]
                log_decay = nn(lower, decay[span], HIGH)
                flat = step_rows(log_decay, dt)
                writer = act[span, chans : chans + NSTATE]
                reader = act[span, chans + NSTATE :]
                cross = nt3(reader, writer)
                for pair in range(sz.padded // 2):
                    cols = slice(pair * LANES, (pair + 1) * LANES)
                    x = act[span, cols]
                    total = jnp.zeros((chunk, LANES), F32)
                    for side in range(2):
                        head = 2 * pair + side
                        gap = log_decay[:, head : head + 1] - flat[head : head + 1, :]
                        weight = cross * jnp.exp(jnp.where(mask, gap, -1e30)) * flat[8 + head : 9 + head, :]
                        part = jnp.where((lane < HDIM) == (side == 0), x, 0.0)
                        total = total + nn3(weight, part)
                    logs = halves(log_decay[:, 2 * pair : 2 * pair + 1], log_decay[:, 2 * pair + 1 : 2 * pair + 2])
                    dts = halves(dt[:, 2 * pair : 2 * pair + 1], dt[:, 2 * pair + 1 : 2 * pair + 2])
                    old = state_ref[:, cols]
                    total = total + jnp.exp(logs) * nn3(reader, old)
                    last = logs[chunk - 1 : chunk, :]
                    moved_in = x * jnp.exp(last - logs) * dts
                    state_ref[:, cols] = jnp.exp(last) * old + tn3(writer, moved_in)
                    y_ref[span, cols] = total + pk_ref[6:7, cols] * x
            z = p_ref[:, :chans]
            gated = y_ref[...] * z * sigmoid(z)
            square = nt(jnp.ones((8, chans), F32), gated * gated, HIGH)
            for k in range(shards):
                sq_ref[c * shards + k] = square[:, k * rows : (k + 1) * rows]
            high, low = split(gated * pk_ref[5:6, :chans])
            part_ref[span_all, :] = (nn(high, wo_ref[...]) + nn(low, wo_ref[...])).astype(BF16)
            for copy in stores(c):
                copy.start()
            if per == 1:
                scatter.step(planes, c + 1, lambda k: k)
            else:
                pl.when(c % per == per - 1)(lambda: scatter.step(planes, c // per + 1, lambda k: k))
            return carry

        lax.fori_loop(0, blocks, one_block, 0)
        me = lax.axis_index("head")
        copies = start_direct(count, lambda peer: sq_ref.at[peer], sums_ref, small_send, small_recv)
        sums_ref[me] = sq_ref[me]
        scatter.finish(planes, lambda k: k)
        wait_direct(count, sums_ref, copies, small_recv, small_send)
        total = jnp.sum(sums_ref[...], axis=0)
        total_ref[...] = total
        scale = lax.rsqrt(column_of(total, rows) / (HEADS * HDIM) + EPS_NORM)
        branch = branch_ref[...] * scale
        branch_ref[...] = branch
        live_col = live_ref[:, 0:1]
        result = (u_ref[...].astype(F32) + live_col * branch).astype(BF16)
        result_ref[...] = result
        stat = None
        if turn:
            stat_ref, stat_send, stat_recv = refs
            out_grad = (live_col * cot_ref[...].astype(F32)).astype(BF16)
            own_ref[...] = out_grad
            write_stats(stat_ref, total, out_grad.astype(F32), branch, rows)
            stat = (stat_ref, stats_ref, stat_send, stat_recv)
        else:
            gain = pks_ref[layer + 1, GAIN_ROW : GAIN_ROW + 1, :]
            own_ref[...] = norm_rows(result.astype(F32), gain).astype(BF16)
        run_gather(count, parts, own_ref, next_ref, ag_sems, stat)
        for c in range(max(blocks - 2, 0), blocks):
            for copy in stores(c):
                copy.wait()
        scatter.drain()

    tokens = sz.tokens
    out_shape = [
        jax.ShapeDtypeStruct((rows, width), BF16),
        jax.ShapeDtypeStruct((rows, width), F32),
        jax.ShapeDtypeStruct((8, rows), F32),
        jax.ShapeDtypeStruct((tokens, width), BF16),
        jax.ShapeDtypeStruct((tokens, sz.cols), F32),
        jax.ShapeDtypeStruct((tokens, chans), F32),
        jax.ShapeDtypeStruct((tokens // chunk, NSTATE, chans), F32),
    ]
    out_specs = [VMEM_SPEC] * 3 + [ANY_SPEC] * 4
    scratch = [
        pltpu.VMEM((block + 8, sz.conv), F32),
        pltpu.VMEM((NSTATE, chans), F32),
        pltpu.VMEM((sz.cols, width), BF16),
        pltpu.VMEM((chans, width), BF16),
        pltpu.VMEM((2, block, width), BF16),
        pltpu.VMEM((2, block, sz.cols), F32),
        pltpu.VMEM((2, block, chans), F32),
        pltpu.VMEM((2, subs, NSTATE, chans), F32),
        pltpu.VMEM((tokens, width), BF16),
        pltpu.VMEM((count, 8, rows), F32),
        DMA((2,)),
        DMA((3, 2)),
        DMA((2,)),
        pltpu.VMEM((count, 8, rows), F32),
        pltpu.VMEM((rows, width), BF16),
    ]
    scratch += scatter.scratch() + gather_scratch(parts, dims, count) + [DMA((count,))] * 2
    operands = [resets, gathered, weights, weight_out, pack, residual, live]
    in_specs = [pl.BlockSpec(memory_space=pltpu.SMEM)] + [ANY_SPEC] * 3 + [VMEM_SPEC] * 3
    if turn:
        out_shape.append(jax.ShapeDtypeStruct((count, 8, LANES), F32))
        out_specs.append(VMEM_SPEC)
        scratch += [pltpu.VMEM((8, LANES), F32)] + [DMA((count,))] * 2
        operands.append(cotangent)
        in_specs.append(VMEM_SPEC)
    return pl.pallas_call(
        kernel,
        out_shape=out_shape,
        in_specs=in_specs,
        out_specs=out_specs,
        scratch_shapes=scratch,
        compiler_params=params(collective_id),
        name="forward_phase",
    )(*operands)


def backward_phase(
    count, sz, layer, resets, out_grads, proj, mixed, states, stats, weights, weight_out, pack, order,
    residual, upstream, live, below, upper, collective_id,
):
    block, chunk, chans = STRETCH, CHUNK, sz.channels
    dims = chip_dims(count)
    rows, width = residual.shape
    subs = block // chunk
    blocks = sz.blocks
    planes = dims[0]
    per = blocks // planes
    parts = column_parts(width, GATHER)
    scatter = PlaneScatter(dims, rows, width)
    more = below is not None
    close = upper is not None
    cols = 256
    steps = width // cols

    def kernel(*refs):
        refs = list(refs)
        take = lambda number: [refs.pop(0) for _ in range(number)]
        reset_ref, g_all, p_all, y_all, s_all, ws_ref, wos_ref, orders_ref = take(8)
        st_ref, pks_ref, sum_ref, u_ref, up_ref, live_ref = take(6)
        if more:
            lower_ref, lower_total = take(2)
        if close:
            gt_upper, q_upper, h_upper, g_upper, h_own = take(5)
            acc_upper, result_own, result_upper, grad_upper = take(4)
            sum_in, sum_out, sum_state, sum_small, outs_ref, grads_ref, squares_ref = take(7)
        else:
            grad_ref, low_grad_ref, acc_ref, gt_out, q_out = take(5)
        if more:
            next_ref, stats_ref = take(2)
        conv_ref, dpre_ref, dact_ref, ddt_ref, dstate_ref = take(5)
        w_ref, wo_ref, order_ref, g_buf, p_buf, halo_buf, y_buf, s_buf, gt_buf, q_buf, part_ref = take(11)
        load_sem, store_sem, weight_sem = take(3)
        scatter_refs = take(3)
        pk_ref = pks_ref.at[layer]
        if close:
            grad_ref, acc_ref, gt_full, q_full, gt_one, q_one, h_cols, g_cols = take(8)
            send_state, box_in, box_out, box_state, box_small, state_own = take(6)
            send_in, send_out = w_ref.at[: sz.master_pad, :], wo_ref
            col_sem, whole_sem, trade_send, trade_recv, few_send, few_recv = take(6)
            section = lax.axis_index("section")
            other = 1 - section
            whole = [
                pltpu.make_async_copy(gt_upper, gt_one, whole_sem.at[0]),
                pltpu.make_async_copy(q_upper, q_one, whole_sem.at[1]),
            ]

        def loads(c):
            slot = c % 2
            span = pl.ds(pl.multiple_of(c * block, block), block)
            before = pl.multiple_of(jnp.maximum(c * block - 8, 0), 8)
            return [
                pltpu.make_async_copy(g_all.at[span, :], g_buf.at[slot], load_sem.at[0, slot]),
                pltpu.make_async_copy(p_all.at[span, :], p_buf.at[slot], load_sem.at[1, slot]),
                pltpu.make_async_copy(p_all.at[pl.ds(before, 8), :], halo_buf.at[slot], load_sem.at[2, slot]),
                pltpu.make_async_copy(y_all.at[span, :], y_buf.at[slot], load_sem.at[3, slot]),
                pltpu.make_async_copy(s_all.at[pl.ds(c * subs, subs)], s_buf.at[slot], load_sem.at[4, slot]),
            ]

        def stores(c):
            slot = c % 2
            span = pl.ds(pl.multiple_of(c * block, block), block)
            if close:
                return []
            return [
                pltpu.make_async_copy(gt_buf.at[slot], gt_out.at[:, span], store_sem.at[0, slot]),
                pltpu.make_async_copy(q_buf.at[slot], q_out.at[span, :], store_sem.at[1, slot]),
            ]

        for copy in loads(blocks - 1):
            copy.start()
        weight_copies = [
            pltpu.make_async_copy(wos_ref.at[layer], wo_ref, weight_sem.at[0]),
            pltpu.make_async_copy(ws_ref.at[layer], w_ref, weight_sem.at[1]),
            pltpu.make_async_copy(orders_ref, order_ref, weight_sem.at[2]),
        ]
        for copy in weight_copies:
            copy.start()
        if close:
            for copy in whole:
                copy.start()
            greet_all(count, "section")
        else:
            greet_all(count)
        dpre_ref[...] = jnp.zeros_like(dpre_ref)
        dstate_ref[...] = jnp.zeros_like(dstate_ref)
        acc_ref[...] = jnp.zeros_like(acc_ref)
        scatter.bind(part_ref, grad_ref, *scatter_refs)
        for copy in weight_copies:
            copy.wait()

        def one_block(i, carry):
            c = blocks - 1 - i
            slot = c % 2
            keep = 1.0 - reset_ref[c]
            after = 1.0 - reset_ref[jnp.minimum(c + 1, blocks - 1)]
            span_all = pl.ds(pl.multiple_of(c * block, block), block)

            @pl.when(c >= 1)
            def _():
                for copy in loads(c - 1):
                    copy.start()

            for copy in loads(c):
                copy.wait()

            if not close:
                @pl.when(i >= 2)
                def _():
                    for copy in stores(c + 2):
                        copy.wait()

            g_ref, p_ref, halo_ref, y_ref, s_ref = (
                buf.at[slot] for buf in (g_buf, p_buf, halo_buf, y_buf, s_buf)
            )
            if close:
                gt_ref, q_ref = gt_full.at[:, span_all], q_full.at[span_all, :]
            else:
                gt_ref, q_ref = gt_buf.at[slot], q_buf.at[slot]
            conv_ref[0:8, :chans] = halo_ref[:, chans : 2 * chans] * keep
            conv_ref[0:8, chans:] = halo_ref[:, 2 * chans : sz.dt].astype(BF16).astype(F32) * keep
            conv_ref[8 : 8 + block, :chans] = p_ref[:, chans : 2 * chans]
            conv_ref[8 : 8 + block, chans:] = p_ref[:, 2 * chans : sz.dt].astype(BF16).astype(F32)
            pre = pk_ref[CONV : CONV + 1, : sz.conv] + pk_ref[0:1, : sz.conv] * conv_ref[8 : 8 + block, :]
            for tap in range(1, CONV):
                pre = pre + pk_ref[tap : tap + 1, : sz.conv] * conv_ref[8 - tap : 8 - tap + block, :]
            gate = sigmoid(pre)
            act = pre * gate
            slope = gate * (1.0 + pre * (1.0 - gate))
            step_in = p_ref[:, sz.dt :] + pk_ref[7:8, :LANES]
            step = softplus(step_in)
            rate = pk_ref[8:9, :LANES]
            decay = step * rate
            z = p_ref[:, :chans]
            zgate = sigmoid(z)
            zsilu = z * zgate
            y = y_ref[...]
            gated = y * zsilu
            gain = pk_ref[5:6, :chans]
            skip = pk_ref[6:7, :chans]
            columns = [to_columns(st_ref[c * (block // rows) + k], rows) for k in range(block // rows)]
            columns = jnp.concatenate(columns, axis=0)
            scale = columns[:, 0:1]
            along = columns[:, 1:2]
            grad_q = nt(g_ref[...], wo_ref[...])
            q_ref[...] = (gated * scale * gain).astype(BF16)
            acc_ref[5:6, :chans] += jnp.sum(grad_q * gated * scale, axis=0, keepdims=True)
            dgated = grad_q * gain * scale - gated * (scale * scale * along * (1.0 / (HEADS * HDIM)))
            dy = dgated * zsilu
            dz = dgated * y * zgate * (1.0 + z * (1.0 - zgate))
            x_all = act[:, :chans]
            acc_ref[6:7, :chans] += jnp.sum(dy * x_all, axis=0, keepdims=True)
            scan_dot = nn(dy * (y - skip * x_all), sum_ref[...], HIGH)
            mask = lower_mask(chunk)
            lower = mask.astype(F32)
            lane = lax.broadcasted_iota(jnp.int32, (chunk, LANES), 1)
            for sub in reversed(range(subs)):
                span = slice(sub * chunk, (sub + 1) * chunk)
                dt = step[span]
                log_decay = nn(lower, decay[span], HIGH)
                flat = step_rows(log_decay, dt)
                writer = act[span, chans : chans + NSTATE]
                reader = act[span, chans + NSTATE :]
                cross = nt3(reader, writer)
                cross_grad = jnp.zeros((chunk, chunk), F32)
                dreader = jnp.zeros((chunk, NSTATE), F32)
                dwriter = jnp.zeros((chunk, NSTATE), F32)
                fall = jnp.zeros((LANES, chunk), F32)
                row = lax.broadcasted_iota(jnp.int32, (LANES, chunk), 0)
                reach = []
                carried = []
                for pair in range(sz.padded // 2):
                    cols = slice(pair * LANES, (pair + 1) * LANES)
                    x = act[span, cols]
                    g = dy[span, cols]
                    logs = halves(log_decay[:, 2 * pair : 2 * pair + 1], log_decay[:, 2 * pair + 1 : 2 * pair + 2])
                    dts = halves(dt[:, 2 * pair : 2 * pair + 1], dt[:, 2 * pair + 1 : 2 * pair + 2])
                    last = logs[chunk - 1 : chunk, :]
                    old = s_ref[sub, :, cols]
                    dnew = dstate_ref[:, cols]
                    faded = g * jnp.exp(logs)
                    tail = jnp.exp(last - logs)
                    dreader = dreader + nt3(faded, old)
                    ahead = nn3(writer, dnew)
                    dx = g * skip[:, cols] + ahead * tail * dts
                    dwriter = dwriter + nt3(x * tail * dts, dnew)
                    reach.append(x * ahead * tail)
                    carried.append(jnp.sum(old * dnew, axis=0, keepdims=True) * jnp.exp(last))
                    dstate_ref[:, cols] = jnp.exp(last) * dnew + tn3(reader, faded)
                    for side in range(2):
                        head = 2 * pair + side
                        own = (lane < HDIM) == (side == 0)
                        g_own = jnp.where(own, g, 0.0)
                        gap = log_decay[:, head : head + 1] - flat[head : head + 1, :]
                        decays = jnp.exp(jnp.where(mask, gap, -1e30))
                        steps = flat[8 + head : 9 + head, :]
                        spread = nt3(g_own, x) * decays
                        weight = cross * decays * steps
                        dx = dx + tn3(weight, g_own)
                        cross_grad = cross_grad + spread * steps
                        sums = jnp.sum(spread * cross, axis=0, keepdims=True)
                        fall = fall + jnp.where(row == head, sums, 0.0)
                    dact_ref[span, cols] = dx
                dact_ref[span, chans : chans + NSTATE] = dwriter + tn3(cross_grad, reader)
                dact_ref[span, chans + NSTATE :] = dreader + nn3(cross_grad, writer)
                reach = nn(jnp.concatenate(reach, axis=1), sum_ref[...], HIGH)
                carried = nn(jnp.concatenate(carried, axis=1), sum_ref[...], HIGH)
                direct = jnp.transpose(fall) + reach
                given = dt * reach
                dlog = scan_dot[span] - dt * direct
                ends = jnp.sum(given, axis=0, keepdims=True) + carried
                at_end = lax.broadcasted_iota(jnp.int32, (chunk, LANES), 0) == chunk - 1
                dlog = dlog + jnp.where(at_end, ends, 0.0)
                ddecay = tn(lower, dlog, HIGH)
                ddt_ref[span, :] = direct + ddecay * rate
                acc_ref[8:9, :LANES] += jnp.sum(ddecay * dt, axis=0, keepdims=True)
            dstate_ref[...] = dstate_ref[...] * keep
            ddt_raw = ddt_ref[...] * sigmoid(step_in)
            acc_ref[7:8, :LANES] += jnp.sum(ddt_raw, axis=0, keepdims=True)
            dpre_ref[block : block + 8, :] = dpre_ref[0:8, :] * after
            dpre_ref[0:block, :] = dact_ref[...] * slope
            raw = conv_ref[8 : 8 + block, :]
            acc_ref[CONV : CONV + 1, : sz.conv] += jnp.sum(dpre_ref[0:block, :], axis=0, keepdims=True)
            draw = jnp.zeros((block, sz.conv), F32)
            for tap in range(CONV):
                later = dpre_ref[tap : tap + block, :]
                draw = draw + pk_ref[tap : tap + 1, : sz.conv] * later
                acc_ref[tap : tap + 1, : sz.conv] += jnp.sum(raw * later, axis=0, keepdims=True)
            low = jnp.concatenate(
                [dz.astype(BF16), draw.astype(BF16), ddt_raw.astype(BF16)], axis=1
            )
            part_ref[span_all, :] = nn(low, w_ref[...]).astype(BF16)
            gt_ref[...] = nt(order_ref[...], low).astype(BF16)
            for copy in stores(c):
                copy.start()
            if per == 1:
                scatter.step(planes, i + 1, lambda k: planes - 1 - k)
            else:
                pl.when(i % per == per - 1)(
                    lambda: scatter.step(planes, i // per + 1, lambda k: planes - 1 - k)
                )
            return carry

        def input_grads():
            gain = pk_ref[GAIN_ROW : GAIN_ROW + 1, :]
            grad, gain_grad = norm_rows_back(u_ref[...].astype(F32), gain, grad_ref[...])
            grad = grad + up_ref[...].astype(F32)
            grad_ref[...] = grad
            acc_ref[GAIN_ROW : GAIN_ROW + 1, :] = gain_grad
            return grad

        lax.fori_loop(0, blocks, one_block, 0)
        if not close:
            scatter.finish(planes, lambda k: planes - 1 - k)
            grad = input_grads()
            low_grad_ref[...] = grad.astype(BF16)
            if more:
                own_ref, stat_ref, stat_send, stat_recv = take(4)
                out_grad = (live_ref[:, 0:1] * grad.astype(BF16).astype(F32)).astype(BF16)
                own_ref[...] = out_grad
                write_stats(stat_ref, lower_total[...], out_grad.astype(F32), lower_ref[...], rows)
                run_gather(count, parts, own_ref, next_ref, refs, (stat_ref, stats_ref, stat_send, stat_recv))
            for c in range(0, min(2, blocks)):
                for copy in stores(c):
                    copy.wait()
            scatter.drain()
            return

        def at(j):
            return pl.ds(pl.multiple_of(j * cols, cols), cols)

        def columns(which, j):
            slot = j % 2
            h_all, g_from = (h_upper, g_upper) if which else (h_own, g_all)
            return [
                pltpu.make_async_copy(h_all.at[:, at(j)], h_cols.at[slot], col_sem.at[0, slot]),
                pltpu.make_async_copy(g_from.at[:, at(j)], g_cols.at[slot], col_sem.at[1, slot]),
            ]

        def passed(src, dst, send_sem, recv_sem):
            return pltpu.make_async_remote_copy(
                src_ref=src, dst_ref=dst, send_sem=send_sem, recv_sem=recv_sem,
                device_id={"section": other}, device_id_type=MESH,
            )

        def traded(j):
            sets = ((send_in, box_in), (send_out, box_out), (send_state, box_state))
            return [
                passed(src.at[:, at(j)], dst.at[:, at(j)], trade_send.at[k, j], trade_recv.at[k, j])
                for k, (src, dst) in enumerate(sets)
            ]

        def weight_steps(which, begin, end):
            gt, q = (gt_one, q_one) if which else (gt_full, q_full)

            def body(j, carry):
                slot = j % 2
                for copy in columns(which, j):
                    copy.wait()

                @pl.when(j + 1 < steps)
                def _():
                    for copy in columns(which, j + 1):
                        copy.start()

                in_grad = nn(gt[: sz.master_pad, :], h_cols[slot])
                state_grad = nn(gt[sz.master_pad :, :], h_cols[slot])
                out_grad = tn(q[...], g_cols[slot])

                @pl.when(section == which)
                def _():
                    sum_in[:, at(j)] = in_grad
                    sum_out[:, at(j)] = out_grad
                    state_own[:, at(j)] = state_grad

                @pl.when(section != which)
                def _():
                    send_in[:, at(j)] = in_grad.astype(BF16)
                    send_out[:, at(j)] = out_grad.astype(BF16)
                    send_state[:, at(j)] = state_grad
                    for copy in traded(j):
                        copy.start()

                return carry

            lax.fori_loop(begin, end, body, 0)

        def begin_columns(which):
            for copy in columns(which, 0):
                copy.start()

        begin_columns(1)
        for copy in whole:
            copy.wait()
        weight_steps(1, 0, steps // 4)
        scatter.step(planes, planes + 1, lambda k: planes - 1 - k)
        weight_steps(1, steps // 4, steps // 2)
        scatter.step(planes, planes + 2, lambda k: planes - 1 - k)
        weight_steps(1, steps // 2, steps)
        begin_columns(0)
        weight_steps(0, 0, steps // 4)
        scatter.last()
        input_grads()
        few = [(acc_ref, acc_upper, box_small), (result_own, result_upper, outs_ref.at[section])]
        few.append((grad_ref, grad_upper, grads_ref.at[section]))

        def few_copies(theirs):
            return [
                passed(entry[theirs], entry[2], few_send.at[k], few_recv.at[k]) for k, entry in enumerate(few)
            ]

        @pl.when(section == 0)
        def _():
            for copy in few_copies(1):
                copy.start()
            outs_ref[0] = result_own[...]
            grads_ref[0] = grad_ref[...]

        @pl.when(section == 1)
        def _():
            for copy in few_copies(0):
                copy.start()
            outs_ref[1] = result_upper[...]
            grads_ref[1] = grad_upper[...]

        weight_steps(0, steps // 4, steps)
        squares_ref[...] = jnp.zeros_like(squares_ref)

        def add_up(j, carry):
            for copy in traded(j):
                copy.wait_recv()
            total = sum_in[:, at(j)] + box_in[:, at(j)].astype(F32)
            sum_in[:, at(j)] = total
            squares_ref[0:1, at(j)] += jnp.sum(total * total, axis=0, keepdims=True)
            total = sum_out[:, at(j)] + box_out[:, at(j)].astype(F32)
            sum_out[:, at(j)] = total
            squares_ref[1:2, at(j)] += jnp.sum(total * total, axis=0, keepdims=True)
            sum_state[:, at(j)] = (state_own[:, at(j)] + box_state[:, at(j)]).astype(BF16)
            return carry

        lax.fori_loop(0, steps, add_up, 0)
        for copy in few_copies(0):
            copy.wait_recv()
        sum_small[...] = jnp.where(section == 0, acc_ref[...], acc_upper[...]) + box_small[...]

        def settle(j, carry):
            for copy in traded(j):
                copy.wait_send()
            return carry

        lax.fori_loop(0, steps, settle, 0)
        for copy in few_copies(0):
            copy.wait_send()
        scatter.drain()

    tokens = sz.tokens
    state = 2 * NSTATE
    if close:
        out_shape = [
            jax.ShapeDtypeStruct((sz.master_pad, width), F32),
            jax.ShapeDtypeStruct((chans, width), F32),
            jax.ShapeDtypeStruct((state, width), BF16),
            jax.ShapeDtypeStruct((16, width), F32),
            jax.ShapeDtypeStruct((2, rows, width), BF16),
            jax.ShapeDtypeStruct((2, rows, width), F32),
            jax.ShapeDtypeStruct((8, width), F32),
        ]
        out_specs = [VMEM_SPEC] * 7
    else:
        out_shape = [
            jax.ShapeDtypeStruct((rows, width), F32),
            jax.ShapeDtypeStruct((rows, width), BF16),
            jax.ShapeDtypeStruct((16, width), F32),
            jax.ShapeDtypeStruct((sz.grad_rows, tokens), BF16),
            jax.ShapeDtypeStruct((tokens, chans), BF16),
        ]
        out_specs = [VMEM_SPEC] * 3 + [ANY_SPEC] * 2
    scratch = [
        pltpu.VMEM((block + 8, sz.conv), F32),
        pltpu.VMEM((block + 8, sz.conv), F32),
        pltpu.VMEM((block, sz.conv), F32),
        pltpu.VMEM((block, LANES), F32),
        pltpu.VMEM((NSTATE, chans), F32),
        pltpu.VMEM((sz.cols, width), BF16),
        pltpu.VMEM((chans, width), BF16),
        pltpu.VMEM((sz.grad_rows, sz.cols), BF16),
        pltpu.VMEM((2, block, width), BF16),
        pltpu.VMEM((2, block, sz.cols), F32),
        pltpu.VMEM((2, 8, sz.cols), F32),
        pltpu.VMEM((2, block, chans), F32),
        pltpu.VMEM((2, subs, NSTATE, chans), F32),
        pltpu.VMEM((8, LANES) if close else (2, sz.grad_rows, block), BF16),
        pltpu.VMEM((8, LANES) if close else (2, block, chans), BF16),
        pltpu.VMEM((tokens, width), BF16),
        DMA((5, 2)),
        DMA((2, 2)),
        DMA((3,)),
    ]
    scratch += scatter.scratch()
    if close:
        scratch += [
            pltpu.VMEM((rows, width), F32),
            pltpu.VMEM((16, width), F32),
            pltpu.VMEM((sz.grad_rows, tokens), BF16),
            pltpu.VMEM((tokens, chans), BF16),
            pltpu.VMEM((sz.grad_rows, tokens), BF16),
            pltpu.VMEM((tokens, chans), BF16),
            pltpu.VMEM((2, tokens, cols), BF16),
            pltpu.VMEM((2, tokens, cols), BF16),
        ]
        scratch += [
            pltpu.VMEM((state, width), F32),
            pltpu.VMEM((sz.master_pad, width), BF16),
            pltpu.VMEM((chans, width), BF16),
            pltpu.VMEM((state, width), F32),
            pltpu.VMEM((16, width), F32),
            pltpu.VMEM((state, width), F32),
        ]
        scratch += [DMA((2, 2)), DMA((2,)), DMA((3, steps)), DMA((3, steps)), DMA((3,)), DMA((3,))]
    operands = [resets, out_grads, proj, mixed, states, weights, weight_out, order]
    in_specs = [pl.BlockSpec(memory_space=pltpu.SMEM)] + [ANY_SPEC] * 7 + [VMEM_SPEC] * 6
    operands += [stats, pack, sz.head_sum(), residual, upstream, live]
    if more:
        out_shape += [
            jax.ShapeDtypeStruct((tokens, width), BF16),
            jax.ShapeDtypeStruct((count, 8, LANES), F32),
        ]
        out_specs += [ANY_SPEC, VMEM_SPEC]
        scratch += [pltpu.VMEM((rows, width), BF16), pltpu.VMEM((8, LANES), F32)]
        scratch += [DMA((count,))] * 2 + gather_scratch(parts, dims, count)
        operands += list(below)
        in_specs += [VMEM_SPEC] * 2
    if close:
        operands += list(upper)
        in_specs += [ANY_SPEC] * 5 + [VMEM_SPEC] * 4
    return pl.pallas_call(
        kernel,
        out_shape=out_shape,
        in_specs=in_specs,
        out_specs=out_specs,
        scratch_shapes=scratch,
        compiler_params=params(collective_id),
        name="last_phase" if close else "backward_phase",
    )(*operands)


def weight_grads(sz, grads_t, gathered, scaled, out_grads):
    cols = 256

    split_row = sz.master_pad

    def kernel(gt_ref, h_ref, q_ref, g_ref, in_ref, state_ref, out_ref):
        in_ref[...] = nn(gt_ref[:split_row, :], h_ref[...]).astype(BF16)
        state_ref[...] = nn(gt_ref[split_row:, :], h_ref[...])
        out_ref[...] = tn(q_ref[...], g_ref[...]).astype(BF16)

    tokens, width, chans = sz.tokens, sz.width, sz.channels
    return pl.pallas_call(
        kernel,
        grid=(width // cols,),
        out_shape=[
            jax.ShapeDtypeStruct((sz.master_pad, width), BF16),
            jax.ShapeDtypeStruct((2 * NSTATE, width), F32),
            jax.ShapeDtypeStruct((chans, width), BF16),
        ],
        in_specs=[
            pl.BlockSpec((sz.grad_rows, tokens), lambda i: (0, 0)),
            pl.BlockSpec((tokens, cols), lambda i: (0, i)),
            pl.BlockSpec((tokens, chans), lambda i: (0, 0)),
            pl.BlockSpec((tokens, cols), lambda i: (0, i)),
        ],
        out_specs=[
            pl.BlockSpec((sz.master_pad, cols), lambda i: (0, i)),
            pl.BlockSpec((2 * NSTATE, cols), lambda i: (0, i)),
            pl.BlockSpec((chans, cols), lambda i: (0, i)),
        ],
        compiler_params=pltpu.CompilerParams(vmem_limit_bytes=VMEM_LIMIT),
        name="weight_grads",
    )(grads_t, gathered, scaled, out_grads)


def adam_update(weight, moment, second, gradient, rate, decay):
    moment_new = BETA_ONE * moment + (1.0 - BETA_ONE) * gradient
    second_new = BETA_TWO * second + (1.0 - BETA_TWO) * gradient * gradient
    corrected = moment_new / (1.0 - BETA_ONE**ADAM_STEP)
    corrected_sq = second_new / (1.0 - BETA_TWO**ADAM_STEP)
    weight_new = weight - rate * (corrected / (jnp.sqrt(corrected_sq) + ADAM_EPS) + decay * weight)
    return (weight_new, moment_new, second_new)


def adam_in(sz, clip, grad, weight, moment, second):
    block = LANES
    width = sz.width

    def kernel(clip_ref, g_ref, w_ref, m_ref, v_ref, wn_ref, mn_ref, vn_ref, low_ref):
        scale = clip_ref[0]

        def body(i, carry):
            made = []
            for half in range(2):
                span = pl.ds(pl.multiple_of(i * 16 + half * 8, 8), 8)
                new = adam_update(
                    w_ref[span, 0, :], m_ref[span, 0, :], v_ref[span, 0, :],
                    scale * g_ref[span, :], LEARN_MATRIX, WEIGHT_DECAY,
                )
                wn_ref[span, 0, :] = new[0]
                mn_ref[span, 0, :] = new[1]
                vn_ref[span, 0, :] = new[2]
                made.append(new[0])
            low_ref[pl.ds(pl.multiple_of(i * 16, 16), 16), :] = jnp.concatenate(made, axis=0).astype(BF16)
            return carry

        lax.fori_loop(0, block // 16, body, 0)

    view = pl.BlockSpec((block, 1, width), lambda i: (i, 0, 0))
    flat = pl.BlockSpec((block, width), lambda i: (i, 0))
    shape = jax.ShapeDtypeStruct((sz.master, 1, width), F32)
    return pl.pallas_call(
        kernel,
        grid=(sz.master_pad // block,),
        out_shape=[shape, shape, shape, jax.ShapeDtypeStruct((sz.master, width), BF16)],
        in_specs=[pl.BlockSpec(memory_space=pltpu.SMEM), flat, view, view, view],
        out_specs=[view, view, view, flat],
        compiler_params=pltpu.CompilerParams(vmem_limit_bytes=VMEM_LIMIT),
        name="adam_in",
    )(clip, grad, weight, moment, second)


def adam_plain(clip, grad, weight, moment, second, transposed):
    rows, width = weight.shape
    block = min(256 if transposed else 64, rows)

    def kernel(clip_ref, g_ref, w_ref, m_ref, v_ref, wn_ref, mn_ref, vn_ref, low_ref):
        if transposed:
            row = lax.broadcasted_iota(jnp.int32, (width, width), 0)
            col = lax.broadcasted_iota(jnp.int32, (width, width), 1)
            grad_value = tn(g_ref[...], (row == col).astype(BF16))
        else:
            grad_value = g_ref[...]
        new = adam_update(
            w_ref[...], m_ref[...], v_ref[...], clip_ref[0] * grad_value, LEARN_MATRIX, WEIGHT_DECAY
        )
        wn_ref[...], mn_ref[...], vn_ref[...] = new
        low_ref[...] = new[0].astype(BF16)

    flat = pl.BlockSpec((block, width), lambda i: (i, 0))
    turned = pl.BlockSpec((width, block), lambda i: (0, i))
    shape = jax.ShapeDtypeStruct((rows, width), F32)
    return pl.pallas_call(
        kernel,
        grid=(rows // block,),
        out_shape=[shape, shape, shape, jax.ShapeDtypeStruct((rows, width), BF16)],
        in_specs=[
            pl.BlockSpec(memory_space=pltpu.SMEM), turned if transposed else flat, flat, flat, flat
        ],
        out_specs=[flat] * 4,
        compiler_params=pltpu.CompilerParams(vmem_limit_bytes=VMEM_LIMIT),
        name="adam_plain",
    )(clip, grad, weight, moment, second)


def columns_first(array):
    return jnp.transpose(array, (2, 0, 1))


def shards(
    inputs,
    cotangent,
    valid_lengths,
    proj_in,
    proj_in_m,
    proj_in_v,
    proj_state,
    proj_state_m,
    proj_state_v,
    proj_out,
    proj_out_m,
    proj_out_v,
    head_params,
    head_m,
    head_v,
    shared_params,
    shared_m,
    shared_v,
):
    section = lax.axis_index("section")
    head_idx = lax.axis_index("head")
    count = lax.axis_size("head")
    rows, width = inputs.shape[1], inputs.shape[2]
    heads = head_params.shape[1]
    tokens = rows * count
    sz = Sizes(heads, tokens, width)
    order = sz.order()
    start_block, seq_length, resets = seq_layout(
        lax.dynamic_index_in_dim(valid_lengths, section, 0, keepdims=False)
    )
    token = head_idx * rows + lax.broadcasted_iota(jnp.int32, (rows, LANES), 0)
    live = jnp.zeros((rows, LANES), F32)
    for block in range(sz.blocks):
        inside = (token // STRETCH == block) & (token - start_block[block] * STRETCH < seq_length[block])
        live = jnp.where(inside, 1.0, live)
    first = lax.dynamic_index_in_dim(inputs, section, 0, keepdims=False)
    cot = lax.dynamic_index_in_dim(cotangent, section, 0, keepdims=False)
    weights, weight_out, pack, rows_zero = opening(
        count, sz, columns_first(proj_in), proj_state[0], proj_out[0], head_params[0], shared_params, order, first, 0
    )

    def run_forward(layer, gathered, residual, cotangent, collective_id):
        return forward_phase(
            count, sz, layer, resets, gathered, weights, weight_out, pack, residual, live, cotangent, collective_id
        )

    def run_backward(layer, out_grads, kept, stats, residual, upstream, below, upper, collective_id):
        proj, mixed, states = kept[4:7]
        return backward_phase(
            count, sz, layer, resets, out_grads, proj, mixed, states, stats, weights, weight_out, pack, order,
            residual, upstream, live, below, upper, collective_id,
        )

    kept_zero = run_forward(0, rows_zero, first, None, 1)
    result_zero, branch_zero, total_zero, rows_one = kept_zero[:4]
    kept_one = run_forward(1, rows_one, result_zero, cot, 2)
    result_one, out_grads_one, stats_one = kept_one[0], kept_one[3], kept_one[7]
    back_one = run_backward(
        1, out_grads_one, kept_one, stats_one, result_zero, cot, (branch_zero, total_zero), None, 3
    )
    grad_one, low_one, acc_one, grads_t_one, scaled_one, out_grads_zero, stats_zero = back_one
    upper = (
        grads_t_one, scaled_one, rows_one, out_grads_one, rows_zero, acc_one, result_zero, result_one, grad_one
    )
    if tokens * width <= 4 << 20:
        grad_in, grad_out, state_part, small, layer_outs, grad_buffer, squares = run_backward(
            0, out_grads_zero, kept_zero, stats_zero, first, low_one, None, upper, 4
        )
    else:
        grad_zero, _, acc_zero, grads_t_zero, scaled_zero = run_backward(
            0, out_grads_zero, kept_zero, stats_zero, first, low_one, None, None, 4
        )
        lower = weight_grads(sz, grads_t_zero, rows_zero, scaled_zero, out_grads_zero)
        higher = weight_grads(sz, grads_t_one, rows_one, scaled_one, out_grads_one)
        grad_in, grad_out, state_sum, small, layer_outs, grad_buffer, squares = trade_sections(
            [(lower[0], higher[0]), (lower[2], higher[2]), (lower[1], higher[1]), (acc_zero, acc_one)],
            [(result_zero, result_one), (grad_zero, grad_one)],
            2,
            6,
        )
        state_part = state_sum.astype(BF16)

    state_all, all_stats, norms = finish_sums(
        count, sz, state_part.reshape(16 * count, -1), small, squares, pack, sz.head_sum(), 5
    )
    grad_state = state_all.reshape(state_part.shape)
    pieces = width // LANES
    shared_rows = all_stats[:pieces].transpose(1, 0, 2).reshape(8, width)
    grad_shared = jnp.concatenate(
        [shared_rows[1 : CONV + 2, : 2 * NSTATE].reshape(-1), shared_rows[0]]
    )
    grad_norm, clip_scale = norms[0, 0], norms[1, 0]
    clip = norms[1, :1]
    chans = heads * HDIM
    head_part = head_params[0]
    taps = small[:CONV, :chans].reshape(CONV, heads, HDIM).transpose(1, 0, 2).reshape(heads, -1)
    grad_head = jnp.concatenate(
        [
            taps,
            small[5, :chans].reshape(heads, HDIM),
            small[CONV, :chans].reshape(heads, HDIM),
            small[7, :heads][:, None],
            (small[8, :heads] * -jnp.exp(head_part[:, -2]))[:, None],
            jnp.sum(small[6, :chans].reshape(heads, HDIM), axis=1)[:, None],
        ],
        axis=1,
    )
    new_in = adam_in(
        sz, clip, grad_in, columns_first(proj_in), columns_first(proj_in_m), columns_first(proj_in_v)
    )
    new_out = adam_plain(
        clip, grad_out, proj_out[0], proj_out_m[0], proj_out_v[0], False
    )
    new_state = adam_plain(
        clip, grad_state, proj_state[0], proj_state_m[0], proj_state_v[0], True
    )
    new_head = adam_update(
        head_part, head_m[0], head_v[0], clip_scale * grad_head, LEARN_VECTOR, 0.0
    )
    new_shared = adam_update(
        shared_params[0], shared_m[0], shared_v[0], clip_scale * grad_shared, LEARN_VECTOR, 0.0
    )
    back_view = [jnp.transpose(array, (1, 2, 0)) for array in new_in[:3]]
    return (
        layer_outs[None],
        grad_buffer[None],
        grad_norm,
        back_view[0],
        back_view[1],
        back_view[2],
        new_in[3].T[None],
        new_state[0][None],
        new_state[1][None],
        new_state[2][None],
        new_state[3][None],
        new_out[0][None],
        new_out[1][None],
        new_out[2][None],
        new_out[3][None],
        new_head[0][None],
        new_head[1][None],
        new_head[2][None],
        new_shared[0][None],
        new_shared[1][None],
        new_shared[2][None],
    )


def solution(mesh):
    in_specs = (
        P(None, "head", None),
        P(None, "head", None),
        P(),
        P("section", None, "head"),
        P("section", None, "head"),
        P("section", None, "head"),
        P("section", None, None),
        P("section", None, None),
        P("section", None, None),
        P("section", "head", None),
        P("section", "head", None),
        P("section", "head", None),
        P("section", "head", None),
        P("section", "head", None),
        P("section", "head", None),
        P("section", None),
        P("section", None),
        P("section", None),
    )
    out_specs = (
        P("section", None, "head", None),
        P("section", None, "head", None),
        P(),
        P("section", None, "head"),
        P("section", None, "head"),
        P("section", None, "head"),
        P("section", None, "head"),
        P("section", None, None),
        P("section", None, None),
        P("section", None, None),
        P("section", None, None),
        P("section", "head", None),
        P("section", "head", None),
        P("section", "head", None),
        P("section", "head", None),
        P("section", "head", None),
        P("section", "head", None),
        P("section", "head", None),
        P("section", None),
        P("section", None),
        P("section", None),
    )
    return jax.shard_map(shards, mesh=mesh, in_specs=in_specs, out_specs=out_specs, check_vma=False)
```

time: 598 us -> 517 us (0.86)
  Pallas kernels: 539 us -> 486 us
  other arithmetic: 23.1 us -> 8.44 us
    pallas_call x15 -> x6, Pallas kernels: 506 us -> 451 us  [the longest x2 192 us: forward_phase(): pl.pallas_call(kernel, out_shape=out_shape, in_specs=in_specs, out_specs=...]
    reduce_sum x6 -> x0, other arithmetic: 7.21 us -> none  [the longest x1 2.22 us: shards(): jnp.sum(state_own * state_own)]
  transfers between devices with their start and end apart: 1 -> 0, of which waited for: 1 -> 0; matrix products, arithmetic and copies ran while one was open for 0% -> 0% of each run, Pallas kernels for 0% -> 0%
where the time goes in v3:
time: 517 us; the launch traced here: 509 us
  Pallas kernels  486 us (94%)
  local copies, waits for them, and re-layouts  10.7 us (2%)
  other arithmetic  8.44 us (2%)
    pallas_call x2, Pallas kernels, forward_phase(): pl.pallas_call(kernel, out_shape=out_shape, in_specs=in_specs, out_specs=...  192 us
    pallas_call x2, Pallas kernels, backward_phase(): pl.pallas_call(kernel, out_shape=out_shape, in_specs=in_specs, out_specs=...  174 us
    pallas_call x1, Pallas kernels, opening(): pl.pallas_call(kernel, out_shape=[jax.ShapeDtypeStruct((2, sz.cols, width...  44.5 us
    pallas_call x1, Pallas kernels, finish_sums(): pl.pallas_call(kernel, out_shape=[jax.ShapeDtypeStruct(state_part.shape,...  40.9 us
    pallas_call x2, Pallas kernels, adam_plain(): pl.pallas_call(kernel, grid=(rows // block,), out_shape=[shape, shape, sh...  18.1 us
    pallas_call x1, Pallas kernels, adam_in(): pl.pallas_call(kernel, grid=(sz.master_pad // block,), out_shape=[shape,...  16.8 us

profile of v3, /device:TPU:0, one launch (start us, length us, event | category | flops | bytes accessed | tf_op | source)
XLA Modules:
  0.0 508.9 jit_solution(13814890386878596218)
XLA Ops:
  0.7 0.7 bitcast_select_fusion
  1.4 0.2 broadcast_in_dim.60
  1.5 1.2 compare_convert_fusion
  2.7 0.2 select_reduce_fusion
  2.9 0.6 fusion.15
  3.5 0.6 fusion.14
  6.7 1.3 subtract_compare_fusion.1
  8.0 0.7 subtract_compare_fusion.3
  8.7 0.7 compare_and_fusion
  9.3 0.7 select_select_fusion.refs_6_.refs_13_
  10.1 1.9 dynamic-slice_bitcast_fusion
  11.9 44.5 %opening.1 = (bf16[2,896,2048]{2,1,0:T(8,128)(2,1)}, bf16[2,256,2048]{2,1,0:T(8,128)(2,1)}, f32[2,16,2048]{2,1,0:T(8,128)}, bf16[1024,2048]{1,0:T(8,128)(2,1)}) custom-call(f32[516,1,2048]{2,1,0:T(1,128)} %bitcast.64, f32[2048,256]{1,0:T(8,128)} %bitcast.68, f32[256,2048]{1,0:T(8,128)} %bitcast.66, bf16[896,896]{1,0:T(8,128)(2,1)} %constant.91.clone.refs_3_.refs_7_, ...), custom_call_target="tpu_custom_call" | custom-call | tf_op jit(solution)/shard_map/opening/pallas_call | solution.py:792
  56.4 97.3 %forward_phase.2 = (bf16[64,2048]{1,0:T(8,128)(2,1)}, f32[64,2048]{1,0:T(8,128)}, f32[8,64]{1,0:T(8,128)}, bf16[1024,2048]{1,0:T(8,128)(2,1)}, f32[1024,896]{1,0...) custom-call(f32[4]{0:T(128)} %get-tuple-element.122.refs_0_, ...), custom_call_target="tpu_custom_call" | custom-call | tf_op jit(solution)/shard_map/forward_phase/pallas_call | solution.py:1211
  153.7 94.6 %forward_phase.3 = (bf16[64,2048]{1,0:T(8,128)(2,1)}, f32[64,2048]{1,0:T(8,128)}, f32[8,64]{1,0:T(8,128)}, bf16[1024,2048]{1,0:T(8,128)(2,1)}, f32[1024,896]{1,0...) custom-call(f32[4]{0:T(128)} %get-tuple-element.122.refs_0_, ...), custom_call_target="tpu_custom_call" | custom-call | tf_op jit(solution)/shard_map/forward_phase/pallas_call | solution.py:1211
  248.3 96.2 %backward_phase.1 = (f32[64,2048]{1,0:T(8,128)}, bf16[64,2048]{1,0:T(8,128)(2,1)}, f32[16,2048]{1,0:T(8,128)}, bf16[896,1024]{1,0:T(8,128)(2,1)}, bf16[1024,256]...) custom-call(f32[4]{0:T(128)} %get-tuple-element.122.refs_0_, ...), custom_call_target="tpu_custom_call" | custom-call | tf_op jit(solution)/shard_map/backward_phase/pallas_call | solution.py:1700
  344.6 0.0 copy-start.3
  344.6 0.0 copy-start.6
  344.6 0.0 copy-start.7
  344.6 0.0 copy-start.2
  344.6 0.0 copy-start.4
  344.6 0.0 copy-start.5
  344.6 77.7 %last_phase.1 = (f32[640,2048]{1,0:T(8,128)}, f32[256,2048]{1,0:T(8,128)}, bf16[256,2048]{1,0:T(8,128)(2,1)}, f32[16,2048]{1,0:T(8,128)}, bf16[2,64,2048]{2,1,0:...) custom-call(f32[4]{0:T(128)} %get-tuple-element.122.refs_0_, bf16[1024,2048]{1,0:T(8,128)(2,1)} %get-tuple-element.80.refs_1_, ...), custom_call_target="tpu_custom_call" | custom-call | tf_op jit(solution)/shard_map/last_phase/pallas_call | solution.py:1700
  422.3 0.7 slice_bitcast_fusion.2
  423.0 0.1 copy.54
  423.1 0.1 fusion.8
  423.2 0.1 copy.55
  423.3 0.8 slice_reduce_fusion
  424.1 0.1 reshape_squeeze.2
  424.2 0.1 reduce_sum.19
  424.3 0.1 copy.57
  424.4 0.1 concatenate.48
  424.5 0.1 concatenate.47
  424.6 0.7 slice.73
  425.3 40.9 %finish_sums.1 = (bf16[256,2048]{1,0:T(8,128)(2,1)}, f32[16,8,128]{2,1,0:T(8,128)}, f32[8,128]{1,0:T(8,128)}) custom-call(bf16[256,2048]{1,0:T(8,128)(2,1)} %get-tuple-element.93.refs_0_, f32[16,2048]{1,0:T(8,128)} %get-tuple-element.94.refs_1_, f32[8,2048]{1,0:T(8,128)} %get-tuple-element.95.refs_2_, ...), custom_call_target="tpu_custom_call" | custom-call | tf_op jit(solution)/shard_map/finish_sums/pallas_call | solution.py:647
  466.2 1.3 fusion.13
  467.5 0.1 reshape.295
  467.6 0.1 concatenate.46
  467.7 0.1 concatenate.52
  467.8 0.8 slice_bitcast_fusion
  468.6 0.7 slice_bitcast_fusion.1
  469.3 0.0 copy-done.6
  469.3 1.3 multiply_subtract_fusion.1
  470.6 1.4 multiply_subtract_fusion
  472.0 7.8 %adam_plain.3 = (f32[256,2048]{1,0:T(8,128)}, f32[256,2048]{1,0:T(8,128)}, f32[256,2048]{1,0:T(8,128)}, bf16[256,2048]{1,0:T(8,128)(2,1)}) custom-call(f32[1]{0:T(128)} %bitcast.20.clip_ref, f32[256,2048]{1,0:T(8,128)} %get-tuple-element.107.g_ref, f32[256,2048]{1,0:T(8,128)} %bitcast.67, f32[256,2048]{1,0:T(8,128)} %bitcast.72, f32[256,2048]{1,0:T(8,128)} %bitcast.73), custom_call_target="tpu_custom_call" | custom-call | tf_op jit(solution)/shard_map/adam_plain/pallas_call | solution.py:1813
  479.8 10.3 %adam_plain.2 = (f32[2048,256]{1,0:T(8,128)}, f32[2048,256]{1,0:T(8,128)}, f32[2048,256]{1,0:T(8,128)}, bf16[2048,256]{1,0:T(8,128)(2,1)}) custom-call(f32[1]{0:T(128)} %bitcast.20.clip_ref, bf16[256,2048]{1,0:T(8,128)(2,1)} %get-tuple-element.102.g_ref, f32[2048,256]{1,0:T(8,128)} %bitcast.69, f32[2048,256]{1,0:T(8,128)} %bitcast.74, f32[2048,256]{1,0:T(8,128)} %bitcast.75), custom_call_target="tpu_custom_call" | custom-call | tf_op jit(solution)/shard_map/adam_plain/pallas_call | solution.py:1813
  490.1 16.8 %adam_in.1 = (f32[516,1,2048]{2,1,0:T(1,128)}, f32[516,1,2048]{2,1,0:T(1,128)}, f32[516,1,2048]{2,1,0:T(1,128)}, bf16[516,2048]{1,0:T(8,128)(2,1)}) custom-call(f32[1]{0:T(128)} %bitcast.20.clip_ref, f32[640,2048]{1,0:T(8,128)} %get-tuple-element.97.g_ref, f32[516,1,2048]{2,1,0:T(1,128)} %bitcast.65, f32[516,1,2048]{2,1,0:T(1,128)} %bitcast.70, ...), custom_call_target="tpu_custom_call" | custom-call | tf_op jit(solution)/shard_map/adam_in/pallas_call | solution.py:1782
  506.9 0.8 copy.61
  507.7 1.0 copy.62
  (12 shorter events, 0.0 us)
Async XLA Ops:
  344.6 78.5 %copy-start.3 = (f32[1,4,387]{2,1,0:T(4,128)S(1)}, f32[1,4,387]{2,1,0:T(4,128)}, u32[]{:S(2)}) copy-start(f32[1,4,387]{2,1,0:T(4,128)} %param.34) | copy-start | bytes 18580
  344.6 124.7 %copy-start.6 = (f32[1,4,387]{2,1,0:T(4,128)S(1)}, f32[1,4,387]{2,1,0:T(4,128)}, u32[]{:S(2)}) copy-start(f32[1,4,387]{2,1,0:T(4,128)} %param.35) | copy-start | bytes 18580
  344.6 124.7 %copy-start.7 = (f32[1,4,387]{2,1,0:T(4,128)S(1)}, f32[1,4,387]{2,1,0:T(4,128)}, u32[]{:S(2)}) copy-start(f32[1,4,387]{2,1,0:T(4,128)} %param.36) | copy-start | bytes 18580
  344.6 126.0 %copy-start.2 = (f32[1,3328]{1,0:T(1,128)S(1)}, f32[1,3328]{1,0:T(1,128)}, u32[]{:S(2)}) copy-start(f32[1,3328]{1,0:T(1,128)} %refs_5_.1) | copy-start | bytes 39940
  344.6 126.0 %copy-start.4 = (f32[1,3328]{1,0:T(1,128)S(1)}, f32[1,3328]{1,0:T(1,128)}, u32[]{:S(2)}) copy-start(f32[1,3328]{1,0:T(1,128)} %param.38) | copy-start | bytes 39940
  344.6 126.0 %copy-start.5 = (f32[1,3328]{1,0:T(1,128)S(1)}, f32[1,3328]{1,0:T(1,128)}, u32[]{:S(2)}) copy-start(f32[1,3328]{1,0:T(1,128)} %param.39) | copy-start | bytes 39940
  490.1 16.8 %copy-start.1 = (bf16[2,64,2048]{2,1,0:T(8,128)(2,1)S(1)}, bf16[2,64,2048]{2,1,0:T(8,128)(2,1)}, u32[]{:S(2)}) copy-start(bf16[2,64,2048]{2,1,0:T(8,128)(2,1)} %get-tuple-element.91) | copy-start | bytes 1572868
  490.1 17.6 %copy-start = (f32[2,64,2048]{2,1,0:T(8,128)S(1)}, f32[2,64,2048]{2,1,0:T(8,128)}, u32[]{:S(2)}) copy-start(f32[2,64,2048]{2,1,0:T(8,128)} %get-tuple-element.92) | copy-start | bytes 3145732

commit v4 on v3

--- a/solution.py
+++ b/solution.py
@@ -33,17 +33,24 @@
 CHUNK = 128
 COLS = HDIM * 2 + 1
 GAIN_ROW = 9
-VMEM_LIMIT = 56 << 20
-
-
-def seq_layout(lengths_row):
-    block_count = lengths_row.shape[0]
-    block_idx = jnp.arange(block_count, dtype=jnp.int32)
-    starts = lengths_row > 0
-    start_block = lax.cummax(jnp.where(starts, block_idx, 0), axis=0)
-    owner_mask = (start_block[:, None] == block_idx[None, :]).astype(jnp.int32)
-    seq_length = jnp.sum(owner_mask * lengths_row[None, :], axis=1)
-    return (start_block, seq_length, starts.astype(jnp.float32))
+VMEM_LIMIT = 58 << 20
+
+
+def keeps(lengths_ref, micro, block):
+    return jnp.where(lengths_ref[micro, block] > 0, 0.0, 1.0)
+
+
+def live_rows_of(lengths_ref, micro, shard, rows):
+    token = shard * rows
+    own_block = token // STRETCH
+    start, length = jnp.int32(0), lengths_ref[micro, 0]
+    for block in range(1, lengths_ref.shape[1]):
+        here = lengths_ref[micro, block]
+        begins = (here > 0) & (block <= own_block)
+        start = jnp.where(begins, block, start)
+        length = jnp.where(begins, here, length)
+    position = token - start * STRETCH + lax.broadcasted_iota(jnp.int32, (rows, 1), 0)
+    return (position < length).astype(F32)
 
 
 def chip_dims(count):
@@ -58,6 +65,57 @@
     return (me // (dims[1] * dims[2]), (me // dims[2]) % dims[1], me % dims[2])
 
 
+class Heads:
+    def __init__(self, count):
+        self.count = count
+        self.dims = chip_dims(count)
+        self.lined = False
+
+    def spot(self):
+        return place(self.dims)
+
+    def device(self, index):
+        return {"head": index}
+
+
+class Team:
+    def __init__(self, count):
+        self.count = count
+        self.chips = chip_dims(count)
+        self.paired = self.chips[2] == 2
+        self.lined = True
+        self.dims = self.chips[:2] + (2,) if self.paired else self.chips
+
+    def spot(self):
+        spot = place(self.chips)
+        return spot[:2] + (lax.axis_index("section"),) if self.paired else spot
+
+    def device(self, index):
+        if not self.paired:
+            return {"head": index}
+        return {"section": index % 2, "head": index // 2 * 2 + lax.axis_index("head") % 2}
+
+    def micro(self):
+        return lax.axis_index("head") % 2 if self.paired else lax.axis_index("section")
+
+    def owner(self, layer):
+        if not self.paired:
+            return {"section": layer}
+        return {"section": layer, "head": lax.axis_index("head") // 2 * 2 + lax.axis_index("section")}
+
+    def user(self, micro):
+        if not self.paired:
+            return {"section": micro}
+        head = lax.axis_index("head")
+        return {"section": head % 2, "head": head // 2 * 2 + micro}
+
+    def alone(self, which):
+        section = lax.axis_index("section")
+        if not self.paired:
+            return section == which
+        return (lax.axis_index("head") % 2 == section) & (section == which)
+
+
 def linear(dims, spot):
     return (spot[0] * dims[1] + spot[1]) * dims[2] + spot[2]
 
@@ -73,33 +131,19 @@
     return out
 
 
-def greet_axes(dims, spot):
-    barrier = pltpu.get_barrier_semaphore()
-    count = 0
-    for axis in range(3):
-        for off in range(1, dims[axis]):
-            peer = linear(dims, moved(dims, spot, shift_of((axis,), (off,))))
-            pl.semaphore_signal(
-                barrier, inc=1, device_id={"head": peer}, device_id_type=MESH
-            )
-            count += 1
-    if count:
-        pl.semaphore_wait(barrier, count)
-
-
-def greet_all(count, pair=None):
+def greet_all(count, pair=False):
     barrier = pltpu.get_barrier_semaphore()
     me = lax.axis_index("head")
-    if pair is not None:
-        other = 1 - lax.axis_index(pair)
-        pl.semaphore_signal(barrier, inc=1, device_id={pair: other}, device_id_type=MESH)
+    section = lax.axis_index("section")
     for off in range(1, count):
-        pl.semaphore_signal(
-            barrier, inc=1, device_id={"head": (me + off) % count}, device_id_type=MESH
-        )
-    expected = count - 1 + (pair is not None)
-    if expected:
-        pl.semaphore_wait(barrier, expected)
+        peer = (me + off) % count
+        pl.semaphore_signal(barrier, inc=1, device_id={"head": peer}, device_id_type=MESH)
+        if pair:
+            there = {"section": 1 - section, "head": peer}
+            pl.semaphore_signal(barrier, inc=1, device_id=there, device_id_type=MESH)
+    if pair:
+        pl.semaphore_signal(barrier, inc=1, device_id={"section": 1 - section}, device_id_type=MESH)
+    pl.semaphore_wait(barrier, 2 * count - 1 if pair else count - 1)
 
 
 def rows_at(shard, rows):
@@ -118,12 +162,14 @@
     return parts
 
 
+TEAM_GATHER = ((3, (1, 0, 2), 0), (7, (0, 1, 2), 0), (6, (0, 1, 2), 0))
 GATHER = ((2, (2, 1, 0), 0), (2, (1, 2, 0), 0), (6, (0, 2, 1), 0), (6, (0, 1, 2), 0))
 GATHER_SMALL = ((8, (0, 2, 1), 0), (8, (0, 1, 2), 0))
 SCATTER = (
     (1, (2, 0, 1), 0), (1, (1, 0, 2), 0), (1, (0, 1, 2), 0), (1, (0, 2, 1), 0),
     (3, (2, 1, 0), 0), (3, (1, 2, 0), 0), (3, (2, 1, 0), 1), (3, (1, 2, 0), 1),
 )
+TEAM_SCATTER_SMALL = ((16, (2, 1, 0), 0),)
 SCATTER_SMALL = ((8, (2, 1, 0), 0), (8, (1, 2, 0), 0))
 SCATTER_PACE = (0.3, 0.9, 0.7, 2.0)
 
@@ -139,14 +185,15 @@
     pl.when(cond)(action)
 
 
-def gather_steps(dims, parts, rows, own_ref, all_ref, send_sem, recv_sem, between=()):
-    spot = place(dims)
+def gather_steps(group, parts, rows, own_ref, all_ref, send_sem, recv_sem, between=()):
+    dims = group.dims
+    spot = group.spot()
     me = linear(dims, spot)
     waits = []
     counter = [0] * len(parts)
 
     def lined(axis):
-        return axis == 0 and dims[0] > 2 and dims[1] == 2
+        return group.lined and axis == 0 and dims[0] > 2 and dims[1] == 2
 
     def above(axis, dist):
         return lambda: spot[axis] + dist < dims[axis]
@@ -188,7 +235,7 @@
                     dst_ref=dst,
                     send_sem=send_sem.at[part, number],
                     recv_sem=recv_sem.at[part, shard],
-                    device_id={"head": peer},
+                    device_id=group.device(peer),
                     device_id_type=MESH,
                 ).start()
 
@@ -203,7 +250,7 @@
                 dst_ref=dst,
                 send_sem=send_sem.at[part, 0],
                 recv_sem=recv_sem.at[part, shard],
-                device_id={"head": me},
+                device_id=group.device(me),
                 device_id_type=MESH,
             ).wait_recv()
             push(part, offsets, pos, preds, None, came)
@@ -246,7 +293,7 @@
                 dst_ref=ref,
                 send_sem=send_sem.at[part, number],
                 recv_sem=recv_sem.at[part, 0],
-                device_id={"head": me},
+                device_id=group.device(me),
                 device_id_type=MESH,
             ).wait_send()
 
@@ -257,8 +304,9 @@
     return 3 * dims[0] * dims[1] * dims[2]
 
 
-def scatter_steps(dims, parts, rows, in_ref, out_ref, box_ref, send_sem, recv_sem):
-    spot = place(dims)
+def scatter_steps(group, parts, rows, in_ref, out_ref, box_ref, send_sem, recv_sem, staged=False):
+    dims = group.dims
+    spot = group.spot()
     me = linear(dims, spot)
     sends = []
 
@@ -289,7 +337,7 @@
             dst_ref=box_ref.at[slot, :, cols(part)],
             send_sem=send_sem.at[part, slot],
             recv_sem=recv_sem.at[part, slot],
-            device_id={"head": peer},
+            device_id=group.device(peer),
             device_id_type=MESH,
         )
         copy.start()
@@ -302,7 +350,7 @@
             dst_ref=ref,
             send_sem=send_sem.at[part, slot],
             recv_sem=recv_sem.at[part, slot],
-            device_id={"head": me},
+            device_id=group.device(me),
             device_id_type=MESH,
         ).wait_recv()
         return ref[...].astype(F32)
@@ -344,44 +392,63 @@
 
     lag, rest, turn, end = SCATTER_PACE
     program = []
-    for part, (_, _, _, group) in enumerate(parts):
+    for part, (_, _, _, late) in enumerate(parts):
         for ob, oc in itertools.product(range(size(part, 1)), range(size(part, 2))):
             for off in range(1, size(part, 0)):
-                rank = (0.0 if ob else rest) + group * lag
+                rank = (0.0 if ob else rest) + late * lag
                 program.append((rank, oc == 0, off, part, first, ob, oc))
             if ob:
-                program.append((turn + group * lag, oc == 0, 0, part, second, ob, oc))
+                program.append((turn + late * lag, oc == 0, 0, part, second, ob, oc))
         for oc in range(1, size(part, 2)):
-            program.append((end + group * lag, False, 0, part, third, 0, oc))
-        program.append((3.0 + group * lag, True, 0, part, last, 0, 0))
+            program.append((end + late * lag, False, 0, part, third, 0, oc))
+        program.append((3.0 + late * lag, True, 0, part, last, 0, 0))
     program.sort(key=lambda step: step[:4])
-    for _, _, off, part, action, ob, oc in program:
-        action(part, ob, oc, off)
+
+    def run(low, high):
+        for rank, _, off, part, action, ob, oc in program:
+            if low <= rank < high:
+                action(part, ob, oc, off)
+
+    if staged:
+        marks = (-1.0, turn, end, 3.0, 9.0)
+        return sends, [lambda k=k: run(marks[k], marks[k + 1]) for k in range(4)]
+    run(-1.0, 99.0)
     return sends
 
 
+PIECES = 1
+
+
 class PlaneScatter:
-    def __init__(self, dims, rows, width):
-        self.dims, self.rows, self.half = dims, rows, width // 2
-        self.orders = ((2, 1), (1, 2))
+    def __init__(self, group, rows, width):
+        self.group, self.dims, self.rows = group, group.dims, rows
+        self.wide = group.paired
+        self.orders = ((2, 1),) * PIECES if self.wide else ((2, 1), (1, 2))
+        self.half = width // len(self.orders)
         self.width = width
-        depth = dims[0]
-        most = max(dims[1], dims[2])
+        depth = self.dims[0]
+        most = max(self.dims[1], self.dims[2])
         self.one = depth * (most - 1) * most
         self.two = depth * (most - 1)
-        self.slots = max(self.one + self.two + depth, 1)
+        self.slots = self.one + self.two + 2 * depth
+        self.first_type = F32 if self.wide else BF16
 
     def scratch(self):
+        parts = len(self.orders)
+        later = self.two + 2 * self.dims[0]
         return [
-            pltpu.VMEM((self.slots, self.rows, self.width), BF16),
-            DMA((2, self.slots)),
-            DMA((2, self.slots)),
+            pltpu.VMEM((self.one, self.rows, self.width), self.first_type),
+            pltpu.VMEM((later, self.rows, self.width), BF16),
+            pltpu.VMEM((self.two + self.dims[0] if self.wide else 1, self.rows, self.width), BF16),
+            DMA((parts, self.slots)),
+            DMA((parts, self.slots)),
         ]
 
-    def bind(self, part_ref, out_ref, box_ref, send_sem, recv_sem):
-        self.part_ref, self.out_ref, self.box_ref = part_ref, out_ref, box_ref
+    def bind(self, part_ref, out_ref, first_ref, later_ref, hold_ref, send_sem, recv_sem):
+        self.part_ref, self.out_ref = part_ref, out_ref
+        self.first_ref, self.later_ref, self.hold_ref = first_ref, later_ref, hold_ref
         self.send_sem, self.recv_sem = send_sem, recv_sem
-        self.spot = place(self.dims)
+        self.spot = self.group.spot()
         self.me = linear(self.dims, self.spot)
 
     def sizes(self, part):
@@ -395,8 +462,8 @@
     def slot_two(self, part, plane, eb):
         return self.one + plane * (self.sizes(part)[1] - 1) + eb - 1
 
-    def slot_three(self, plane):
-        return self.one + self.two + plane
+    def slot_three(self, plane, below):
+        return self.one + self.two + 2 * plane + below
 
     def cols(self, part):
         return pl.ds(part * self.half, self.half)
@@ -406,28 +473,37 @@
         spot = moved(self.dims, (plane, self.spot[1], self.spot[2]), shift)
         return self.part_ref.at[rows_at(linear(self.dims, spot), self.rows), self.cols(part)]
 
-    def copy(self, part, src, slot, sent, peer):
-        return pltpu.make_async_remote_copy(
-            src_ref=src,
-            dst_ref=self.box_ref.at[slot, :, self.cols(part)],
-            send_sem=self.send_sem.at[part, sent],
-            recv_sem=self.recv_sem.at[part, slot],
-            device_id={"head": peer},
-            device_id_type=MESH,
+    def box(self, part, slot, begun):
+        if begun:
+            return self.first_ref.at[slot, :, self.cols(part)]
+        return self.later_ref.at[slot - self.one, :, self.cols(part)]
+
+    def copy(self, part, src, slot, sent, peer, begun=False):
+        return remote(
+            src,
+            self.box(part, slot, begun),
+            self.send_sem.at[part, sent],
+            self.recv_sem.at[part, slot],
+            self.group.device(peer),
         )
+
+    def hold(self, part, plane, oa, ob, slot):
+        if self.wide:
+            return self.hold_ref.at[slot - self.one, :, self.cols(part)]
+        return self.mine(part, plane, oa, ob)
 
     def peer(self, part, pos, off):
         shift = shift_of((self.orders[part][pos],), (off,))
         return linear(self.dims, moved(self.dims, self.spot, shift))
 
-    def arrived(self, part, slot):
-        ref = self.box_ref.at[slot, :, self.cols(part)]
-        self.copy(part, ref, slot, slot, self.me).wait_recv()
+    def arrived(self, part, slot, begun=False):
+        ref = self.box(part, slot, begun)
+        self.copy(part, ref, slot, slot, self.me, begun).wait_recv()
         return ref[...].astype(F32)
 
     def first(self, plane):
         for inner in (1, 0):
-            for part in range(2):
+            for part in range(len(self.orders)):
                 size_a, size_b = self.sizes(part)
                 for ob in range(size_b):
                     if (ob != 0) != bool(inner):
@@ -435,51 +511,70 @@
                     for off in range(1, size_a):
                         slot = self.slot_one(part, plane, size_a - off, ob)
                         src = self.mine(part, plane, off, ob)
-                        self.copy(part, src, slot, slot, self.peer(part, 0, off)).start()
+                        self.copy(part, src, slot, slot, self.peer(part, 0, off), True).start()
 
     def second(self, plane):
-        for part in range(2):
+        for part in range(len(self.orders)):
             size_a, size_b = self.sizes(part)
             for ob in range(1, size_b):
-                hold = self.mine(part, plane, 0, ob)
-                total = hold[...].astype(F32)
+                slot = self.slot_two(part, plane, size_b - ob)
+                total = self.mine(part, plane, 0, ob)[...].astype(F32)
                 for ea in range(1, size_a):
-                    total = total + self.arrived(part, self.slot_one(part, plane, ea, ob))
+                    total = total + self.arrived(part, self.slot_one(part, plane, ea, ob), True)
+                hold = self.hold(part, plane, 0, ob, slot)
                 hold[...] = total.astype(BF16)
-                slot = self.slot_two(part, plane, size_b - ob)
                 self.copy(part, hold, slot, slot, self.peer(part, 1, ob)).start()
 
-    def third(self, plane):
+    def third(self, plane, place_in_line):
         depth = self.spot[0]
-        for part in range(2):
+        above = depth > plane
+        place_here = jnp.where(above, self.dims[0] - 1 - depth, depth)
+
+        def own_total(part):
             size_a, size_b = self.sizes(part)
-            hold = self.mine(part, plane, 0, 0)
-            total = hold[...].astype(F32)
+            total = self.mine(part, plane, 0, 0)[...].astype(F32)
             for ea in range(1, size_a):
-                total = total + self.arrived(part, self.slot_one(part, plane, ea, 0))
+                total = total + self.arrived(part, self.slot_one(part, plane, ea, 0), True)
             for eb in range(1, size_b):
                 total = total + self.arrived(part, self.slot_two(part, plane, eb))
+            return total
+
+        if place_in_line == 0:
 
             @pl.when(plane == depth)
-            def _(part=part, total=total):
-                self.out_ref[:, self.cols(part)] = total
-
-            @pl.when(plane != depth)
-            def _(part=part, total=total, hold=hold):
+            def _():
+                for part in range(len(self.orders)):
+                    self.out_ref[:, self.cols(part)] = own_total(part)
+
+        @pl.when((plane != depth) & (place_here == place_in_line))
+        def _():
+            below = jnp.where(above, 0, 1)
+            onward = jnp.where(above, depth - 1, depth + 1)
+            peer = linear(self.dims, (onward, self.spot[1], self.spot[2]))
+            slot = self.slot_three(plane, below)
+            for part in range(len(self.orders)):
+                total = own_total(part)
+                if place_in_line > 0:
+                    total = total + self.arrived(part, slot)
+                hold = self.hold(part, plane, 0, 0, self.one + self.two + plane)
                 hold[...] = total.astype(BF16)
-                peer = linear(self.dims, (plane, self.spot[1], self.spot[2]))
-                self.copy(part, hold, self.slot_three(depth), self.slot_three(plane), peer).start()
+                self.copy(part, hold, slot, slot, peer).start()
 
     def last(self):
-        for part in range(2):
-            total = self.out_ref[:, self.cols(part)]
-            for off in range(1, self.dims[0]):
-                plane = (self.spot[0] + off) % self.dims[0]
-                total = total + self.arrived(part, self.slot_three(plane))
-            self.out_ref[:, self.cols(part)] = total
+        depth = self.spot[0]
+        for below, there in ((0, depth < self.dims[0] - 1), (1, depth > 0)):
+
+            @pl.when(there)
+            def _(below=below):
+                for part in range(len(self.orders)):
+                    total = self.out_ref[:, self.cols(part)]
+                    total = total + self.arrived(part, self.slot_three(depth, below))
+                    self.out_ref[:, self.cols(part)] = total
 
     def step(self, number, made, plane_of):
-        for back, action in ((0, self.first), (1, self.second), (2, self.third)):
+        actions = [self.first, self.second]
+        actions += [lambda plane, k=k: self.third(plane, k) for k in range(max(self.dims[0] - 1, 1))]
+        for back, action in enumerate(actions):
             k = made - 1 - back
             if isinstance(made, int):
                 if 0 <= k < number:
@@ -487,27 +582,35 @@
             else:
                 pl.when(k >= 0)(lambda k=k, action=action: action(plane_of(k)))
 
-    def finish(self, number, plane_of):
-        for extra in (1, 2):
+    def extra_steps(self):
+        return 1 + max(self.dims[0] - 1, 1)
+
+    def finish(self, number, plane_of, begun=0):
+        for extra in range(1 + begun, self.extra_steps() + 1):
             self.step(number, number + extra, plane_of)
         self.last()
 
     def drain(self):
-        ref_of = lambda part: self.box_ref.at[0, :, self.cols(part)]
-        for part in range(2):
+        for part in range(len(self.orders)):
             size_a, size_b = self.sizes(part)
+            early, late = self.box(part, 0, True), self.box(part, self.one, False)
             for plane in range(self.dims[0]):
-                slots = [self.slot_one(part, plane, ea, ob) for ea in range(1, size_a) for ob in range(size_b)]
-                slots += [self.slot_two(part, plane, eb) for eb in range(1, size_b)]
-                for slot in slots:
-                    self.copy(part, ref_of(part), slot, slot, self.me).wait_send()
+                for ea in range(1, size_a):
+                    for ob in range(size_b):
+                        slot = self.slot_one(part, plane, ea, ob)
+                        self.copy(part, early, slot, slot, self.me, True).wait_send()
+                for eb in range(1, size_b):
+                    slot = self.slot_two(part, plane, eb)
+                    self.copy(part, late, slot, slot, self.me).wait_send()
             for off in range(1, self.dims[0]):
-                slot = self.slot_three((self.spot[0] + off) % self.dims[0])
-                self.copy(part, ref_of(part), slot, slot, self.me).wait_send()
-
-
-def start_direct(count, own_ref_of, box_ref, send_sem, recv_sem):
-    me = lax.axis_index("head")
+                plane = (self.spot[0] + off) % self.dims[0]
+                slot = self.slot_three(plane, jnp.where(self.spot[0] > plane, 0, 1))
+                self.copy(part, late, slot, slot, self.me).wait_send()
+
+
+def start_direct(group, own_ref_of, box_ref, send_sem, recv_sem):
+    count = group.count
+    me = linear(group.dims, group.spot())
     copies = []
     for off in range(1, count):
         peer = (me + off) % count
@@ -516,7 +619,7 @@
             dst_ref=box_ref.at[me],
             send_sem=send_sem.at[off],
             recv_sem=recv_sem.at[count - off],
-            device_id={"head": peer},
+            device_id=group.device(peer),
             device_id_type=MESH,
         )
         copy.start()
@@ -524,8 +627,9 @@
     return copies
 
 
-def wait_direct(count, box_ref, copies, recv_sem, send_sem):
-    me = lax.axis_index("head")
+def wait_direct(group, box_ref, copies, recv_sem, send_sem):
+    count = group.count
+    me = linear(group.dims, group.spot())
     for off in range(1, count):
         ref = box_ref.at[(me + off) % count]
         pltpu.make_async_remote_copy(
@@ -533,13 +637,42 @@
             dst_ref=ref,
             send_sem=send_sem.at[off],
             recv_sem=recv_sem.at[off],
-            device_id={"head": me},
+            device_id=group.device(me),
             device_id_type=MESH,
         ).wait_recv()
     for copy in copies:
         copy.wait_send()
 
 
+def remote(src, dst, send_sem, recv_sem, device):
+    return pltpu.make_async_remote_copy(
+        src_ref=src, dst_ref=dst, send_sem=send_sem, recv_sem=recv_sem, device_id=device, device_id_type=MESH
+    )
+
+
+class Delivery:
+    def __init__(self, src, dst, send_sem, recv_sem, device, alone):
+        self.alone = alone
+        self.ends = src, dst, send_sem, recv_sem, device
+
+    def near(self):
+        return pltpu.make_async_copy(*self.ends[:3])
+
+    def far(self):
+        return remote(*self.ends)
+
+    def start(self):
+        pl.when(self.alone)(lambda: self.near().start())
+        pl.when(jnp.logical_not(self.alone))(lambda: self.far().start())
+
+    def wait_sent(self):
+        pl.when(self.alone)(lambda: self.near().wait())
+        pl.when(jnp.logical_not(self.alone))(lambda: self.far().wait_send())
+
+    def wait_got(self):
+        pl.when(jnp.logical_not(self.alone))(lambda: self.far().wait_recv())
+
+
 VMEM_SPEC = pl.BlockSpec(memory_space=pltpu.VMEM)
 ANY_SPEC = pl.BlockSpec(memory_space=pl.ANY)
 DMA = pltpu.SemaphoreType.DMA
@@ -555,20 +688,19 @@
     return [DMA((len(parts), gather_sends(dims))), DMA((len(parts), count)), DMA]
 
 
-def run_gather(count, parts, own_ref, all_ref, sems, stat=None, between=()):
-    dims = chip_dims(count)
+def run_gather(group, parts, own_ref, all_ref, sems, stat=None, between=()):
     rows = own_ref.shape[0]
-    me = lax.axis_index("head")
+    me = linear(group.dims, group.spot())
     send_sem, recv_sem, local_sem = sems
     local = pltpu.make_async_copy(own_ref, all_ref.at[rows_at(me, rows)], local_sem)
     local.start()
     if stat is not None:
         stat_ref, box_ref, small_send, small_recv = stat
-        copies = start_direct(count, lambda peer: stat_ref, box_ref, small_send, small_recv)
+        copies = start_direct(group, lambda peer: stat_ref, box_ref, small_send, small_recv)
         box_ref[me] = stat_ref[...]
-    gather_steps(dims, parts, rows, own_ref, all_ref, send_sem, recv_sem, between)
+    gather_steps(group, parts, rows, own_ref, all_ref, send_sem, recv_sem, between)
     if stat is not None:
-        wait_direct(count, box_ref, copies, small_recv, small_send)
+        wait_direct(group, box_ref, copies, small_recv, small_send)
     local.wait()
 
 
@@ -577,11 +709,13 @@
     return [pltpu.VMEM((slots, rows, width), BF16), DMA((len(parts), slots)), DMA((len(parts), slots))]
 
 
-def finish_sums(count, sz, state_part, small, squares, pack, head_sum, collective_id):
-    dims = chip_dims(count)
-    width = state_part.shape[1]
-    rows = state_part.shape[0] // count
-    back, parts = column_parts(width, SCATTER_SMALL), column_parts(width, GATHER_SMALL)
+def finish_sums(count, sz, states, small, squares, rates, head_sum, collective_id):
+    team, heads = Team(count), Heads(count)
+    width = states[0].shape[1]
+    rows = states[0].shape[0] // count
+    layers = len(states)
+    back = column_parts(width, TEAM_SCATTER_SMALL if layers > 1 else SCATTER_SMALL)
+    parts = column_parts(width, GATHER_SMALL)
     chans, state = sz.channels, 2 * NSTATE
     pieces = sz.width // LANES
     threshold = CLIP_COEF * PARAMS**0.5
@@ -589,10 +723,13 @@
     def kernel(*refs):
         refs = list(refs)
         take = lambda number: [refs.pop(0) for _ in range(number)]
-        in_ref, small_ref, squares_ref, pks_ref, sum_ref = take(5)
+        in_refs = take(layers)
+        small_ref, squares_ref, rates_ref, sum_ref = take(4)
         all_ref, stats_ref, norm_ref = take(3)
         share_ref, sums_ref, out_ref, own_ref, stat_ref, mine_ref, got_ref = take(7)
         scatter_refs, ag_sems = take(3), take(3)
+        if layers > 1:
+            both_ref, pieces_ref, piece_send, piece_recv = take(4)
         small_send, small_recv, stat_send, stat_recv, pair_send, pair_recv = take(6)
         me = lax.axis_index("head")
         section = lax.axis_index("section")
@@ -603,19 +740,42 @@
         def piece(peer):
             return share_ref.at[:, pl.ds(pl.multiple_of((peer % pieces) * LANES, LANES), LANES)]
 
-        greet_all(count, "section")
-        copies = start_direct(count, piece, sums_ref, small_send, small_recv)
+        greet_all(count, True)
+        copies = start_direct(heads, piece, sums_ref, small_send, small_recv)
         sums_ref[me] = piece(me)[...]
-        sends = scatter_steps(dims, back, rows, in_ref, out_ref, *scatter_refs)
-        wait_direct(count, sums_ref, copies, small_recv, small_send)
+        if layers > 1:
+            for k in range(count):
+                for layer in range(layers):
+                    to = slice((k * layers + layer) * rows, (k * layers + layer + 1) * rows)
+                    both_ref[to, :] = in_refs[layer][k * rows : (k + 1) * rows, :]
+            sends = scatter_steps(team, back, rows * layers, both_ref, out_ref, *scatter_refs)
+            micro = team.micro()
+            passed = [
+                Delivery(
+                    out_ref.at[pl.ds(layer * rows, rows), :], pieces_ref.at[micro],
+                    piece_send.at[layer], piece_recv.at[micro], team.owner(layer), team.alone(layer),
+                )
+                for layer in range(layers)
+            ]
+            for copy in passed:
+                copy.start()
+            for copy in passed:
+                copy.wait_sent()
+            for m in range(2):
+                ref = pieces_ref.at[m]
+                Delivery(ref, ref, piece_send.at[0], piece_recv.at[m], team.user(m), team.alone(m)).wait_got()
+            state_own = pieces_ref[0] + pieces_ref[1]
+        else:
+            sends = scatter_steps(heads, back, rows, in_refs[0], out_ref, *scatter_refs)
+            state_own = out_ref[...]
+        wait_direct(heads, sums_ref, copies, small_recv, small_send)
         shared = jnp.sum(sums_ref[...], axis=0)
         shared_sq = jnp.where(me < pieces, jnp.sum(shared * shared), 0.0)
-        state_own = out_ref[...]
         own_ref[...] = state_own.astype(BF16)
         taps = small_ref[: CONV + 2, :chans]
         skip = nn(small_ref[6:7, :chans], sum_ref[...], HIGH)
         bias = small_ref[7:8, :LANES]
-        rate = small_ref[8:9, :LANES] * pks_ref[section, 8:9, :LANES]
+        rate = small_ref[8:9, :LANES] * rates_ref[...]
         lane = lax.broadcasted_iota(jnp.int32, (1, LANES), 1)
         of_heads = jnp.where(lane < sz.heads, bias * bias + rate * rate + skip * skip, 0.0)
         if chans > sz.heads * HDIM:
@@ -624,7 +784,7 @@
         total = total + jnp.sum(state_own * state_own) + shared_sq
         row = lax.broadcasted_iota(jnp.int32, (8, LANES), 0)
         stat_ref[...] = jnp.where(row == 7, total, shared)
-        run_gather(count, parts, own_ref, all_ref, ag_sems, (stat_ref, stats_ref, stat_send, stat_recv))
+        run_gather(heads, parts, own_ref, all_ref, ag_sems, (stat_ref, stats_ref, stat_send, stat_recv))
         section_sq = stats_ref[0, 7:8, :]
         for k in range(1, count):
             section_sq = section_sq + stats_ref[k, 7:8, :]
@@ -647,26 +807,31 @@
     return pl.pallas_call(
         kernel,
         out_shape=[
-            jax.ShapeDtypeStruct(state_part.shape, BF16),
+            jax.ShapeDtypeStruct(states[0].shape, BF16),
             jax.ShapeDtypeStruct((count, 8, LANES), F32),
             jax.ShapeDtypeStruct((8, LANES), F32),
         ],
-        in_specs=[VMEM_SPEC] * 5,
+        in_specs=[VMEM_SPEC] * (4 + layers),
         out_specs=[ANY_SPEC, VMEM_SPEC, VMEM_SPEC],
         scratch_shapes=[
             pltpu.VMEM((8, sz.width), F32),
             pltpu.VMEM((count, 8, LANES), F32),
-            pltpu.VMEM((rows, width), F32),
+            pltpu.VMEM((rows * layers, width), F32),
             pltpu.VMEM((rows, width), BF16),
         ]
         + [pltpu.VMEM((8, LANES), F32)] * 3
-        + scatter_scratch(back, count, rows, width)
-        + gather_scratch(parts, dims, count)
+        + scatter_scratch(back, count, rows * layers, width)
+        + gather_scratch(parts, heads.dims, count)
+        + (
+            [pltpu.VMEM((count * rows * layers, width), BF16), pltpu.VMEM((2, rows, width), F32), DMA((2,)), DMA((2,))]
+            if layers > 1
+            else []
+        )
         + [DMA((count,))] * 4
         + [DMA, DMA],
         compiler_params=params(collective_id),
         name="finish_sums",
-    )(state_part, small, squares, pack, head_sum)
+    )(*states, small, squares, rates, head_sum)
 
 
 def norm_rows(value, gain):
@@ -707,10 +872,54 @@
     pack_ref[GAIN_ROW : GAIN_ROW + 1, :] = shared_ref[:, (CONV + 1) * state :]
 
 
-def opening(count, sz, proj_in_t, proj_state, proj_out, head_part, shared_part, order, first, collective_id):
-    dims = chip_dims(count)
-    rows, width = first.shape
-    parts = column_parts(width, GATHER)
+def give_weights(team, number, w_ref, wo_ref, ws_ref, wos_ref, zero_ref, sems, sz, steps, cols):
+    send, recv = sems
+    section = lax.axis_index("section")
+    head_rows = (pl.ds(0, 2 * sz.channels), pl.ds(sz.dt, 16))
+    state_rows = pl.ds(2 * sz.channels, 2 * NSTATE)
+
+    def for_users(src, dst, k):
+        return [
+            Delivery(src, dst, send.at[k, micro], recv.at[k], team.user(micro), team.alone(micro))
+            for micro in range(2)
+        ]
+
+    def block(step):
+        span = pl.ds(step * cols, cols)
+        out = []
+        for k, rows in enumerate(head_rows):
+            out += for_users(w_ref.at[rows, span], ws_ref.at[rows, span], 3 * step + k)
+        pair = w_ref.at[state_rows, span], ws_ref.at[state_rows, span]
+        k = 3 * step + 2
+        for there in range(2):
+            out.append(
+                Delivery(*pair, send.at[k, there], recv.at[k], {"section": there}, section == there)
+            )
+        return out
+
+    def matrix():
+        return for_users(wo_ref, wos_ref, 3 * steps)
+
+    def receive():
+        for step in range(steps):
+            span = pl.ds(step * cols, cols)
+            for k, rows in enumerate(head_rows):
+                got = ws_ref.at[rows, span]
+                Delivery(got, got, send.at[0, 0], recv.at[3 * step + k], team.owner(number), team.alone(number)).wait_got()
+            got = ws_ref.at[state_rows, span]
+            Delivery(got, got, send.at[0, 0], recv.at[3 * step + 2], {"section": number}, section == number).wait_got()
+        Delivery(wos_ref, wos_ref, send.at[0, 0], recv.at[3 * steps], team.owner(number), team.alone(number)).wait_got()
+
+    def blank(sem):
+        return pltpu.make_async_copy(zero_ref, ws_ref.at[pl.ds(sz.dt + 16, LANES - 16), :], sem)
+
+    return block, matrix, receive, blank
+
+
+def opening(count, sz, proj_in_t, proj_state, proj_out, head_part, shared_part, order, inputs, cotangent, collective_id):
+    team = Team(count)
+    rows, width = inputs.shape[1:]
+    parts = column_parts(width, TEAM_GATHER if team.paired else GATHER)
     cols = 256
     steps = width // cols
     full = sz.master // 16 * 16
@@ -719,13 +928,13 @@
     def kernel(*refs):
         refs = list(refs)
         take = lambda number: [refs.pop(0) for _ in range(number)]
-        in_hbm, state_hbm, out_hbm, order_hbm, head_ref, shared_ref, x_ref = take(7)
-        ws_ref, wos_ref, pks_ref, all_ref = take(4)
-        own_ref, in_ref, state_ref, out_ref, order_ref, low_ref, w_ref, wo_ref = take(8)
+        in_hbm, state_hbm, out_hbm, order_hbm, head_ref, shared_ref, x_ref, cot_ref = take(8)
+        w_own, wo_own, ws_ref, wos_ref, pks_ref, rates_ref, first_ref, cot_own, all_ref = take(9)
+        own_ref, in_ref, state_ref, out_ref, order_ref, low_ref, w_ref, wo_ref, zero_ref = take(9)
         ag_sems = take(3)
-        load_sem, pair_send, pair_recv, pair_local = take(4)
+        load_sem, pack_send, pack_recv, swap_send, swap_recv, give_send, give_recv, local_sem = take(8)
         section = lax.axis_index("section")
-        other = 1 - section
+        micro = team.micro()
         loads = [
             pltpu.make_async_copy(src, dst, load_sem.at[k])
             for k, (src, dst) in enumerate(
@@ -734,41 +943,68 @@
         ]
         for copy in loads:
             copy.start()
-        write_pack(sz, pks_ref.at[section], head_ref, shared_ref)
-        greet_all(count, "section")
-        sent = []
-
-        def share(src, dst, k):
-            copy = pltpu.make_async_remote_copy(
-                src_ref=src,
-                dst_ref=dst,
-                send_sem=pair_send.at[k],
-                recv_sem=pair_recv.at[k],
-                device_id={"section": other},
-                device_id_type=MESH,
+        write_pack(sz, own_pack_ref := refs[0], head_ref, shared_ref)
+        rates_ref[...] = own_pack_ref[8:9, :LANES]
+        zero_ref[...] = jnp.zeros_like(zero_ref)
+        greet_all(count, True)
+        packs = [
+            Delivery(
+                own_pack_ref, pks_ref.at[section], pack_send.at[m], pack_recv.at[section], team.user(m), team.alone(m)
             )
+            for m in range(2)
+        ]
+        for copy in packs:
             copy.start()
-            return copy
-
-        pack_copy = share(pks_ref.at[section], pks_ref.at[section], 0)
-        pack_copy.wait()
-        gain = pks_ref[0, GAIN_ROW : GAIN_ROW + 1, :]
-        own_ref[...] = norm_rows(x_ref[...].astype(F32), gain).astype(BF16)
-
-        def keep(src, dst, k):
-            local = pltpu.make_async_copy(src, dst, pair_local.at[k])
-            local.start()
-            sent.extend([share(src, dst, k), local])
+        straight = micro == section
+        if team.paired:
+            head = lax.axis_index("head")
+            partner = {"section": head % 2, "head": head // 2 * 2 + section}
+            swaps = [
+                remote(x_ref.at[section], first_ref, swap_send.at[0], swap_recv.at[0], partner),
+                remote(cot_ref.at[section], cot_own, swap_send.at[1], swap_recv.at[1], partner),
+            ]
+
+            @pl.when(jnp.logical_not(straight))
+            def _():
+                for copy in swaps:
+                    copy.start()
+
+            @pl.when(straight)
+            def _():
+                first_ref[...] = x_ref[micro]
+                cot_own[...] = cot_ref[micro]
+
+        else:
+            first_ref[...] = x_ref[micro]
+            cot_own[...] = cot_ref[micro]
+
+        block, matrix, receive, blank = give_weights(
+            team, 0, w_ref, wo_ref, ws_ref, wos_ref, zero_ref, (give_send, give_recv), sz, steps, cols
+        )
+        keeps = [
+            pltpu.make_async_copy(w_ref, w_own, local_sem.at[0]),
+            pltpu.make_async_copy(wo_ref, wo_own, local_sem.at[1]),
+        ]
+
+        def lower(copies):
+            @pl.when(section == 0)
+            def _():
+                for copy in copies():
+                    copy.start()
 
         def low_out():
-            for copy in loads:
-                copy.wait()
+            loads[3].wait()
             if own_rows < sz.channels:
                 wo_ref[...] = jnp.zeros_like(wo_ref)
             wo_ref[:own_rows, :] = out_ref[...].astype(BF16)
-            keep(wo_ref, wos_ref.at[section], 1)
+            keeps[1].start()
+            lower(matrix)
 
         def low_in(step):
+            if step == 0:
+                for copy in loads[:3]:
+                    copy.wait()
+                blank(local_sem.at[2]).start()
             span = slice(step * cols, (step + 1) * cols)
             low_ref[:full, :] = in_ref[:full, 0, span].astype(BF16)
             if full < sz.master_pad:
@@ -782,23 +1018,66 @@
             col = lax.broadcasted_iota(jnp.int32, (2 * NSTATE, 2 * NSTATE), 1)
             one = (row == col).astype(BF16)
             w_ref[2 * sz.channels : sz.dt, span] = nt(one, state_ref[span, :].astype(BF16)).astype(BF16)
-            keep(w_ref.at[:, span], ws_ref.at[section, :, span], 2 + step)
-
-        work = [low_out] + [lambda step=step: low_in(step) for step in range(steps)]
-        run_gather(count, parts, own_ref, all_ref, ag_sems, None, work)
-        for copy in sent:
+            lower(lambda: block(step))
+
+        low_out()
+        ahead = 3
+        for step in range(ahead):
+            low_in(step)
+        if team.paired:
+            pl.when(jnp.logical_not(straight))(lambda: swaps[0].wait_recv())
+
+        def got_pack(layer):
+            ref = pks_ref.at[layer]
+            Delivery(ref, ref, pack_send.at[0], pack_recv.at[layer], team.owner(layer), team.alone(layer)).wait_got()
+
+        got_pack(0)
+        pl.when(team.alone(0))(lambda: packs[0].near().wait())
+        gain = pks_ref[0, GAIN_ROW : GAIN_ROW + 1, :]
+        own_ref[...] = norm_rows(first_ref[...].astype(F32), gain).astype(BF16)
+        work = [lambda step=step: low_in(step) for step in range(ahead, steps)]
+        run_gather(team, parts, own_ref, all_ref, ag_sems, None, work)
+        keeps[0].start()
+        got_pack(1)
+        if team.paired:
+
+            @pl.when(jnp.logical_not(straight))
+            def _():
+                swaps[1].wait_recv()
+                for copy in swaps:
+                    copy.wait_send()
+
+        for m, copy in enumerate(packs):
+            done = team.alone(0) if m == 0 else jnp.bool_(False)
+            pl.when(jnp.logical_not(done))(copy.wait_sent)
+        receive()
+
+        @pl.when(section == 0)
+        def _():
+            for step in range(steps):
+                for copy in block(step):
+                    copy.wait_sent()
+            for copy in matrix():
+                copy.wait_sent()
+
+        blank(local_sem.at[2]).wait()
+        for copy in keeps:
             copy.wait()
 
+    w_shape = jax.ShapeDtypeStruct((sz.cols, width), BF16)
+    wo_shape = jax.ShapeDtypeStruct((sz.channels, width), BF16)
+    row_shape = jax.ShapeDtypeStruct((rows, width), BF16)
     return pl.pallas_call(
         kernel,
         out_shape=[
-            jax.ShapeDtypeStruct((2, sz.cols, width), BF16),
-            jax.ShapeDtypeStruct((2, sz.channels, width), BF16),
+            w_shape, wo_shape, w_shape, wo_shape,
             jax.ShapeDtypeStruct((2, 16, width), F32),
+            jax.ShapeDtypeStruct((1, LANES), F32),
+            row_shape, row_shape,
             jax.ShapeDtypeStruct((count * rows, width), BF16),
         ],
-        in_specs=[ANY_SPEC] * 4 + [VMEM_SPEC] * 3,
-        out_specs=[ANY_SPEC, ANY_SPEC, VMEM_SPEC, ANY_SPEC],
+        in_specs=[ANY_SPEC] * 4 + [VMEM_SPEC] * 4,
+        out_specs=[ANY_SPEC] * 4 + [VMEM_SPEC] * 4 + [ANY_SPEC],
         scratch_shapes=[
             pltpu.VMEM((rows, width), BF16),
             pltpu.VMEM(proj_in_t.shape, F32),
@@ -808,12 +1087,15 @@
             pltpu.VMEM((sz.master_pad, cols), BF16),
             pltpu.VMEM((sz.cols, width), BF16),
             pltpu.VMEM((sz.channels, width), BF16),
+            pltpu.VMEM((LANES - 16, width), BF16),
         ]
-        + gather_scratch(parts, dims, count)
-        + [DMA((4,)), DMA((2 + steps,)), DMA((2 + steps,)), DMA((2 + steps,))],
+        + gather_scratch(parts, team.dims, count)
+        + [DMA((4,)), DMA((2,)), DMA((2,)), DMA((2,)), DMA((2,))]
+        + [DMA((3 * steps + 1, 2)), DMA((3 * steps + 1,)), DMA((3,))]
+        + [pltpu.VMEM((16, width), F32)],
         compiler_params=params(collective_id),
         name="opening",
-    )(proj_in_t, proj_state, proj_out, order, head_part, shared_part, first)
+    )(proj_in_t, proj_state, proj_out, order, head_part, shared_part, inputs, cotangent)
 
 
 def column_of(tile, rows):
@@ -907,8 +1189,13 @@
     )(*[a for pair in pairs for a in pair])
 
 
+def fits(sz):
+    return Team(sz.count).paired and sz.tokens * sz.width <= 4 << 20
+
+
 class Sizes:
-    def __init__(self, heads, tokens, width):
+    def __init__(self, count, heads, tokens, width):
+        self.count = count
         self.heads = heads
         self.padded = heads + heads % 2
         self.channels = self.padded * HDIM
@@ -1014,32 +1301,42 @@
     return nt((row == lane).astype(F32), tile, HIGH)
 
 
-def forward_phase(count, sz, layer, resets, gathered, weights, weight_out, pack, residual, live, cotangent, collective_id):
+def forward_phase(
+    count, sz, layer, lengths, gathered, weights, weight_out, pack, residual, cotangent, own, collective_id
+):
     block, chunk, chans = STRETCH, CHUNK, sz.channels
-    dims = chip_dims(count)
+    team = Team(count)
+    dims = team.dims
     rows, width = residual.shape
     subs = block // chunk
     shards = block // rows
     blocks = sz.blocks
     planes = dims[0]
     per = blocks // planes
-    parts = column_parts(width, GATHER)
-    scatter = PlaneScatter(dims, rows, width)
+    parts = column_parts(width, TEAM_GATHER if team.paired else GATHER)
+    scatter = PlaneScatter(team, rows, width)
     turn = cotangent is not None
+    passing = own is not None
+    cols = 256
+    steps = width // cols
 
     def kernel(*refs):
         refs = list(refs)
         take = lambda number: [refs.pop(0) for _ in range(number)]
-        reset_ref, rows_ref, ws_ref, wos_ref, pks_ref, u_ref, live_ref = take(7)
+        reset_ref, rows_ref, ws_ref, wos_ref, pks_ref, u_ref = take(6)
         cot_ref = refs.pop(0) if turn else None
+        w_own, wo_own = take(2) if passing else (None, None)
         result_ref, branch_ref, total_ref, next_ref, p_out, y_out, s_out = take(7)
         stats_ref = refs.pop(0) if turn else None
+        ws_next, wos_next = take(2) if passing else (None, None)
         conv_ref, state_ref, w_ref, wo_ref, h_buf, p_buf, y_buf, s_buf, part_ref, sq_ref = take(10)
         load_sem, store_sem, weight_sem = take(3)
         sums_ref, own_ref = take(2)
-        scatter_refs = take(3)
+        scatter_refs = take(5)
         ag_sems = take(3)
         small_send, small_recv = take(2)
+        if passing:
+            w_mine, wo_mine, zero_ref, own_sem, give_send, give_recv = take(6)
         pk_ref = pks_ref.at[layer]
 
         def load(c):
@@ -1057,12 +1354,37 @@
 
         load(0).start()
         weight_copies = [
-            pltpu.make_async_copy(ws_ref.at[layer], w_ref, weight_sem.at[0]),
-            pltpu.make_async_copy(wos_ref.at[layer], wo_ref, weight_sem.at[1]),
+            pltpu.make_async_copy(ws_ref, w_ref, weight_sem.at[0]),
+            pltpu.make_async_copy(wos_ref, wo_ref, weight_sem.at[1]),
         ]
         for copy in weight_copies:
             copy.start()
-        greet_all(count)
+        if passing:
+            section = lax.axis_index("section")
+            own_copies = [
+                pltpu.make_async_copy(w_own, w_mine, own_sem.at[0]),
+                pltpu.make_async_copy(wo_own, wo_mine, own_sem.at[1]),
+            ]
+            for copy in own_copies:
+                copy.start()
+            zero_ref[...] = jnp.zeros_like(zero_ref)
+            give_block, give_matrix, receive, blank = give_weights(
+                team, 1, w_mine, wo_mine, ws_next, wos_next, zero_ref, (give_send, give_recv), sz, steps, cols
+            )
+            blank(own_sem.at[2]).start()
+        greet_all(count, True)
+        if passing:
+            for copy in own_copies:
+                copy.wait()
+
+            @pl.when(section == 1)
+            def _():
+                for step in range(steps):
+                    for copy in give_block(step):
+                        copy.start()
+                for copy in give_matrix():
+                    copy.start()
+
         conv_ref[...] = jnp.zeros_like(conv_ref)
         state_ref[...] = jnp.zeros_like(state_ref)
         scatter.bind(part_ref, branch_ref, *scatter_refs)
@@ -1071,7 +1393,7 @@
 
         def one_block(c, carry):
             slot = c % 2
-            keep = 1.0 - reset_ref[c]
+            keep = keeps(reset_ref, team.micro(), c)
             span_all = pl.ds(pl.multiple_of(c * block, block), block)
             pl.when(c + 1 < blocks)(lambda: load(c + 1).start())
             load(c).wait()
@@ -1132,7 +1454,7 @@
             for k in range(shards):
                 sq_ref[c * shards + k] = square[:, k * rows : (k + 1) * rows]
             high, low = split(gated * pk_ref[5:6, :chans])
-            part_ref[span_all, :] = (nn(high, wo_ref[...]) + nn(low, wo_ref[...])).astype(BF16)
+            part_ref[span_all, :] = (nn(high, wo_ref[...]) + nn(low, wo_ref[...])).astype(part_ref.dtype)
             for copy in stores(c):
                 copy.start()
             if per == 1:
@@ -1142,17 +1464,17 @@
             return carry
 
         lax.fori_loop(0, blocks, one_block, 0)
-        me = lax.axis_index("head")
-        copies = start_direct(count, lambda peer: sq_ref.at[peer], sums_ref, small_send, small_recv)
+        me = linear(dims, team.spot())
+        copies = start_direct(team, lambda peer: sq_ref.at[peer], sums_ref, small_send, small_recv)
         sums_ref[me] = sq_ref[me]
         scatter.finish(planes, lambda k: k)
-        wait_direct(count, sums_ref, copies, small_recv, small_send)
+        wait_direct(team, sums_ref, copies, small_recv, small_send)
         total = jnp.sum(sums_ref[...], axis=0)
         total_ref[...] = total
         scale = lax.rsqrt(column_of(total, rows) / (HEADS * HDIM) + EPS_NORM)
         branch = branch_ref[...] * scale
         branch_ref[...] = branch
-        live_col = live_ref[:, 0:1]
+        live_col = live_rows_of(reset_ref, team.micro(), me, rows)
         result = (u_ref[...].astype(F32) + live_col * branch).astype(BF16)
         result_ref[...] = result
         stat = None
@@ -1165,11 +1487,23 @@
         else:
             gain = pks_ref[layer + 1, GAIN_ROW : GAIN_ROW + 1, :]
             own_ref[...] = norm_rows(result.astype(F32), gain).astype(BF16)
-        run_gather(count, parts, own_ref, next_ref, ag_sems, stat)
+        run_gather(team, parts, own_ref, next_ref, ag_sems, stat)
         for c in range(max(blocks - 2, 0), blocks):
             for copy in stores(c):
                 copy.wait()
         scatter.drain()
+        if passing:
+            receive()
+
+            @pl.when(section == 1)
+            def _():
+                for step in range(steps):
+                    for copy in give_block(step):
+                        copy.wait_sent()
+                for copy in give_matrix():
+                    copy.wait_sent()
+
+            blank(own_sem.at[2]).wait()
 
     tokens = sz.tokens
     out_shape = [
@@ -1191,7 +1525,7 @@
         pltpu.VMEM((2, block, sz.cols), F32),
         pltpu.VMEM((2, block, chans), F32),
         pltpu.VMEM((2, subs, NSTATE, chans), F32),
-        pltpu.VMEM((tokens, width), BF16),
+        pltpu.VMEM((tokens, width), scatter.first_type),
         pltpu.VMEM((count, 8, rows), F32),
         DMA((2,)),
         DMA((3, 2)),
@@ -1200,14 +1534,22 @@
         pltpu.VMEM((rows, width), BF16),
     ]
     scratch += scatter.scratch() + gather_scratch(parts, dims, count) + [DMA((count,))] * 2
-    operands = [resets, gathered, weights, weight_out, pack, residual, live]
-    in_specs = [pl.BlockSpec(memory_space=pltpu.SMEM)] + [ANY_SPEC] * 3 + [VMEM_SPEC] * 3
+    operands = [lengths, gathered, weights, weight_out, pack, residual]
+    in_specs = [pl.BlockSpec(memory_space=pltpu.SMEM)] + [ANY_SPEC] * 3 + [VMEM_SPEC] * 2
     if turn:
         out_shape.append(jax.ShapeDtypeStruct((count, 8, LANES), F32))
         out_specs.append(VMEM_SPEC)
         scratch += [pltpu.VMEM((8, LANES), F32)] + [DMA((count,))] * 2
         operands.append(cotangent)
         in_specs.append(VMEM_SPEC)
+    if passing:
+        out_shape += [jax.ShapeDtypeStruct(array.shape, array.dtype) for array in own]
+        out_specs += [ANY_SPEC] * 2
+        scratch += [pltpu.VMEM(array.shape, array.dtype) for array in own]
+        scratch += [pltpu.VMEM((LANES - 16, width), BF16), DMA((3,))]
+        scratch += [DMA((3 * steps + 1, 2)), DMA((3 * steps + 1,))]
+        operands += list(own)
+        in_specs += [ANY_SPEC] * 2
     return pl.pallas_call(
         kernel,
         out_shape=out_shape,
@@ -1220,20 +1562,22 @@
 
 
 def backward_phase(
-    count, sz, layer, resets, out_grads, proj, mixed, states, stats, weights, weight_out, pack, order,
-    residual, upstream, live, below, upper, collective_id,
+    count, sz, layer, lengths, out_grads, proj, mixed, states, stats, weights, weight_out, pack, order,
+    residual, upstream, below, gathered, upper, collective_id,
 ):
     block, chunk, chans = STRETCH, CHUNK, sz.channels
-    dims = chip_dims(count)
+    team = Team(count)
+    dims = team.dims
     rows, width = residual.shape
     subs = block // chunk
     blocks = sz.blocks
     planes = dims[0]
     per = blocks // planes
-    parts = column_parts(width, GATHER)
-    scatter = PlaneScatter(dims, rows, width)
+    parts = column_parts(width, TEAM_GATHER if team.paired else GATHER)
+    scatter = PlaneScatter(team, rows, width)
     more = below is not None
     close = upper is not None
+    early = more and fits(sz)
     cols = 256
     steps = width // cols
 
@@ -1241,13 +1585,16 @@
         refs = list(refs)
         take = lambda number: [refs.pop(0) for _ in range(number)]
         reset_ref, g_all, p_all, y_all, s_all, ws_ref, wos_ref, orders_ref = take(8)
-        st_ref, pks_ref, sum_ref, u_ref, up_ref, live_ref = take(6)
+        st_ref, pks_ref, sum_ref, u_ref, up_ref = take(5)
         if more:
             lower_ref, lower_total = take(2)
         if close:
-            gt_upper, q_upper, h_upper, g_upper, h_own = take(5)
-            acc_upper, result_own, result_upper, grad_upper = take(4)
-            sum_in, sum_out, sum_state, sum_small, outs_ref, grads_ref, squares_ref = take(7)
+            h_own, in_upper, out_upper, acc_upper, result_own, result_upper, grad_upper = take(7)
+            state_upper, rates_ref = take(2)
+            sum_in, sum_out, state_all, sum_small, outs_ref, grads_ref, stats_ref, norm_ref = take(8)
+        elif early:
+            h_own = refs.pop(0)
+            grad_ref, low_grad_ref, acc_ref, in_out, out_out, state_out = take(6)
         else:
             grad_ref, low_grad_ref, acc_ref, gt_out, q_out = take(5)
         if more:
@@ -1255,26 +1602,33 @@
         conv_ref, dpre_ref, dact_ref, ddt_ref, dstate_ref = take(5)
         w_ref, wo_ref, order_ref, g_buf, p_buf, halo_buf, y_buf, s_buf, gt_buf, q_buf, part_ref = take(11)
         load_sem, store_sem, weight_sem = take(3)
-        scatter_refs = take(3)
+        scatter_refs = take(5)
         pk_ref = pks_ref.at[layer]
+        if close or early:
+            gt_full, q_full, h_cols, g_cols, col_sem = take(5)
         if close:
-            grad_ref, acc_ref, gt_full, q_full, gt_one, q_one, h_cols, g_cols = take(8)
-            send_state, box_in, box_out, box_state, box_small, state_own = take(6)
-            send_in, send_out = w_ref.at[: sz.master_pad, :], wo_ref
-            col_sem, whole_sem, trade_send, trade_recv, few_send, few_recv = take(6)
+            grad_ref, acc_ref, box_in, box_out, box_small = take(5)
+            in_out, out_out = w_ref.at[: sz.master_pad, :], wo_ref
+            live_rows = pl.ds(0, -(-sz.master // 16) * 16)
+            trade_send, trade_recv, few_send, few_recv = take(4)
+            in_buf, out_buf, keep_sem = take(3)
+            state_out, squares_ref, state_sums, state_box, pieces_ref, state_own = take(6)
+            share_ref, shares_ref, stat_ref, mine_ref, got_ref = take(5)
+            state_send, state_recv, piece_send, piece_recv = take(4)
+            head_sems = take(3)
+            share_send, share_recv, stat_send, stat_recv, pair_send, pair_recv = take(6)
             section = lax.axis_index("section")
-            other = 1 - section
-            whole = [
-                pltpu.make_async_copy(gt_upper, gt_one, whole_sem.at[0]),
-                pltpu.make_async_copy(q_upper, q_one, whole_sem.at[1]),
-            ]
+            micro = team.micro()
+
+        def g_slot(slot):
+            return g_buf.at[pl.ds(pl.multiple_of(slot * block, block), block), :]
 
         def loads(c):
             slot = c % 2
             span = pl.ds(pl.multiple_of(c * block, block), block)
             before = pl.multiple_of(jnp.maximum(c * block - 8, 0), 8)
             return [
-                pltpu.make_async_copy(g_all.at[span, :], g_buf.at[slot], load_sem.at[0, slot]),
+                pltpu.make_async_copy(g_all.at[span, :], g_slot(slot), load_sem.at[0, slot]),
                 pltpu.make_async_copy(p_all.at[span, :], p_buf.at[slot], load_sem.at[1, slot]),
                 pltpu.make_async_copy(p_all.at[pl.ds(before, 8), :], halo_buf.at[slot], load_sem.at[2, slot]),
                 pltpu.make_async_copy(y_all.at[span, :], y_buf.at[slot], load_sem.at[3, slot]),
@@ -1284,7 +1638,7 @@
         def stores(c):
             slot = c % 2
             span = pl.ds(pl.multiple_of(c * block, block), block)
-            if close:
+            if close or early:
                 return []
             return [
                 pltpu.make_async_copy(gt_buf.at[slot], gt_out.at[:, span], store_sem.at[0, slot]),
@@ -1294,18 +1648,13 @@
         for copy in loads(blocks - 1):
             copy.start()
         weight_copies = [
-            pltpu.make_async_copy(wos_ref.at[layer], wo_ref, weight_sem.at[0]),
-            pltpu.make_async_copy(ws_ref.at[layer], w_ref, weight_sem.at[1]),
+            pltpu.make_async_copy(wos_ref, wo_ref, weight_sem.at[0]),
+            pltpu.make_async_copy(ws_ref, w_ref, weight_sem.at[1]),
             pltpu.make_async_copy(orders_ref, order_ref, weight_sem.at[2]),
         ]
         for copy in weight_copies:
             copy.start()
-        if close:
-            for copy in whole:
-                copy.start()
-            greet_all(count, "section")
-        else:
-            greet_all(count)
+        greet_all(count, True)
         dpre_ref[...] = jnp.zeros_like(dpre_ref)
         dstate_ref[...] = jnp.zeros_like(dstate_ref)
         acc_ref[...] = jnp.zeros_like(acc_ref)
@@ -1316,8 +1665,8 @@
         def one_block(i, carry):
             c = blocks - 1 - i
             slot = c % 2
-            keep = 1.0 - reset_ref[c]
-            after = 1.0 - reset_ref[jnp.minimum(c + 1, blocks - 1)]
+            keep = keeps(reset_ref, team.micro(), c)
+            after = keeps(reset_ref, team.micro(), jnp.minimum(c + 1, blocks - 1))
             span_all = pl.ds(pl.multiple_of(c * block, block), block)
 
             @pl.when(c >= 1)
@@ -1328,16 +1677,16 @@
             for copy in loads(c):
                 copy.wait()
 
-            if not close:
+            if not (close or early):
+
                 @pl.when(i >= 2)
                 def _():
                     for copy in stores(c + 2):
                         copy.wait()
 
-            g_ref, p_ref, halo_ref, y_ref, s_ref = (
-                buf.at[slot] for buf in (g_buf, p_buf, halo_buf, y_buf, s_buf)
-            )
-            if close:
+            g_ref = g_slot(slot)
+            p_ref, halo_ref, y_ref, s_ref = (buf.at[slot] for buf in (p_buf, halo_buf, y_buf, s_buf))
+            if close or early:
                 gt_ref, q_ref = gt_full.at[:, span_all], q_full.at[span_all, :]
             else:
                 gt_ref, q_ref = gt_buf.at[slot], q_buf.at[slot]
@@ -1453,7 +1802,7 @@
             low = jnp.concatenate(
                 [dz.astype(BF16), draw.astype(BF16), ddt_raw.astype(BF16)], axis=1
             )
-            part_ref[span_all, :] = nn(low, w_ref[...]).astype(BF16)
+            part_ref[span_all, :] = nn(low, w_ref[...]).astype(part_ref.dtype)
             gt_ref[...] = nt(order_ref[...], low).astype(BF16)
             for copy in stores(c):
                 copy.start()
@@ -1473,147 +1822,240 @@
             acc_ref[GAIN_ROW : GAIN_ROW + 1, :] = gain_grad
             return grad
 
+        def at(j):
+            return pl.ds(pl.multiple_of(j * cols, cols), cols)
+
+        def columns(j):
+            slot = j % 2
+            return [
+                pltpu.make_async_copy(h_own.at[:, at(j)], h_cols.at[slot], col_sem.at[0, slot]),
+                pltpu.make_async_copy(g_all.at[:, at(j)], g_cols.at[slot], col_sem.at[1, slot]),
+            ]
+
+        def weight_step(j, then=None):
+            slot = j % 2
+            for copy in columns(j):
+                copy.wait()
+
+            @pl.when(j + 1 < steps)
+            def _():
+                for copy in columns(j + 1):
+                    copy.start()
+
+            in_out[:, at(j)] = nn(gt_full[: sz.master_pad, :], h_cols[slot]).astype(BF16)
+            out_out[:, at(j)] = tn(q_full[...], g_cols[slot]).astype(BF16)
+            if then is not None:
+                then(j)
+            state_out[:, at(j)] = nn(gt_full[sz.master_pad :, :], h_cols[slot]).astype(BF16)
+
+        if close:
+            def trade(layer, j):
+                ins, outs = (in_upper, out_upper) if layer else (in_out, out_out)
+                sets = ((ins, box_in, live_rows), (outs, box_out, slice(None)))
+                return [
+                    Delivery(
+                        src.at[cut, at(j)], dst.at[micro, cut, at(j)],
+                        trade_send.at[k, layer, j], trade_recv.at[k, micro, j],
+                        team.owner(layer), team.alone(layer),
+                    )
+                    for k, (src, dst, cut) in enumerate(sets)
+                ]
+
+            def each(action):
+                def body(j, carry):
+                    action(j)
+                    return carry
+
+                lax.fori_loop(0, steps, body, 0)
+
+            def begin(layer):
+                def action(j):
+                    for copy in trade(layer, j):
+                        copy.start()
+
+                return action
+
+            each(begin(1))
+            few = {}
+            for layer_now, sources in (
+                (0, (acc_ref, result_own, grad_ref)), (1, (acc_upper, result_upper, grad_upper))
+            ):
+                for k, (src, dst) in enumerate(zip(sources, (box_small, outs_ref, grads_ref))):
+                    few[layer_now, k] = Delivery(
+                        src, dst.at[micro], few_send.at[k, layer_now], few_recv.at[k, micro],
+                        team.owner(layer_now), team.alone(layer_now),
+                    )
+            late = ((0, 0), (0, 2))
+            for key, copy in few.items():
+                if key not in late:
+                    copy.start()
+
         lax.fori_loop(0, blocks, one_block, 0)
         if not close:
+            if early:
+                for copy in columns(0):
+                    copy.start()
             scatter.finish(planes, lambda k: planes - 1 - k)
             grad = input_grads()
             low_grad_ref[...] = grad.astype(BF16)
             if more:
                 own_ref, stat_ref, stat_send, stat_recv = take(4)
-                out_grad = (live_ref[:, 0:1] * grad.astype(BF16).astype(F32)).astype(BF16)
+                out_grad = (live_rows_of(reset_ref, team.micro(), linear(dims, team.spot()), rows) * grad.astype(BF16).astype(F32)).astype(BF16)
                 own_ref[...] = out_grad
                 write_stats(stat_ref, lower_total[...], out_grad.astype(F32), lower_ref[...], rows)
-                run_gather(count, parts, own_ref, next_ref, refs, (stat_ref, stats_ref, stat_send, stat_recv))
-            for c in range(0, min(2, blocks)):
-                for copy in stores(c):
-                    copy.wait()
+                work = [lambda j=j: weight_step(j) for j in range(steps)] if early else []
+                run_gather(team, parts, own_ref, next_ref, refs, (stat_ref, stats_ref, stat_send, stat_recv), work)
+            if not early:
+                for c in range(0, min(2, blocks)):
+                    for copy in stores(c):
+                        copy.wait()
             scatter.drain()
             return
 
-        def at(j):
-            return pl.ds(pl.multiple_of(j * cols, cols), cols)
-
-        def columns(which, j):
-            slot = j % 2
-            h_all, g_from = (h_upper, g_upper) if which else (h_own, g_all)
-            return [
-                pltpu.make_async_copy(h_all.at[:, at(j)], h_cols.at[slot], col_sem.at[0, slot]),
-                pltpu.make_async_copy(g_from.at[:, at(j)], g_cols.at[slot], col_sem.at[1, slot]),
-            ]
-
-        def passed(src, dst, send_sem, recv_sem):
-            return pltpu.make_async_remote_copy(
-                src_ref=src, dst_ref=dst, send_sem=send_sem, recv_sem=recv_sem,
-                device_id={"section": other}, device_id_type=MESH,
-            )
-
-        def traded(j):
-            sets = ((send_in, box_in), (send_out, box_out), (send_state, box_state))
-            return [
-                passed(src.at[:, at(j)], dst.at[:, at(j)], trade_send.at[k, j], trade_recv.at[k, j])
-                for k, (src, dst) in enumerate(sets)
-            ]
-
-        def weight_steps(which, begin, end):
-            gt, q = (gt_one, q_one) if which else (gt_full, q_full)
-
+        def made(begin_at, end_at):
             def body(j, carry):
-                slot = j % 2
-                for copy in columns(which, j):
-                    copy.wait()
-
-                @pl.when(j + 1 < steps)
-                def _():
-                    for copy in columns(which, j + 1):
-                        copy.start()
-
-                in_grad = nn(gt[: sz.master_pad, :], h_cols[slot])
-                state_grad = nn(gt[sz.master_pad :, :], h_cols[slot])
-                out_grad = tn(q[...], g_cols[slot])
-
-                @pl.when(section == which)
-                def _():
-                    sum_in[:, at(j)] = in_grad
-                    sum_out[:, at(j)] = out_grad
-                    state_own[:, at(j)] = state_grad
-
-                @pl.when(section != which)
-                def _():
-                    send_in[:, at(j)] = in_grad.astype(BF16)
-                    send_out[:, at(j)] = out_grad.astype(BF16)
-                    send_state[:, at(j)] = state_grad
-                    for copy in traded(j):
-                        copy.start()
-
+                weight_step(j, begin(0))
                 return carry
 
-            lax.fori_loop(begin, end, body, 0)
-
-        def begin_columns(which):
-            for copy in columns(which, 0):
-                copy.start()
-
-        begin_columns(1)
-        for copy in whole:
-            copy.wait()
-        weight_steps(1, 0, steps // 4)
-        scatter.step(planes, planes + 1, lambda k: planes - 1 - k)
-        weight_steps(1, steps // 4, steps // 2)
-        scatter.step(planes, planes + 2, lambda k: planes - 1 - k)
-        weight_steps(1, steps // 2, steps)
-        begin_columns(0)
-        weight_steps(0, 0, steps // 4)
+            lax.fori_loop(begin_at, end_at, body, 0)
+
+        for copy in columns(0):
+            copy.start()
+        order_of = lambda k: planes - 1 - k
+        stops = scatter.extra_steps()
+        for extra in range(1, stops + 1):
+            scatter.step(planes, planes + extra, order_of)
+            made(steps * (extra - 1) // stops, steps * extra // stops)
+        squares_ref[...] = jnp.zeros_like(squares_ref)
+        each_rows = 16
+        for k in range(count):
+            for layer_now, ref in enumerate((state_out, state_upper)):
+                to = (2 * k + layer_now) * each_rows
+                g_buf[to : to + each_rows, :] = ref[k * each_rows : (k + 1) * each_rows, :]
+        state_sends, stages = scatter_steps(
+            team, column_parts(width, TEAM_SCATTER_SMALL), 2 * each_rows, g_buf, state_sums, state_box,
+            state_send, state_recv, True,
+        )
+        stages[0]()
         scatter.last()
         input_grads()
-        few = [(acc_ref, acc_upper, box_small), (result_own, result_upper, outs_ref.at[section])]
-        few.append((grad_ref, grad_upper, grads_ref.at[section]))
-
-        def few_copies(theirs):
+        for key in late:
+            few[key].start()
+        for stage in stages[1:]:
+            stage()
+        passed = [
+            Delivery(
+                state_sums.at[pl.ds(layer_now * each_rows, each_rows), :], pieces_ref.at[micro],
+                piece_send.at[layer_now], piece_recv.at[micro], team.owner(layer_now), team.alone(layer_now),
+            )
+            for layer_now in range(2)
+        ]
+        for copy in passed:
+            copy.start()
+
+        def sent(layer):
+            def action(j):
+                for copy in trade(layer, j):
+                    copy.wait_sent()
+
+            return action
+
+        for copy in few.values():
+            copy.wait_sent()
+        for copy in passed:
+            copy.wait_sent()
+
+        def got(src, sem, m):
+            Delivery(src, src, trade_send.at[0, 0, 0], sem, team.user(m), team.alone(m)).wait_got()
+
+        for m in range(2):
+            for k, box in enumerate((box_small, outs_ref, grads_ref)):
+                got(box.at[m], few_recv.at[k, m], m)
+        sum_small[...] = box_small[0] + box_small[1]
+        heads = Heads(count)
+        pieces = width // LANES
+        me = lax.axis_index("head")
+        share_ref[...] = jnp.zeros_like(share_ref)
+        share_ref[0:1, :] = sum_small[GAIN_ROW : GAIN_ROW + 1, :]
+        share_ref[1 : CONV + 2, : 2 * NSTATE] = sum_small[: CONV + 1, chans : sz.conv]
+
+        def piece(peer):
+            return share_ref.at[:, pl.ds(pl.multiple_of((peer % pieces) * LANES, LANES), LANES)]
+
+        shares = start_direct(heads, piece, shares_ref, share_send, share_recv)
+        shares_ref[me] = piece(me)[...]
+        for m in range(2):
+            got(pieces_ref.at[m], piece_recv.at[m], m)
+        state_total = pieces_ref[0] + pieces_ref[1]
+        state_own[...] = state_total.astype(BF16)
+        def kept(j):
+            slot = j % 2
             return [
-                passed(entry[theirs], entry[2], few_send.at[k], few_recv.at[k]) for k, entry in enumerate(few)
+                pltpu.make_async_copy(in_buf.at[slot, live_rows, :], sum_in.at[live_rows, at(j)], keep_sem.at[0, slot]),
+                pltpu.make_async_copy(out_buf.at[slot], sum_out.at[:, at(j)], keep_sem.at[1, slot]),
             ]
 
-        @pl.when(section == 0)
-        def _():
-            for copy in few_copies(1):
-                copy.start()
-            outs_ref[0] = result_own[...]
-            grads_ref[0] = grad_ref[...]
-
-        @pl.when(section == 1)
-        def _():
-            for copy in few_copies(0):
-                copy.start()
-            outs_ref[1] = result_upper[...]
-            grads_ref[1] = grad_upper[...]
-
-        weight_steps(0, steps // 4, steps)
-        squares_ref[...] = jnp.zeros_like(squares_ref)
-
-        def add_up(j, carry):
-            for copy in traded(j):
-                copy.wait_recv()
-            total = sum_in[:, at(j)] + box_in[:, at(j)].astype(F32)
-            sum_in[:, at(j)] = total
-            squares_ref[0:1, at(j)] += jnp.sum(total * total, axis=0, keepdims=True)
-            total = sum_out[:, at(j)] + box_out[:, at(j)].astype(F32)
-            sum_out[:, at(j)] = total
-            squares_ref[1:2, at(j)] += jnp.sum(total * total, axis=0, keepdims=True)
-            sum_state[:, at(j)] = (state_own[:, at(j)] + box_state[:, at(j)]).astype(BF16)
-            return carry
-
-        lax.fori_loop(0, steps, add_up, 0)
-        for copy in few_copies(0):
-            copy.wait_recv()
-        sum_small[...] = jnp.where(section == 0, acc_ref[...], acc_upper[...]) + box_small[...]
-
-        def settle(j, carry):
-            for copy in traded(j):
-                copy.wait_send()
-            return carry
-
-        lax.fori_loop(0, steps, settle, 0)
-        for copy in few_copies(0):
+        stat_copies = []
+
+        def begin_norm():
+            each(sent(1))
+            each(sent(0))
+
+            def add_up(j, carry):
+                @pl.when(j >= 2)
+                def _():
+                    for copy in kept(j - 2):
+                        copy.wait()
+
+                for k, (box, total_ref) in enumerate(((box_in, in_buf), (box_out, out_buf))):
+                    for m in range(2):
+                        cut = slice(None) if k else live_rows
+                        got(box.at[m, cut, at(j)], trade_recv.at[k, m, j], m)
+                    count_rows = chans if k else -(-sz.master // 16) * 16
+                    total = box[0, :count_rows, at(j)].astype(F32) + box[1, :count_rows, at(j)].astype(F32)
+                    total_ref[j % 2, :count_rows, :] = total
+                    squares_ref[k : k + 1, at(j)] += jnp.sum(total * total, axis=0, keepdims=True)
+                for copy in kept(j):
+                    copy.start()
+                return carry
+
+            lax.fori_loop(0, steps, add_up, 0)
+            wait_direct(heads, shares_ref, shares, share_recv, share_send)
+            shared = jnp.sum(shares_ref[...], axis=0)
+            taps = sum_small[: CONV + 2, : sz.heads * HDIM]
+            skip_sums = nn(sum_small[6:7, :chans], sum_ref[...], HIGH)
+            bias = sum_small[7:8, :LANES]
+            rate = sum_small[8:9, :LANES] * rates_ref[...]
+            lane = lax.broadcasted_iota(jnp.int32, (1, LANES), 1)
+            of_heads = jnp.where(lane < sz.heads, bias * bias + rate * rate + skip_sums * skip_sums, 0.0)
+            total = jnp.sum(squares_ref[...]) + jnp.sum(taps * taps) + jnp.sum(of_heads)
+            total = total + jnp.sum(state_total * state_total)
+            total = total + jnp.where(me < pieces, jnp.sum(shared * shared), 0.0)
+            row = lax.broadcasted_iota(jnp.int32, (8, LANES), 0)
+            stat_ref[...] = jnp.where(row == 7, total, shared)
+            stat_copies.extend(start_direct(heads, lambda peer: stat_ref, stats_ref, stat_send, stat_recv))
+            stats_ref[me] = stat_ref[...]
+
+        run_gather(
+            heads, column_parts(width, GATHER_SMALL), state_own, state_all, head_sems, None,
+            [lambda: None] * 4 + [begin_norm],
+        )
+        wait_direct(heads, stats_ref, stat_copies, stat_recv, stat_send)
+        row = lax.broadcasted_iota(jnp.int32, (8, LANES), 0)
+        section_sq = stats_ref[0, 7:8, :]
+        for k in range(1, count):
+            section_sq = section_sq + stats_ref[k, 7:8, :]
+        mine_ref[...] = jnp.broadcast_to(section_sq, (8, LANES))
+        pair = remote(mine_ref, got_ref, pair_send, pair_recv, {"section": 1 - section})
+        pair.start()
+        pair.wait()
+        norm = jnp.sqrt(mine_ref[...] + got_ref[...])
+        threshold = CLIP_COEF * PARAMS**0.5
+        norm_ref[...] = jnp.where(row == 0, norm, threshold / jnp.maximum(norm, threshold))
+        for j in range(max(steps - 2, 0), steps):
+            for copy in kept(j):
+                copy.wait()
+        for copy in state_sends:
             copy.wait_send()
         scatter.drain()
 
@@ -1627,9 +2069,20 @@
             jax.ShapeDtypeStruct((16, width), F32),
             jax.ShapeDtypeStruct((2, rows, width), BF16),
             jax.ShapeDtypeStruct((2, rows, width), F32),
-            jax.ShapeDtypeStruct((8, width), F32),
+            jax.ShapeDtypeStruct((count, 8, LANES), F32),
+            jax.ShapeDtypeStruct((8, LANES), F32),
         ]
-        out_specs = [VMEM_SPEC] * 7
+        out_specs = [ANY_SPEC] * 3 + [VMEM_SPEC] * 5
+    elif early:
+        out_shape = [
+            jax.ShapeDtypeStruct((rows, width), F32),
+            jax.ShapeDtypeStruct((rows, width), BF16),
+            jax.ShapeDtypeStruct((16, width), F32),
+            jax.ShapeDtypeStruct((sz.master_pad, width), BF16),
+            jax.ShapeDtypeStruct((chans, width), BF16),
+            jax.ShapeDtypeStruct((state, width), BF16),
+        ]
+        out_specs = [VMEM_SPEC] * 6
     else:
         out_shape = [
             jax.ShapeDtypeStruct((rows, width), F32),
@@ -1648,42 +2101,57 @@
         pltpu.VMEM((sz.cols, width), BF16),
         pltpu.VMEM((chans, width), BF16),
         pltpu.VMEM((sz.grad_rows, sz.cols), BF16),
-        pltpu.VMEM((2, block, width), BF16),
+        pltpu.VMEM((max(2 * block, 2 * 16 * count) if close else 2 * block, width), BF16),
         pltpu.VMEM((2, block, sz.cols), F32),
         pltpu.VMEM((2, 8, sz.cols), F32),
         pltpu.VMEM((2, block, chans), F32),
         pltpu.VMEM((2, subs, NSTATE, chans), F32),
-        pltpu.VMEM((8, LANES) if close else (2, sz.grad_rows, block), BF16),
-        pltpu.VMEM((8, LANES) if close else (2, block, chans), BF16),
-        pltpu.VMEM((tokens, width), BF16),
+        pltpu.VMEM((8, LANES) if close or early else (2, sz.grad_rows, block), BF16),
+        pltpu.VMEM((8, LANES) if close or early else (2, block, chans), BF16),
+        pltpu.VMEM((tokens, width), scatter.first_type),
         DMA((5, 2)),
         DMA((2, 2)),
         DMA((3,)),
     ]
     scratch += scatter.scratch()
+    if close or early:
+        scratch += [
+            pltpu.VMEM((sz.grad_rows, tokens), BF16),
+            pltpu.VMEM((tokens, chans), BF16),
+            pltpu.VMEM((2, tokens, cols), BF16),
+            pltpu.VMEM((2, tokens, cols), BF16),
+            DMA((2, 2)),
+        ]
     if close:
         scratch += [
             pltpu.VMEM((rows, width), F32),
             pltpu.VMEM((16, width), F32),
-            pltpu.VMEM((sz.grad_rows, tokens), BF16),
-            pltpu.VMEM((tokens, chans), BF16),
-            pltpu.VMEM((sz.grad_rows, tokens), BF16),
-            pltpu.VMEM((tokens, chans), BF16),
-            pltpu.VMEM((2, tokens, cols), BF16),
-            pltpu.VMEM((2, tokens, cols), BF16),
+            pltpu.VMEM((2, sz.master_pad, width), BF16),
+            pltpu.VMEM((2, chans, width), BF16),
+            pltpu.VMEM((2, 16, width), F32),
+            DMA((2, 2, steps)),
+            DMA((2, 2, steps)),
+            DMA((3, 2)),
+            DMA((3, 2)),
+            pltpu.VMEM((2, sz.master_pad, cols), F32),
+            pltpu.VMEM((2, chans, cols), F32),
+            DMA((2, 2)),
+            pltpu.VMEM((state, width), BF16),
+            pltpu.VMEM((8, width), F32),
+            pltpu.VMEM((32, width), F32),
+            pltpu.VMEM((count - 1, 32, width), BF16),
+            pltpu.VMEM((2, 16, width), F32),
+            pltpu.VMEM((16, width), BF16),
+            pltpu.VMEM((8, width), F32),
+            pltpu.VMEM((count, 8, LANES), F32),
         ]
-        scratch += [
-            pltpu.VMEM((state, width), F32),
-            pltpu.VMEM((sz.master_pad, width), BF16),
-            pltpu.VMEM((chans, width), BF16),
-            pltpu.VMEM((state, width), F32),
-            pltpu.VMEM((16, width), F32),
-            pltpu.VMEM((state, width), F32),
-        ]
-        scratch += [DMA((2, 2)), DMA((2,)), DMA((3, steps)), DMA((3, steps)), DMA((3,)), DMA((3,))]
-    operands = [resets, out_grads, proj, mixed, states, weights, weight_out, order]
-    in_specs = [pl.BlockSpec(memory_space=pltpu.SMEM)] + [ANY_SPEC] * 7 + [VMEM_SPEC] * 6
-    operands += [stats, pack, sz.head_sum(), residual, upstream, live]
+        scratch += [pltpu.VMEM((8, LANES), F32)] * 3
+        scratch += [DMA((1, count - 1)), DMA((1, count - 1)), DMA((2,)), DMA((2,))]
+        scratch += gather_scratch(column_parts(width, GATHER_SMALL), Heads(count).dims, count)
+        scratch += [DMA((count,))] * 4 + [DMA, DMA]
+    operands = [lengths, out_grads, proj, mixed, states, weights, weight_out, order]
+    in_specs = [pl.BlockSpec(memory_space=pltpu.SMEM)] + [ANY_SPEC] * 7 + [VMEM_SPEC] * 5
+    operands += [stats, pack, sz.head_sum(), residual, upstream]
     if more:
         out_shape += [
             jax.ShapeDtypeStruct((tokens, width), BF16),
@@ -1696,7 +2164,10 @@
         in_specs += [VMEM_SPEC] * 2
     if close:
         operands += list(upper)
-        in_specs += [ANY_SPEC] * 5 + [VMEM_SPEC] * 4
+        in_specs += [ANY_SPEC] * 3 + [VMEM_SPEC] * 6
+    elif early:
+        operands.append(gathered)
+        in_specs.append(ANY_SPEC)
     return pl.pallas_call(
         kernel,
         out_shape=out_shape,
@@ -1746,8 +2217,8 @@
 def adam_update(weight, moment, second, gradient, rate, decay):
     moment_new = BETA_ONE * moment + (1.0 - BETA_ONE) * gradient
     second_new = BETA_TWO * second + (1.0 - BETA_TWO) * gradient * gradient
-    corrected = moment_new / (1.0 - BETA_ONE**ADAM_STEP)
-    corrected_sq = second_new / (1.0 - BETA_TWO**ADAM_STEP)
+    corrected = moment_new * (1.0 / (1.0 - BETA_ONE**ADAM_STEP))
+    corrected_sq = second_new * (1.0 / (1.0 - BETA_TWO**ADAM_STEP))
     weight_new = weight - rate * (corrected / (jnp.sqrt(corrected_sq) + ADAM_EPS) + decay * weight)
     return (weight_new, moment_new, second_new)
 
@@ -1821,6 +2292,49 @@
         compiler_params=pltpu.CompilerParams(vmem_limit_bytes=VMEM_LIMIT),
         name="adam_plain",
     )(clip, grad, weight, moment, second)
+
+
+def adam_few(sz, norms, small, stats, rates, head, shared):
+    state = 2 * NSTATE
+    pieces = sz.width // LANES
+    conv = (CONV + 1) * state
+    last = (CONV + 2) * HDIM
+
+    def kernel(norm_ref, small_ref, stats_ref, rates_ref, *refs):
+        ins, outs, (head_grad, shared_grad) = refs[:6], refs[6:12], refs[12:]
+        scale = norm_ref[1:2, 0:1]
+        lane = lax.broadcasted_iota(jnp.int32, (1, LANES), 1)
+        rate_grad = small_ref[8:9, :LANES] * rates_ref[...]
+        for head_at in range(sz.heads):
+            row = slice(head_at, head_at + 1)
+            cols = slice(head_at * HDIM, (head_at + 1) * HDIM)
+            for tap in range(CONV):
+                head_grad[row, tap * HDIM : (tap + 1) * HDIM] = small_ref[tap : tap + 1, cols]
+            head_grad[row, CONV * HDIM : (CONV + 1) * HDIM] = small_ref[5:6, cols]
+            head_grad[row, (CONV + 1) * HDIM : last] = small_ref[CONV : CONV + 1, cols]
+            head_grad[row, last : last + 1] = small_ref[7:8, head_at : head_at + 1]
+            head_grad[row, last + 1 : last + 2] = rate_grad[:, head_at : head_at + 1]
+            head_grad[row, last + 2 : last + 3] = jnp.sum(small_ref[6:7, cols], axis=1, keepdims=True)
+        for tap in range(CONV + 1):
+            for k in range(state // LANES):
+                to = tap * state + k * LANES
+                shared_grad[:, to : to + LANES] = stats_ref[k, tap + 1 : tap + 2, :]
+        for k in range(pieces):
+            shared_grad[:, conv + k * LANES : conv + (k + 1) * LANES] = stats_ref[k, 0:1, :]
+        for k, grad in enumerate((head_grad, shared_grad)):
+            new = adam_update(*(ref[...] for ref in ins[3 * k : 3 * k + 3]), scale * grad[...], LEARN_VECTOR, 0.0)
+            for ref, value in zip(outs[3 * k : 3 * k + 3], new):
+                ref[...] = value
+
+    arrays = list(head) + list(shared)
+    return pl.pallas_call(
+        kernel,
+        out_shape=[jax.ShapeDtypeStruct(array.shape, F32) for array in arrays],
+        in_specs=[VMEM_SPEC] * 10,
+        out_specs=[VMEM_SPEC] * 6,
+        scratch_shapes=[pltpu.VMEM(head[0].shape, F32), pltpu.VMEM(shared[0].shape, F32)],
+        name="adam_few",
+    )(norms, small, stats, rates, *arrays)
 
 
 def columns_first(array):
@@ -1847,59 +2361,46 @@
     shared_m,
     shared_v,
 ):
-    section = lax.axis_index("section")
-    head_idx = lax.axis_index("head")
     count = lax.axis_size("head")
     rows, width = inputs.shape[1], inputs.shape[2]
     heads = head_params.shape[1]
     tokens = rows * count
-    sz = Sizes(heads, tokens, width)
+    sz = Sizes(count, heads, tokens, width)
     order = sz.order()
-    start_block, seq_length, resets = seq_layout(
-        lax.dynamic_index_in_dim(valid_lengths, section, 0, keepdims=False)
+    own_in, own_out, lower_in, lower_out, pack, rates, first, cot, rows_zero = opening(
+        count, sz, columns_first(proj_in), proj_state[0], proj_out[0], head_params[0], shared_params, order,
+        inputs, cotangent, 0,
     )
-    token = head_idx * rows + lax.broadcasted_iota(jnp.int32, (rows, LANES), 0)
-    live = jnp.zeros((rows, LANES), F32)
-    for block in range(sz.blocks):
-        inside = (token // STRETCH == block) & (token - start_block[block] * STRETCH < seq_length[block])
-        live = jnp.where(inside, 1.0, live)
-    first = lax.dynamic_index_in_dim(inputs, section, 0, keepdims=False)
-    cot = lax.dynamic_index_in_dim(cotangent, section, 0, keepdims=False)
-    weights, weight_out, pack, rows_zero = opening(
-        count, sz, columns_first(proj_in), proj_state[0], proj_out[0], head_params[0], shared_params, order, first, 0
+
+    kept_zero = forward_phase(
+        count, sz, 0, valid_lengths, rows_zero, lower_in, lower_out, pack, first, None, (own_in, own_out), 1
     )
-
-    def run_forward(layer, gathered, residual, cotangent, collective_id):
-        return forward_phase(
-            count, sz, layer, resets, gathered, weights, weight_out, pack, residual, live, cotangent, collective_id
+    result_zero, branch_zero, total_zero, rows_one = kept_zero[:4]
+    upper_in, upper_out = kept_zero[7:]
+    kept_one = forward_phase(
+        count, sz, 1, valid_lengths, rows_one, upper_in, upper_out, pack, result_zero, cot, None, 2
+    )
+    result_one, out_grads_one, stats_one = kept_one[0], kept_one[3], kept_one[7]
+    back_one = backward_phase(
+        count, sz, 1, valid_lengths, out_grads_one, *kept_one[4:7], stats_one, upper_in, upper_out, pack, order,
+        result_zero, cot, (branch_zero, total_zero), rows_one, None, 3,
+    )
+    out_grads_zero, stats_zero = back_one[-2:]
+    grad_one, low_one, acc_one = back_one[:3]
+
+    def run_last(upper):
+        return backward_phase(
+            count, sz, 0, valid_lengths, out_grads_zero, *kept_zero[4:7], stats_zero, lower_in, lower_out, pack, order,
+            first, low_one, None, rows_zero, upper, 4,
         )
 
-    def run_backward(layer, out_grads, kept, stats, residual, upstream, below, upper, collective_id):
-        proj, mixed, states = kept[4:7]
-        return backward_phase(
-            count, sz, layer, resets, out_grads, proj, mixed, states, stats, weights, weight_out, pack, order,
-            residual, upstream, live, below, upper, collective_id,
-        )
-
-    kept_zero = run_forward(0, rows_zero, first, None, 1)
-    result_zero, branch_zero, total_zero, rows_one = kept_zero[:4]
-    kept_one = run_forward(1, rows_one, result_zero, cot, 2)
-    result_one, out_grads_one, stats_one = kept_one[0], kept_one[3], kept_one[7]
-    back_one = run_backward(
-        1, out_grads_one, kept_one, stats_one, result_zero, cot, (branch_zero, total_zero), None, 3
-    )
-    grad_one, low_one, acc_one, grads_t_one, scaled_one, out_grads_zero, stats_zero = back_one
-    upper = (
-        grads_t_one, scaled_one, rows_one, out_grads_one, rows_zero, acc_one, result_zero, result_one, grad_one
-    )
-    if tokens * width <= 4 << 20:
-        grad_in, grad_out, state_part, small, layer_outs, grad_buffer, squares = run_backward(
-            0, out_grads_zero, kept_zero, stats_zero, first, low_one, None, upper, 4
-        )
+    if fits(sz):
+        in_one, out_one, state_one = back_one[3:6]
+        upper = (rows_zero, in_one, out_one, acc_one, result_zero, result_one, grad_one, state_one, rates)
+        grad_in, grad_out, grad_state, small, layer_outs, grad_buffer, all_stats, norms = run_last(upper)
     else:
-        grad_zero, _, acc_zero, grads_t_zero, scaled_zero = run_backward(
-            0, out_grads_zero, kept_zero, stats_zero, first, low_one, None, None, 4
-        )
+        grads_t_one, scaled_one = back_one[3:5]
+        grad_zero, _, acc_zero, grads_t_zero, scaled_zero = run_last(None)
         lower = weight_grads(sz, grads_t_zero, rows_zero, scaled_zero, out_grads_zero)
         higher = weight_grads(sz, grads_t_one, rows_one, scaled_one, out_grads_one)
         grad_in, grad_out, state_sum, small, layer_outs, grad_buffer, squares = trade_sections(
@@ -1909,31 +2410,14 @@
             6,
         )
         state_part = state_sum.astype(BF16)
-
-    state_all, all_stats, norms = finish_sums(
-        count, sz, state_part.reshape(16 * count, -1), small, squares, pack, sz.head_sum(), 5
-    )
-    grad_state = state_all.reshape(state_part.shape)
-    pieces = width // LANES
-    shared_rows = all_stats[:pieces].transpose(1, 0, 2).reshape(8, width)
-    grad_shared = jnp.concatenate(
-        [shared_rows[1 : CONV + 2, : 2 * NSTATE].reshape(-1), shared_rows[0]]
-    )
-    grad_norm, clip_scale = norms[0, 0], norms[1, 0]
-    clip = norms[1, :1]
-    chans = heads * HDIM
-    head_part = head_params[0]
-    taps = small[:CONV, :chans].reshape(CONV, heads, HDIM).transpose(1, 0, 2).reshape(heads, -1)
-    grad_head = jnp.concatenate(
-        [
-            taps,
-            small[5, :chans].reshape(heads, HDIM),
-            small[CONV, :chans].reshape(heads, HDIM),
-            small[7, :heads][:, None],
-            (small[8, :heads] * -jnp.exp(head_part[:, -2]))[:, None],
-            jnp.sum(small[6, :chans].reshape(heads, HDIM), axis=1)[:, None],
-        ],
-        axis=1,
+        state_all, all_stats, norms = finish_sums(
+            count, sz, [state_part.reshape(16 * count, -1)], small, squares, rates, sz.head_sum(), 5
+        )
+        grad_state = state_all.reshape(state_part.shape)
+    grad_norm, clip = norms[0, 0], norms[1, :1]
+    few = adam_few(
+        sz, norms, small, all_stats, rates,
+        (head_params[0], head_m[0], head_v[0]), (shared_params, shared_m, shared_v),
     )
     new_in = adam_in(
         sz, clip, grad_in, columns_first(proj_in), columns_first(proj_in_m), columns_first(proj_in_v)
@@ -1943,12 +2427,6 @@
     )
     new_state = adam_plain(
         clip, grad_state, proj_state[0], proj_state_m[0], proj_state_v[0], True
-    )
-    new_head = adam_update(
-        head_part, head_m[0], head_v[0], clip_scale * grad_head, LEARN_VECTOR, 0.0
-    )
-    new_shared = adam_update(
-        shared_params[0], shared_m[0], shared_v[0], clip_scale * grad_shared, LEARN_VECTOR, 0.0
     )
     back_view = [jnp.transpose(array, (1, 2, 0)) for array in new_in[:3]]
     return (
@@ -1967,12 +2445,12 @@
         new_out[1][None],
         new_out[2][None],
         new_out[3][None],
-        new_head[0][None],
-        new_head[1][None],
-        new_head[2][None],
-        new_shared[0][None],
-        new_shared[1][None],
-        new_shared[2][None],
+        few[0][None],
+        few[1][None],
+        few[2][None],
+        few[3],
+        few[4],
+        few[5],
     )
 
 

time: 517 us -> 500 us (0.967)
  the two profiles are of different devices: /device:TPU:0 before, /device:TPU:13 now
where the time goes in v4:
time: 500 us; the launch traced here: 491 us
  Pallas kernels  487 us (97%)
    pallas_call x2, Pallas kernels, backward_phase(): pl.pallas_call(kernel, out_shape=out_shape, in_specs=in_specs, out_specs=...  229 us
    pallas_call x2, Pallas kernels, forward_phase(): pl.pallas_call(kernel, out_shape=out_shape, in_specs=in_specs, out_specs=...  169 us
    pallas_call x1, Pallas kernels, opening(): pl.pallas_call(kernel, out_shape=[w_shape, wo_shape, w_shape, wo_shape, j...  52.9 us
    pallas_call x2, Pallas kernels, adam_plain(): pl.pallas_call(kernel, grid=(rows // block,), out_shape=[shape, shape, sh...  18.1 us
    pallas_call x1, Pallas kernels, adam_in(): pl.pallas_call(kernel, grid=(sz.master_pad // block,), out_shape=[shape,...  16.8 us

profile of v4, /device:TPU:13, one launch (start us, length us, event | category | flops | bytes accessed | tf_op | source)
XLA Modules:
  0.0 491.3 jit_solution(10909756054201807755)
XLA Ops:
  0.7 52.9 %opening.1 = (bf16[896,2048]{1,0:T(8,128)(2,1)}, bf16[256,2048]{1,0:T(8,128)(2,1)}, bf16[896,2048]{1,0:T(8,128)(2,1)}, bf16[256,2048]{1,0:T(8,128)(2,1)}, f32[2,...) custom-call(f32[516,1,2048]{2,1,0:T(1,128)} %bitcast.33, ...), custom_call_target="tpu_custom_call" | custom-call | tf_op jit(solution)/shard_map/opening/pallas_call | solution.py:1070
  53.6 83.2 %forward_phase.2 = (bf16[64,2048]{1,0:T(8,128)(2,1)}, f32[64,2048]{1,0:T(8,128)}, f32[8,64]{1,0:T(8,128)}, bf16[1024,2048]{1,0:T(8,128)(2,1)}, f32[1024,896]{1,0...) custom-call(s32[2,4]{1,0:T(2,128)} %refs_0_.7, ...), custom_call_target="tpu_custom_call" | custom-call | tf_op jit(solution)/shard_map/forward_phase/pallas_call | solution.py:1553
  136.7 85.7 %forward_phase.3 = (bf16[64,2048]{1,0:T(8,128)(2,1)}, f32[64,2048]{1,0:T(8,128)}, f32[8,64]{1,0:T(8,128)}, bf16[1024,2048]{1,0:T(8,128)(2,1)}, f32[1024,896]{1,0...) custom-call(s32[2,4]{1,0:T(2,128)} %refs_0_.7, ...), custom_call_target="tpu_custom_call" | custom-call | tf_op jit(solution)/shard_map/forward_phase/pallas_call | solution.py:1553
  222.5 95.7 %backward_phase.1 = (f32[64,2048]{1,0:T(8,128)}, bf16[64,2048]{1,0:T(8,128)(2,1)}, f32[16,2048]{1,0:T(8,128)}, bf16[640,2048]{1,0:T(8,128)(2,1)}, bf16[256,2048]...) custom-call(s32[2,4]{1,0:T(2,128)} %refs_0_.7, ...), custom_call_target="tpu_custom_call" | custom-call | tf_op jit(solution)/shard_map/backward_phase/pallas_call | solution.py:2171
  318.2 132.8 %last_phase.1 = (f32[640,2048]{1,0:T(8,128)}, f32[256,2048]{1,0:T(8,128)}, bf16[256,2048]{1,0:T(8,128)(2,1)}, f32[16,2048]{1,0:T(8,128)}, bf16[2,64,2048]{2,1,0:...) custom-call(s32[2,4]{1,0:T(2,128)} %refs_0_.7, ...), custom_call_target="tpu_custom_call" | custom-call | tf_op jit(solution)/shard_map/last_phase/pallas_call | solution.py:2171
  451.1 1.3 fusion
  452.3 1.7 adam_few.1
  454.1 7.8 %adam_plain.3 = (f32[256,2048]{1,0:T(8,128)}, f32[256,2048]{1,0:T(8,128)}, f32[256,2048]{1,0:T(8,128)}, bf16[256,2048]{1,0:T(8,128)(2,1)}) custom-call(f32[1]{0:T(128)} %bitcast.7.clip_ref, f32[256,2048]{1,0:T(8,128)} %get-tuple-element.124.g_ref, f32[256,2048]{1,0:T(8,128)} %bitcast.36, f32[256,2048]{1,0:T(8,128)} %bitcast.41, f32[256,2048]{1,0:T(8,128)} %bitcast.42), custom_call_target="tpu_custom_call" | custom-call | tf_op jit(solution)/shard_map/adam_plain/pallas_call | solution.py:2284
  461.9 10.3 %adam_plain.2 = (f32[2048,256]{1,0:T(8,128)}, f32[2048,256]{1,0:T(8,128)}, f32[2048,256]{1,0:T(8,128)}, bf16[2048,256]{1,0:T(8,128)(2,1)}) custom-call(f32[1]{0:T(128)} %bitcast.7.clip_ref, bf16[256,2048]{1,0:T(8,128)(2,1)} %get-tuple-element.119.g_ref, f32[2048,256]{1,0:T(8,128)} %bitcast.38, f32[2048,256]{1,0:T(8,128)} %bitcast.43, f32[2048,256]{1,0:T(8,128)} %bitcast.44), custom_call_target="tpu_custom_call" | custom-call | tf_op jit(solution)/shard_map/adam_plain/pallas_call | solution.py:2284
  472.2 0.0 copy-start.1
  472.2 0.0 copy-start
  472.2 16.8 %adam_in.1 = (f32[516,1,2048]{2,1,0:T(1,128)}, f32[516,1,2048]{2,1,0:T(1,128)}, f32[516,1,2048]{2,1,0:T(1,128)}, bf16[516,2048]{1,0:T(8,128)(2,1)}) custom-call(f32[1]{0:T(128)} %bitcast.7.clip_ref, f32[640,2048]{1,0:T(8,128)} %get-tuple-element.114.g_ref, f32[516,1,2048]{2,1,0:T(1,128)} %bitcast.34, f32[516,1,2048]{2,1,0:T(1,128)} %bitcast.39, ...), custom_call_target="tpu_custom_call" | custom-call | tf_op jit(solution)/shard_map/adam_in/pallas_call | solution.py:2253
  489.0 0.0 copy-done.1
  489.0 0.8 copy.44
  489.8 0.0 copy-done
  489.8 1.0 copy.45
Async XLA Ops:
  472.2 16.8 %copy-start.1 = (bf16[2,64,2048]{2,1,0:T(8,128)(2,1)S(1)}, bf16[2,64,2048]{2,1,0:T(8,128)(2,1)}, u32[]{:S(2)}) copy-start(bf16[2,64,2048]{2,1,0:T(8,128)(2,1)} %get-tuple-element.111) | copy-start | bytes 1572868
  472.2 17.6 %copy-start = (f32[2,64,2048]{2,1,0:T(8,128)S(1)}, f32[2,64,2048]{2,1,0:T(8,128)}, u32[]{:S(2)}) copy-start(f32[2,64,2048]{2,1,0:T(8,128)} %get-tuple-element.112) | copy-start | bytes 3145732

commit v5 on v4

--- a/solution.py
+++ b/solution.py
@@ -933,7 +933,9 @@
         own_ref, in_ref, state_ref, out_ref, order_ref, low_ref, w_ref, wo_ref, zero_ref = take(9)
         ag_sems = take(3)
         load_sem, pack_send, pack_recv, swap_send, swap_recv, give_send, give_recv, local_sem = take(8)
+        relay_ref, relay_sem = take(2)
         section = lax.axis_index("section")
+        other = 1 - section
         micro = team.micro()
         loads = [
             pltpu.make_async_copy(src, dst, load_sem.at[k])
@@ -992,13 +994,35 @@
                 for copy in copies():
                     copy.start()
 
+        x = lax.axis_index("head") % 2
+        far = {"section": x, "head": lax.axis_index("head") // 2 * 2 + 1 - x}
+
+        def by_way():
+            return remote(wo_ref, relay_ref, relay_sem.at[0], relay_sem.at[1], {"section": other})
+
+        def on_from():
+            return remote(relay_ref, wos_ref, relay_sem.at[2], give_recv.at[3 * steps], far)
+
+        def matrix_near():
+            there = {"section": x}
+            return Delivery(wo_ref, wos_ref, give_send.at[3 * steps, 0], give_recv.at[3 * steps], there, section == x)
+
+        def pass_on():
+            @pl.when(section == 1)
+            def _():
+                by_way().wait_recv()
+                on_from().start()
+
         def low_out():
             loads[3].wait()
             if own_rows < sz.channels:
                 wo_ref[...] = jnp.zeros_like(wo_ref)
             wo_ref[:own_rows, :] = out_ref[...].astype(BF16)
             keeps[1].start()
-            lower(matrix)
+            if team.paired:
+                lower(lambda: [by_way(), matrix_near()])
+            else:
+                lower(matrix)
 
         def low_in(step):
             if step == 0:
@@ -1025,6 +1049,8 @@
         for step in range(ahead):
             low_in(step)
         if team.paired:
+            pass_on()
+        if team.paired:
             pl.when(jnp.logical_not(straight))(lambda: swaps[0].wait_recv())
 
         def got_pack(layer):
@@ -1057,9 +1083,15 @@
             for step in range(steps):
                 for copy in block(step):
                     copy.wait_sent()
-            for copy in matrix():
-                copy.wait_sent()
-
+            if team.paired:
+                matrix_near().wait_sent()
+                by_way().wait_send()
+            else:
+                for copy in matrix():
+                    copy.wait_sent()
+
+        if team.paired:
+            pl.when(section == 1)(lambda: on_from().wait_send())
         blank(local_sem.at[2]).wait()
         for copy in keeps:
             copy.wait()
@@ -1092,6 +1124,7 @@
         + gather_scratch(parts, team.dims, count)
         + [DMA((4,)), DMA((2,)), DMA((2,)), DMA((2,)), DMA((2,))]
         + [DMA((3 * steps + 1, 2)), DMA((3 * steps + 1,)), DMA((3,))]
+        + [pltpu.VMEM((sz.channels, width), BF16), DMA((3,))]
         + [pltpu.VMEM((16, width), F32)],
         compiler_params=params(collective_id),
         name="opening",
@@ -1257,6 +1290,15 @@
     )
 
 
+def exact(dot, ones, value, axis, ones_first=True):
+    ones = ones.astype(BF16)
+    high, low = split(value)
+    ones_axis = {(nn, True): 1, (nn, False): 0, (nt, True): 1, (nt, False): 1, (tn, True): 0}[dot, ones_first]
+    both = jnp.concatenate([ones, ones], axis=ones_axis)
+    halves_of = jnp.concatenate([high, low], axis=axis)
+    return dot(both, halves_of) if ones_first else dot(halves_of, both)
+
+
 def nt3(left, right):
     return fine(nt, left, right, 1, 1)
 
@@ -1298,7 +1340,7 @@
 def to_columns(tile, rows):
     row = lax.broadcasted_iota(jnp.int32, (rows, LANES), 0)
     lane = lax.broadcasted_iota(jnp.int32, (rows, LANES), 1)
-    return nt((row == lane).astype(F32), tile, HIGH)
+    return exact(nt, (row == lane).astype(F32), tile, 1)
 
 
 def forward_phase(
@@ -1425,7 +1467,7 @@
                     state_ref[...] = state_ref[...] * keep
                 s_ref[sub] = state_ref[...]
                 dt = step[span]
-                log_decay = nn(lower, decay[span], HIGH)
+                log_decay = exact(nn, lower, decay[span], 0)
                 flat = step_rows(log_decay, dt)
                 writer = act[span, chans : chans + NSTATE]
                 reader = act[span, chans + NSTATE :]
@@ -1450,7 +1492,7 @@
                     y_ref[span, cols] = total + pk_ref[6:7, cols] * x
             z = p_ref[:, :chans]
             gated = y_ref[...] * z * sigmoid(z)
-            square = nt(jnp.ones((8, chans), F32), gated * gated, HIGH)
+            square = exact(nt, jnp.ones((8, chans), F32), gated * gated, 1)
             for k in range(shards):
                 sq_ref[c * shards + k] = square[:, k * rows : (k + 1) * rows]
             high, low = split(gated * pk_ref[5:6, :chans])
@@ -1580,6 +1622,7 @@
     early = more and fits(sz)
     cols = 256
     steps = width // cols
+    ranges = steps
 
     def kernel(*refs):
         refs = list(refs)
@@ -1723,14 +1766,14 @@
             dz = dgated * y * zgate * (1.0 + z * (1.0 - zgate))
             x_all = act[:, :chans]
             acc_ref[6:7, :chans] += jnp.sum(dy * x_all, axis=0, keepdims=True)
-            scan_dot = nn(dy * (y - skip * x_all), sum_ref[...], HIGH)
+            scan_dot = exact(nn, sum_ref[...], dy * (y - skip * x_all), 1, False)
             mask = lower_mask(chunk)
             lower = mask.astype(F32)
             lane = lax.broadcasted_iota(jnp.int32, (chunk, LANES), 1)
             for sub in reversed(range(subs)):
                 span = slice(sub * chunk, (sub + 1) * chunk)
                 dt = step[span]
-                log_decay = nn(lower, decay[span], HIGH)
+                log_decay = exact(nn, lower, decay[span], 0)
                 flat = step_rows(log_decay, dt)
                 writer = act[span, chans : chans + NSTATE]
                 reader = act[span, chans + NSTATE :]
@@ -1776,15 +1819,15 @@
                     dact_ref[span, cols] = dx
                 dact_ref[span, chans : chans + NSTATE] = dwriter + tn3(cross_grad, reader)
                 dact_ref[span, chans + NSTATE :] = dreader + nn3(cross_grad, writer)
-                reach = nn(jnp.concatenate(reach, axis=1), sum_ref[...], HIGH)
-                carried = nn(jnp.concatenate(carried, axis=1), sum_ref[...], HIGH)
+                reach = exact(nn, sum_ref[...], jnp.concatenate(reach, axis=1), 1, False)
+                carried = exact(nn, sum_ref[...], jnp.broadcast_to(jnp.concatenate(carried, axis=1), (8, chans)), 1, False)[0:1]
                 direct = jnp.transpose(fall) + reach
                 given = dt * reach
                 dlog = scan_dot[span] - dt * direct
                 ends = jnp.sum(given, axis=0, keepdims=True) + carried
                 at_end = lax.broadcasted_iota(jnp.int32, (chunk, LANES), 0) == chunk - 1
                 dlog = dlog + jnp.where(at_end, ends, 0.0)
-                ddecay = tn(lower, dlog, HIGH)
+                ddecay = exact(tn, lower, dlog, 0)
                 ddt_ref[span, :] = direct + ddecay * rate
                 acc_ref[8:9, :LANES] += jnp.sum(ddecay * dt, axis=0, keepdims=True)
             dstate_ref[...] = dstate_ref[...] * keep
@@ -1812,6 +1855,11 @@
                 pl.when(i % per == per - 1)(
                     lambda: scatter.step(planes, i // per + 1, lambda k: planes - 1 - k)
                 )
+            if close:
+                share = -(-ranges // blocks)
+                for k in range(share):
+                    j = i * share + k
+                    pl.when(j < ranges)(lambda j=j: begin(1)(j))
             return carry
 
         def input_grads():
@@ -1875,7 +1923,6 @@
 
                 return action
 
-            each(begin(1))
             few = {}
             for layer_now, sources in (
                 (0, (acc_ref, result_own, grad_ref)), (1, (acc_upper, result_upper, grad_upper))

time: 500 us -> 497 us (level)
  no operation moved by 1% of the time
where the time goes in v5:
time: 497 us; the launch traced here: 489 us
  Pallas kernels  484 us (97%)
    pallas_call x2, Pallas kernels, backward_phase(): pl.pallas_call(kernel, out_shape=out_shape, in_specs=in_specs, out_specs=...  226 us
    pallas_call x2, Pallas kernels, forward_phase(): pl.pallas_call(kernel, out_shape=out_shape, in_specs=in_specs, out_specs=...  169 us
    pallas_call x1, Pallas kernels, opening(): pl.pallas_call(kernel, out_shape=[w_shape, wo_shape, w_shape, wo_shape, j...  52.9 us
    pallas_call x2, Pallas kernels, adam_plain(): pl.pallas_call(kernel, grid=(rows // block,), out_shape=[shape, shape, sh...  18.1 us
    pallas_call x1, Pallas kernels, adam_in(): pl.pallas_call(kernel, grid=(sz.master_pad // block,), out_shape=[shape,...  16.8 us

profile of v5, /device:TPU:13, one launch (start us, length us, event | category | flops | bytes accessed | tf_op | source)
XLA Modules:
  0.0 488.6 jit_solution(14870066583959665700)
XLA Ops:
  0.7 52.9 %opening.1 = (bf16[896,2048]{1,0:T(8,128)(2,1)}, bf16[256,2048]{1,0:T(8,128)(2,1)}, bf16[896,2048]{1,0:T(8,128)(2,1)}, bf16[256,2048]{1,0:T(8,128)(2,1)}, f32[2,...) custom-call(f32[516,1,2048]{2,1,0:T(1,128)} %bitcast.33, ...), custom_call_target="tpu_custom_call" | custom-call | tf_op jit(solution)/shard_map/opening/pallas_call | solution.py:1102
  53.6 81.3 %forward_phase.2 = (bf16[64,2048]{1,0:T(8,128)(2,1)}, f32[64,2048]{1,0:T(8,128)}, f32[8,64]{1,0:T(8,128)}, bf16[1024,2048]{1,0:T(8,128)(2,1)}, f32[1024,896]{1,0...) custom-call(s32[2,4]{1,0:T(2,128)} %refs_0_.7, ...), custom_call_target="tpu_custom_call" | custom-call | tf_op jit(solution)/shard_map/forward_phase/pallas_call | solution.py:1595
  134.9 87.5 %forward_phase.3 = (bf16[64,2048]{1,0:T(8,128)(2,1)}, f32[64,2048]{1,0:T(8,128)}, f32[8,64]{1,0:T(8,128)}, bf16[1024,2048]{1,0:T(8,128)(2,1)}, f32[1024,896]{1,0...) custom-call(s32[2,4]{1,0:T(2,128)} %refs_0_.7, ...), custom_call_target="tpu_custom_call" | custom-call | tf_op jit(solution)/shard_map/forward_phase/pallas_call | solution.py:1595
  222.4 93.0 %backward_phase.1 = (f32[64,2048]{1,0:T(8,128)}, bf16[64,2048]{1,0:T(8,128)(2,1)}, f32[16,2048]{1,0:T(8,128)}, bf16[640,2048]{1,0:T(8,128)(2,1)}, bf16[256,2048]...) custom-call(s32[2,4]{1,0:T(2,128)} %refs_0_.7, ...), custom_call_target="tpu_custom_call" | custom-call | tf_op jit(solution)/shard_map/backward_phase/pallas_call | solution.py:2218
  315.4 133.1 %last_phase.1 = (f32[640,2048]{1,0:T(8,128)}, f32[256,2048]{1,0:T(8,128)}, bf16[256,2048]{1,0:T(8,128)(2,1)}, f32[16,2048]{1,0:T(8,128)}, bf16[2,64,2048]{2,1,0:...) custom-call(s32[2,4]{1,0:T(2,128)} %refs_0_.7, ...), custom_call_target="tpu_custom_call" | custom-call | tf_op jit(solution)/shard_map/last_phase/pallas_call | solution.py:2218
  448.5 1.3 fusion
  449.8 1.7 adam_few.1
  451.5 7.8 %adam_plain.3 = (f32[256,2048]{1,0:T(8,128)}, f32[256,2048]{1,0:T(8,128)}, f32[256,2048]{1,0:T(8,128)}, bf16[256,2048]{1,0:T(8,128)(2,1)}) custom-call(f32[1]{0:T(128)} %bitcast.7.clip_ref, f32[256,2048]{1,0:T(8,128)} %get-tuple-element.124.g_ref, f32[256,2048]{1,0:T(8,128)} %bitcast.36, f32[256,2048]{1,0:T(8,128)} %bitcast.41, f32[256,2048]{1,0:T(8,128)} %bitcast.42), custom_call_target="tpu_custom_call" | custom-call | tf_op jit(solution)/shard_map/adam_plain/pallas_call | solution.py:2331
  459.3 10.3 %adam_plain.2 = (f32[2048,256]{1,0:T(8,128)}, f32[2048,256]{1,0:T(8,128)}, f32[2048,256]{1,0:T(8,128)}, bf16[2048,256]{1,0:T(8,128)(2,1)}) custom-call(f32[1]{0:T(128)} %bitcast.7.clip_ref, bf16[256,2048]{1,0:T(8,128)(2,1)} %get-tuple-element.119.g_ref, f32[2048,256]{1,0:T(8,128)} %bitcast.38, f32[2048,256]{1,0:T(8,128)} %bitcast.43, f32[2048,256]{1,0:T(8,128)} %bitcast.44), custom_call_target="tpu_custom_call" | custom-call | tf_op jit(solution)/shard_map/adam_plain/pallas_call | solution.py:2331
  469.6 0.0 copy-start.1
  469.6 0.0 copy-start
  469.6 16.8 %adam_in.1 = (f32[516,1,2048]{2,1,0:T(1,128)}, f32[516,1,2048]{2,1,0:T(1,128)}, f32[516,1,2048]{2,1,0:T(1,128)}, bf16[516,2048]{1,0:T(8,128)(2,1)}) custom-call(f32[1]{0:T(128)} %bitcast.7.clip_ref, f32[640,2048]{1,0:T(8,128)} %get-tuple-element.114.g_ref, f32[516,1,2048]{2,1,0:T(1,128)} %bitcast.34, f32[516,1,2048]{2,1,0:T(1,128)} %bitcast.39, ...), custom_call_target="tpu_custom_call" | custom-call | tf_op jit(solution)/shard_map/adam_in/pallas_call | solution.py:2300
  486.4 0.0 copy-done.1
  486.4 0.8 copy.44
  487.2 0.0 copy-done
  487.2 1.0 copy.45
Async XLA Ops:
  469.6 16.8 %copy-start.1 = (bf16[2,64,2048]{2,1,0:T(8,128)(2,1)S(1)}, bf16[2,64,2048]{2,1,0:T(8,128)(2,1)}, u32[]{:S(2)}) copy-start(bf16[2,64,2048]{2,1,0:T(8,128)(2,1)} %get-tuple-element.111) | copy-start | bytes 1572868
  469.6 17.6 %copy-start = (f32[2,64,2048]{2,1,0:T(8,128)S(1)}, f32[2,64,2048]{2,1,0:T(8,128)}, u32[]{:S(2)}) copy-start(f32[2,64,2048]{2,1,0:T(8,128)} %get-tuple-element.112) | copy-start | bytes 3145732

commit v6 on v5

--- a/solution.py
+++ b/solution.py
@@ -2310,7 +2310,7 @@
 
 def adam_plain(clip, grad, weight, moment, second, transposed):
     rows, width = weight.shape
-    block = min(256 if transposed else 64, rows)
+    block = min(512 if transposed else 64, rows)
 
     def kernel(clip_ref, g_ref, w_ref, m_ref, v_ref, wn_ref, mn_ref, vn_ref, low_ref):
         if transposed:

time: 497 us -> 495 us (level)
  no operation moved by 1% of the time
where the time goes in v6:
time: 495 us; the launch traced here: 486 us
  Pallas kernels  482 us (97%)
    pallas_call x2, Pallas kernels, backward_phase(): pl.pallas_call(kernel, out_shape=out_shape, in_specs=in_specs, out_specs=...  226 us
    pallas_call x2, Pallas kernels, forward_phase(): pl.pallas_call(kernel, out_shape=out_shape, in_specs=in_specs, out_specs=...  169 us
    pallas_call x1, Pallas kernels, opening(): pl.pallas_call(kernel, out_shape=[w_shape, wo_shape, w_shape, wo_shape, j...  52.9 us
    pallas_call x1, Pallas kernels, adam_in(): pl.pallas_call(kernel, grid=(sz.master_pad // block,), out_shape=[shape,...  16.8 us
    pallas_call x2, Pallas kernels, adam_plain(): pl.pallas_call(kernel, grid=(rows // block,), out_shape=[shape, shape, sh...  15.7 us

profile of v6, /device:TPU:13, one launch (start us, length us, event | category | flops | bytes accessed | tf_op | source)
XLA Modules:
  0.0 486.3 jit_solution(13547202196488552749)
XLA Ops:
  0.7 52.9 %opening.1 = (bf16[896,2048]{1,0:T(8,128)(2,1)}, bf16[256,2048]{1,0:T(8,128)(2,1)}, bf16[896,2048]{1,0:T(8,128)(2,1)}, bf16[256,2048]{1,0:T(8,128)(2,1)}, f32[2,...) custom-call(f32[516,1,2048]{2,1,0:T(1,128)} %bitcast.33, ...), custom_call_target="tpu_custom_call" | custom-call | tf_op jit(solution)/shard_map/opening/pallas_call | solution.py:1102
  53.6 81.3 %forward_phase.2 = (bf16[64,2048]{1,0:T(8,128)(2,1)}, f32[64,2048]{1,0:T(8,128)}, f32[8,64]{1,0:T(8,128)}, bf16[1024,2048]{1,0:T(8,128)(2,1)}, f32[1024,896]{1,0...) custom-call(s32[2,4]{1,0:T(2,128)} %refs_0_.7, ...), custom_call_target="tpu_custom_call" | custom-call | tf_op jit(solution)/shard_map/forward_phase/pallas_call | solution.py:1595
  134.9 87.5 %forward_phase.3 = (bf16[64,2048]{1,0:T(8,128)(2,1)}, f32[64,2048]{1,0:T(8,128)}, f32[8,64]{1,0:T(8,128)}, bf16[1024,2048]{1,0:T(8,128)(2,1)}, f32[1024,896]{1,0...) custom-call(s32[2,4]{1,0:T(2,128)} %refs_0_.7, ...), custom_call_target="tpu_custom_call" | custom-call | tf_op jit(solution)/shard_map/forward_phase/pallas_call | solution.py:1595
  222.4 93.0 %backward_phase.1 = (f32[64,2048]{1,0:T(8,128)}, bf16[64,2048]{1,0:T(8,128)(2,1)}, f32[16,2048]{1,0:T(8,128)}, bf16[640,2048]{1,0:T(8,128)(2,1)}, bf16[256,2048]...) custom-call(s32[2,4]{1,0:T(2,128)} %refs_0_.7, ...), custom_call_target="tpu_custom_call" | custom-call | tf_op jit(solution)/shard_map/backward_phase/pallas_call | solution.py:2218
  315.4 133.1 %last_phase.1 = (f32[640,2048]{1,0:T(8,128)}, f32[256,2048]{1,0:T(8,128)}, bf16[256,2048]{1,0:T(8,128)(2,1)}, f32[16,2048]{1,0:T(8,128)}, bf16[2,64,2048]{2,1,0:...) custom-call(s32[2,4]{1,0:T(2,128)} %refs_0_.7, ...), custom_call_target="tpu_custom_call" | custom-call | tf_op jit(solution)/shard_map/last_phase/pallas_call | solution.py:2218
  448.5 1.3 fusion
  449.8 1.7 adam_few.1
  451.5 7.8 %adam_plain.3 = (f32[256,2048]{1,0:T(8,128)}, f32[256,2048]{1,0:T(8,128)}, f32[256,2048]{1,0:T(8,128)}, bf16[256,2048]{1,0:T(8,128)(2,1)}) custom-call(f32[1]{0:T(128)} %bitcast.7.clip_ref, f32[256,2048]{1,0:T(8,128)} %get-tuple-element.124.g_ref, f32[256,2048]{1,0:T(8,128)} %bitcast.36, f32[256,2048]{1,0:T(8,128)} %bitcast.41, f32[256,2048]{1,0:T(8,128)} %bitcast.42), custom_call_target="tpu_custom_call" | custom-call | tf_op jit(solution)/shard_map/adam_plain/pallas_call | solution.py:2331
  459.3 7.9 %adam_plain.2 = (f32[2048,256]{1,0:T(8,128)}, f32[2048,256]{1,0:T(8,128)}, f32[2048,256]{1,0:T(8,128)}, bf16[2048,256]{1,0:T(8,128)(2,1)}) custom-call(f32[1]{0:T(128)} %bitcast.7.clip_ref, bf16[256,2048]{1,0:T(8,128)(2,1)} %get-tuple-element.119.g_ref, f32[2048,256]{1,0:T(8,128)} %bitcast.38, f32[2048,256]{1,0:T(8,128)} %bitcast.43, f32[2048,256]{1,0:T(8,128)} %bitcast.44), custom_call_target="tpu_custom_call" | custom-call | tf_op jit(solution)/shard_map/adam_plain/pallas_call | solution.py:2331
  467.2 0.0 copy-start.1
  467.2 0.0 copy-start
  467.3 16.8 %adam_in.1 = (f32[516,1,2048]{2,1,0:T(1,128)}, f32[516,1,2048]{2,1,0:T(1,128)}, f32[516,1,2048]{2,1,0:T(1,128)}, bf16[516,2048]{1,0:T(8,128)(2,1)}) custom-call(f32[1]{0:T(128)} %bitcast.7.clip_ref, f32[640,2048]{1,0:T(8,128)} %get-tuple-element.114.g_ref, f32[516,1,2048]{2,1,0:T(1,128)} %bitcast.34, f32[516,1,2048]{2,1,0:T(1,128)} %bitcast.39, ...), custom_call_target="tpu_custom_call" | custom-call | tf_op jit(solution)/shard_map/adam_in/pallas_call | solution.py:2300
  484.1 0.0 copy-done.1
  484.1 0.8 copy.44
  484.9 0.0 copy-done
  484.9 1.0 copy.45
Async XLA Ops:
  467.2 16.8 %copy-start.1 = (bf16[2,64,2048]{2,1,0:T(8,128)(2,1)S(1)}, bf16[2,64,2048]{2,1,0:T(8,128)(2,1)}, u32[]{:S(2)}) copy-start(bf16[2,64,2048]{2,1,0:T(8,128)(2,1)} %get-tuple-element.111) | copy-start | bytes 1572868
  467.2 17.6 %copy-start = (f32[2,64,2048]{2,1,0:T(8,128)S(1)}, f32[2,64,2048]{2,1,0:T(8,128)}, u32[]{:S(2)}) copy-start(f32[2,64,2048]{2,1,0:T(8,128)} %get-tuple-element.112) | copy-start | bytes 3145732
